TPU v7x, 32 devices: a whole 2x2x4 slice. The times are simulated.
32 devices in a mesh: group: 4 (over y, x), seq: 4 (over z), wshard: 2 (over core).
Axes of the slice: x: 2, y: 2, z: 4, core: 2. Of those that a mesh axis runs over, the one named last changes fastest.
Arguments:
- tokens: bfloat16 [6144, 2048], P(('group', 'seq', 'wshard')), may hold values from -6 to 6
- cotangent: bfloat16 [6144, 2048], P(('group', 'seq', 'wshard')), may hold values from -6 to 6
- dealing: int32 [6144], P(('group', 'seq', 'wshard')), may hold values from 0 to 3, as said below
- lengths: int32 [4, 2, 4], P('group', 'wshard'), may hold values from 1 to 624, as said below
- attn_gain: bfloat16 [2048], P(('seq', 'wshard')), may hold values from 0.5 to 1.5
- w_in: bfloat16 [2048, 12288], P(('seq', 'wshard')), may hold values from -0.125 to 0.125
- w_ab: bfloat16 [2048, 32], P(('seq', 'wshard')), may hold values from -0.125 to 0.125
- conv_w: bfloat16 [4, 8192], P(None, ('seq', 'wshard')), may hold values from -3 to 3
- decay_log: float32 [16], replicated, may hold values from -6 to 1
- dt_bias: float32 [16], replicated, may hold values from -5 to -1
- o_gain: bfloat16 [256], P(('seq', 'wshard')), may hold values from 0.5 to 1.5
- w_out: bfloat16 [4096, 2048], P(('seq', 'wshard')), may hold values from -0.09375 to 0.09375
- ffn_gain: bfloat16 [2048], P(('seq', 'wshard')), may hold values from 0.5 to 1.5
- w_gu: bfloat16 [2048, 11264], P(('seq', 'wshard')), may hold values from -0.125 to 0.125
- w_down: bfloat16 [5632, 2048], P(('seq', 'wshard')), may hold values from -0.078125 to 0.078125
Outputs:
- output: bfloat16 [6144, 2048], P(('group', 'seq', 'wshard'))
- input_grad: bfloat16 [6144, 2048], P(('group', 'seq', 'wshard'))
- grad_attn_gain: float32 [2048], P(('seq', 'wshard'))
- grad_w_in: float32 [2048, 12288], P(('seq', 'wshard'))
- grad_w_ab: float32 [2048, 32], P(('seq', 'wshard'))
- grad_conv_w: float32 [4, 8192], P(None, ('seq', 'wshard'))
- grad_decay_log: float32 [16], replicated
- grad_dt_bias: float32 [16], replicated
- grad_o_gain: float32 [256], P(('seq', 'wshard'))
- grad_w_out: float32 [4096, 2048], P(('seq', 'wshard'))
- grad_ffn_gain: float32 [2048], P(('seq', 'wshard'))
- grad_w_gu: float32 [2048, 11264], P(('seq', 'wshard'))
- grad_w_down: float32 [5632, 2048], P(('seq', 'wshard'))
Inputs may be any that keep to these rules, and one draw needn't show every extreme that they name: `dealing`: on every device each group index appears exactly 192 // 4 times. The lengths of a lane sum to 768 or less, the positions after them are padding; one length of each lane, at a place drawn from the seed, is at least 577, and the others are at most 48.
All inputs are finite; a program needn't handle non-finite values.
Results may differ from a plain program's by a relative error of at most 0.023.
The roundings to bfloat16 on the way count: a program that leaves them out, or rounds other values in their place, can miss the bound.
Values may be sent and summed in bfloat16 or wider, within the bound.
A program may use at most 576 MiB of HBM per device.

v0:
```python
import jax
import jax.numpy as jnp
from jax import lax
from jax.sharding import PartitionSpec as P

H = 16
DK = 128
DV = 256
FF = 5632
CONV = 4
SPAN = 64
HK = 2048
HV = 4096


mixer_precision = lax.Precision.HIGH
eps_norm = 1e-06


def passed_along(value, axis, steps):
    count = lax.axis_size(axis)
    first, last = (max(0, -steps), min(count, count - steps))
    return lax.ppermute(value, axis, [(source, source + steps) for source in range(first, last)])


def rms_scale(values, gain):
    return values * lax.rsqrt(jnp.mean(values * values, axis=-1, keepdims=True) + eps_norm) * gain


def unit_rows(values):
    return values * lax.rsqrt(jnp.sum(values * values, axis=-1, keepdims=True) + eps_norm)


def delta_block(carried, inputs):
    query_rows, key_rows, value_rows, beta_rows, decay_rows, start_rows = inputs
    width = query_rows.shape[0]
    counted = jnp.cumsum(start_rows)
    same_seq = counted[:, None] == counted[None, :]
    keeping = (counted == 0).astype(jnp.float32)
    cumulative = jnp.cumsum(decay_rows, axis=0)
    places = jnp.arange(width)
    lower_eq = (places[:, None] >= places[None, :]) & same_seq
    lower_st = (places[:, None] > places[None, :]) & same_seq
    spread = (cumulative[:, None, :] - cumulative[None, :, :]).transpose(2, 0, 1)
    weights_eq = jnp.where(lower_eq[None], jnp.exp(jnp.where(lower_eq[None], spread, 0.0)), 0.0)
    key_prod = jnp.einsum("ihd,jhd->hij", key_rows, key_rows, precision=mixer_precision)
    coupling = jnp.where(lower_st[None], beta_rows.T[:, :, None] * key_prod * weights_eq, 0.0)
    system = coupling + jnp.eye(width, dtype=jnp.float32)
    growth = jnp.exp(cumulative) * keeping[:, None]
    key_state = jnp.einsum("chd,hde->che", key_rows, carried, precision=mixer_precision)
    right_side = beta_rows[:, :, None] * (value_rows - growth[:, :, None] * key_state)
    solved = lax.linalg.triangular_solve(
        system, right_side.transpose(1, 0, 2), left_side=True, lower=True, unit_diagonal=True
    )
    mixing = (
        jnp.einsum("ihd,jhd->hij", query_rows, key_rows, precision=mixer_precision) * weights_eq
    )
    scale = query_rows.shape[2] ** (-0.5)
    outputs = growth[:, :, None] * jnp.einsum(
        "chd,hde->che", query_rows, carried, precision=mixer_precision
    )
    outputs = scale * (
        outputs + jnp.einsum("hij,hje->ihe", mixing, solved, precision=mixer_precision)
    )
    last_row = weights_eq[:, -1, :]
    new_carried = growth[-1][:, None, None] * carried + jnp.einsum(
        "hj,jhd,hje->hde", last_row, key_rows, solved, precision=mixer_precision
    )
    return (new_carried, outputs)


def local_mixer(query_rows, key_rows, value_rows, beta_rows, decay_rows, start_rows, carried):
    blocks = query_rows.shape[0] // SPAN

    def in_blocks(array):
        return array.reshape((blocks, SPAN) + array.shape[1:])

    final_state, outputs = lax.scan(
        delta_block,
        carried,
        (
            in_blocks(query_rows),
            in_blocks(key_rows),
            in_blocks(value_rows),
            in_blocks(beta_rows),
            in_blocks(decay_rows),
            in_blocks(start_rows),
        ),
    )
    return (outputs.reshape((blocks * SPAN,) + outputs.shape[2:]), final_state)


def short_conv(extended, conv_w, segment):
    rows_here = extended.shape[0] - (CONV - 1)
    own_seg = segment[CONV - 1 :]
    conv_sum = jnp.zeros((rows_here, extended.shape[1]), jnp.float32)
    for shift_by in range(CONV):
        begin = CONV - 1 - shift_by
        same = (segment[begin : begin + rows_here] == own_seg).astype(jnp.float32)
        conv_sum = conv_sum + conv_w[shift_by] * extended[begin : begin + rows_here] * same[:, None]
    return conv_sum


def mixer_inputs(extended, conv_w, segment):
    rows_here = extended.shape[0] - (CONV - 1)
    act = jax.nn.silu(short_conv(extended, conv_w, segment))
    queries = unit_rows(act[:, :HK].reshape(rows_here, H, DK))
    keys_all = unit_rows(act[:, HK : 2 * HK].reshape(rows_here, H, DK))
    values = act[:, 2 * HK :].reshape(rows_here, H, DV)
    return (queries, keys_all, values)


def decay_inputs(gates_ab, decay_log, dt_bias):
    beta_rows = jax.nn.sigmoid(gates_ab[:, H:])
    decay_rows = -jnp.exp(decay_log) * jax.nn.softplus(gates_ab[:, :H] + dt_bias)
    return (beta_rows, decay_rows)


def gated_norm(mixed, out_gate, gain):
    rows_here = mixed.shape[0]
    gated = rms_scale(mixed, gain) * jax.nn.silu(out_gate.reshape(mixed.shape))
    return gated.reshape(rows_here, -1)


def swiglu(gate_up):
    return jax.nn.silu(gate_up[:, :FF]) * gate_up[:, FF:]


def gather_weights(weights):
    return (
        lax.all_gather(weights[0], ("seq", "wshard"), axis=0, tiled=True),
        lax.all_gather(weights[1], ("seq", "wshard"), axis=0, tiled=True),
        lax.all_gather(weights[2], ("seq", "wshard"), axis=0, tiled=True),
        lax.all_gather(weights[3], ("seq", "wshard"), axis=1, tiled=True),
        lax.all_gather(weights[4], ("seq", "wshard"), axis=0, tiled=True),
        lax.all_gather(weights[5], ("seq", "wshard"), axis=0, tiled=True),
        lax.all_gather(weights[6], ("seq", "wshard"), axis=0, tiled=True),
        lax.all_gather(weights[7], ("seq", "wshard"), axis=0, tiled=True),
        lax.all_gather(weights[8], ("seq", "wshard"), axis=0, tiled=True),
    )


def segment_info(lane_lengths, seq_index, rows_here):
    ends = jnp.cumsum(lane_lengths)
    bounds = jnp.concatenate([jnp.zeros((1,), jnp.int32), ends])
    places = seq_index * rows_here + jnp.arange(-(CONV - 1), rows_here, dtype=jnp.int32)
    segment = jnp.sum((places[:, None] >= bounds[None, :]).astype(jnp.int32), axis=1)
    segment = jnp.where(places >= 0, segment, -1)
    own_places = places[CONV - 1 :]
    starts = jnp.any(own_places[:, None] == bounds[None, :], axis=1).astype(jnp.int32)
    valid = (own_places < ends[-1]).astype(jnp.float32)
    return (segment, starts, valid)


def chain_forward(transfer, offset, seq_count):

    def relay(step_index, carried_pair):
        incoming, leaving = carried_pair
        incoming = passed_along(leaving, "seq", 1)
        leaving = jnp.einsum("hij,hje->hie", transfer, incoming, precision=mixer_precision) + offset
        return (incoming, leaving)

    incoming, leaving = lax.fori_loop(0, seq_count - 1, relay, (jnp.zeros_like(offset), offset))
    return incoming


def chain_backward(transfer, local_grad, seq_count):

    def relay_back(step_index, carried_pair):
        leaving_grad, entering_grad = carried_pair
        leaving_grad = passed_along(entering_grad.astype(jnp.bfloat16), "seq", -1).astype(
            entering_grad.dtype
        )
        entering_grad = (
            jnp.einsum("hji,hje->hie", transfer, leaving_grad, precision=mixer_precision)
            + local_grad
        )
        return (leaving_grad, entering_grad)

    leaving_grad, entering_grad = lax.fori_loop(
        0, seq_count - 1, relay_back, (jnp.zeros_like(local_grad), local_grad)
    )
    return leaving_grad


def forward_pass(tokens_dst, lane_lengths, weights, decay_log, dt_bias):
    attn_gain, w_in, w_ab, conv_w, o_gain, w_out, ffn_gain, w_gu, w_down = weights
    rows_here = tokens_dst.shape[0]
    seq_count = lax.axis_size("seq")
    segment, starts, valid = segment_info(lane_lengths, lax.axis_index("seq"), rows_here)
    tokens_f = tokens_dst.astype(jnp.float32)
    normed = rms_scale(tokens_f, attn_gain.astype(jnp.float32)).astype(jnp.bfloat16)
    proj = jnp.dot(normed, w_in, preferred_element_type=jnp.float32)
    gates_ab = jnp.dot(normed, w_ab, preferred_element_type=jnp.float32)
    width_qkv = 2 * HK + HV
    conv_in = proj[:, :width_qkv].astype(jnp.bfloat16)
    out_gate = proj[:, width_qkv:]
    edge_rows = passed_along(conv_in[rows_here - (CONV - 1) :], "seq", 1)
    extended = jnp.concatenate([edge_rows, conv_in], axis=0).astype(jnp.float32)
    queries, keys_all, values = mixer_inputs(extended, conv_w.astype(jnp.float32), segment)
    query_rows = queries.astype(jnp.bfloat16).astype(jnp.float32)
    key_rows = keys_all.astype(jnp.bfloat16).astype(jnp.float32)
    value_rows = values.astype(jnp.bfloat16).astype(jnp.float32)
    beta_rows, decay_rows = decay_inputs(gates_ab, decay_log, dt_bias)
    value_aug = jnp.concatenate([value_rows, jnp.zeros((rows_here, H, DK), jnp.float32)], axis=2)
    eye_maps = jnp.broadcast_to(jnp.eye(DK, dtype=jnp.float32), (H, DK, DK))
    carried_aug = jnp.concatenate([jnp.zeros((H, DK, DV), jnp.float32), eye_maps], axis=2)
    outputs_aug, final_aug = local_mixer(
        query_rows, key_rows, value_aug, beta_rows, decay_rows, starts, carried_aug
    )
    base_out = outputs_aug[..., :DV]
    reach = outputs_aug[..., DV:]
    offset = final_aug[..., :DV]
    transfer = final_aug[..., DV:]
    incoming = chain_forward(transfer, offset, seq_count)
    mixed = (
        base_out + jnp.einsum("thd,hde->the", reach, incoming, precision=mixer_precision)
    ) * valid[:, None, None]
    gated = gated_norm(mixed, out_gate, o_gain.astype(jnp.float32)).astype(jnp.bfloat16)
    branch = jnp.dot(gated, w_out, preferred_element_type=jnp.float32)
    resid = tokens_f + branch
    normed2 = rms_scale(resid, ffn_gain.astype(jnp.float32)).astype(jnp.bfloat16)
    gate_up = jnp.dot(normed2, w_gu, preferred_element_type=jnp.float32)
    hidden = swiglu(gate_up).astype(jnp.bfloat16)
    output = (resid + jnp.dot(hidden, w_down, preferred_element_type=jnp.float32)).astype(
        jnp.bfloat16
    )
    saved = (
        tokens_f,
        normed,
        extended,
        segment,
        starts,
        valid,
        query_rows,
        key_rows,
        value_rows,
        beta_rows,
        decay_rows,
        gates_ab,
        reach,
        transfer,
        incoming,
        mixed,
        out_gate,
        gated,
        resid,
        normed2,
        gate_up,
        hidden,
    )
    return (output, saved)


def backward_pass(saved, weights, cot_dst, decay_log, dt_bias):
    attn_gain, w_in, w_ab, conv_w, o_gain, w_out, ffn_gain, w_gu, w_down = weights
    (
        tokens_f,
        normed,
        extended,
        segment,
        starts,
        valid,
        query_rows,
        key_rows,
        value_rows,
        beta_rows,
        decay_rows,
        gates_ab,
        reach,
        transfer,
        incoming,
        mixed,
        out_gate,
        gated,
        resid,
        normed2,
        gate_up,
        hidden,
    ) = saved
    rows_here = tokens_f.shape[0]
    seq_count = lax.axis_size("seq")
    cot_f = cot_dst.astype(jnp.float32)
    d_hidden = jnp.dot(cot_dst, w_down.T, preferred_element_type=jnp.float32)
    d_down = jnp.einsum("tf,td->fd", hidden, cot_dst, preferred_element_type=jnp.float32)
    value_ffn, pull_ffn = jax.vjp(swiglu, gate_up)
    d_gate_up = pull_ffn(d_hidden)[0].astype(jnp.bfloat16)
    grad_w_gu = lax.psum_scatter(
        jnp.einsum("tr,tf->rf", normed2, d_gate_up, preferred_element_type=jnp.float32).astype(
            jnp.bfloat16
        ),
        ("seq", "wshard"),
        scatter_dimension=0,
        tiled=True,
    )
    d_normed2 = jnp.dot(d_gate_up, w_gu.T, preferred_element_type=jnp.float32)
    value_norm2, pull_norm2 = jax.vjp(rms_scale, resid, ffn_gain.astype(jnp.float32))
    d_resid_norm, d_ffn_gain = pull_norm2(d_normed2)
    d_resid = cot_f + d_resid_norm
    grad_w_down, grad_ffn_gain = (
        lax.psum_scatter(
            d_down.astype(jnp.bfloat16), ("seq", "wshard"), scatter_dimension=0, tiled=True
        ).astype(jnp.float32),
        lax.psum_scatter(
            d_ffn_gain.astype(jnp.bfloat16), ("seq", "wshard"), scatter_dimension=0, tiled=True
        ).astype(jnp.float32),
    )
    d_branch = d_resid.astype(jnp.bfloat16)
    d_w_out = jnp.einsum("th,td->hd", gated, d_branch, preferred_element_type=jnp.float32)
    d_gated = jnp.dot(d_branch, w_out.T, preferred_element_type=jnp.float32)
    value_gate, pull_gate = jax.vjp(gated_norm, mixed, out_gate, o_gain.astype(jnp.float32))
    d_mixed, d_out_gate, d_o_gain = pull_gate(d_gated)
    d_mixed = d_mixed * valid[:, None, None]
    local_grad = jnp.einsum("thd,the->hde", reach, d_mixed, precision=mixer_precision)
    d_leaving = chain_backward(transfer, local_grad, seq_count)

    def mixer_part(query_in, key_in, value_in, beta_in, decay_in, carried):
        return local_mixer(query_in, key_in, value_in, beta_in, decay_in, starts, carried)

    value_mix, pull_mix = jax.vjp(
        mixer_part, query_rows, key_rows, value_rows, beta_rows, decay_rows, incoming
    )
    d_query, d_key, d_value, d_beta, d_decay, d_entering = pull_mix((d_mixed, d_leaving))

    def conv_part(extended_in, conv_in_w):
        return mixer_inputs(extended_in, conv_in_w, segment)

    value_conv, pull_conv = jax.vjp(conv_part, extended, conv_w.astype(jnp.float32))
    d_extended, d_conv_w = pull_conv((d_query, d_key, d_value))
    back_edge = passed_along(d_extended[: CONV - 1].astype(jnp.bfloat16), "seq", -1).astype(
        jnp.float32
    )
    d_conv_in = d_extended[CONV - 1 :] + jnp.pad(back_edge, ((rows_here - (CONV - 1), 0), (0, 0)))
    value_decay, pull_decay = jax.vjp(decay_inputs, gates_ab, decay_log, dt_bias)
    d_gates_ab, d_decay_log, d_dt_bias = pull_decay((d_beta, d_decay))
    d_proj = jnp.concatenate([d_conv_in, d_out_gate], axis=1).astype(jnp.bfloat16)
    d_ab = d_gates_ab.astype(jnp.bfloat16)
    d_w_in = jnp.einsum("td,tf->df", normed, d_proj, preferred_element_type=jnp.float32)
    d_w_ab = jnp.einsum("td,tf->df", normed, d_ab, preferred_element_type=jnp.float32)
    d_normed = jnp.dot(d_proj, w_in.T, preferred_element_type=jnp.float32) + jnp.dot(
        d_ab, w_ab.T, preferred_element_type=jnp.float32
    )
    value_norm, pull_norm = jax.vjp(rms_scale, tokens_f, attn_gain.astype(jnp.float32))
    d_tokens_norm, d_attn_gain = pull_norm(d_normed)
    d_tokens = d_resid + d_tokens_norm
    mixer_shards = (
        lax.psum_scatter(
            d_attn_gain.astype(jnp.bfloat16), ("seq", "wshard"), scatter_dimension=0, tiled=True
        ).astype(jnp.float32),
        lax.psum_scatter(
            d_w_in.astype(jnp.bfloat16), ("seq", "wshard"), scatter_dimension=0, tiled=True
        ).astype(jnp.float32),
        lax.psum_scatter(
            d_w_ab.astype(jnp.bfloat16), ("seq", "wshard"), scatter_dimension=0, tiled=True
        ).astype(jnp.float32),
        lax.psum_scatter(
            d_conv_w.astype(jnp.bfloat16), ("seq", "wshard"), scatter_dimension=1, tiled=True
        ).astype(jnp.float32),
        lax.psum_scatter(
            d_o_gain.astype(jnp.bfloat16), ("seq", "wshard"), scatter_dimension=0, tiled=True
        ).astype(jnp.float32),
        lax.psum_scatter(
            d_w_out.astype(jnp.bfloat16), ("seq", "wshard"), scatter_dimension=0, tiled=True
        ).astype(jnp.float32),
    )
    grad_decay_log, grad_dt_bias = lax.psum((d_decay_log, d_dt_bias), ("group", "seq", "wshard"))
    summed = (
        lax.psum(mixer_shards[0].astype(jnp.bfloat16), "group").astype(jnp.float32),
        lax.psum(mixer_shards[1].astype(jnp.bfloat16), "group").astype(jnp.float32),
        lax.psum(mixer_shards[2].astype(jnp.bfloat16), "group").astype(jnp.float32),
        lax.psum(mixer_shards[3].astype(jnp.bfloat16), "group").astype(jnp.float32),
        lax.psum(mixer_shards[4].astype(jnp.bfloat16), "group").astype(jnp.float32),
        lax.psum(mixer_shards[5].astype(jnp.bfloat16), "group").astype(jnp.float32),
        lax.psum(grad_ffn_gain.astype(jnp.bfloat16), "group").astype(jnp.float32),
        lax.psum(grad_w_gu, "group").astype(jnp.float32),
        lax.psum(grad_w_down.astype(jnp.bfloat16), "group").astype(jnp.float32),
    )
    grads = (
        summed[0],
        summed[1],
        summed[2],
        summed[3],
        grad_decay_log,
        grad_dt_bias,
        summed[4],
        summed[5],
        summed[6],
        summed[7],
        summed[8],
    )
    return (d_tokens, grads)


def shards(
    tokens,
    cotangent,
    dealing,
    lengths,
    attn_gain,
    w_in,
    w_ab,
    conv_w,
    decay_log,
    dt_bias,
    o_gain,
    w_out,
    ffn_gain,
    w_gu,
    w_down,
):
    sorting = jnp.argsort(dealing)
    tokens_dst, cot_dst = (
        lax.all_to_all(tokens[sorting], "group", split_axis=0, concat_axis=0, tiled=True),
        lax.all_to_all(cotangent[sorting], "group", split_axis=0, concat_axis=0, tiled=True),
    )
    lane_lengths = lengths.reshape(-1)
    shard_weights = (attn_gain, w_in, w_ab, conv_w, o_gain, w_out, ffn_gain, w_gu, w_down)
    weights = gather_weights(shard_weights)
    output, saved = forward_pass(tokens_dst, lane_lengths, weights, decay_log, dt_bias)
    weights_back = gather_weights(shard_weights)
    unused_output, saved = forward_pass(tokens_dst, lane_lengths, weights_back, decay_log, dt_bias)
    d_tokens, grads = backward_pass(saved, weights_back, cot_dst, decay_log, dt_bias)
    returned = (
        lax.all_to_all(output, "group", split_axis=0, concat_axis=0, tiled=True),
        lax.all_to_all(
            d_tokens.astype(jnp.bfloat16), "group", split_axis=0, concat_axis=0, tiled=True
        ),
    )
    inverse = jnp.argsort(sorting)
    return (returned[0][inverse], returned[1][inverse]) + grads


def solution(mesh):
    placed = (
        P(("group", "seq", "wshard"), None),
        P(("group", "seq", "wshard"), None),
        P(("group", "seq", "wshard")),
        P("group", "wshard", None),
        P(("seq", "wshard")),
        P(("seq", "wshard"), None),
        P(("seq", "wshard"), None),
        P(None, ("seq", "wshard")),
        P(),
        P(),
        P(("seq", "wshard")),
        P(("seq", "wshard"), None),
        P(("seq", "wshard")),
        P(("seq", "wshard"), None),
        P(("seq", "wshard"), None),
    )
    return jax.shard_map(
        shards,
        mesh=mesh,
        in_specs=placed,
        out_specs=(
            P(("group", "seq", "wshard"), None),
            P(("group", "seq", "wshard"), None),
            P(("seq", "wshard")),
            P(("seq", "wshard"), None),
            P(("seq", "wshard"), None),
            P(None, ("seq", "wshard")),
            P(),
            P(),
            P(("seq", "wshard")),
            P(("seq", "wshard"), None),
            P(("seq", "wshard")),
            P(("seq", "wshard"), None),
            P(("seq", "wshard"), None),
        ),
        check_vma=False,
    )
```

profile of v0, /device:TPU:0, one launch (start us, length us, event | category | flops | bytes accessed | tf_op | source)
XLA Modules:
  0.0 3278.4 jit_solution(5489503391643655986)
XLA Ops:
  162.3 279.3 %all-gather.7.cloned.1.call-done = bf16[2048,12288]{1,0:T(8,128)(2,1)} async-done(((bf16[256,12288]{1,0:T(8,128)(2,1)}), bf16[2048,12288]{1,0:T(8,128)(2,1)}) %all-gather.7.cloned.1.call-update) | async-done | bytes 50331664 | tf_op jit(solution)/shard_map/all_gather | solution.py:132
  502.2 302.7 %while.134 = (s32[]{:T(128)}, f32[16,128,384]{2,1,0:T(8,128)S(1)}, f32[3,64,16,384]{3,1,0,2:T(8,128)}, f32[3,64,16]{2,1,0:T(8,128)S(1)}, s32[3,64]{1,0:T(4,128)S...) while((s32[]{:T(128)}, f32[16,128,384]{2,1,0:T(8,128)S(1)}, ...), condition=%wide.region_10.12_spmd, body=%wide.region_7.11_spmd.sunk | while | flops 1464840320 | bytes 47208796 | solution.py:78
  512.1 80.0 %custom-call.61 = f32[16,1,64,64]{2,3,1,0:T(8,128)} custom-call(f32[16,1,64,64]{3,2,1,0:T(8,128)} %fusion.380), custom_call_target="InvertDiagBlocksLowerTriangular" | custom-call | tf_op jit(solution)/shard_map/while/body/eval_jaxpr/triangular_solve/custom-call.1 | solution.py:52
  613.4 80.0 %custom-call.61 = f32[16,1,64,64]{2,3,1,0:T(8,128)} custom-call(f32[16,1,64,64]{3,2,1,0:T(8,128)} %fusion.380), custom_call_target="InvertDiagBlocksLowerTriangular" | custom-call | tf_op jit(solution)/shard_map/while/body/eval_jaxpr/triangular_solve/custom-call.1 | solution.py:52
  713.9 80.0 %custom-call.61 = f32[16,1,64,64]{2,3,1,0:T(8,128)} custom-call(f32[16,1,64,64]{3,2,1,0:T(8,128)} %fusion.380), custom_call_target="InvertDiagBlocksLowerTriangular" | custom-call | tf_op jit(solution)/shard_map/while/body/eval_jaxpr/triangular_solve/custom-call.1 | solution.py:52
  815.2 352.0 %while.135 = (s32[]{:T(128)}, f32[16,128,256]{2,1,0:T(8,128)}, f32[16,128,256]{2,1,0:T(8,128)}, f32[16,128,128]{2,1,0:T(8,128)S(1)}, f32[16,128,256]{2,1,0:T(8,128)}, /*index=5*/s32[]{:T(128)}) while((s32[]{:T(128)}, f32[16,128,256]{2,1,0:T(8,128)}, f32[16,128,256]{2,1,0:T(8,128)}, f32[16,128,128]{2,1,0:T(8,128)S(1)}, ...), condition=%wide.region_12.14_spmd, body=%wide.region_11.13_spmd.sunk | while | flops 403177472 | bytes 24117384 | solution.py:163
  819.6 90.7 %collective-permute-done = f32[16,128,256]{2,1,0:T(8,128)S(1)} collective-permute-done((f32[16,128,256]{2,1,0:T(8,128)}, f32[16,128,256]{2,1,0:T(8,128)S(1)}, u32[]{:S(2)}, u32[]{:S(2)}) %collective-permute-start) | collective-permute-done | bytes 2097184 | tf_op jit(solution)/shard_map/while/body/eval_jaxpr/ppermute | solution.py:23
  915.2 51.9 %collective-permute-start = (f32[16,128,256]{2,1,0:T(8,128)}, f32[16,128,256]{2,1,0:T(8,128)S(1)}, u32[]{:S(2)}, u32[]{:S(2)}) collective-permute-start(f32[16,128,256]{2,1,0:T(8,128)} %get-tuple-element.3005), channel_id=1, source_target_pairs={{0,2},{2,4},{4,6},{1,3},{3,5},{5,7},{8,10},{10,12},{12,14},{9,11},... | collective-permute-start | bytes 6291464 | tf_op jit(solution)/shard_map/while/body/eval_jaxpr/ppermute | solution.py:23
  967.1 88.9 %collective-permute-done = f32[16,128,256]{2,1,0:T(8,128)S(1)} collective-permute-done((f32[16,128,256]{2,1,0:T(8,128)}, f32[16,128,256]{2,1,0:T(8,128)S(1)}, u32[]{:S(2)}, u32[]{:S(2)}) %collective-permute-start) | collective-permute-done | bytes 2097184 | tf_op jit(solution)/shard_map/while/body/eval_jaxpr/ppermute | solution.py:23
  1078.8 83.4 %collective-permute-done = f32[16,128,256]{2,1,0:T(8,128)S(1)} collective-permute-done((f32[16,128,256]{2,1,0:T(8,128)}, f32[16,128,256]{2,1,0:T(8,128)S(1)}, u32[]{:S(2)}, u32[]{:S(2)}) %collective-permute-start) | collective-permute-done | bytes 2097184 | tf_op jit(solution)/shard_map/while/body/eval_jaxpr/ppermute | solution.py:23
  1208.1 100.6 %all-gather.13.cloned.1.call-done = bf16[5632,2048]{1,0:T(8,128)(2,1)} async-done(((bf16[704,2048]{1,0:T(8,128)(2,1)}), bf16[5632,2048]{1,0:T(8,128)(2,1)}) %all-gather.13.cloned.1.call-update) | async-done | bytes 23068688 | tf_op jit(solution)/shard_map/all_gather | solution.py:139
  1437.6 328.4 %while.137 = (s32[]{:T(128)}, f32[16,128,256]{2,1,0:T(8,128)S(1)}, pred[3,16,64,64]{3,2,1,0:T(32,128)(4,1)}, f32[3,16,64,64]{3,2,1,0:T(8,128)}, f32[3,16,64,64]{...) while((s32[]{:T(128)}, f32[16,128,256]{2,1,0:T(8,128)S(1)}, ...), condition=%wide.region_23.25_spmd.clone, body=%wide.region_20.24_spmd.clone.sunk | while | flops 910013696 | bytes 44190532 | solution.py:78
  1453.2 80.0 %custom-call.62 = f32[16,1,64,64]{2,3,1,0:T(8,128)} custom-call(f32[16,1,64,64]{3,2,1,0:T(8,128)} %get-tuple-element.2895), custom_call_target="InvertDiagBlocksLowerTriangular" | custom-call | tf_op jit(solution)/shard_map/jvp()/while/body/eval_jaxpr/triangular_solve | solution.py:52
  1562.7 80.0 %custom-call.62 = f32[16,1,64,64]{2,3,1,0:T(8,128)} custom-call(f32[16,1,64,64]{3,2,1,0:T(8,128)} %get-tuple-element.2895), custom_call_target="InvertDiagBlocksLowerTriangular" | custom-call | tf_op jit(solution)/shard_map/jvp()/while/body/eval_jaxpr/triangular_solve | solution.py:52
  1672.1 80.0 %custom-call.62 = f32[16,1,64,64]{2,3,1,0:T(8,128)} custom-call(f32[16,1,64,64]{3,2,1,0:T(8,128)} %get-tuple-element.2895), custom_call_target="InvertDiagBlocksLowerTriangular" | custom-call | tf_op jit(solution)/shard_map/jvp()/while/body/eval_jaxpr/triangular_solve | solution.py:52
  1767.5 160.5 %while.136 = (s32[]{:T(128)}, f32[16,128,256]{2,1,0:T(8,128)}, bf16[16,128,256]{2,1,0:T(8,128)(2,1)}, f32[16,128,128]{1,2,0:T(8,128)}, f32[16,128,256]{2,1,0:T(8,128)}, /*index=5*/s32[]{:T(128)}) while((s32[]{:T(128)}, f32[16,128,256]{2,1,0:T(8,128)}, bf16[16,128,256]{2,1,0:T(8,128)(2,1)}, f32[16,128,128]{1,2,0:T(8,128)}, ...), condition=%wide.region_19.21_spmd, body=%wide.region_18.20_spmd.sunk | while | flops 404226048 | bytes 25165988 | solution.py:180
  1820.9 49.7 %collective-permute-done.1 = bf16[16,128,256]{2,1,0:T(8,128)(2,1)S(1)} collective-permute-done((bf16[16,128,256]{2,1,0:T(8,128)(2,1)}, bf16[16,128,256]{2,1,0:T(8,128)(2,1)S(1)}, u32[]{:S(2)}, u32[]{:S(2)}) %collective-permute-start.1) | collective-permute-done | bytes 1048608 | tf_op jit(solution)/shard_map/while/body/eval_jaxpr/ppermute | solution.py:23
  1875.4 49.3 %collective-permute-done.1 = bf16[16,128,256]{2,1,0:T(8,128)(2,1)S(1)} collective-permute-done((bf16[16,128,256]{2,1,0:T(8,128)(2,1)}, bf16[16,128,256]{2,1,0:T(8,128)(2,1)S(1)}, u32[]{:S(2)}, u32[]{:S(2)}) %collective-permute-start.1) | collective-permute-done | bytes 1048608 | tf_op jit(solution)/shard_map/while/body/eval_jaxpr/ppermute | solution.py:23
  1932.7 368.0 %while.138 = (s32[]{:T(128)}, f32[16,128,256]{2,1,0:T(8,128)S(1)}, f32[3,64,16,128]{3,2,1,0:T(8,128)}, f32[3,64,16,128]{3,2,1,0:T(8,128)}, f32[3,64,16,256]{3,2,...) while((s32[]{:T(128)}, f32[16,128,256]{2,1,0:T(8,128)S(1)}, ...), condition=%wide.region_33.35_spmd.clone, body=%wide.region_24.34_spmd.clone.sunk | while | flops 2074096640 | bytes 118558400 | solution.py:78
  1947.8 80.0 %custom-call.63 = f32[16,1,64,64]{2,3,1,0:T(8,128)} custom-call(f32[16,1,64,64]{3,2,1,0:T(8,128)} %add_bitcast_fusion.3), custom_call_target="InvertDiagBlocksLowerTriangular" | custom-call | tf_op jit(solution)/shard_map/transpose(jvp())/while/body/eval_jaxpr/triangular_solve | solution.py:52
  2070.4 80.0 %custom-call.63 = f32[16,1,64,64]{2,3,1,0:T(8,128)} custom-call(f32[16,1,64,64]{3,2,1,0:T(8,128)} %add_bitcast_fusion.3), custom_call_target="InvertDiagBlocksLowerTriangular" | custom-call | tf_op jit(solution)/shard_map/transpose(jvp())/while/body/eval_jaxpr/triangular_solve | solution.py:52
  2193.0 80.0 %custom-call.63 = f32[16,1,64,64]{2,3,1,0:T(8,128)} custom-call(f32[16,1,64,64]{3,2,1,0:T(8,128)} %add_bitcast_fusion.3), custom_call_target="InvertDiagBlocksLowerTriangular" | custom-call | tf_op jit(solution)/shard_map/transpose(jvp())/while/body/eval_jaxpr/triangular_solve | solution.py:52
  2380.2 481.9 %reduce-scatter.21.cloned.1.call-done = bf16[256,12288]{1,0:T(8,128)(2,1)} async-done(((bf16[2048,12288]{1,0:T(8,128)(2,1)}), bf16[256,12288]{1,0:T(8,128)(2,1)}) %reduce-scatter.21.cloned.1.call-update) | async-done | bytes 6291472
  3003.3 245.6 %all-reduce.32.cloned.1.call-done = (bf16[256,12288]{1,0:T(8,128)(2,1)}, bf16[512,2048]{1,0:T(8,128)(2,1)}, bf16[256,11264]{1,0:T(8,128)(2,1)}, bf16[704,2048]{1,0:T(8,128)(2,1)}) async-done(((bf16[256,12288]{1,0:T(8,128)(2,1)}, bf16[512,2048]{1,0:T(8,128)(2,1)}, bf16[256,11264]{1,0:T(8,128)(2,1)}, bf16[704,2048]{1,0:T(8,128)(2,1)}), (bf16[256,12288]{1,0:T(8,128)(2,1)}, bf16[512,2048]{1,0:T(8,128)(2,1)}, ...) | async-done | bytes 17039376 | tf_op jit(solution)/shard_map/psum | solution.py:369
  (807 shorter events, 1016.7 us)
Async XLA Ops:
  7.2 434.4 %all-gather.7.cloned.1.call-start = ((), (), s32[]{:S(2)}) async-start(), calls=%async_computation.10 | async-start | bytes 56623104 | tf_op jit(solution)/shard_map/all_gather | solution.py:132
  7.9 1166.9 %all-gather.9.cloned.1.call-start = ((), (), s32[]{:S(2)}) async-start(), calls=%async_computation.11 | async-start | bytes 18874368 | tf_op jit(solution)/shard_map/all_gather | solution.py:136
  8.7 1177.2 %all-gather.11.cloned.1.call-start = ((), (), s32[]{:S(2)}) async-start(), calls=%async_computation.12 | async-start | bytes 51904512 | tf_op jit(solution)/shard_map/all_gather | solution.py:138
  9.4 1299.3 %all-gather.13.cloned.1.call-start = ((), (), s32[]{:S(2)}) async-start(), calls=%async_computation.13 | async-start | bytes 25952256 | tf_op jit(solution)/shard_map/all_gather | solution.py:139
  15.4 105.3 %all-to-all-start = ((bf16[4,48,2048]{2,1,0:T(8,128)(2,1)}), bf16[4,48,2048]{2,1,0:T(8,128)(2,1)}, u32[]{:S(2)}, u32[]{:S(2)}) async-start(bf16[4,48,2048]{2,1,0:T(8,128)(2,1)} %bitcast.20), calls=%async_computation | async-start | bytes 1572864 | tf_op jit(solution)/shard_map/all_to_all | solution.py:413
  37.4 441.0 %copy-start.50 = (f32[1,8192]{1,0:T(1,128)}, f32[1,8192]{1,0:T(1,128)S(1)}, u32[]{:S(2)}) copy-start(f32[1,8192]{1,0:T(1,128)S(1)} %get-tuple-element.2347) | copy-start | bytes 98308
  120.7 1087.5 %all-to-all-start.2 = ((bf16[4,48,2048]{2,1,0:T(8,128)(2,1)}), bf16[4,48,2048]{2,1,0:T(8,128)(2,1)}, u32[]{:S(2)}, u32[]{:S(2)}) async-start(bf16[4,48,2048]{2,1,0:T(8,128)(2,1)} %bitcast.877), calls=%async_computation.2 | async-start | bytes 1572864 | tf_op jit(solution)/shard_map/all_to_all | solution.py:414
  158.1 2222.0 %reduce-scatter.15.cloned.1.call-start = ((), (), s32[]{:S(2)}) async-start(), calls=%async_computation.15 | async-start | bytes 18874368 | tf_op jit(solution)/shard_map/reduce_scatter | solution.py:362
  469.6 7.9 collective-permute-start.2
  815.3 95.0 %collective-permute-start = (f32[16,128,256]{2,1,0:T(8,128)}, f32[16,128,256]{2,1,0:T(8,128)S(1)}, u32[]{:S(2)}, u32[]{:S(2)}) collective-permute-start(f32[16,128,256]{2,1,0:T(8,128)} %get-tuple-element.3005), channel_id=1, source_target_pairs={{0,2},{2,4},{4,6},{1,3},{3,5},{5,7},{8,10},{10,12},{12,14},{9,11},... | collective-permute-start | bytes 6291464 | tf_op jit(solution)/shard_map/while/body/eval_jaxpr/ppermute | solution.py:23
  915.2 140.8 %collective-permute-start = (f32[16,128,256]{2,1,0:T(8,128)}, f32[16,128,256]{2,1,0:T(8,128)S(1)}, u32[]{:S(2)}, u32[]{:S(2)}) collective-permute-start(f32[16,128,256]{2,1,0:T(8,128)} %get-tuple-element.3005), channel_id=1, source_target_pairs={{0,2},{2,4},{4,6},{1,3},{3,5},{5,7},{8,10},{10,12},{12,14},{9,11},... | collective-permute-start | bytes 6291464 | tf_op jit(solution)/shard_map/while/body/eval_jaxpr/ppermute | solution.py:23
  1060.9 101.4 %collective-permute-start = (f32[16,128,256]{2,1,0:T(8,128)}, f32[16,128,256]{2,1,0:T(8,128)S(1)}, u32[]{:S(2)}, u32[]{:S(2)}) collective-permute-start(f32[16,128,256]{2,1,0:T(8,128)} %get-tuple-element.3005), channel_id=1, source_target_pairs={{0,2},{2,4},{4,6},{1,3},{3,5},{5,7},{8,10},{10,12},{12,14},{9,11},... | collective-permute-start | bytes 6291464 | tf_op jit(solution)/shard_map/while/body/eval_jaxpr/ppermute | solution.py:23
  1368.0 1012.2 %reduce-scatter.17.cloned.1.call-start = ((), (), s32[]{:S(2)}) async-start(), calls=%async_computation.16 | async-start | bytes 25952256 | tf_op jit(solution)/shard_map/reduce_scatter | solution.py:301
  1381.5 998.7 %reduce-scatter.23.cloned.1.call-start = ((), (), s32[]{:S(2)}) async-start(), calls=%async_computation.19 | async-start | bytes 51904512
  1403.9 1458.2 %reduce-scatter.21.cloned.1.call-start = ((), (), s32[]{:S(2)}) async-start(), calls=%async_computation.18 | async-start | bytes 56623104
  1767.5 48.7 %collective-permute-start.1 = (bf16[16,128,256]{2,1,0:T(8,128)(2,1)}, bf16[16,128,256]{2,1,0:T(8,128)(2,1)S(1)}, u32[]{:S(2)}, u32[]{:S(2)}) collective-permute-start(bf16[16,128,256]{2,1,0:T(8,128)(2,1)} %get-tuple-element.3023), channel_id=1, source_target_pairs={{2,0},{4,2},{6,4},{3,1},{5,3},{7,5},{10,8},{12,10},{14,12},{11,9},... | collective-permute-start | bytes 3145736 | tf_op jit(solution)/shard_map/while/body/eval_jaxpr/ppermute | solution.py:23
  1819.5 51.1 %collective-permute-start.1 = (bf16[16,128,256]{2,1,0:T(8,128)(2,1)}, bf16[16,128,256]{2,1,0:T(8,128)(2,1)S(1)}, u32[]{:S(2)}, u32[]{:S(2)}) collective-permute-start(bf16[16,128,256]{2,1,0:T(8,128)(2,1)} %get-tuple-element.3023), channel_id=1, source_target_pairs={{2,0},{4,2},{6,4},{3,1},{5,3},{7,5},{10,8},{12,10},{14,12},{11,9},... | collective-permute-start | bytes 3145736 | tf_op jit(solution)/shard_map/while/body/eval_jaxpr/ppermute | solution.py:23
  1874.0 50.7 %collective-permute-start.1 = (bf16[16,128,256]{2,1,0:T(8,128)(2,1)}, bf16[16,128,256]{2,1,0:T(8,128)(2,1)S(1)}, u32[]{:S(2)}, u32[]{:S(2)}) collective-permute-start(bf16[16,128,256]{2,1,0:T(8,128)(2,1)} %get-tuple-element.3023), channel_id=1, source_target_pairs={{2,0},{4,2},{6,4},{3,1},{5,3},{7,5},{10,8},{12,10},{14,12},{11,9},... | collective-permute-start | bytes 3145736 | tf_op jit(solution)/shard_map/while/body/eval_jaxpr/ppermute | solution.py:23
  2346.0 6.2 collective-permute-start.3
  2376.4 602.3 %reduce-scatter.19.cloned.1.call-start = ((), (), s32[]{:S(2)}) async-start(), calls=%async_computation.17 | async-start | bytes 2359296
  2378.8 600.9 %reduce-scatter.13.cloned.1.call-start = ((), (), s32[]{:S(2)}) async-start(), calls=%async_computation.14 | async-start | bytes 147456 | tf_op jit(solution)/shard_map/reduce_scatter | solution.py:353
  2379.8 869.1 %all-reduce.32.cloned.1.call-start = ((), (), s32[]{:S(2)}) async-start(), calls=%async_computation.20 | async-start | bytes 34078720 | tf_op jit(solution)/shard_map/psum | solution.py:369
  2877.5 37.7 %all-to-all-start.1 = ((bf16[4,48,2048]{2,1,0:T(8,128)(2,1)}), bf16[4,48,2048]{2,1,0:T(8,128)(2,1)S(1)}, u32[]{:S(2)}, u32[]{:S(2)}) async-start(bf16[4,48,2048]{2,1,0:T(8,128)(2,1)} %bitcast.35), calls=%async_computation.1 | async-start | bytes 1572864 | tf_op jit(solution)/shard_map/all_to_all | solution.py:424
  2915.1 86.2 %all-to-all-start.3 = ((bf16[4,48,2048]{2,1,0:T(8,128)(2,1)}), bf16[4,48,2048]{2,1,0:T(8,128)(2,1)S(1)}, u32[]{:S(2)}, u32[]{:S(2)}) async-start(bf16[4,48,2048]{2,1,0:T(8,128)(2,1)} %bitcast.43), calls=%async_computation.3 | async-start | bytes 1572864 | tf_op jit(solution)/shard_map/all_to_all | solution.py:425
  (130 other events, 5554.5 us)
Sparse Core Ops, SparseCore 0:
  9.7 431.8 all-gather.6
  443.2 149.2 all-gather.8
  594.1 476.3 all-gather.10
  1072.0 236.6 all-gather.12
  1368.1 173.9 reduce-scatter.14
  1544.3 225.7 reduce-scatter.16
  1772.4 506.6 reduce-scatter.22
  2376.5 485.5 reduce-scatter.20
  2865.0 34.1 reduce-scatter.18
  2901.8 28.7 reduce-scatter.12
  2935.1 313.7 all-reduce.31
where the time goes:
time: 3290 us; the launch traced here: 3280 us
  waiting for transfers between devices  1520 us (46%)
  other arithmetic  863 us (26%)
  matrix products  459 us (14%)
  blocking collectives  165 us (5%)
  starting transfers between devices  133 us (4%)
  local copies, waits for them, and re-layouts  115 us (3%)
    another operation x30, other arithmetic, delta_block(): lax.linalg.triangular_solve(system, right_side.transpose(1, 0, 2), left_s...  726 us
    unnamed x14, waiting for transfers between devices  485 us
    ppermute x8, waiting for transfers between devices, passed_along(): lax.ppermute(value, axis, [(source, source + steps) for source in range(f...  414 us
    all_gather x1, waiting for transfers between devices, gather_weights(): lax.all_gather(weights[1], ('seq', 'wshard'), axis=0, tiled=True)  279 us
    psum x1, waiting for transfers between devices, backward_pass(): lax.psum(mixer_shards[1].astype(jnp.bfloat16), 'group').astype(jnp.float32)  246 us
    all_gather x1, waiting for transfers between devices, gather_weights(): lax.all_gather(weights[8], ('seq', 'wshard'), axis=0, tiled=True)  101 us
    ppermute x8, starting transfers between devices, passed_along(): lax.ppermute(value, axis, [(source, source + steps) for source in range(f...  81.1 us
  transfers between devices with their start and end apart: 23, of which 11 were waited for; matrix products, arithmetic and copies ran while one was open for 41% of the time, Pallas kernels for 0%

commit v1 on v0

v1 whole, which is shorter than its diff:
```python
import functools

import jax
import jax.numpy as jnp
from jax import lax
from jax.experimental import pallas as pl
from jax.experimental.pallas import tpu as pltpu
from jax.sharding import PartitionSpec as P

H = 16
DK = 128
DV = 256
FF = 5632
CONV = 4
SPAN = 64
HK = 2048
HV = 4096
SIDE = 16

bf16 = jnp.bfloat16
f32 = jnp.float32
eps_norm = 1e-06


def mm(left, right, over=((1,), (0,))):
    return lax.dot_general(left, right, (over, ((), ())), preferred_element_type=f32)


def halves(value):
    high = value.astype(bf16)
    return high, (value - high.astype(f32)).astype(bf16)


def mm_right(left, right, over=((1,), (0,))):
    high, low = halves(right)
    return mm(left, high, over) + mm(left, low, over)


def mm_both(left, right, over=((1,), (0,))):
    left_high, left_low = halves(left)
    right_high, right_low = halves(right)
    return (
        mm(left_high, right_high, over)
        + mm(left_low, right_high, over)
        + mm(left_high, right_low, over)
    )


ROWS = ((1,), (1,))
COLS = ((0,), (0,))


def unit_lower_inverse(strict):
    parts = SPAN // 8
    places = lax.broadcasted_iota(jnp.int32, (8, SPAN), 0)
    columns = lax.broadcasted_iota(jnp.int32, (8, SPAN), 1)
    done = [(places + 8 * part == columns).astype(f32) for part in range(parts)]
    for row in range(SPAN - 1):
        first = row // 8
        line = done[first][row - 8 * first : row - 8 * first + 1, :]
        for part in range(first, parts):
            column = strict[8 * part : 8 * part + 8, row : row + 1]
            done[part] = done[part] - column * line
    return jnp.concatenate(done, axis=0)


def block_terms(head, heads, qkv, cols, rows):
    queries = qkv[:, head * DK : (head + 1) * DK]
    keys = qkv[:, (heads + head) * DK : (heads + head + 1) * DK]
    begin = 2 * heads * DK + head * DV
    values = qkv[:, begin : begin + DV]
    cum_c = cols[:, head : head + 1]
    beta_c = cols[:, heads + head : heads + head + 1]
    count_c = cols[:, 2 * heads : 2 * heads + 1]
    cum_r = rows[head : head + 1, :]
    count_r = rows[2 * heads : 2 * heads + 1, :]
    at_i = lax.broadcasted_iota(jnp.int32, (SPAN, SPAN), 0)
    at_j = lax.broadcasted_iota(jnp.int32, (SPAN, SPAN), 1)
    same = count_c == count_r
    lower_eq = same & (at_i >= at_j)
    lower_st = same & (at_i > at_j)
    fall = jnp.where(lower_eq, jnp.exp(jnp.where(lower_eq, cum_c - cum_r, 0.0)), 0.0)
    growth = jnp.where(count_c == 0.0, jnp.exp(cum_c), 0.0)
    last = SPAN - 1
    tail = jnp.where(
        count_c == count_c[last : last + 1, :], jnp.exp(cum_c[last : last + 1, :] - cum_c), 0.0
    )
    return queries, keys, values, beta_c, lower_st, fall, growth, tail, growth[last : last + 1, :]


def mixer_forward_kernel(heads, qkv_ref, cols_ref, rows_ref, mixed_ref, state_ref, inv_ref, solved_ref, carried):
    @pl.when(pl.program_id(0) == 0)
    def _():
        carried[...] = jnp.zeros_like(carried)

    qkv = qkv_ref[...]
    cols = cols_ref[...]
    rows = rows_ref[0]
    scale = DK ** (-0.5)
    for head in range(heads):
        queries, keys, values, beta_c, lower_st, fall, growth, tail, kept = block_terms(
            head, heads, qkv, cols, rows
        )
        state = carried[head]
        state_ref[0, head] = state
        key_prod = mm(keys, keys, ROWS)
        query_prod = mm(queries, keys, ROWS)
        strict = jnp.where(lower_st, beta_c * key_prod * fall, 0.0)
        inverse = unit_lower_inverse(strict)
        inv_ref[0, head] = inverse
        key_state = mm_right(keys, state)
        query_state = mm_right(queries, state)
        right_side = beta_c * (values.astype(f32) - growth * key_state)
        solved = mm_both(inverse, right_side)
        mixed = scale * (growth * query_state + mm_both(query_prod * fall, solved))
        mixed_ref[:, head * DV : (head + 1) * DV] = mixed
        solved_ref[:, head * DV : (head + 1) * DV] = solved
        carried[head] = kept * state + mm_both(tail * keys.astype(f32), solved, COLS)


def mixer_backward_kernel(
    heads, qkv_ref, cols_ref, rows_ref, state_ref, inv_ref, solved_ref, cot_ref, dqkv_ref, dcols_ref, carried
):
    @pl.when(pl.program_id(0) == 0)
    def _():
        carried[...] = jnp.zeros_like(carried)

    qkv = qkv_ref[...]
    cols = cols_ref[...]
    rows = rows_ref[0]
    scale = DK ** (-0.5)
    at_last = lax.broadcasted_iota(jnp.int32, (SPAN, 1), 0) == SPAN - 1
    d_betas, d_cums = [], []
    for head in range(heads):
        queries, keys, values, beta_c, lower_st, fall, growth, tail, kept = block_terms(
            head, heads, qkv, cols, rows
        )
        keys_f = keys.astype(f32)
        queries_f = queries.astype(f32)
        state = state_ref[0, head]
        inverse = inv_ref[0, head]
        solved = solved_ref[:, head * DV : (head + 1) * DV]
        d_mixed = scale * cot_ref[:, head * DV : (head + 1) * DV]
        d_state = carried[head]
        key_prod = mm(keys, keys, ROWS)
        query_prod = mm(queries, keys, ROWS)
        strict = jnp.where(lower_st, beta_c * key_prod * fall, 0.0)
        mixing = query_prod * fall
        key_state = mm_right(keys, state)
        query_state = mm_right(queries, state)
        d_solved = mm_both(mixing, d_mixed, COLS) + mm_both(tail * keys_f, d_state)
        d_right = mm_both(inverse, d_solved, COLS)
        d_mixing = mm_both(d_mixed, solved, ROWS)
        d_query_prod = d_mixing * fall
        d_strict = jnp.where(lower_st, -mm_both(d_right, solved, ROWS), 0.0)
        d_key_prod = d_strict * beta_c * fall
        d_key_state = -(beta_c * growth) * d_right
        d_query = mm_both(growth * d_mixed, state, ROWS) + mm_right(keys, d_query_prod, ((0,), (1,))).T
        both = d_key_prod + d_key_prod.T
        from_tail = mm_both(solved, d_state, ROWS)
        d_key = (
            mm_both(d_key_state, state, ROWS)
            + mm_both(both, keys_f)
            + mm_both(d_query_prod, queries_f, COLS)
            + tail * from_tail
        )
        residual = values.astype(f32) - growth * key_state
        d_betas.append(
            jnp.sum(d_right * residual, axis=1, keepdims=True)
            + jnp.sum(d_strict * key_prod * fall, axis=1, keepdims=True)
        )
        spread = d_strict * strict + d_mixing * mixing
        from_last = tail * jnp.sum(keys_f * from_tail, axis=1, keepdims=True)
        d_growth = jnp.sum(d_mixed * query_state, axis=1, keepdims=True) - beta_c * jnp.sum(
            d_right * key_state, axis=1, keepdims=True
        )
        at_end = jnp.sum(from_last, axis=0, keepdims=True) + kept * jnp.sum(
            jnp.sum(d_state * state, axis=1, keepdims=True), axis=0, keepdims=True
        )
        d_cums.append(
            jnp.sum(spread, axis=1, keepdims=True)
            - jnp.sum(spread.T, axis=1, keepdims=True)
            + growth * d_growth
            - from_last
            + jnp.where(at_last, at_end, 0.0)
        )
        dqkv_ref[:, head * DK : (head + 1) * DK] = d_query
        dqkv_ref[:, (heads + head) * DK : (heads + head + 1) * DK] = d_key
        begin = 2 * heads * DK + head * DV
        dqkv_ref[:, begin : begin + DV] = beta_c * d_right
        carried[head] = (
            kept * d_state
            + mm_both(growth * queries_f, d_mixed, COLS)
            + mm_right(keys, d_key_state, COLS)
        )
    dcols_ref[...] = jnp.concatenate(
        d_betas + d_cums + [jnp.zeros((SPAN, SIDE - 2 * heads), f32)], axis=1
    )


def side_arrays(beta_rows, decay_rows, starts):
    length, heads = beta_rows.shape
    blocks = length // SPAN
    lower = jnp.tril(jnp.ones((SPAN, SPAN), f32))
    running = jnp.einsum(
        "ij,bjh->bih", lower, decay_rows.reshape(blocks, SPAN, heads), precision=lax.Precision.HIGHEST
    )
    counted = jnp.einsum("ij,bj->bi", lower, starts.astype(f32).reshape(blocks, SPAN))
    cols = jnp.concatenate(
        [
            running,
            beta_rows.reshape(blocks, SPAN, heads),
            counted[..., None],
            jnp.zeros((blocks, SPAN, SIDE - 2 * heads - 1), f32),
        ],
        axis=2,
    )
    return cols.reshape(length, SIDE), cols.transpose(0, 2, 1)


def mixer_forward(qkv, cols, rows):
    length, width = qkv.shape
    heads = width // (2 * DK + DV)
    blocks = length // SPAN
    return pl.pallas_call(
        functools.partial(mixer_forward_kernel, heads),
        grid=(blocks,),
        in_specs=[
            pl.BlockSpec((SPAN, width), lambda i: (i, 0)),
            pl.BlockSpec((SPAN, SIDE), lambda i: (i, 0)),
            pl.BlockSpec((1, SIDE, SPAN), lambda i: (i, 0, 0)),
        ],
        out_specs=[
            pl.BlockSpec((SPAN, heads * DV), lambda i: (i, 0)),
            pl.BlockSpec((1, heads, DK, DV), lambda i: (i, 0, 0, 0)),
            pl.BlockSpec((1, heads, SPAN, SPAN), lambda i: (i, 0, 0, 0)),
            pl.BlockSpec((SPAN, heads * DV), lambda i: (i, 0)),
        ],
        out_shape=[
            jax.ShapeDtypeStruct((length, heads * DV), f32),
            jax.ShapeDtypeStruct((blocks, heads, DK, DV), f32),
            jax.ShapeDtypeStruct((blocks, heads, SPAN, SPAN), f32),
            jax.ShapeDtypeStruct((length, heads * DV), f32),
        ],
        scratch_shapes=[pltpu.VMEM((heads, DK, DV), f32)],
        compiler_params=pltpu.CompilerParams(vmem_limit_bytes=32 * 1024 * 1024),
        name="mixer_forward",
    )(qkv, cols, rows)


def mixer_backward(qkv, cols, rows, states, inverses, solved, d_mixed):
    length, width = qkv.shape
    heads = width // (2 * DK + DV)
    blocks = length // SPAN
    end = blocks - 1
    return pl.pallas_call(
        functools.partial(mixer_backward_kernel, heads),
        grid=(blocks,),
        in_specs=[
            pl.BlockSpec((SPAN, width), lambda i: (end - i, 0)),
            pl.BlockSpec((SPAN, SIDE), lambda i: (end - i, 0)),
            pl.BlockSpec((1, SIDE, SPAN), lambda i: (end - i, 0, 0)),
            pl.BlockSpec((1, heads, DK, DV), lambda i: (end - i, 0, 0, 0)),
            pl.BlockSpec((1, heads, SPAN, SPAN), lambda i: (end - i, 0, 0, 0)),
            pl.BlockSpec((SPAN, heads * DV), lambda i: (end - i, 0)),
            pl.BlockSpec((SPAN, heads * DV), lambda i: (end - i, 0)),
        ],
        out_specs=[
            pl.BlockSpec((SPAN, width), lambda i: (end - i, 0)),
            pl.BlockSpec((SPAN, SIDE), lambda i: (end - i, 0)),
        ],
        out_shape=[
            jax.ShapeDtypeStruct((length, width), f32),
            jax.ShapeDtypeStruct((length, SIDE), f32),
        ],
        scratch_shapes=[pltpu.VMEM((heads, DK, DV), f32)],
        compiler_params=pltpu.CompilerParams(vmem_limit_bytes=32 * 1024 * 1024),
        name="mixer_backward",
    )(qkv, cols, rows, states, inverses, solved, d_mixed)


def decay_back(d_cums):
    length, heads = d_cums.shape
    upper = jnp.triu(jnp.ones((SPAN, SPAN), f32))
    return jnp.einsum(
        "ij,bjh->bih",
        upper,
        d_cums.reshape(length // SPAN, SPAN, heads),
        precision=lax.Precision.HIGHEST,
    ).reshape(length, heads)


def rms_scale(values, gain):
    return values * lax.rsqrt(jnp.mean(values * values, axis=-1, keepdims=True) + eps_norm) * gain


def unit_rows(values):
    return values * lax.rsqrt(jnp.sum(values * values, axis=-1, keepdims=True) + eps_norm)


def short_conv(extended, conv_w, segment):
    rows_here = extended.shape[0] - (CONV - 1)
    own_seg = segment[CONV - 1 :]
    conv_sum = jnp.zeros((rows_here, extended.shape[1]), f32)
    for shift_by in range(CONV):
        begin = CONV - 1 - shift_by
        same = (segment[begin : begin + rows_here] == own_seg).astype(f32)
        conv_sum = conv_sum + conv_w[shift_by] * extended[begin : begin + rows_here] * same[:, None]
    return conv_sum


def mixer_inputs(heads, extended, conv_w, segment):
    rows_here = extended.shape[0] - (CONV - 1)
    act = jax.nn.silu(short_conv(extended, conv_w, segment))
    width = heads * DK
    queries = unit_rows(act[:, :width].reshape(rows_here, heads, DK)).reshape(rows_here, -1)
    keys_all = unit_rows(act[:, width : 2 * width].reshape(rows_here, heads, DK)).reshape(
        rows_here, -1
    )
    return jnp.concatenate([queries, keys_all, act[:, 2 * width :]], axis=1)


def decay_inputs(gates_ab, decay_log, dt_bias):
    heads = decay_log.shape[0]
    beta_rows = jax.nn.sigmoid(gates_ab[:, heads:])
    decay_rows = -jnp.exp(decay_log) * jax.nn.softplus(gates_ab[:, :heads] + dt_bias)
    return (beta_rows, decay_rows)


def gated_norm(mixed, out_gate, gain):
    rows_here = mixed.shape[0]
    per_head = mixed.reshape(rows_here, -1, DV)
    gated = rms_scale(per_head, gain) * jax.nn.silu(out_gate.reshape(per_head.shape))
    return gated.reshape(rows_here, -1)


def swiglu(gate_up):
    half = gate_up.shape[1] // 2
    return jax.nn.silu(gate_up[:, :half]) * gate_up[:, half:]


def dot(left, right):
    return jnp.dot(left, right, preferred_element_type=f32)


def dot_t(left, right):
    return lax.dot_general(left, right, (((0,), (0,)), ((), ())), preferred_element_type=f32)


def dot_back(left, right):
    return lax.dot_general(left, right, (((1,), (1,)), ((), ())), preferred_element_type=f32)


SHARDED = ("seq", "wshard")


class Place:
    def __init__(self, rows):
        self.group = lax.axis_size("group")
        self.seq = lax.axis_size("seq")
        self.cores = lax.axis_size("wshard")
        self.part = lax.axis_index("group")
        self.at_seq = lax.axis_index("seq")
        self.core = lax.axis_index("wshard")
        self.rows = rows
        self.per = rows // self.group
        self.subs = self.seq // self.group
        self.sources = self.seq // self.subs
        self.sub = self.at_seq % self.subs
        self.heads = H // self.group
        self.lane = self.seq * rows

    def deal(self, sorted_rows):
        width = sorted_rows.shape[1]
        if self.subs == 1:
            return lax.all_to_all(sorted_rows, "seq", split_axis=0, concat_axis=0, tiled=True)
        sent = jnp.zeros((self.group, self.subs, self.per, width), sorted_rows.dtype)
        sent = lax.dynamic_update_slice(
            sent,
            sorted_rows.reshape(self.group, 1, self.per, width),
            (0, self.at_seq // self.sources, 0, 0),
        )
        got = lax.all_to_all(
            sent.reshape(-1, width), "seq", split_axis=0, concat_axis=0, tiled=True
        )
        return lax.dynamic_slice(got, (self.sub * self.rows, 0), (self.rows, width))

    def undeal(self, rows):
        width = rows.shape[1]
        if self.subs == 1:
            return lax.all_to_all(rows, "seq", split_axis=0, concat_axis=0, tiled=True)
        sent = jnp.zeros((self.subs * self.rows, width), rows.dtype)
        sent = lax.dynamic_update_slice(sent, rows, (self.sub * self.rows, 0))
        got = lax.all_to_all(sent, "seq", split_axis=0, concat_axis=0, tiled=True)
        got = got.reshape(self.group, self.subs, self.per, width)
        got = lax.dynamic_slice(
            got, (0, self.at_seq // self.sources, 0, 0), (self.group, 1, self.per, width)
        )
        return got.reshape(self.rows, width)

    def swap(self, value, turn):
        if turn == 0:
            return value
        return lax.ppermute(value, "group", [(i, i ^ turn) for i in range(self.group)])

    def gather_any(self, rows):
        return jnp.concatenate([self.swap(rows, turn) for turn in range(self.group)], axis=0)

    def reduce_any(self, partial):
        total = partial[: self.rows]
        for turn in range(1, self.group):
            sent = partial[turn * self.rows : (turn + 1) * self.rows].astype(bf16)
            total = total + self.swap(sent, turn).astype(f32)
        return total

    def gather_places(self, rows):
        width = rows.shape[1]
        lane = jnp.zeros((self.sources, self.group, self.per, width), rows.dtype)
        for turn in range(self.group):
            got = self.swap(rows, turn).reshape(self.sources, 1, self.per, width)
            lane = lax.dynamic_update_slice(lane, got, (0, self.part ^ turn, 0, 0))
        return lane.reshape(-1, width)

    def reduce_places(self, partial):
        width = partial.shape[1]
        lane = partial.reshape(self.sources, self.group, self.per, width)
        total = None
        for turn in range(self.group):
            mine = lax.dynamic_slice(
                lane, (0, self.part ^ turn, 0, 0), (self.sources, 1, self.per, width)
            ).reshape(self.rows, width)
            if turn == 0:
                total = mine
            else:
                total = total + self.swap(mine.astype(bf16), turn).astype(f32)
        return total

    def gather_parts(self, value):
        parts = jnp.zeros((self.group,) + value.shape, value.dtype)
        for turn in range(self.group):
            parts = lax.dynamic_update_slice(
                parts, self.swap(value, turn)[None], (self.part ^ turn,) + (0,) * value.ndim
            )
        return parts

    def to_lane(self, rows):
        if self.subs == 1:
            return rows
        every = lax.all_gather(rows, "seq", axis=0, tiled=True)
        length = rows.shape[0] * self.subs
        return lax.dynamic_slice(
            every, ((self.at_seq // self.subs) * length, 0), (length, rows.shape[1])
        )

    def to_own(self, lane_rows):
        if self.subs == 1:
            return lane_rows
        length = lane_rows.shape[0] // self.subs
        return lax.dynamic_slice(lane_rows, (self.sub * length, 0), (length, lane_rows.shape[1]))

    def head_columns(self, array, sections):
        pieces = []
        for begin, width in sections:
            for turn in range(self.heads):
                pieces.append(
                    lax.dynamic_slice(
                        array,
                        (0, begin + (turn * self.group + self.part) * width),
                        (array.shape[0], width),
                    )
                )
        return jnp.concatenate(pieces, axis=1)

    def join_heads(self, parts, sections):
        group, rows = parts.shape[:2]
        out, begin = [], 0
        for _, width in sections:
            section = parts[:, :, begin : begin + self.heads * width]
            begin += self.heads * width
            section = section.reshape(group, rows, self.heads, width).transpose(1, 2, 0, 3)
            out.append(section.reshape(rows, self.heads * group * width))
        return jnp.concatenate(out, axis=1)

    def hidden_columns(self, array, unit_rows_here):
        rows = array.shape[0]
        blocks = self.seq * self.cores
        piece = unit_rows_here // self.group
        split = array.reshape(rows, 2 * blocks, self.group, piece)
        mine = lax.dynamic_slice(split, (0, 0, self.part, 0), (rows, 2 * blocks, 1, piece))
        return mine.reshape(rows, 2 * blocks * piece)

    def join_hidden(self, parts, unit_rows_here):
        group, rows = parts.shape[:2]
        blocks = self.seq * self.cores
        piece = unit_rows_here // group
        split = parts.reshape(group, rows, 2 * blocks, piece).transpose(1, 2, 0, 3)
        return split.reshape(rows, 2 * blocks * group * piece)

    def out_rows(self, w_out):
        width = w_out.shape[1]
        if self.subs == 1 and self.cores == 2:
            mine = lax.dynamic_slice(w_out, ((self.part % 2) * DV, 0), (DV, width))
            half = DV // 2
            kept = lax.dynamic_slice(mine, (self.core * half, 0), (half, width))
            other = lax.dynamic_slice(mine, ((1 - self.core) * half, 0), (half, width))
            got = lax.ppermute(other, "wshard", [(0, 1), (1, 0)])
            piece = jnp.where(self.core == self.part // 2, kept, got)
            return lax.all_gather(piece, SHARDED, axis=0, tiled=True)
        every = lax.all_gather(w_out, SHARDED, axis=0, tiled=True)
        every = every.reshape(self.heads, self.group, DV, width)
        return lax.dynamic_slice(
            every, (0, self.part, 0, 0), (self.heads, 1, DV, width)
        ).reshape(-1, width)

    def out_rows_back(self, grad):
        width = grad.shape[1]
        grad = grad.astype(bf16)
        if self.subs == 1 and self.cores == 2:
            half = lax.psum_scatter(grad, SHARDED, scatter_dimension=0, tiled=True)
            halves_all = self.gather_parts(half)
            here = lax.dynamic_slice(halves_all, (2 * self.core, 0, 0), (2, DV // 2, width))
            there = lax.dynamic_slice(halves_all, (2 - 2 * self.core, 0, 0), (2, DV // 2, width))
            got = lax.ppermute(there, "wshard", [(0, 1), (1, 0)])
            first = jnp.where(self.core == 0, here, got)
            second = jnp.where(self.core == 0, got, here)
            return jnp.stack([first, second], axis=1).reshape(2 * DV, width).astype(f32)
        every = jnp.zeros((self.heads, self.group, DV, width), bf16)
        every = lax.dynamic_update_slice(
            every, grad.reshape(self.heads, 1, DV, width), (0, self.part, 0, 0)
        )
        shard = lax.psum_scatter(every.reshape(-1, width), SHARDED, scatter_dimension=0, tiled=True)
        return lax.psum(shard, "group").astype(f32)


QKV = ((0, DK), (HK, DK), (2 * HK, DV))
GATE = ((2 * HK + HV, DV),)


def segment_info(lane_lengths, length):
    ends = jnp.cumsum(lane_lengths)
    bounds = jnp.concatenate([jnp.zeros((1,), jnp.int32), ends])
    places = jnp.arange(-(CONV - 1), length, dtype=jnp.int32)
    segment = jnp.sum((places[:, None] >= bounds[None, :]).astype(jnp.int32), axis=1)
    segment = jnp.where(places >= 0, segment, -1)
    own_places = places[CONV - 1 :]
    starts = jnp.any(own_places[:, None] == bounds[None, :], axis=1).astype(jnp.int32)
    valid = (own_places < ends[-1]).astype(f32)
    return (segment, starts, valid)


def shards(
    tokens,
    cotangent,
    dealing,
    lengths,
    attn_gain,
    w_in,
    w_ab,
    conv_w,
    decay_log,
    dt_bias,
    o_gain,
    w_out,
    ffn_gain,
    w_gu,
    w_down,
):
    rows, width = tokens.shape
    at = Place(rows)
    heads = at.heads
    device_rows = w_down.shape[0]
    devices = at.seq * at.cores

    small = (attn_gain, ffn_gain, o_gain, w_ab.reshape(-1), conv_w.reshape(-1))
    packed = lax.all_gather(jnp.concatenate(small), SHARDED, axis=0).reshape(devices, -1)
    full, begin = [], 0
    for array in small:
        full.append(packed[:, begin : begin + array.shape[0]])
        begin += array.shape[0]
    attn_f, ffn_f, o_f = (array.reshape(-1).astype(f32) for array in full[:3])
    ab_all = full[3].reshape(width, 2, heads, at.group)
    ab_mine = lax.dynamic_slice(ab_all, (0, 0, 0, at.part), (width, 2, heads, 1)).reshape(width, -1)
    conv_all = full[4].reshape(devices, CONV, -1).transpose(1, 0, 2).reshape(CONV, -1)
    conv_mine = at.head_columns(conv_all, QKV).astype(f32)

    def my_heads(values):
        return lax.dynamic_slice(values.reshape(heads, at.group), (0, at.part), (heads, 1)).reshape(-1)

    decay_mine, dt_mine = my_heads(decay_log), my_heads(dt_bias)

    in_qkv = lax.all_gather(at.head_columns(w_in, QKV), SHARDED, axis=0, tiled=True)
    in_gate = lax.all_gather(at.head_columns(w_in, GATE), SHARDED, axis=0, tiled=True)
    out_mine = at.out_rows(w_out)
    gu_mine = lax.all_gather(at.hidden_columns(w_gu, device_rows), SHARDED, axis=0, tiled=True)
    piece = device_rows // at.group
    down_mine = lax.all_gather(
        lax.dynamic_slice(w_down, (at.part * piece, 0), (piece, width)), SHARDED, axis=0, tiled=True
    )

    member = (dealing[:, None] == jnp.arange(at.group, dtype=jnp.int32)[None, :]).astype(jnp.int32)
    before = lax.dot_general(
        jnp.tril(jnp.ones((rows, rows), f32), -1).astype(bf16),
        member.astype(bf16),
        (((1,), (0,)), ((), ())),
        preferred_element_type=f32,
    ).astype(jnp.int32)
    target = jnp.sum((before + at.per * jnp.arange(at.group, dtype=jnp.int32)) * member, axis=1)
    sorting = (target[None, :] == jnp.arange(rows, dtype=jnp.int32)[:, None]).astype(bf16)
    dealt = at.deal(dot(sorting, jnp.concatenate([tokens, cotangent], axis=1)).astype(bf16))
    tokens_f = dealt[:, :width].astype(f32)
    cot_own = dealt[:, width:]
    cot_all = at.gather_any(cot_own)

    lane_lengths = lax.dynamic_index_in_dim(
        at.gather_parts(lengths.reshape(-1)), at.at_seq // at.subs, 0, keepdims=False
    )
    segment, starts, valid_lane = segment_info(lane_lengths, at.lane)
    valid = at.to_own(valid_lane[:, None])
    normed = rms_scale(tokens_f, attn_f).astype(bf16)
    normed_all = at.gather_places(normed)
    conv_in = dot(normed_all, in_qkv).astype(bf16)
    gates_ab = dot(normed_all, ab_mine)
    out_gate = dot(normed_all, in_gate)
    extended = jnp.pad(at.to_lane(conv_in), ((CONV - 1, 0), (0, 0))).astype(f32)
    qkv_f, pull_conv = jax.vjp(
        lambda extended_in, conv_in_w: mixer_inputs(heads, extended_in, conv_in_w, segment),
        extended,
        conv_mine,
    )
    qkv = qkv_f.astype(bf16)
    (beta_rows, decay_rows), pull_decay = jax.vjp(decay_inputs, gates_ab, decay_mine, dt_mine)
    cols, side_rows = side_arrays(at.to_lane(beta_rows), at.to_lane(decay_rows), starts)
    mixed_lane, states, inverses, solved = mixer_forward(qkv, cols, side_rows)
    mixed = at.to_own(mixed_lane) * valid
    gated_f, pull_gate = jax.vjp(gated_norm, mixed, out_gate, o_f)
    gated = gated_f.astype(bf16)
    branch = at.reduce_places(dot(gated, out_mine))
    resid = tokens_f + branch

    normed2_f, pull_norm2 = jax.vjp(rms_scale, resid, ffn_f)
    normed2_all = at.gather_any(normed2_f.astype(bf16))
    gate_up = dot(normed2_all, gu_mine)
    hidden_f, pull_ffn = jax.vjp(swiglu, gate_up)
    hidden = hidden_f.astype(bf16)
    output = (resid + at.reduce_any(dot(hidden, down_mine))).astype(bf16)

    d_hidden = dot_back(cot_all, down_mine)
    d_gate_up = pull_ffn(d_hidden)[0].astype(bf16)
    d_down = dot_t(hidden, cot_all)
    d_gu = dot_t(normed2_all, d_gate_up)
    d_normed2 = at.reduce_any(dot_back(d_gate_up, gu_mine))
    d_resid_norm, d_ffn_gain = pull_norm2(d_normed2)
    d_resid = cot_own.astype(f32) + d_resid_norm
    down_shard = lax.psum_scatter(d_down.astype(bf16), SHARDED, scatter_dimension=0, tiled=True)
    gu_shard = lax.psum_scatter(d_gu.astype(bf16), SHARDED, scatter_dimension=0, tiled=True)

    d_branch_all = at.gather_places(d_resid.astype(bf16))
    d_gated = dot_back(d_branch_all, out_mine)
    grad_w_out = at.out_rows_back(dot_t(gated, d_branch_all))
    d_mixed, d_out_gate, d_o_gain = pull_gate(d_gated)
    d_gate_cols = d_out_gate.astype(bf16)
    gate_shard = lax.psum_scatter(
        dot_t(normed_all, d_gate_cols).astype(bf16), SHARDED, scatter_dimension=0, tiled=True
    )
    d_qkv, d_cols = mixer_backward(
        qkv, cols, side_rows, states, inverses, solved, at.to_lane(d_mixed * valid)
    )
    d_beta = at.to_own(d_cols[:, :heads])
    d_decay = at.to_own(decay_back(d_cols[:, heads : 2 * heads]))
    d_extended, d_conv_w = pull_conv(d_qkv)
    d_conv_w = d_conv_w * (at.sub == 0).astype(f32)
    d_conv_in = at.to_own(d_extended[CONV - 1 :]).astype(bf16)
    d_gates_ab, d_decay_log, d_dt_bias = pull_decay((d_beta, d_decay))
    d_ab = d_gates_ab.astype(bf16)
    d_in = dot_t(normed_all, d_conv_in)
    d_w_ab = dot_t(normed_all, d_ab)
    d_normed = at.reduce_places(
        dot_back(d_conv_in, in_qkv) + dot_back(d_gate_cols, in_gate) + dot_back(d_ab, ab_mine)
    )
    value_norm, pull_norm = jax.vjp(rms_scale, tokens_f, attn_f)
    d_tokens_norm, d_attn_gain = pull_norm(d_normed)
    d_tokens = (d_resid + d_tokens_norm).astype(bf16)
    in_shard = lax.psum_scatter(d_in.astype(bf16), SHARDED, scatter_dimension=0, tiled=True)

    returned = at.undeal(jnp.concatenate([output, d_tokens], axis=1))
    returned = dot_t(sorting, returned).astype(bf16)

    grad_w_down = at.gather_parts(down_shard).reshape(device_rows, width).astype(f32)
    grad_w_gu = at.join_hidden(at.gather_parts(gu_shard), device_rows).astype(f32)
    grad_w_in = jnp.concatenate(
        [
            at.join_heads(at.gather_parts(in_shard), QKV),
            at.join_heads(at.gather_parts(gate_shard), GATE),
        ],
        axis=1,
    ).astype(f32)

    mine = (jnp.arange(at.group) == at.part).astype(f32)

    def own_columns(array, piece_width):
        count = array.shape[0]
        spread = array.reshape(count, heads, 1, piece_width) * mine[:, None]
        return spread.reshape(count, -1)

    conv_parts = [
        own_columns(d_conv_w[:, : heads * DK], DK),
        own_columns(d_conv_w[:, heads * DK : 2 * heads * DK], DK),
        own_columns(d_conv_w[:, 2 * heads * DK :], DV),
    ]
    totals = (
        d_attn_gain,
        d_ffn_gain,
        d_o_gain,
        jnp.concatenate(conv_parts, axis=1).reshape(-1),
        own_columns(d_w_ab.reshape(-1, heads), 1).reshape(-1),
        own_columns(d_decay_log[None], 1).reshape(-1),
        own_columns(d_dt_bias[None], 1).reshape(-1),
    )
    sizes = [array.shape[0] for array in totals]
    summed = lax.psum(jnp.concatenate(totals), ("group", "seq", "wshard"))
    parts, begin = [], 0
    for size in sizes:
        parts.append(summed[begin : begin + size])
        begin += size
    me = at.at_seq * at.cores + at.core

    def own_rows(array, axis=0):
        count = array.shape[axis] // devices
        return lax.dynamic_slice_in_dim(array, me * count, count, axis)

    return (
        returned[:, :width],
        returned[:, width:],
        own_rows(parts[0]),
        grad_w_in,
        own_rows(parts[4].reshape(width, 2 * H)),
        own_rows(parts[3].reshape(CONV, -1), 1),
        parts[5],
        parts[6],
        own_rows(parts[2]),
        grad_w_out,
        own_rows(parts[1]),
        grad_w_gu,
        grad_w_down,
    )


def solution(mesh):
    placed = (
        P(("group", "seq", "wshard"), None),
        P(("group", "seq", "wshard"), None),
        P(("group", "seq", "wshard")),
        P("group", "wshard", None),
        P(("seq", "wshard")),
        P(("seq", "wshard"), None),
        P(("seq", "wshard"), None),
        P(None, ("seq", "wshard")),
        P(),
        P(),
        P(("seq", "wshard")),
        P(("seq", "wshard"), None),
        P(("seq", "wshard")),
        P(("seq", "wshard"), None),
        P(("seq", "wshard"), None),
    )
    return jax.shard_map(
        shards,
        mesh=mesh,
        in_specs=placed,
        out_specs=(
            P(("group", "seq", "wshard"), None),
            P(("group", "seq", "wshard"), None),
            P(("seq", "wshard")),
            P(("seq", "wshard"), None),
            P(("seq", "wshard"), None),
            P(None, ("seq", "wshard")),
            P(),
            P(),
            P(("seq", "wshard")),
            P(("seq", "wshard"), None),
            P(("seq", "wshard")),
            P(("seq", "wshard"), None),
            P(("seq", "wshard"), None),
        ),
        check_vma=False,
    )
```

time: 3290 us -> 1450 us (0.44)
  waiting for transfers between devices: 1520 us -> 676 us
  other arithmetic: 863 us -> 145 us
  matrix products: 459 us -> 161 us
  blocking collectives: 165 us -> 0 us
  local copies, waits for them, and re-layouts: 115 us -> 277 us
  Pallas kernels: 0 us -> 95.9 us
  starting transfers between devices: 133 us -> 63.6 us
    another operation x67 -> x5, other arithmetic: 731 us -> 12.9 us  [the longest x30 726 us: delta_block(): lax.linalg.triangular_solve(system, right_side.transpose(1, 0, 2), left_s...]
    unnamed x14 -> x13, waiting for transfers between devices: 485 us -> 0.86 us
    all_gather x4 -> x5, waiting for transfers between devices: 380 us -> 39.8 us  [the longest x1 39.8 us: shards(): lax.all_gather(at.head_columns(w_in, QKV), SHARDED, axis=0, tiled=True)]
    dot_general x95 -> x24, matrix products: 418 us -> 161 us  [the longest x7 54 us: dot(): return jnp.dot(left, right, preferred_element_type=f32)]
    reduce_scatter x3 -> x5, waiting for transfers between devices: 0.05 us -> 222 us  [the longest x1 61.6 us: shards(): lax.psum_scatter(d_gu.astype(bf16), SHARDED, scatter_dimension=0, tiled=T...]
    psum x1, waiting for transfers between devices: 246 us -> 75 us  [shards(): summed = lax.psum(jnp.concatenate(totals), ('group', 'seq', 'wshard'))]
    ppermute x8 -> x44, waiting for transfers between devices: 414 us -> 301 us  [the longest x42 299 us: swap(): lax.ppermute(value, 'group', [(i, i ^ turn) for i in range(self.group)])]
    pallas_call x0 -> x2, Pallas kernels: none -> 95.9 us  [the longest x1 49.9 us: mixer_backward(): pl.pallas_call(functools.partial(mixer_backward_kernel, heads), grid=(blo...]
  transfers between devices with their start and end apart: 23 -> 58, of which waited for: 11 -> 32; matrix products, arithmetic and copies ran while one was open for 41% -> 26% of each run, Pallas kernels for 0% -> 3%
where the time goes in v1:
time: 1450 us; the launch traced here: 1440 us
  waiting for transfers between devices  676 us (47%)
  local copies, waits for them, and re-layouts  277 us (19%)
  matrix products  161 us (11%)
  other arithmetic  145 us (10%)
  Pallas kernels  95.9 us (7%)
  starting transfers between devices  63.6 us (4%)
  between operations  17.5 us (1%)
    ppermute x42, waiting for transfers between devices, swap(): lax.ppermute(value, 'group', [(i, i ^ turn) for i in range(self.group)])  299 us
    unnamed x275, local copies, waits for them, and re-layouts  79.8 us
    psum x1, waiting for transfers between devices, shards(): summed = lax.psum(jnp.concatenate(totals), ('group', 'seq', 'wshard'))  75 us
    reduce_scatter x1, waiting for transfers between devices, shards(): lax.psum_scatter(d_gu.astype(bf16), SHARDED, scatter_dimension=0, tiled=T...  61.6 us
    reduce_scatter x1, waiting for transfers between devices, shards(): lax.psum_scatter(d_in.astype(bf16), SHARDED, scatter_dimension=0, tiled=T...  58.2 us
    dot_general x7, matrix products, dot(): return jnp.dot(left, right, preferred_element_type=f32)  54 us
    dot_general x7, matrix products, dot_t(): lax.dot_general(left, right, (((0,), (0,)), ((), ())), preferred_element_...  53.3 us
    ppermute x42, starting transfers between devices, swap(): lax.ppermute(value, 'group', [(i, i ^ turn) for i in range(self.group)])  53 us
  transfers between devices with their start and end apart: 58, of which 32 were waited for; matrix products, arithmetic and copies ran while one was open for 26% of the time, Pallas kernels for 3%

profile of v1, /device:TPU:0, one launch (start us, length us, event | category | flops | bytes accessed | tf_op | source)
XLA Modules:
  0.0 1435.8 jit_solution(9306853353641268165)
XLA Ops:
  86.8 37.3 %all-to-all-done = bf16[4,48,4096]{2,1,0:T(8,128)(2,1)} async-done(((bf16[4,48,4096]{2,1,0:T(8,128)(2,1)}), bf16[4,48,4096]{2,1,0:T(8,128)(2,1)}, u32[]{:S(2)}, u32[]{:S(2)}) %all-to-all-start) | async-done | bytes 1572896 | tf_op jit(solution)/shard_map/all_to_all | solution.py:376
  180.8 39.8 %all-gather.7.cloned.1.call-done = bf16[2048,2048]{1,0:T(8,128)(2,1)} async-done(((bf16[256,2048]{1,0:T(8,128)(2,1)}), bf16[2048,2048]{1,0:T(8,128)(2,1)}) %all-gather.7.cloned.1.call-update) | async-done | bytes 8388624 | tf_op jit(solution)/shard_map/all_gather | solution.py:591
  258.2 46.0 %mixer_forward.1 = (f32[768,1024]{1,0:T(8,128)S(1)}, f32[12,4,128,256]{3,2,1,0:T(8,128)S(1)}, f32[12,4,64,64]{3,2,1,0:T(8,128)S(1)}, f32[768,1024]{1,0:T(8,128)S(1)}) custom-call(bf16[768,2048]{1,0:T(8,128)(2,1)S(1)} %pad_maximum_fusion.qkv_ref, f32[768,16]{1,0:T(8,128)S(1)} %maximum_maximum_fusion.cols_ref, f32[12,16,64]{2,1,0:T(8,128)S(1)} %copy-done.9), custom_call_target="tpu_custom_call" | custom-call | tf_op jit(solution)/shard_map/mixer_forward/pallas_call | solution.py:225
  354.0 17.6 %collective-permute-done.9 = bf16[192,2048]{1,0:T(8,128)(2,1)S(1)} collective-permute-done((bf16[192,2048]{1,0:T(8,128)(2,1)S(1)}, bf16[192,2048]{1,0:T(8,128)(2,1)S(1)}, u32[]{:S(2)}, u32[]{:S(2)}) %collective-permute-start.9) | collective-permute-done | bytes 786464 | tf_op jit(solution)/shard_map/ppermute | solution.py:404
  371.7 16.3 %collective-permute-done.8 = bf16[192,2048]{1,0:T(8,128)(2,1)S(1)} collective-permute-done((bf16[192,2048]{1,0:T(8,128)(2,1)S(1)}, bf16[192,2048]{1,0:T(8,128)(2,1)S(1)}, u32[]{:S(2)}, u32[]{:S(2)}) %collective-permute-start.8) | collective-permute-done | bytes 786464 | tf_op jit(solution)/shard_map/ppermute | solution.py:404
  414.3 15.5 %collective-permute-done.11 = bf16[192,2048]{1,0:T(8,128)(2,1)S(1)} collective-permute-done((bf16[192,2048]{1,0:T(8,128)(2,1)S(1)}, bf16[192,2048]{1,0:T(8,128)(2,1)S(1)}, u32[]{:S(2)}, u32[]{:S(2)}) %collective-permute-start.11) | collective-permute-done | bytes 786464 | tf_op jit(solution)/shard_map/ppermute | solution.py:404
  430.7 17.7 %fusion.43 = f32[768,2816]{1,0:T(8,128)} fusion(bf16[2048,2816]{0,1:T(8,128)(2,1)} %all-gather.13.cloned.1.call-done, bf16[192,2048]{1,0:T(8,128)(2,1)} %copy-done.110, bf16[192,2048]{1,0:T(8,128)(2,1)} %copy-done.112, bf16[192,2048]{1,0:T(8,128)(2,1)} %collective-permute-done.10, bf16[192,2048]{1,0:T(8,128)(2,1)} %copy-done.43), kind=kOutput, calls=%fused_computation.136 | convolution fusion | flops 8870952960 | bytes 23330816 | tf_op jit(solution)/shard_map/dot_general | solution.py:343
  476.6 15.4 %fusion.108 = (bf16[768,2048]{1,0:T(8,128)(2,1)S(1)}, f32[768,2048]{1,0:T(8,128)S(1)}) fusion(bf16[2048,2816]{0,1:T(8,128)(2,1)} %all-gather.13.cloned.1.call-done, f32[768,1408]{1,0:T(8,128)} %get-tuple-element.120, f32[768,1408]{1,0:T(8,128)} %get-tuple-element.119), kind=kOutput, calls=%fused_computation.334 | convolution fusion | flops 8864268288 | bytes 29622272 | tf_op jit(solution)/shard_map/dot_general | solution.py:351
  514.9 15.6 %collective-permute-done.20 = bf16[192,2048]{1,0:T(8,128)(2,1)S(1)} collective-permute-done((bf16[192,2048]{1,0:T(8,128)(2,1)S(1)}, bf16[192,2048]{1,0:T(8,128)(2,1)S(1)}, u32[]{:S(2)}, u32[]{:S(2)}) %collective-permute-start.20) | collective-permute-done | bytes 786464 | tf_op jit(solution)/shard_map/ppermute | solution.py:404
  530.5 16.8 %collective-permute-done.15 = bf16[192,2048]{1,0:T(8,128)(2,1)S(1)} collective-permute-done((bf16[192,2048]{1,0:T(8,128)(2,1)S(1)}, bf16[192,2048]{1,0:T(8,128)(2,1)S(1)}, u32[]{:S(2)}, u32[]{:S(2)}) %collective-permute-start.15) | collective-permute-done | bytes 786464 | tf_op jit(solution)/shard_map/ppermute | solution.py:404
  547.4 15.4 %collective-permute-done.14 = bf16[192,2048]{1,0:T(8,128)(2,1)S(1)} collective-permute-done((bf16[192,2048]{1,0:T(8,128)(2,1)S(1)}, bf16[192,2048]{1,0:T(8,128)(2,1)S(1)}, u32[]{:S(2)}, u32[]{:S(2)}) %collective-permute-start.14) | collective-permute-done | bytes 786464 | tf_op jit(solution)/shard_map/ppermute | solution.py:404
  573.7 15.2 %collective-permute-done.22 = bf16[192,2048]{1,0:T(8,128)(2,1)S(1)} collective-permute-done((bf16[192,2048]{1,0:T(8,128)(2,1)S(1)}, bf16[192,2048]{1,0:T(8,128)(2,1)S(1)}, u32[]{:S(2)}, u32[]{:S(2)}) %collective-permute-start.22) | collective-permute-done | bytes 786464 | tf_op jit(solution)/shard_map/ppermute | solution.py:404
  588.9 16.9 %collective-permute-done.23 = bf16[192,2048]{1,0:T(8,128)(2,1)S(1)} collective-permute-done((bf16[192,2048]{1,0:T(8,128)(2,1)S(1)}, bf16[192,2048]{1,0:T(8,128)(2,1)S(1)}, u32[]{:S(2)}, u32[]{:S(2)}) %collective-permute-start.23) | collective-permute-done | bytes 786464 | tf_op jit(solution)/shard_map/ppermute | solution.py:404
  622.6 49.9 %mixer_backward.1 = (f32[768,2048]{1,0:T(8,128)}, f32[768,16]{1,0:T(8,128)S(1)}) custom-call(bf16[768,2048]{1,0:T(8,128)(2,1)S(1)} %pad_maximum_fusion.qkv_ref, f32[768,16]{1,0:T(8,128)S(1)} %maximum_maximum_fusion.cols_ref, f32[12,16,64]{2,1,0:T(8,128)S(1)} %copy-done.10, f32[12,4,128,256]{3,2,1,0:T(8,128)} %copy-done.2, f32[12,4,64,64]{3,2,1,0:T(8,128)S(1)} %copy-done.6, ...), custom_call_target="tpu_custom_call" | custom-call | tf_op jit(solution)/shard_map/mixer_backward/pallas_call | solution.py:256
  844.5 15.7 %convolution_convert_fusion = bf16[2048,2816]{1,0:T(8,128)(2,1)} fusion(f32[768,1408]{1,0:T(8,128)} %get-tuple-element.120, f32[768,1408]{1,0:T(8,128)} %get-tuple-element.119, bf16[192,2048]{1,0:T(8,128)(2,1)S(1)} %copy-done.111, bf16[192,2048]{1,0:T(8,128)(2,1)S(1)} %copy-done.113, bf16[192,2048]{1,0:T(8,128)(2,1)} %collective-permute-done.10, ...), kind=kOutput, calls=%fused_computation.1 | convolution fusion | flops 8881045504 | bytes 23330816 | tf_op jit(solution)/shard_map/dot_general | solution.py:347
  870.2 75.0 %all-reduce.20.cloned.1.call-done = f32[102688]{0:T(1024)} async-done(((f32[102688]{0:T(1024)}), f32[102688]{0:T(1024)}) %all-reduce.20.cloned.1.call-update) | async-done | bytes 410768 | tf_op jit(solution)/shard_map/psum | solution.py:720
  953.3 45.2 %reduce-scatter.10.cloned.1.call-done = bf16[128,2048]{1,0:T(8,128)(2,1)} async-done(((bf16[1024,2048]{1,0:T(8,128)(2,1)}), bf16[128,2048]{1,0:T(8,128)(2,1)}) %reduce-scatter.10.cloned.1.call-update) | async-done | bytes 524304 | tf_op jit(solution)/shard_map/reduce_scatter | solution.py:519
  1000.6 48.9 %reduce-scatter.8.cloned.1.call-done = bf16[256,1024]{1,0:T(8,128)(2,1)} async-done(((bf16[2048,1024]{1,0:T(8,128)(2,1)}), bf16[256,1024]{1,0:T(8,128)(2,1)}) %reduce-scatter.8.cloned.1.call-update) | async-done | bytes 524304 | tf_op jit(solution)/shard_map/reduce_scatter | solution.py:662
  1058.5 37.7 %collective-permute-done.35 = bf16[128,2048]{1,0:T(8,128)(2,1)S(1)} collective-permute-done((bf16[128,2048]{1,0:T(8,128)(2,1)}, bf16[128,2048]{1,0:T(8,128)(2,1)S(1)}, u32[]{:S(2)}, u32[]{:S(2)}) %collective-permute-start.35) | collective-permute-done | bytes 524320 | tf_op jit(solution)/shard_map/ppermute | solution.py:404
  1148.0 58.2 %reduce-scatter.6.cloned.1.call-done = bf16[256,2048]{1,0:T(8,128)(2,1)} async-done(((bf16[2048,2048]{1,0:T(8,128)(2,1)}), bf16[256,2048]{1,0:T(8,128)(2,1)}) %reduce-scatter.6.cloned.1.call-update) | async-done | bytes 1048592 | tf_op jit(solution)/shard_map/reduce_scatter | solution.py:683
  1234.1 18.8 %collective-permute-done.29 = bf16[256,2048]{1,0:T(8,128)(2,1)} collective-permute-done((bf16[256,2048]{1,0:T(8,128)(2,1)}, bf16[256,2048]{1,0:T(8,128)(2,1)}, u32[]{:S(2)}, u32[]{:S(2)}) %collective-permute-start.29) | collective-permute-done | bytes 1048608 | tf_op jit(solution)/shard_map/ppermute | solution.py:404
  1265.0 61.6 %reduce-scatter.12.cloned.1.call-done = bf16[256,2816]{1,0:T(8,128)(2,1)} async-done(((bf16[2048,2816]{1,0:T(8,128)(2,1)}), bf16[256,2816]{1,0:T(8,128)(2,1)}) %reduce-scatter.12.cloned.1.call-update) | async-done | bytes 1441808 | tf_op jit(solution)/shard_map/reduce_scatter | solution.py:655
  1330.1 21.2 %maximum_convert_fusion = f32[256,12288]{0,1:T(8,128)} fusion(bf16[256,4096]{0,1:T(8,128)(2,1)S(1)} %bitcast.280, bf16[256,4096]{0,1:T(8,128)(2,1)} %bitcast.281, bf16[256,2048]{0,1:T(8,128)(2,1)S(1)} %bitcast.288, bf16[256,2048]{0,1:T(8,128)(2,1)} %bitcast.289), kind=kLoop, calls=%fused_computation.13 | loop fusion | flops 25165824 | bytes 18874368 | tf_op jit(solution)/shard_map/convert_element_type | solution.py:696
  1370.4 19.8 %collective-permute-done.39 = bf16[256,2816]{1,0:T(8,128)(2,1)} collective-permute-done((bf16[256,2816]{1,0:T(8,128)(2,1)}, bf16[256,2816]{1,0:T(8,128)(2,1)}, u32[]{:S(2)}, u32[]{:S(2)}) %collective-permute-start.39) | collective-permute-done | bytes 1441824 | tf_op jit(solution)/shard_map/ppermute | solution.py:404
  (637 shorter events, 680.7 us)
Async XLA Ops:
  7.2 65.7 %all-reduce.22.cloned.1.call-start = ((), (), s32[]{:S(2)}) async-start(), calls=%async_computation.18 | async-start | bytes 413696
  14.3 160.0 %all-gather.9.cloned.1.call-start = ((), (), s32[]{:S(2)}) async-start(), calls=%async_computation.8 | async-start | bytes 4718592 | tf_op jit(solution)/shard_map/all_gather | solution.py:592
  33.6 186.9 %all-gather.7.cloned.1.call-start = ((), (), s32[]{:S(2)}) async-start(), calls=%async_computation.7 | async-start | bytes 9437184 | tf_op jit(solution)/shard_map/all_gather | solution.py:591
  34.4 309.9 %all-gather.11.cloned.1.call-start = ((), (), s32[]{:S(2)}) async-start(), calls=%async_computation.9 | async-start | bytes 4718592 | tf_op jit(solution)/shard_map/all_gather | solution.py:508
  39.9 390.8 %all-gather.13.cloned.1.call-start = ((), (), s32[]{:S(2)}) async-start(), calls=%async_computation.10 | async-start | bytes 12976128 | tf_op jit(solution)/shard_map/all_gather | solution.py:594
  59.4 64.8 %all-to-all-start = ((bf16[4,48,4096]{2,1,0:T(8,128)(2,1)}), bf16[4,48,4096]{2,1,0:T(8,128)(2,1)}, u32[]{:S(2)}, u32[]{:S(2)}) async-start(bf16[4,48,4096]{2,1,0:T(8,128)(2,1)} %bitcast.299), calls=%async_computation | async-start | bytes 3145728 | tf_op jit(solution)/shard_map/all_to_all | solution.py:376
  64.7 398.0 %all-gather.15.cloned.1.call-start = ((), (), s32[]{:S(2)}) async-start(), calls=%async_computation.11 | async-start | bytes 6488064 | tf_op jit(solution)/shard_map/all_gather | solution.py:596
  65.6 879.5 %all-reduce.20.cloned.1.call-start = ((), (), s32[]{:S(2)}) async-start(), calls=%async_computation.12 | async-start | bytes 827392 | tf_op jit(solution)/shard_map/psum | solution.py:720
  397.1 51.3 %collective-permute-start.18 = (bf16[192,2048]{1,0:T(8,128)(2,1)}, bf16[192,2048]{1,0:T(8,128)(2,1)}, u32[]{:S(2)}, u32[]{:S(2)}) collective-permute-start(bf16[192,2048]{1,0:T(8,128)(2,1)} %slice.261), channel_id=1, source_target_pairs={{0,24},{8,16},{16,8},{24,0},{1,25},{9,17},{17,9},{25,1},{2,26},{10... | collective-permute-start | bytes 2359304 | tf_op jit(solution)/shard_map/ppermute | solution.py:404
  398.6 63.7 %collective-permute-start.17 = (bf16[192,2048]{1,0:T(8,128)(2,1)}, bf16[192,2048]{1,0:T(8,128)(2,1)}, u32[]{:S(2)}, u32[]{:S(2)}) collective-permute-start(bf16[192,2048]{1,0:T(8,128)(2,1)} %slice.261), channel_id=1, source_target_pairs={{0,16},{8,24},{16,0},{24,8},{1,17},{9,25},{17,1},{25,9},{2,18},{10... | collective-permute-start | bytes 2359304 | tf_op jit(solution)/shard_map/ppermute | solution.py:404
  505.0 57.8 %collective-permute-start.14 = (bf16[192,2048]{1,0:T(8,128)(2,1)S(1)}, bf16[192,2048]{1,0:T(8,128)(2,1)S(1)}, u32[]{:S(2)}, u32[]{:S(2)}) collective-permute-start(bf16[192,2048]{1,0:T(8,128)(2,1)S(1)} %get-tuple-element.150), channel_id=1, source_target_pairs={{0,16},{8,24},{16,0},{24,8},{1,17},{9,25},{17,1},{25,9},{2,18},{10... | collective-permute-start | bytes 2359304 | tf_op jit(solution)/shard_map/ppermute | solution.py:404
  807.5 191.0 %reduce-scatter.10.cloned.1.call-start = ((), (), s32[]{:S(2)}) async-start(), calls=%async_computation.15 | async-start | bytes 4718592 | tf_op jit(solution)/shard_map/reduce_scatter | solution.py:519
  815.4 234.2 %reduce-scatter.8.cloned.1.call-start = ((), (), s32[]{:S(2)}) async-start(), calls=%async_computation.14 | async-start | bytes 4718592 | tf_op jit(solution)/shard_map/reduce_scatter | solution.py:662
  821.9 293.4 %reduce-scatter.14.cloned.1.call-start = ((), (), s32[]{:S(2)}) async-start(), calls=%async_computation.17 | async-start | bytes 6488064 | tf_op jit(solution)/shard_map/reduce_scatter | solution.py:654
  831.9 374.3 %reduce-scatter.6.cloned.1.call-start = ((), (), s32[]{:S(2)}) async-start(), calls=%async_computation.13 | async-start | bytes 9437184 | tf_op jit(solution)/shard_map/reduce_scatter | solution.py:683
  842.9 483.7 %reduce-scatter.12.cloned.1.call-start = ((), (), s32[]{:S(2)}) async-start(), calls=%async_computation.16 | async-start | bytes 12976128 | tf_op jit(solution)/shard_map/reduce_scatter | solution.py:655
  866.2 133.7 %all-to-all-start.1 = ((bf16[4,48,4096]{2,1,0:T(8,128)(2,1)}), bf16[4,48,4096]{2,1,0:T(8,128)(2,1)S(1)}, u32[]{:S(2)}, u32[]{:S(2)}) async-start(bf16[4,48,4096]{2,1,0:T(8,128)(2,1)} %bitcast.65), calls=%async_computation.1 | async-start | bytes 3145728 | tf_op jit(solution)/shard_map/all_to_all | solution.py:391
  998.5 57.4 %collective-permute-start.34 = (bf16[128,2048]{1,0:T(8,128)(2,1)}, bf16[128,2048]{1,0:T(8,128)(2,1)}, u32[]{:S(2)}, u32[]{:S(2)}) collective-permute-start(bf16[128,2048]{1,0:T(8,128)(2,1)} %reduce-scatter.10.cloned.1.call-done), channel_id=1, source_target_pairs={{0,8},{8,0},{16,24},{24,16},{1,9},{9,1},{17,25},{25,17},{2,10},{10... | collective-permute-start | bytes 1572872 | tf_op jit(solution)/shard_map/ppermute | solution.py:404
  1049.5 50.8 %collective-permute-start.31 = (bf16[256,1024]{1,0:T(8,128)(2,1)}, bf16[256,1024]{1,0:T(8,128)(2,1)}, u32[]{:S(2)}, u32[]{:S(2)}) collective-permute-start(bf16[256,1024]{1,0:T(8,128)(2,1)} %reduce-scatter.8.cloned.1.call-done), channel_id=1, source_target_pairs={{0,8},{8,0},{16,24},{24,16},{1,9},{9,1},{17,25},{25,17},{2,10},{10... | collective-permute-start | bytes 1572872 | tf_op jit(solution)/shard_map/ppermute | solution.py:404
  1051.0 50.5 %collective-permute-start.32 = (bf16[256,1024]{1,0:T(8,128)(2,1)}, bf16[256,1024]{1,0:T(8,128)(2,1)}, u32[]{:S(2)}, u32[]{:S(2)}) collective-permute-start(bf16[256,1024]{1,0:T(8,128)(2,1)} %reduce-scatter.8.cloned.1.call-done), channel_id=1, source_target_pairs={{0,16},{8,24},{16,0},{24,8},{1,17},{9,25},{17,1},{25,9},{2,18},{10... | collective-permute-start | bytes 1572872 | tf_op jit(solution)/shard_map/ppermute | solution.py:404
  1052.5 50.3 %collective-permute-start.33 = (bf16[256,1024]{1,0:T(8,128)(2,1)}, bf16[256,1024]{1,0:T(8,128)(2,1)}, u32[]{:S(2)}, u32[]{:S(2)}) collective-permute-start(bf16[256,1024]{1,0:T(8,128)(2,1)} %reduce-scatter.8.cloned.1.call-done), channel_id=1, source_target_pairs={{0,24},{8,16},{16,8},{24,0},{1,25},{9,17},{17,9},{25,1},{2,26},{10... | collective-permute-start | bytes 1572872 | tf_op jit(solution)/shard_map/ppermute | solution.py:404
  1118.3 91.4 %collective-permute-start.43 = (bf16[176,2048]{1,0:T(8,128)(2,1)}, bf16[176,2048]{1,0:T(8,128)(2,1)}, u32[]{:S(2)}, u32[]{:S(2)}) collective-permute-start(bf16[176,2048]{1,0:T(8,128)(2,1)} %reduce-scatter.14.cloned.1.call-done), channel_id=1, source_target_pairs={{0,24},{8,16},{16,8},{24,0},{1,25},{9,17},{17,9},{25,1},{2,26},{10... | collective-permute-start | bytes 2162696 | tf_op jit(solution)/shard_map/ppermute | solution.py:404
  1328.1 62.1 %collective-permute-start.39 = (bf16[256,2816]{1,0:T(8,128)(2,1)}, bf16[256,2816]{1,0:T(8,128)(2,1)}, u32[]{:S(2)}, u32[]{:S(2)}) collective-permute-start(bf16[256,2816]{1,0:T(8,128)(2,1)} %reduce-scatter.12.cloned.1.call-done), channel_id=1, source_target_pairs={{0,16},{8,24},{16,0},{24,8},{1,17},{9,25},{17,1},{25,9},{2,18},{10... | collective-permute-start | bytes 4325384 | tf_op jit(solution)/shard_map/ppermute | solution.py:404
  1329.6 62.3 %collective-permute-start.40 = (bf16[256,2816]{1,0:T(8,128)(2,1)}, bf16[256,2816]{1,0:T(8,128)(2,1)}, u32[]{:S(2)}, u32[]{:S(2)}) collective-permute-start(bf16[256,2816]{1,0:T(8,128)(2,1)} %reduce-scatter.12.cloned.1.call-done), channel_id=1, source_target_pairs={{0,24},{8,16},{16,8},{24,0},{1,25},{9,17},{17,9},{25,1},{2,26},{10... | collective-permute-start | bytes 4325384 | tf_op jit(solution)/shard_map/ppermute | solution.py:404
  (153 other events, 2977.3 us)
Sparse Core Ops, SparseCore 0:
  14.4 55.2 all-reduce.21
  71.9 65.0 all-gather.8
  139.3 81.2 all-gather.6
  222.1 45.7 all-gather.10
  269.4 107.1 all-gather.12
  378.2 58.6 all-gather.14
  807.6 137.5 all-reduce.19
  947.5 50.9 reduce-scatter.9
  1001.3 48.1 reduce-scatter.7
  1052.3 63.0 reduce-scatter.13
  1118.2 87.9 reduce-scatter.5
  1208.9 117.6 reduce-scatter.11

commit v2 on v1

--- a/solution.py
+++ b/solution.py
@@ -64,11 +64,51 @@
     return jnp.concatenate(done, axis=0)
 
 
-def block_terms(head, heads, qkv, cols, rows):
-    queries = qkv[:, head * DK : (head + 1) * DK]
-    keys = qkv[:, (heads + head) * DK : (heads + head + 1) * DK]
-    begin = 2 * heads * DK + head * DV
-    values = qkv[:, begin : begin + DV]
+def silu_parts(value):
+    rate = 1.0 / (1.0 + jnp.exp(-value))
+    return value * rate, rate
+
+
+def gate_terms(heads, gates, decay_log, dt_bias):
+    shifted = gates[:, :heads] + dt_bias
+    beta = 1.0 / (1.0 + jnp.exp(-gates[:, heads:]))
+    soft = jnp.maximum(shifted, 0.0) + jnp.log1p(jnp.exp(-jnp.abs(shifted)))
+    return shifted, beta, -jnp.exp(decay_log) * soft
+
+
+def ones_left(ones, value):
+    high, rest = halves(value)
+    high_f = high.astype(f32)
+    rest, low = halves(value - high_f)
+    return mm(ones, high) + mm(ones, rest) + mm(ones, low)
+
+
+def triangle(upper):
+    at_i = lax.broadcasted_iota(jnp.int32, (SPAN, SPAN), 0)
+    at_j = lax.broadcasted_iota(jnp.int32, (SPAN, SPAN), 1)
+    return jnp.where(at_i <= at_j if upper else at_i >= at_j, 1.0, 0.0).astype(bf16)
+
+
+def side_columns(heads, gates, side, decay_log, dt_bias):
+    shifted, beta, decay = gate_terms(heads, gates, decay_log, dt_bias)
+    running = ones_left(triangle(False), decay)
+    cols = jnp.concatenate(
+        [running, beta, side[:, :1], jnp.zeros((SPAN, 128 - 2 * heads - 1), f32)], axis=1
+    )
+    return cols, cols.T, shifted, beta, decay
+
+
+def conv_forward(current, before, taps, side):
+    extended = jnp.concatenate([before, current], axis=0)
+    total = taps[0:1, :] * current
+    for back in range(1, CONV):
+        total = total + taps[back : back + 1, :] * (
+            extended[8 - back : 8 - back + SPAN, :] * side[:, back : back + 1]
+        )
+    return total
+
+
+def block_terms(head, heads, cols, rows):
     cum_c = cols[:, head : head + 1]
     beta_c = cols[:, heads + head : heads + head + 1]
     count_c = cols[:, 2 * heads : 2 * heads + 1]
@@ -85,22 +125,54 @@
     tail = jnp.where(
         count_c == count_c[last : last + 1, :], jnp.exp(cum_c[last : last + 1, :] - cum_c), 0.0
     )
-    return queries, keys, values, beta_c, lower_st, fall, growth, tail, growth[last : last + 1, :]
-
-
-def mixer_forward_kernel(heads, qkv_ref, cols_ref, rows_ref, mixed_ref, state_ref, inv_ref, solved_ref, carried):
+    return beta_c, lower_st, fall, growth, tail, growth[last : last + 1, :]
+
+
+def mixer_forward_kernel(
+    heads,
+    conv_ref,
+    gate_ref,
+    gates_ref,
+    side_ref,
+    taps_ref,
+    gain_ref,
+    log_ref,
+    bias_ref,
+    gated_ref,
+    mixed_ref,
+    qkv_ref,
+    state_ref,
+    inv_ref,
+    solved_ref,
+    carried,
+    before,
+):
     @pl.when(pl.program_id(0) == 0)
     def _():
         carried[...] = jnp.zeros_like(carried)
-
-    qkv = qkv_ref[...]
-    cols = cols_ref[...]
-    rows = rows_ref[0]
+        before[...] = jnp.zeros_like(before)
+
+    side = side_ref[...]
+    current = conv_ref[...].astype(f32)
+    act, _ = silu_parts(conv_forward(current, before[...], taps_ref[...], side))
+    before[...] = current[SPAN - 8 :, :]
+    cols, rows, _, _, _ = side_columns(heads, gates_ref[...], side, log_ref[...], bias_ref[...])
+    valid = side[:, CONV : CONV + 1]
+    gain = gain_ref[...]
     scale = DK ** (-0.5)
     for head in range(heads):
-        queries, keys, values, beta_c, lower_st, fall, growth, tail, kept = block_terms(
-            head, heads, qkv, cols, rows
-        )
+        beta_c, lower_st, fall, growth, tail, kept = block_terms(head, heads, cols, rows)
+        unit = []
+        for begin in (head * DK, (heads + head) * DK):
+            row = act[:, begin : begin + DK]
+            row = row * lax.rsqrt(jnp.sum(row * row, axis=1, keepdims=True) + eps_norm)
+            row = row.astype(bf16)
+            qkv_ref[:, begin : begin + DK] = row
+            unit.append(row)
+        queries, keys = unit
+        begin = 2 * heads * DK + head * DV
+        values = act[:, begin : begin + DV].astype(bf16)
+        qkv_ref[:, begin : begin + DV] = values
         state = carried[head]
         state_ref[0, head] = state
         key_prod = mm(keys, keys, ROWS)
@@ -112,35 +184,95 @@
         query_state = mm_right(queries, state)
         right_side = beta_c * (values.astype(f32) - growth * key_state)
         solved = mm_both(inverse, right_side)
-        mixed = scale * (growth * query_state + mm_both(query_prod * fall, solved))
-        mixed_ref[:, head * DV : (head + 1) * DV] = mixed
-        solved_ref[:, head * DV : (head + 1) * DV] = solved
+        mixed = scale * (growth * query_state + mm_both(query_prod * fall, solved)) * valid
+        part = slice(head * DV, (head + 1) * DV)
+        mixed_ref[:, part] = mixed
+        solved_ref[:, part] = solved
         carried[head] = kept * state + mm_both(tail * keys.astype(f32), solved, COLS)
+        shrink = lax.rsqrt(jnp.mean(mixed * mixed, axis=1, keepdims=True) + eps_norm)
+        open_gate, _ = silu_parts(gate_ref[:, part])
+        gated_ref[:, part] = (mixed * shrink * gain * open_gate).astype(bf16)
 
 
 def mixer_backward_kernel(
-    heads, qkv_ref, cols_ref, rows_ref, state_ref, inv_ref, solved_ref, cot_ref, dqkv_ref, dcols_ref, carried
+    heads,
+    conv_ref,
+    ahead_ref,
+    gate_ref,
+    gates_ref,
+    side_ref,
+    taps_ref,
+    gain_ref,
+    log_ref,
+    bias_ref,
+    mixed_ref,
+    qkv_ref,
+    state_ref,
+    inv_ref,
+    solved_ref,
+    cot_ref,
+    dconv_ref,
+    dgate_ref,
+    dgates_ref,
+    dtaps_ref,
+    dgain_ref,
+    dheads_ref,
+    carried,
+    after,
+    after_side,
 ):
     @pl.when(pl.program_id(0) == 0)
     def _():
         carried[...] = jnp.zeros_like(carried)
-
-    qkv = qkv_ref[...]
-    cols = cols_ref[...]
-    rows = rows_ref[0]
+        after[...] = jnp.zeros_like(after)
+        after_side[...] = jnp.zeros_like(after_side)
+        dtaps_ref[...] = jnp.zeros_like(dtaps_ref)
+        dgain_ref[...] = jnp.zeros_like(dgain_ref)
+        dheads_ref[...] = jnp.zeros_like(dheads_ref)
+
+    side = side_ref[...]
+    taps = taps_ref[...]
+    gain = gain_ref[...]
+    valid = side[:, CONV : CONV + 1]
+    current = conv_ref[...].astype(f32)
+    ahead = ahead_ref[8:, :].astype(f32)
+    conv_out = conv_forward(current, ahead, taps, side)
+    act, rate = silu_parts(conv_out)
+    slope = rate * (1.0 + conv_out * (1.0 - rate))
+    cols, rows, shifted, beta_all, decay_all = side_columns(
+        heads, gates_ref[...], side, log_ref[...], bias_ref[...]
+    )
     scale = DK ** (-0.5)
     at_last = lax.broadcasted_iota(jnp.int32, (SPAN, 1), 0) == SPAN - 1
     d_betas, d_cums = [], []
+    d_queries, d_keys, d_values = [], [], []
+    d_gain = jnp.zeros((1, DV), f32)
     for head in range(heads):
-        queries, keys, values, beta_c, lower_st, fall, growth, tail, kept = block_terms(
-            head, heads, qkv, cols, rows
-        )
+        beta_c, lower_st, fall, growth, tail, kept = block_terms(head, heads, cols, rows)
+        part = slice(head * DV, (head + 1) * DV)
+        mixed = mixed_ref[:, part]
+        gate = gate_ref[:, part]
+        d_gated = cot_ref[:, part]
+        shrink = lax.rsqrt(jnp.mean(mixed * mixed, axis=1, keepdims=True) + eps_norm)
+        normal = mixed * shrink
+        open_gate, gate_rate = silu_parts(gate)
+        with_normal = d_gated * normal
+        d_gain = d_gain + jnp.sum(with_normal * open_gate, axis=0, keepdims=True)
+        dgate_ref[:, part] = (
+            with_normal * gain * (gate_rate * (1.0 + gate * (1.0 - gate_rate)))
+        ).astype(bf16)
+        d_normal = d_gated * gain * open_gate
+        d_mixed = shrink * (d_normal - normal * jnp.mean(d_normal * normal, axis=1, keepdims=True))
+        d_mixed = (scale * valid) * d_mixed
+        queries = qkv_ref[:, head * DK : (head + 1) * DK]
+        keys = qkv_ref[:, (heads + head) * DK : (heads + head + 1) * DK]
+        begin = 2 * heads * DK + head * DV
+        values = qkv_ref[:, begin : begin + DV]
         keys_f = keys.astype(f32)
         queries_f = queries.astype(f32)
         state = state_ref[0, head]
         inverse = inv_ref[0, head]
-        solved = solved_ref[:, head * DV : (head + 1) * DV]
-        d_mixed = scale * cot_ref[:, head * DV : (head + 1) * DV]
+        solved = solved_ref[:, part]
         d_state = carried[head]
         key_prod = mm(keys, keys, ROWS)
         query_prod = mm(queries, keys, ROWS)
@@ -155,7 +287,7 @@
         d_strict = jnp.where(lower_st, -mm_both(d_right, solved, ROWS), 0.0)
         d_key_prod = d_strict * beta_c * fall
         d_key_state = -(beta_c * growth) * d_right
-        d_query = mm_both(growth * d_mixed, state, ROWS) + mm_right(keys, d_query_prod, ((0,), (1,))).T
+        d_query = mm_both(growth * d_mixed, state, ROWS) + mm_both(d_query_prod, keys_f)
         both = d_key_prod + d_key_prod.T
         from_tail = mm_both(solved, d_state, ROWS)
         d_key = (
@@ -184,82 +316,115 @@
             - from_last
             + jnp.where(at_last, at_end, 0.0)
         )
-        dqkv_ref[:, head * DK : (head + 1) * DK] = d_query
-        dqkv_ref[:, (heads + head) * DK : (heads + head + 1) * DK] = d_key
-        begin = 2 * heads * DK + head * DV
-        dqkv_ref[:, begin : begin + DV] = beta_c * d_right
         carried[head] = (
             kept * d_state
             + mm_both(growth * queries_f, d_mixed, COLS)
             + mm_right(keys, d_key_state, COLS)
         )
-    dcols_ref[...] = jnp.concatenate(
-        d_betas + d_cums + [jnp.zeros((SPAN, SIDE - 2 * heads), f32)], axis=1
-    )
-
-
-def side_arrays(beta_rows, decay_rows, starts):
-    length, heads = beta_rows.shape
-    blocks = length // SPAN
-    lower = jnp.tril(jnp.ones((SPAN, SPAN), f32))
-    running = jnp.einsum(
-        "ij,bjh->bih", lower, decay_rows.reshape(blocks, SPAN, heads), precision=lax.Precision.HIGHEST
-    )
-    counted = jnp.einsum("ij,bj->bi", lower, starts.astype(f32).reshape(blocks, SPAN))
-    cols = jnp.concatenate(
+        for grads, grad, start in ((d_queries, d_query, head * DK), (d_keys, d_key, (heads + head) * DK)):
+            row = act[:, start : start + DK]
+            small = lax.rsqrt(jnp.sum(row * row, axis=1, keepdims=True) + eps_norm)
+            along = jnp.sum(row * grad, axis=1, keepdims=True) * small * small
+            grads.append(small * (grad - row * along))
+        d_values.append(beta_c * d_right)
+    dgain_ref[...] += d_gain
+    d_conv = jnp.concatenate(d_queries + d_keys + d_values, axis=1) * slope
+    extended = jnp.concatenate([ahead, current], axis=0)
+    later, later_side = after[...], after_side[...]
+    d_in = taps[0:1, :] * d_conv
+    d_taps = [jnp.sum(d_conv * current, axis=0, keepdims=True)]
+    for back in range(1, CONV):
+        masked = d_conv * side[:, back : back + 1]
+        d_taps.append(
+            jnp.sum(masked * extended[8 - back : 8 - back + SPAN, :], axis=0, keepdims=True)
+        )
+        reach = jnp.concatenate([masked, later * later_side[:, back : back + 1]], axis=0)
+        d_in = d_in + taps[back : back + 1, :] * reach[back : back + SPAN, :]
+    dtaps_ref[...] += jnp.concatenate(d_taps, axis=0)
+    dconv_ref[...] = d_in.astype(bf16)
+    after[...] = d_conv[:8, :]
+    after_side[...] = side[:8, :]
+    d_decay = ones_left(triangle(True), jnp.concatenate(d_cums, axis=1))
+    d_beta = jnp.concatenate(d_betas, axis=1)
+    d_shifted = -d_decay * jnp.exp(log_ref[...]) / (1.0 + jnp.exp(-shifted))
+    dgates_ref[...] = jnp.concatenate([d_shifted, d_beta * beta_all * (1.0 - beta_all)], axis=1)
+    dheads_ref[...] += jnp.concatenate(
         [
-            running,
-            beta_rows.reshape(blocks, SPAN, heads),
-            counted[..., None],
-            jnp.zeros((blocks, SPAN, SIDE - 2 * heads - 1), f32),
+            jnp.sum(d_decay * decay_all, axis=0, keepdims=True),
+            jnp.sum(d_shifted, axis=0, keepdims=True),
         ],
-        axis=2,
-    )
-    return cols.reshape(length, SIDE), cols.transpose(0, 2, 1)
-
-
-def mixer_forward(qkv, cols, rows):
-    length, width = qkv.shape
-    heads = width // (2 * DK + DV)
+        axis=1,
+    )
+
+
+def whole_block(shape):
+    return pl.BlockSpec(shape, lambda i: (0,) * len(shape))
+
+
+MIXER_PARAMS = pltpu.CompilerParams(vmem_limit_bytes=48 * 1024 * 1024)
+
+
+def mixer_forward(conv_in, out_gate, gates, side, taps, gain, decay_log, dt_bias):
+    length, width = conv_in.shape
+    heads = decay_log.shape[1]
     blocks = length // SPAN
     return pl.pallas_call(
         functools.partial(mixer_forward_kernel, heads),
         grid=(blocks,),
         in_specs=[
             pl.BlockSpec((SPAN, width), lambda i: (i, 0)),
+            pl.BlockSpec((SPAN, heads * DV), lambda i: (i, 0)),
+            pl.BlockSpec((SPAN, 2 * heads), lambda i: (i, 0)),
             pl.BlockSpec((SPAN, SIDE), lambda i: (i, 0)),
-            pl.BlockSpec((1, SIDE, SPAN), lambda i: (i, 0, 0)),
+            whole_block((CONV, width)),
+            whole_block((1, DV)),
+            whole_block((1, heads)),
+            whole_block((1, heads)),
         ],
         out_specs=[
             pl.BlockSpec((SPAN, heads * DV), lambda i: (i, 0)),
+            pl.BlockSpec((SPAN, heads * DV), lambda i: (i, 0)),
+            pl.BlockSpec((SPAN, width), lambda i: (i, 0)),
             pl.BlockSpec((1, heads, DK, DV), lambda i: (i, 0, 0, 0)),
             pl.BlockSpec((1, heads, SPAN, SPAN), lambda i: (i, 0, 0, 0)),
             pl.BlockSpec((SPAN, heads * DV), lambda i: (i, 0)),
         ],
         out_shape=[
+            jax.ShapeDtypeStruct((length, heads * DV), bf16),
             jax.ShapeDtypeStruct((length, heads * DV), f32),
+            jax.ShapeDtypeStruct((length, width), bf16),
             jax.ShapeDtypeStruct((blocks, heads, DK, DV), f32),
             jax.ShapeDtypeStruct((blocks, heads, SPAN, SPAN), f32),
             jax.ShapeDtypeStruct((length, heads * DV), f32),
         ],
-        scratch_shapes=[pltpu.VMEM((heads, DK, DV), f32)],
-        compiler_params=pltpu.CompilerParams(vmem_limit_bytes=32 * 1024 * 1024),
+        scratch_shapes=[pltpu.VMEM((heads, DK, DV), f32), pltpu.VMEM((8, width), f32)],
+        compiler_params=MIXER_PARAMS,
         name="mixer_forward",
-    )(qkv, cols, rows)
-
-
-def mixer_backward(qkv, cols, rows, states, inverses, solved, d_mixed):
-    length, width = qkv.shape
-    heads = width // (2 * DK + DV)
+    )(conv_in, out_gate, gates, side, taps, gain, decay_log, dt_bias)
+
+
+def mixer_backward(conv_in, out_gate, gates, side, taps, gain, decay_log, dt_bias, kept, d_gated):
+    length, width = conv_in.shape
+    heads = decay_log.shape[1]
     blocks = length // SPAN
     end = blocks - 1
+    ahead_rows = 16
+    per = SPAN // ahead_rows
     return pl.pallas_call(
         functools.partial(mixer_backward_kernel, heads),
         grid=(blocks,),
         in_specs=[
             pl.BlockSpec((SPAN, width), lambda i: (end - i, 0)),
+            pl.BlockSpec((ahead_rows, width), lambda i: (jnp.maximum((end - i) * per - 1, 0), 0)),
+            pl.BlockSpec((SPAN, heads * DV), lambda i: (end - i, 0)),
+            pl.BlockSpec((SPAN, 2 * heads), lambda i: (end - i, 0)),
             pl.BlockSpec((SPAN, SIDE), lambda i: (end - i, 0)),
-            pl.BlockSpec((1, SIDE, SPAN), lambda i: (end - i, 0, 0)),
+            whole_block((CONV, width)),
+            whole_block((1, DV)),
+            whole_block((1, heads)),
+            whole_block((1, heads)),
+            pl.BlockSpec((SPAN, heads * DV), lambda i: (end - i, 0)),
+            pl.BlockSpec((SPAN, width), lambda i: (end - i, 0)),
             pl.BlockSpec((1, heads, DK, DV), lambda i: (end - i, 0, 0, 0)),
             pl.BlockSpec((1, heads, SPAN, SPAN), lambda i: (end - i, 0, 0, 0)),
             pl.BlockSpec((SPAN, heads * DV), lambda i: (end - i, 0)),
@@ -267,71 +432,146 @@
         ],
         out_specs=[
             pl.BlockSpec((SPAN, width), lambda i: (end - i, 0)),
-            pl.BlockSpec((SPAN, SIDE), lambda i: (end - i, 0)),
+            pl.BlockSpec((SPAN, heads * DV), lambda i: (end - i, 0)),
+            pl.BlockSpec((SPAN, 2 * heads), lambda i: (end - i, 0)),
+            whole_block((CONV, width)),
+            whole_block((1, DV)),
+            whole_block((1, 2 * heads)),
         ],
         out_shape=[
-            jax.ShapeDtypeStruct((length, width), f32),
-            jax.ShapeDtypeStruct((length, SIDE), f32),
+            jax.ShapeDtypeStruct((length, width), bf16),
+            jax.ShapeDtypeStruct((length, heads * DV), bf16),
+            jax.ShapeDtypeStruct((length, 2 * heads), f32),
+            jax.ShapeDtypeStruct((CONV, width), f32),
+            jax.ShapeDtypeStruct((1, DV), f32),
+            jax.ShapeDtypeStruct((1, 2 * heads), f32),
         ],
-        scratch_shapes=[pltpu.VMEM((heads, DK, DV), f32)],
-        compiler_params=pltpu.CompilerParams(vmem_limit_bytes=32 * 1024 * 1024),
+        scratch_shapes=[
+            pltpu.VMEM((heads, DK, DV), f32),
+            pltpu.VMEM((8, width), f32),
+            pltpu.VMEM((8, SIDE), f32),
+        ],
+        compiler_params=MIXER_PARAMS,
         name="mixer_backward",
-    )(qkv, cols, rows, states, inverses, solved, d_mixed)
-
-
-def decay_back(d_cums):
-    length, heads = d_cums.shape
-    upper = jnp.triu(jnp.ones((SPAN, SPAN), f32))
-    return jnp.einsum(
-        "ij,bjh->bih",
-        upper,
-        d_cums.reshape(length // SPAN, SPAN, heads),
-        precision=lax.Precision.HIGHEST,
-    ).reshape(length, heads)
+    )(conv_in, conv_in, out_gate, gates, side, taps, gain, decay_log, dt_bias, *kept, d_gated)
+
+
+MESH = pl.DeviceIdType.MESH
+
+
+def column_peers(seq, cores):
+    count = seq * cores
+    me = lax.axis_index("seq") * cores + lax.axis_index("wshard")
+    peers = []
+    for step in range(1, count):
+        place = lax.rem(me + step, count)
+        peers.append((place, {"seq": place // cores, "wshard": lax.rem(place, cores)}))
+    return me, peers
+
+
+def greet(ids):
+    barrier = pltpu.get_barrier_semaphore()
+    for device in ids:
+        pl.semaphore_signal(barrier, inc=1, device_id=device, device_id_type=MESH)
+    pl.semaphore_wait(barrier, len(ids))
+
+
+def small_gather_kernel(seq, cores, in_ref, out_ref, send_sem, recv_sem):
+    me, peers = column_peers(seq, cores)
+    greet([device for _, device in peers])
+    copies = []
+    for at, (_, device) in enumerate(peers):
+        copies.append(
+            pltpu.make_async_remote_copy(
+                src_ref=in_ref,
+                dst_ref=out_ref.at[me],
+                send_sem=send_sem.at[at],
+                recv_sem=recv_sem.at[at],
+                device_id=device,
+                device_id_type=MESH,
+            )
+        )
+        copies[-1].start()
+    out_ref[me] = in_ref[...]
+    for copy in copies:
+        copy.wait()
+
+
+def small_gather(values, seq, cores):
+    count = seq * cores
+    return pl.pallas_call(
+        functools.partial(small_gather_kernel, seq, cores),
+        out_shape=jax.ShapeDtypeStruct((count,) + values.shape, values.dtype),
+        in_specs=[pl.BlockSpec(memory_space=pltpu.VMEM)],
+        out_specs=pl.BlockSpec(memory_space=pltpu.VMEM),
+        scratch_shapes=[pltpu.SemaphoreType.DMA((count - 1,)), pltpu.SemaphoreType.DMA((count - 1,))],
+        compiler_params=pltpu.CompilerParams(collective_id=0, has_side_effects=True),
+        name="small_gather",
+    )(values)
+
+
+def small_sum_kernel(seq, cores, group, in_ref, out_ref, landed, send_sem, recv_sem, plane_send, plane_recv):
+    me, peers = column_peers(seq, cores)
+    part = lax.axis_index("group")
+    plane = [{"group": lax.rem(part + step, group)} for step in range(1, group)]
+    greet([device for _, device in peers] + plane)
+    copies = []
+    for at, (place, device) in enumerate(peers):
+        copies.append(
+            pltpu.make_async_remote_copy(
+                src_ref=in_ref.at[place],
+                dst_ref=landed.at[at],
+                send_sem=send_sem.at[at],
+                recv_sem=recv_sem.at[at],
+                device_id=device,
+                device_id_type=MESH,
+            )
+        )
+        copies[-1].start()
+    total = in_ref[me]
+    for at, copy in enumerate(copies):
+        copy.wait()
+        total = total + landed[at]
+    out_ref[part] = total
+    copies = []
+    for at, device in enumerate(plane):
+        copies.append(
+            pltpu.make_async_remote_copy(
+                src_ref=out_ref.at[part],
+                dst_ref=out_ref.at[part],
+                send_sem=plane_send.at[at],
+                recv_sem=plane_recv.at[at],
+                device_id=device,
+                device_id_type=MESH,
+            )
+        )
+        copies[-1].start()
+    for copy in copies:
+        copy.wait()
+
+
+def small_sum(values, seq, cores, group):
+    count = seq * cores
+    shape = values.shape[1:]
+    return pl.pallas_call(
+        functools.partial(small_sum_kernel, seq, cores, group),
+        out_shape=jax.ShapeDtypeStruct((group,) + shape, values.dtype),
+        in_specs=[pl.BlockSpec(memory_space=pltpu.VMEM)],
+        out_specs=pl.BlockSpec(memory_space=pltpu.VMEM),
+        scratch_shapes=[
+            pltpu.VMEM((count - 1,) + shape, values.dtype),
+            pltpu.SemaphoreType.DMA((count - 1,)),
+            pltpu.SemaphoreType.DMA((count - 1,)),
+            pltpu.SemaphoreType.DMA((group - 1,)),
+            pltpu.SemaphoreType.DMA((group - 1,)),
+        ],
+        compiler_params=pltpu.CompilerParams(collective_id=1, has_side_effects=True),
+        name="small_sum",
+    )(values)
 
 
 def rms_scale(values, gain):
     return values * lax.rsqrt(jnp.mean(values * values, axis=-1, keepdims=True) + eps_norm) * gain
-
-
-def unit_rows(values):
-    return values * lax.rsqrt(jnp.sum(values * values, axis=-1, keepdims=True) + eps_norm)
-
-
-def short_conv(extended, conv_w, segment):
-    rows_here = extended.shape[0] - (CONV - 1)
-    own_seg = segment[CONV - 1 :]
-    conv_sum = jnp.zeros((rows_here, extended.shape[1]), f32)
-    for shift_by in range(CONV):
-        begin = CONV - 1 - shift_by
-        same = (segment[begin : begin + rows_here] == own_seg).astype(f32)
-        conv_sum = conv_sum + conv_w[shift_by] * extended[begin : begin + rows_here] * same[:, None]
-    return conv_sum
-
-
-def mixer_inputs(heads, extended, conv_w, segment):
-    rows_here = extended.shape[0] - (CONV - 1)
-    act = jax.nn.silu(short_conv(extended, conv_w, segment))
-    width = heads * DK
-    queries = unit_rows(act[:, :width].reshape(rows_here, heads, DK)).reshape(rows_here, -1)
-    keys_all = unit_rows(act[:, width : 2 * width].reshape(rows_here, heads, DK)).reshape(
-        rows_here, -1
-    )
-    return jnp.concatenate([queries, keys_all, act[:, 2 * width :]], axis=1)
-
-
-def decay_inputs(gates_ab, decay_log, dt_bias):
-    heads = decay_log.shape[0]
-    beta_rows = jax.nn.sigmoid(gates_ab[:, heads:])
-    decay_rows = -jnp.exp(decay_log) * jax.nn.softplus(gates_ab[:, :heads] + dt_bias)
-    return (beta_rows, decay_rows)
-
-
-def gated_norm(mixed, out_gate, gain):
-    rows_here = mixed.shape[0]
-    per_head = mixed.reshape(rows_here, -1, DV)
-    gated = rms_scale(per_head, gain) * jax.nn.silu(out_gate.reshape(per_head.shape))
-    return gated.reshape(rows_here, -1)
 
 
 def swiglu(gate_up):
@@ -512,40 +752,97 @@
             every, (0, self.part, 0, 0), (self.heads, 1, DV, width)
         ).reshape(-1, width)
 
-    def out_rows_back(self, grad):
+    def out_rows_scatter(self, grad):
+        if self.subs == 1 and self.cores == 2:
+            return lax.psum_scatter(grad, SHARDED, scatter_dimension=0, tiled=True)
         width = grad.shape[1]
-        grad = grad.astype(bf16)
+        every = jnp.zeros((self.heads, self.group, DV, width), bf16)
+        every = lax.dynamic_update_slice(
+            every, grad.reshape(self.heads, 1, DV, width), (0, self.part, 0, 0)
+        )
+        return lax.psum_scatter(every.reshape(-1, width), SHARDED, scatter_dimension=0, tiled=True)
+
+    def out_rows_join(self, shard):
+        width = shard.shape[1]
         if self.subs == 1 and self.cores == 2:
-            half = lax.psum_scatter(grad, SHARDED, scatter_dimension=0, tiled=True)
-            halves_all = self.gather_parts(half)
+            halves_all = self.gather_parts(shard)
             here = lax.dynamic_slice(halves_all, (2 * self.core, 0, 0), (2, DV // 2, width))
             there = lax.dynamic_slice(halves_all, (2 - 2 * self.core, 0, 0), (2, DV // 2, width))
             got = lax.ppermute(there, "wshard", [(0, 1), (1, 0)])
             first = jnp.where(self.core == 0, here, got)
             second = jnp.where(self.core == 0, got, here)
             return jnp.stack([first, second], axis=1).reshape(2 * DV, width).astype(f32)
-        every = jnp.zeros((self.heads, self.group, DV, width), bf16)
-        every = lax.dynamic_update_slice(
-            every, grad.reshape(self.heads, 1, DV, width), (0, self.part, 0, 0)
-        )
-        shard = lax.psum_scatter(every.reshape(-1, width), SHARDED, scatter_dimension=0, tiled=True)
         return lax.psum(shard, "group").astype(f32)
+
+    def conv_pieces(self, conv_w):
+        if self.subs > 1:
+            return conv_w
+        columns = conv_w.shape[1]
+        wide = lax.dynamic_slice(conv_w, (0, self.part * DV), (CONV, DV))
+        narrow = self.head_columns_of(conv_w, DK)
+        return jnp.where(self.at_seq * self.cores + self.core >= 2 * HK // columns, wide, narrow)
+
+    def head_columns_of(self, array, head_width):
+        count = array.shape[1] // (self.group * head_width)
+        return jnp.concatenate(
+            [
+                lax.dynamic_slice(
+                    array,
+                    (0, (turn * self.group + self.part) * head_width),
+                    (array.shape[0], head_width),
+                )
+                for turn in range(count)
+            ],
+            axis=1,
+        )
+
+    def join_conv(self, pieces):
+        pieces = pieces.reshape(self.seq * self.cores, CONV, -1).transpose(1, 0, 2)
+        pieces = pieces.reshape(CONV, -1)
+        return self.head_columns(pieces, QKV) if self.subs > 1 else pieces
+
+    def split_conv(self, grad):
+        devices = self.seq * self.cores
+        if self.subs > 1:
+            pieces, begin = [], 0
+            mine = (jnp.arange(self.group) == self.part).astype(f32)[:, None]
+            for _, head_width in QKV:
+                end = begin + self.heads * head_width
+                section = grad[:, begin:end].reshape(CONV, self.heads, 1, head_width) * mine
+                pieces.append(section.reshape(CONV, -1))
+                begin = end
+            grad = jnp.concatenate(pieces, axis=1)
+        return grad.reshape(CONV, devices, -1).transpose(1, 0, 2).reshape(devices, -1)
+
+    def join_own_conv(self, parts):
+        parts = parts.reshape(self.group, CONV, -1)
+        if self.subs > 1:
+            return jnp.sum(parts, axis=0)
+        columns = parts.shape[2] * self.group
+        wide = parts.transpose(1, 0, 2).reshape(CONV, columns)
+        narrow = parts.reshape(self.group, CONV, -1, DK).transpose(1, 2, 0, 3).reshape(CONV, columns)
+        return jnp.where(self.at_seq * self.cores + self.core >= 2 * HK // columns, wide, narrow)
 
 
 QKV = ((0, DK), (HK, DK), (2 * HK, DV))
 GATE = ((2 * HK + HV, DV),)
 
 
-def segment_info(lane_lengths, length):
+def side_array(lane_lengths, length):
     ends = jnp.cumsum(lane_lengths)
     bounds = jnp.concatenate([jnp.zeros((1,), jnp.int32), ends])
-    places = jnp.arange(-(CONV - 1), length, dtype=jnp.int32)
-    segment = jnp.sum((places[:, None] >= bounds[None, :]).astype(jnp.int32), axis=1)
-    segment = jnp.where(places >= 0, segment, -1)
-    own_places = places[CONV - 1 :]
-    starts = jnp.any(own_places[:, None] == bounds[None, :], axis=1).astype(jnp.int32)
-    valid = (own_places < ends[-1]).astype(f32)
-    return (segment, starts, valid)
+    places = jnp.arange(length, dtype=jnp.int32)
+    crossed = places[:, None] >= bounds[None, :]
+    block_begin = (places // SPAN) * SPAN
+    counted = jnp.sum((crossed & (bounds[None, :] >= block_begin[:, None])).astype(jnp.int32), axis=1)
+    segment = jnp.sum(crossed.astype(jnp.int32), axis=1)
+    columns = [counted.astype(f32)]
+    for back in range(1, CONV):
+        earlier = jnp.sum((places[:, None] - back >= bounds[None, :]).astype(jnp.int32), axis=1)
+        columns.append(((earlier == segment) & (places >= back)).astype(f32))
+    columns.append((places < ends[-1]).astype(f32))
+    columns += [jnp.zeros((length,), f32)] * (SIDE - len(columns))
+    return jnp.stack(columns, axis=1)
 
 
 def shards(
@@ -571,20 +868,26 @@
     device_rows = w_down.shape[0]
     devices = at.seq * at.cores
 
-    small = (attn_gain, ffn_gain, o_gain, w_ab.reshape(-1), conv_w.reshape(-1))
-    packed = lax.all_gather(jnp.concatenate(small), SHARDED, axis=0).reshape(devices, -1)
+    at_device = at.at_seq * at.cores + at.core
+
+    ab_shard = at.head_columns(w_ab, ((0, 1), (H, 1)))
+    conv_pieces = at.conv_pieces(conv_w)
+    small = (attn_gain, ffn_gain, o_gain, ab_shard.reshape(-1), conv_pieces.reshape(-1))
+    lengths_small = [array.shape[0] for array in small]
+    filled = sum(lengths_small)
+    rows_small = -(-filled // (16 * 128)) * 16
+    packed = jnp.concatenate(small + (jnp.zeros((rows_small * 128 - filled,), bf16),))
+    packed = small_gather(packed.reshape(rows_small, 128), at.seq, at.cores).reshape(devices, -1)
     full, begin = [], 0
-    for array in small:
-        full.append(packed[:, begin : begin + array.shape[0]])
-        begin += array.shape[0]
+    for count in lengths_small:
+        full.append(packed[:, begin : begin + count])
+        begin += count
     attn_f, ffn_f, o_f = (array.reshape(-1).astype(f32) for array in full[:3])
-    ab_all = full[3].reshape(width, 2, heads, at.group)
-    ab_mine = lax.dynamic_slice(ab_all, (0, 0, 0, at.part), (width, 2, heads, 1)).reshape(width, -1)
-    conv_all = full[4].reshape(devices, CONV, -1).transpose(1, 0, 2).reshape(CONV, -1)
-    conv_mine = at.head_columns(conv_all, QKV).astype(f32)
+    ab_mine = full[3].reshape(width, 2 * heads)
+    conv_mine = at.join_conv(full[4]).astype(f32)
 
     def my_heads(values):
-        return lax.dynamic_slice(values.reshape(heads, at.group), (0, at.part), (heads, 1)).reshape(-1)
+        return lax.dynamic_slice(values.reshape(heads, at.group), (0, at.part), (heads, 1)).reshape(1, -1)
 
     decay_mine, dt_mine = my_heads(decay_log), my_heads(dt_bias)
 
@@ -598,95 +901,84 @@
     )
 
     member = (dealing[:, None] == jnp.arange(at.group, dtype=jnp.int32)[None, :]).astype(jnp.int32)
-    before = lax.dot_general(
-        jnp.tril(jnp.ones((rows, rows), f32), -1).astype(bf16),
-        member.astype(bf16),
-        (((1,), (0,)), ((), ())),
-        preferred_element_type=f32,
-    ).astype(jnp.int32)
+    before = dot(jnp.tril(jnp.ones((rows, rows), f32), -1).astype(bf16), member.astype(bf16))
+    before = before.astype(jnp.int32)
     target = jnp.sum((before + at.per * jnp.arange(at.group, dtype=jnp.int32)) * member, axis=1)
     sorting = (target[None, :] == jnp.arange(rows, dtype=jnp.int32)[:, None]).astype(bf16)
     dealt = at.deal(dot(sorting, jnp.concatenate([tokens, cotangent], axis=1)).astype(bf16))
     tokens_f = dealt[:, :width].astype(f32)
     cot_own = dealt[:, width:]
-    cot_all = at.gather_any(cot_own)
 
     lane_lengths = lax.dynamic_index_in_dim(
         at.gather_parts(lengths.reshape(-1)), at.at_seq // at.subs, 0, keepdims=False
     )
-    segment, starts, valid_lane = segment_info(lane_lengths, at.lane)
-    valid = at.to_own(valid_lane[:, None])
+    side = side_array(lane_lengths, at.lane)
     normed = rms_scale(tokens_f, attn_f).astype(bf16)
     normed_all = at.gather_places(normed)
-    conv_in = dot(normed_all, in_qkv).astype(bf16)
-    gates_ab = dot(normed_all, ab_mine)
-    out_gate = dot(normed_all, in_gate)
-    extended = jnp.pad(at.to_lane(conv_in), ((CONV - 1, 0), (0, 0))).astype(f32)
-    qkv_f, pull_conv = jax.vjp(
-        lambda extended_in, conv_in_w: mixer_inputs(heads, extended_in, conv_in_w, segment),
-        extended,
-        conv_mine,
-    )
-    qkv = qkv_f.astype(bf16)
-    (beta_rows, decay_rows), pull_decay = jax.vjp(decay_inputs, gates_ab, decay_mine, dt_mine)
-    cols, side_rows = side_arrays(at.to_lane(beta_rows), at.to_lane(decay_rows), starts)
-    mixed_lane, states, inverses, solved = mixer_forward(qkv, cols, side_rows)
-    mixed = at.to_own(mixed_lane) * valid
-    gated_f, pull_gate = jax.vjp(gated_norm, mixed, out_gate, o_f)
-    gated = gated_f.astype(bf16)
+    conv_in = at.to_lane(dot(normed_all, in_qkv).astype(bf16))
+    gates_ab = at.to_lane(dot(normed_all, ab_mine))
+    out_gate = at.to_lane(dot(normed_all, in_gate))
+    mixer_args = (conv_in, out_gate, gates_ab, side, conv_mine, o_f[None], decay_mine, dt_mine)
+    gated_lane, *kept = mixer_forward(*mixer_args)
+    gated = at.to_own(gated_lane)
     branch = at.reduce_places(dot(gated, out_mine))
     resid = tokens_f + branch
 
     normed2_f, pull_norm2 = jax.vjp(rms_scale, resid, ffn_f)
     normed2_all = at.gather_any(normed2_f.astype(bf16))
+    cot_all = at.gather_any(cot_own)
     gate_up = dot(normed2_all, gu_mine)
     hidden_f, pull_ffn = jax.vjp(swiglu, gate_up)
     hidden = hidden_f.astype(bf16)
-    output = (resid + at.reduce_any(dot(hidden, down_mine))).astype(bf16)
 
     d_hidden = dot_back(cot_all, down_mine)
     d_gate_up = pull_ffn(d_hidden)[0].astype(bf16)
-    d_down = dot_t(hidden, cot_all)
-    d_gu = dot_t(normed2_all, d_gate_up)
-    d_normed2 = at.reduce_any(dot_back(d_gate_up, gu_mine))
+    d_normed2_parts = dot_back(d_gate_up, gu_mine)
+    d_gu = dot_t(normed2_all, d_gate_up).astype(bf16)
+    d_down = dot_t(hidden, cot_all).astype(bf16)
+    d_normed2_parts, d_gu, d_down = lax.optimization_barrier((d_normed2_parts, d_gu, d_down))
+    gu_shard = lax.psum_scatter(d_gu, SHARDED, scatter_dimension=0, tiled=True)
+    down_shard = lax.psum_scatter(d_down, SHARDED, scatter_dimension=0, tiled=True)
+    d_normed2 = at.reduce_any(d_normed2_parts)
+    output_parts = dot(hidden, down_mine)
     d_resid_norm, d_ffn_gain = pull_norm2(d_normed2)
     d_resid = cot_own.astype(f32) + d_resid_norm
-    down_shard = lax.psum_scatter(d_down.astype(bf16), SHARDED, scatter_dimension=0, tiled=True)
-    gu_shard = lax.psum_scatter(d_gu.astype(bf16), SHARDED, scatter_dimension=0, tiled=True)
 
     d_branch_all = at.gather_places(d_resid.astype(bf16))
     d_gated = dot_back(d_branch_all, out_mine)
-    grad_w_out = at.out_rows_back(dot_t(gated, d_branch_all))
-    d_mixed, d_out_gate, d_o_gain = pull_gate(d_gated)
-    d_gate_cols = d_out_gate.astype(bf16)
-    gate_shard = lax.psum_scatter(
-        dot_t(normed_all, d_gate_cols).astype(bf16), SHARDED, scatter_dimension=0, tiled=True
-    )
-    d_qkv, d_cols = mixer_backward(
-        qkv, cols, side_rows, states, inverses, solved, at.to_lane(d_mixed * valid)
-    )
-    d_beta = at.to_own(d_cols[:, :heads])
-    d_decay = at.to_own(decay_back(d_cols[:, heads : 2 * heads]))
-    d_extended, d_conv_w = pull_conv(d_qkv)
-    d_conv_w = d_conv_w * (at.sub == 0).astype(f32)
-    d_conv_in = at.to_own(d_extended[CONV - 1 :]).astype(bf16)
-    d_gates_ab, d_decay_log, d_dt_bias = pull_decay((d_beta, d_decay))
-    d_ab = d_gates_ab.astype(bf16)
-    d_in = dot_t(normed_all, d_conv_in)
+    d_out = dot_t(gated, d_branch_all).astype(bf16)
+    d_gated, d_out, output_parts = lax.optimization_barrier((d_gated, d_out, output_parts))
+    output = (resid + at.reduce_any(output_parts)).astype(bf16)
+    out_shard = at.out_rows_scatter(d_out)
+    d_conv_lane, d_gate_lane, d_gates_lane, d_conv_w, d_o_gain, d_heads = mixer_backward(
+        *mixer_args, tuple(kept), at.to_lane(d_gated)
+    )
+    once = (at.sub == 0).astype(f32)
+    d_conv_w, d_o_gain, d_heads = d_conv_w * once, d_o_gain * once, d_heads * once
+    d_conv_in = at.to_own(d_conv_lane)
+    d_gate = at.to_own(d_gate_lane)
+    d_ab = at.to_own(d_gates_lane).astype(bf16)
+    d_in_gate = dot_t(normed_all, d_gate).astype(bf16)
+    d_in = dot_t(normed_all, d_conv_in).astype(bf16)
+    d_in, d_in_gate, d_conv_in, d_gate, d_ab = lax.optimization_barrier(
+        (d_in, d_in_gate, d_conv_in, d_gate, d_ab)
+    )
+    in_shard = lax.psum_scatter(d_in, SHARDED, scatter_dimension=0, tiled=True)
+    gate_shard = lax.psum_scatter(d_in_gate, SHARDED, scatter_dimension=0, tiled=True)
     d_w_ab = dot_t(normed_all, d_ab)
     d_normed = at.reduce_places(
-        dot_back(d_conv_in, in_qkv) + dot_back(d_gate_cols, in_gate) + dot_back(d_ab, ab_mine)
+        dot_back(d_conv_in, in_qkv) + dot_back(d_gate, in_gate) + dot_back(d_ab, ab_mine)
     )
     value_norm, pull_norm = jax.vjp(rms_scale, tokens_f, attn_f)
     d_tokens_norm, d_attn_gain = pull_norm(d_normed)
     d_tokens = (d_resid + d_tokens_norm).astype(bf16)
-    in_shard = lax.psum_scatter(d_in.astype(bf16), SHARDED, scatter_dimension=0, tiled=True)
 
     returned = at.undeal(jnp.concatenate([output, d_tokens], axis=1))
     returned = dot_t(sorting, returned).astype(bf16)
 
+    grad_w_gu = at.join_hidden(at.gather_parts(gu_shard), device_rows).astype(f32)
     grad_w_down = at.gather_parts(down_shard).reshape(device_rows, width).astype(f32)
-    grad_w_gu = at.join_hidden(at.gather_parts(gu_shard), device_rows).astype(f32)
+    grad_w_out = at.out_rows_join(out_shard)
     grad_w_in = jnp.concatenate(
         [
             at.join_heads(at.gather_parts(in_shard), QKV),
@@ -695,51 +987,43 @@
         axis=1,
     ).astype(f32)
 
-    mine = (jnp.arange(at.group) == at.part).astype(f32)
-
-    def own_columns(array, piece_width):
-        count = array.shape[0]
-        spread = array.reshape(count, heads, 1, piece_width) * mine[:, None]
-        return spread.reshape(count, -1)
-
-    conv_parts = [
-        own_columns(d_conv_w[:, : heads * DK], DK),
-        own_columns(d_conv_w[:, heads * DK : 2 * heads * DK], DK),
-        own_columns(d_conv_w[:, 2 * heads * DK :], DV),
-    ]
-    totals = (
-        d_attn_gain,
-        d_ffn_gain,
-        d_o_gain,
-        jnp.concatenate(conv_parts, axis=1).reshape(-1),
-        own_columns(d_w_ab.reshape(-1, heads), 1).reshape(-1),
-        own_columns(d_decay_log[None], 1).reshape(-1),
-        own_columns(d_dt_bias[None], 1).reshape(-1),
-    )
-    sizes = [array.shape[0] for array in totals]
-    summed = lax.psum(jnp.concatenate(totals), ("group", "seq", "wshard"))
+    def to_blocks(array):
+        return array.reshape(devices, -1)
+
+    blocks = (
+        to_blocks(d_attn_gain),
+        to_blocks(d_ffn_gain),
+        to_blocks(d_o_gain),
+        to_blocks(d_w_ab),
+        at.split_conv(d_conv_w),
+        jnp.broadcast_to(d_heads, (devices, 2 * heads)),
+    )
+    sizes = [array.shape[1] for array in blocks]
+    filled = sum(sizes)
+    rows_small = -(-filled // 1024) * 8
+    packed = jnp.concatenate(
+        blocks + (jnp.zeros((devices, rows_small * 128 - filled), f32),), axis=1
+    )
+    summed = small_sum(packed.reshape(devices, rows_small, 128), at.seq, at.cores, at.group)
+    summed = summed.reshape(at.group, -1)
     parts, begin = [], 0
     for size in sizes:
-        parts.append(summed[begin : begin + size])
+        parts.append(summed[:, begin : begin + size])
         begin += size
-    me = at.at_seq * at.cores + at.core
-
-    def own_rows(array, axis=0):
-        count = array.shape[axis] // devices
-        return lax.dynamic_slice_in_dim(array, me * count, count, axis)
-
+    grad_w_ab = parts[3].reshape(at.group, width // devices, 2, heads).transpose(1, 2, 3, 0)
+    grad_heads = parts[5].reshape(at.group, 2, heads).transpose(1, 2, 0).reshape(2, H)
     return (
         returned[:, :width],
         returned[:, width:],
-        own_rows(parts[0]),
+        jnp.sum(parts[0], axis=0),
         grad_w_in,
-        own_rows(parts[4].reshape(width, 2 * H)),
-        own_rows(parts[3].reshape(CONV, -1), 1),
-        parts[5],
-        parts[6],
-        own_rows(parts[2]),
+        grad_w_ab.reshape(width // devices, 2 * H),
+        at.join_own_conv(parts[4]),
+        grad_heads[0],
+        grad_heads[1],
+        jnp.sum(parts[2], axis=0),
         grad_w_out,
-        own_rows(parts[1]),
+        jnp.sum(parts[1], axis=0),
         grad_w_gu,
         grad_w_down,
     )

time: 1450 us -> 1100 us (0.76)
  waiting for transfers between devices: 676 us -> 436 us
  local copies, waits for them, and re-layouts: 277 us -> 149 us
  Pallas kernels: 95.9 us -> 207 us
  other arithmetic: 145 us -> 65.5 us
    reduce_scatter x5, waiting for transfers between devices: 222 us -> 27.2 us  [the longest x1 27.1 us: shards(): gu_shard = lax.psum_scatter(d_gu, SHARDED, scatter_dimension=0, tiled=True)]
    pallas_call x0 -> x2, Pallas kernels: none -> 95.4 us  [the longest x1 50.5 us: small_gather(): pl.pallas_call(functools.partial(small_gather_kernel, seq, cores), out_sh...]
    psum x1 -> x0, waiting for transfers between devices: 75 us -> none  [shards(): summed = lax.psum(jnp.concatenate(totals), ('group', 'seq', 'wshard'))]
    ppermute x42, waiting for transfers between devices: 299 us -> 346 us  [swap(): lax.ppermute(value, 'group', [(i, i ^ turn) for i in range(self.group)])]
    all_to_all x1, waiting for transfers between devices: 37.3 us -> 0.01 us  [deal(): lax.all_to_all(sorted_rows, 'seq', split_axis=0, concat_axis=0, tiled=True)]
    all_gather x1, waiting for transfers between devices: 0.01 us -> 35.2 us  [shards(): lax.all_gather(lax.dynamic_slice(w_down, (at.part * piece, 0), (piece, wi...]
    mul x14 -> x1, other arithmetic: 32.6 us -> 0.01 us  [side_array(): block_begin = places // SPAN * SPAN]
    reshape x12 -> x11, local copies, waits for them, and re-layouts: 30.1 us -> 5.88 us  [the longest x1 2.56 us: shards(): parts[3].reshape(at.group, width // devices, 2, heads).transpose(1, 2, 3, 0)]
  transfers between devices with their start and end apart: 58 -> 56, of which waited for: 32 -> 30; matrix products, arithmetic and copies ran while one was open for 26% -> 21% of each run, Pallas kernels for 3% -> 19%
where the time goes in v2:
time: 1100 us
  waiting for transfers between devices  436 us (40%)
  Pallas kernels  207 us (19%)
  matrix products  163 us (15%)
  local copies, waits for them, and re-layouts  149 us (14%)
  other arithmetic  65.5 us (6%)
  starting transfers between devices  59.5 us (5%)
  between operations  16 us (1%)
    ppermute x42, waiting for transfers between devices, swap(): lax.ppermute(value, 'group', [(i, i ^ turn) for i in range(self.group)])  346 us
    unnamed x129, local copies, waits for them, and re-layouts  60.5 us
    pallas_call x1, Pallas kernels, mixer_backward(): pl.pallas_call(functools.partial(mixer_backward_kernel, heads), grid=(blo...  60.4 us
    dot_general x8, matrix products, dot(): return jnp.dot(left, right, preferred_element_type=f32)  55.3 us
    dot_general x6, matrix products, dot_back(): lax.dot_general(left, right, (((1,), (1,)), ((), ())), preferred_element_...  54.6 us
    dot_general x7, matrix products, dot_t(): lax.dot_general(left, right, (((0,), (0,)), ((), ())), preferred_element_...  52.9 us
    pallas_call x1, Pallas kernels, mixer_forward(): pl.pallas_call(functools.partial(mixer_forward_kernel, heads), grid=(bloc...  51.3 us
    pallas_call x1, Pallas kernels, small_gather(): pl.pallas_call(functools.partial(small_gather_kernel, seq, cores), out_sh...  50.5 us
  transfers between devices with their start and end apart: 56, of which 30 were waited for; matrix products, arithmetic and copies ran while one was open for 21% of the time, Pallas kernels for 19%

profile of v2, /device:TPU:0, one launch (start us, length us, event | category | flops | bytes accessed | tf_op | source)
XLA Modules:
  0.0 1095.7 jit_solution(11983790828827273823)
XLA Ops:
  60.1 50.5 %small_gather.1 = bf16[8,32,128]{2,1,0:T(8,128)(2,1)} custom-call(bf16[32,128]{1,0:T(8,128)(2,1)} %bitcast.286), custom_call_target="tpu_custom_call" | custom-call | tf_op jit(solution)/shard_map/small_gather/pallas_call | solution.py:502
  137.9 16.6 %collective-permute-done.1 = bf16[192,2048]{1,0:T(8,128)(2,1)} collective-permute-done((bf16[192,2048]{1,0:T(8,128)(2,1)S(1)}, bf16[192,2048]{1,0:T(8,128)(2,1)}, u32[]{:S(2)}, u32[]{:S(2)}) %collective-permute-start.1) | collective-permute-done | bytes 786464 | tf_op jit(solution)/shard_map/ppermute | solution.py:644
  167.9 16.5 %all-gather.6.cloned.1.call-done = bf16[2048,2048]{1,0:T(8,128)(2,1)} async-done(((bf16[256,2048]{1,0:T(8,128)(2,1)}), bf16[2048,2048]{1,0:T(8,128)(2,1)}) %all-gather.6.cloned.1.call-update) | async-done | bytes 8388624 | tf_op jit(solution)/shard_map/all_gather | solution.py:894
  196.4 51.3 %mixer_forward.1 = (bf16[768,1024]{1,0:T(8,128)(2,1)S(1)}, f32[768,1024]{1,0:T(8,128)}, bf16[768,2048]{1,0:T(8,128)(2,1)}, f32[12,4,128,256]{3,2,1,0:T(8,128)}, ...) custom-call(bf16[768,2048]{1,0:T(8,128)(2,1)} %convolution_convert_fusion.7.conv_ref.ahead_ref, ...), custom_call_target="tpu_custom_call" | custom-call | tf_op jit(solution)/shard_map/mixer_forward/pallas_call | solution.py:371
  258.8 17.7 %collective-permute-done.9 = bf16[192,2048]{1,0:T(8,128)(2,1)S(1)} collective-permute-done((bf16[192,2048]{1,0:T(8,128)(2,1)S(1)}, bf16[192,2048]{1,0:T(8,128)(2,1)S(1)}, u32[]{:S(2)}, u32[]{:S(2)}) %collective-permute-start.9) | collective-permute-done | bytes 786464 | tf_op jit(solution)/shard_map/ppermute | solution.py:644
  276.4 16.1 %collective-permute-done.8 = bf16[192,2048]{1,0:T(8,128)(2,1)S(1)} collective-permute-done((bf16[192,2048]{1,0:T(8,128)(2,1)S(1)}, bf16[192,2048]{1,0:T(8,128)(2,1)S(1)}, u32[]{:S(2)}, u32[]{:S(2)}) %collective-permute-start.8) | collective-permute-done | bytes 786464 | tf_op jit(solution)/shard_map/ppermute | solution.py:644
  318.7 15.4 %collective-permute-done.11 = bf16[192,2048]{1,0:T(8,128)(2,1)S(1)} collective-permute-done((bf16[192,2048]{1,0:T(8,128)(2,1)S(1)}, bf16[192,2048]{1,0:T(8,128)(2,1)S(1)}, u32[]{:S(2)}, u32[]{:S(2)}) %collective-permute-start.11) | collective-permute-done | bytes 786464 | tf_op jit(solution)/shard_map/ppermute | solution.py:644
  341.5 17.8 %fusion.24 = f32[768,2816]{1,0:T(8,128)} fusion(bf16[2048,2816]{0,1:T(8,128)(2,1)} %all-gather.12.cloned.1.call-done, bf16[192,2048]{1,0:T(8,128)(2,1)} %copy-done.43, bf16[192,2048]{1,0:T(8,128)(2,1)} %copy-done.45, bf16[192,2048]{1,0:T(8,128)(2,1)} %collective-permute-done.10, bf16[192,2048]{1,0:T(8,128)(2,1)} %copy-done.23), kind=kOutput, calls=%fused_computation.73 | convolution fusion | flops 8870952960 | bytes 23330816 | tf_op jit(solution)/shard_map/dot_general | solution.py:583
  367.1 35.2 %all-gather.14.cloned.1.call-done = bf16[1408,2048]{1,0:T(8,128)(2,1)} async-done(((bf16[176,2048]{1,0:T(8,128)(2,1)}), bf16[1408,2048]{1,0:T(8,128)(2,1)}) %all-gather.14.cloned.1.call-update) | async-done | bytes 5767184 | tf_op jit(solution)/shard_map/all_gather | solution.py:899
  416.5 16.8 %fusion.22 = f32[768,2048]{1,0:T(8,128)} fusion(bf16[2048,2816]{0,1:T(8,128)(2,1)} %all-gather.12.cloned.1.call-done, f32[768,1408]{1,0:T(8,128)} %get-tuple-element.124, f32[768,1408]{1,0:T(8,128)} %get-tuple-element.123), kind=kOutput, calls=%fused_computation.71 | convolution fusion | flops 8862695424 | bytes 26476544 | tf_op jit(solution)/shard_map/dot_general | solution.py:591
  433.3 16.0 %convolution_convert_fusion = bf16[2048,2816]{1,0:T(8,128)(2,1)} fusion(f32[768,1408]{1,0:T(8,128)} %get-tuple-element.124, f32[768,1408]{1,0:T(8,128)} %get-tuple-element.123, bf16[192,2048]{1,0:T(8,128)(2,1)S(1)} %copy-done.44, bf16[192,2048]{1,0:T(8,128)(2,1)S(1)} %copy-done.46, bf16[192,2048]{1,0:T(8,128)(2,1)} %collective-permute-done.10, ...), kind=kOutput, calls=%fused_computation.1 | convolution fusion | flops 8881045504 | bytes 23330816 | tf_op jit(solution)/shard_map/dot_general | solution.py:587
  466.1 17.8 %collective-permute-done.18 = bf16[192,2048]{1,0:T(8,128)(2,1)S(1)} collective-permute-done((bf16[192,2048]{1,0:T(8,128)(2,1)S(1)}, bf16[192,2048]{1,0:T(8,128)(2,1)S(1)}, u32[]{:S(2)}, u32[]{:S(2)}) %collective-permute-start.18) | collective-permute-done | bytes 786464 | tf_op jit(solution)/shard_map/ppermute | solution.py:644
  484.0 16.1 %collective-permute-done.17 = bf16[192,2048]{1,0:T(8,128)(2,1)S(1)} collective-permute-done((bf16[192,2048]{1,0:T(8,128)(2,1)S(1)}, bf16[192,2048]{1,0:T(8,128)(2,1)S(1)}, u32[]{:S(2)}, u32[]{:S(2)}) %collective-permute-start.17) | collective-permute-done | bytes 786464 | tf_op jit(solution)/shard_map/ppermute | solution.py:644
  525.3 17.0 %collective-permute-done.20 = bf16[192,2048]{1,0:T(8,128)(2,1)S(1)} collective-permute-done((bf16[192,2048]{1,0:T(8,128)(2,1)S(1)}, bf16[192,2048]{1,0:T(8,128)(2,1)S(1)}, u32[]{:S(2)}, u32[]{:S(2)}) %collective-permute-start.20) | collective-permute-done | bytes 786464 | tf_op jit(solution)/shard_map/ppermute | solution.py:644
  557.6 60.4 %mixer_backward.1 = (bf16[768,2048]{1,0:T(8,128)(2,1)}, bf16[768,1024]{1,0:T(8,128)(2,1)S(1)}, f32[768,8]{1,0:T(8,128)S(1)}, f32[4,2048]{1,0:T(4,128)S(1)}, f32[1,256]{1,0:T(1,128)S(1)}, /*index=5*/f32[1,8]{1,0:T(1,128)S(1)}) custom-call(bf16[768,2048]{1,0:T(8,128)(2,1)} %convolution_convert_fusion.7.conv_ref.ahead_ref, ...), custom_call_target="tpu_custom_call" | custom-call | tf_op jit(solution)/shard_map/mixer_backward/pallas_call | solution.py:413
  663.2 15.4 %collective-permute-done.27 = bf16[192,2048]{1,0:T(8,128)(2,1)S(1)} collective-permute-done((bf16[192,2048]{1,0:T(8,128)(2,1)S(1)}, bf16[192,2048]{1,0:T(8,128)(2,1)S(1)}, u32[]{:S(2)}, u32[]{:S(2)}) %collective-permute-start.27) | collective-permute-done | bytes 786464 | tf_op jit(solution)/shard_map/ppermute | solution.py:644
  679.2 16.3 %collective-permute-done.26 = bf16[192,2048]{1,0:T(8,128)(2,1)S(1)} collective-permute-done((bf16[192,2048]{1,0:T(8,128)(2,1)S(1)}, bf16[192,2048]{1,0:T(8,128)(2,1)S(1)}, u32[]{:S(2)}, u32[]{:S(2)}) %collective-permute-start.26) | collective-permute-done | bytes 786464 | tf_op jit(solution)/shard_map/ppermute | solution.py:644
  743.4 45.0 %small_sum.1 = f32[4,32,128]{2,1,0:T(8,128)} custom-call(f32[8,32,128]{2,1,0:T(8,128)} %bitcast.262), custom_call_target="tpu_custom_call" | custom-call | tf_op jit(solution)/shard_map/small_sum/pallas_call | solution.py:556
  813.4 34.7 %collective-permute-done.35 = bf16[128,2048]{1,0:T(8,128)(2,1)S(1)} collective-permute-done((bf16[128,2048]{1,0:T(8,128)(2,1)}, bf16[128,2048]{1,0:T(8,128)(2,1)S(1)}, u32[]{:S(2)}, u32[]{:S(2)}) %collective-permute-start.35) | collective-permute-done | bytes 524320 | tf_op jit(solution)/shard_map/ppermute | solution.py:644
  881.7 14.9 %collective-permute-done.42 = bf16[176,2048]{1,0:T(8,128)(2,1)S(1)} collective-permute-done((bf16[176,2048]{1,0:T(8,128)(2,1)}, bf16[176,2048]{1,0:T(8,128)(2,1)S(1)}, u32[]{:S(2)}, u32[]{:S(2)}) %collective-permute-start.42) | collective-permute-done | bytes 720928 | tf_op jit(solution)/shard_map/ppermute | solution.py:644
  924.7 20.9 %collective-permute-done.29 = bf16[256,2048]{1,0:T(8,128)(2,1)} collective-permute-done((bf16[256,2048]{1,0:T(8,128)(2,1)}, bf16[256,2048]{1,0:T(8,128)(2,1)}, u32[]{:S(2)}, u32[]{:S(2)}) %collective-permute-start.29) | collective-permute-done | bytes 1048608 | tf_op jit(solution)/shard_map/ppermute | solution.py:644
  959.5 27.1 %reduce-scatter.12.cloned.1.call-done = bf16[256,2816]{1,0:T(8,128)(2,1)} async-done(((bf16[2048,2816]{1,0:T(8,128)(2,1)}), bf16[256,2816]{1,0:T(8,128)(2,1)}) %reduce-scatter.12.cloned.1.call-update) | async-done | bytes 1441808 | tf_op jit(solution)/shard_map/reduce_scatter | solution.py:940
  990.2 19.2 %maximum_convert_fusion = f32[256,12288]{0,1:T(8,128)} fusion(bf16[256,4096]{0,1:T(8,128)(2,1)S(1)} %bitcast.231, bf16[256,4096]{0,1:T(8,128)(2,1)} %bitcast.232, bf16[256,2048]{0,1:T(8,128)(2,1)} %bitcast.237, bf16[256,2048]{0,1:T(8,128)(2,1)} %bitcast.238), kind=kLoop, calls=%fused_computation.6 | loop fusion | flops 25165824 | bytes 18874368 | tf_op jit(solution)/shard_map/convert_element_type | solution.py:988
  1028.5 21.7 %collective-permute-done.39 = bf16[256,2816]{1,0:T(8,128)(2,1)} collective-permute-done((bf16[256,2816]{1,0:T(8,128)(2,1)}, bf16[256,2816]{1,0:T(8,128)(2,1)}, u32[]{:S(2)}, u32[]{:S(2)}) %collective-permute-start.39) | collective-permute-done | bytes 1441824 | tf_op jit(solution)/shard_map/ppermute | solution.py:644
  (416 shorter events, 483.3 us)
Async XLA Ops:
  7.2 152.4 %all-gather.8.cloned.1.call-start = ((), (), s32[]{:S(2)}) async-start(), calls=%async_computation.8 | async-start | bytes 4718592 | tf_op jit(solution)/shard_map/all_gather | solution.py:895
  26.7 157.7 %all-gather.6.cloned.1.call-start = ((), (), s32[]{:S(2)}) async-start(), calls=%async_computation.7 | async-start | bytes 9437184 | tf_op jit(solution)/shard_map/all_gather | solution.py:894
  27.4 221.6 %all-gather.10.cloned.1.call-start = ((), (), s32[]{:S(2)}) async-start(), calls=%async_computation.9 | async-start | bytes 4718592 | tf_op jit(solution)/shard_map/all_gather | solution.py:748
  32.9 308.6 %all-gather.12.cloned.1.call-start = ((), (), s32[]{:S(2)}) async-start(), calls=%async_computation.10 | async-start | bytes 12976128 | tf_op jit(solution)/shard_map/all_gather | solution.py:897
  47.9 65.4 %all-to-all-start = ((bf16[4,48,4096]{2,1,0:T(8,128)(2,1)}), bf16[4,48,4096]{2,1,0:T(8,128)(2,1)}, u32[]{:S(2)}, u32[]{:S(2)}) async-start(bf16[4,48,4096]{2,1,0:T(8,128)(2,1)} %bitcast.248), calls=%async_computation | async-start | bytes 3145728 | tf_op jit(solution)/shard_map/all_to_all | solution.py:616
  54.3 347.9 %all-gather.14.cloned.1.call-start = ((), (), s32[]{:S(2)}) async-start(), calls=%async_computation.11 | async-start | bytes 6488064 | tf_op jit(solution)/shard_map/all_gather | solution.py:899
  54.3 58.4 %collective-permute-start.3 = (s32[4]{0:T(128)S(1)}, s32[4]{0:T(128)S(1)}, u32[]{:S(2)}, u32[]{:S(2)}) collective-permute-start(s32[4]{0:T(128)S(1)} %bitcast.289), channel_id=1, source_target_pairs={{0,8},{8,0},{16,24},{24,16},{1,9},{9,1},{17,25},{25,17},{2,10},{10... | collective-permute-start | bytes 56 | tf_op jit(solution)/shard_map/ppermute | solution.py:644
  55.9 56.9 %collective-permute-start.4 = (s32[4]{0:T(128)S(1)}, s32[4]{0:T(128)S(1)}, u32[]{:S(2)}, u32[]{:S(2)}) collective-permute-start(s32[4]{0:T(128)S(1)} %bitcast.290), channel_id=1, source_target_pairs={{0,16},{8,24},{16,0},{24,8},{1,17},{9,25},{17,1},{25,9},{2,18},{10... | collective-permute-start | bytes 56 | tf_op jit(solution)/shard_map/ppermute | solution.py:644
  57.6 55.3 %collective-permute-start.5 = (s32[4]{0:T(128)S(1)}, s32[4]{0:T(128)S(1)}, u32[]{:S(2)}, u32[]{:S(2)}) collective-permute-start(s32[4]{0:T(128)S(1)} %bitcast.291), channel_id=1, source_target_pairs={{0,24},{8,16},{16,8},{24,0},{1,25},{9,17},{17,9},{25,1},{2,26},{10... | collective-permute-start | bytes 56 | tf_op jit(solution)/shard_map/ppermute | solution.py:644
  58.9 738.5 %reduce-scatter.10.cloned.1.call-start = ((), (), s32[]{:S(2)}) async-start(), calls=%async_computation.14 | async-start | bytes 4718592 | tf_op jit(solution)/shard_map/reduce_scatter | solution.py:757
  301.5 57.9 %collective-permute-start.15 = (bf16[192,2048]{1,0:T(8,128)(2,1)}, bf16[192,2048]{1,0:T(8,128)(2,1)}, u32[]{:S(2)}, u32[]{:S(2)}) collective-permute-start(bf16[192,2048]{1,0:T(8,128)(2,1)} %slice.138), channel_id=1, source_target_pairs={{0,24},{8,16},{16,8},{24,0},{1,25},{9,17},{17,9},{25,1},{2,26},{10... | collective-permute-start | bytes 2359304 | tf_op jit(solution)/shard_map/ppermute | solution.py:644
  303.1 63.8 %collective-permute-start.14 = (bf16[192,2048]{1,0:T(8,128)(2,1)}, bf16[192,2048]{1,0:T(8,128)(2,1)}, u32[]{:S(2)}, u32[]{:S(2)}) collective-permute-start(bf16[192,2048]{1,0:T(8,128)(2,1)} %slice.138), channel_id=1, source_target_pairs={{0,16},{8,24},{16,0},{24,8},{1,17},{9,25},{17,1},{25,9},{2,18},{10... | collective-permute-start | bytes 2359304 | tf_op jit(solution)/shard_map/ppermute | solution.py:644
  557.5 242.4 %reduce-scatter.8.cloned.1.call-start = ((), (), s32[]{:S(2)}) async-start(), calls=%async_computation.13 | async-start | bytes 4718592 | tf_op jit(solution)/shard_map/reduce_scatter | solution.py:967
  635.5 227.0 %reduce-scatter.14.cloned.1.call-start = ((), (), s32[]{:S(2)}) async-start(), calls=%async_computation.16 | async-start | bytes 6488064 | tf_op jit(solution)/shard_map/reduce_scatter | solution.py:941
  636.3 260.5 %reduce-scatter.6.cloned.1.call-start = ((), (), s32[]{:S(2)}) async-start(), calls=%async_computation.12 | async-start | bytes 9437184 | tf_op jit(solution)/shard_map/reduce_scatter | solution.py:966
  637.0 349.7 %reduce-scatter.12.cloned.1.call-start = ((), (), s32[]{:S(2)}) async-start(), calls=%async_computation.15 | async-start | bytes 12976128 | tf_op jit(solution)/shard_map/reduce_scatter | solution.py:940
  661.0 51.4 %collective-permute-start.24 = (bf16[192,2048]{1,0:T(8,128)(2,1)S(1)}, bf16[192,2048]{1,0:T(8,128)(2,1)S(1)}, u32[]{:S(2)}, u32[]{:S(2)}) collective-permute-start(bf16[192,2048]{1,0:T(8,128)(2,1)S(1)} %get-tuple-element.142), channel_id=1, source_target_pairs={{0,24},{8,16},{16,8},{24,0},{1,25},{9,17},{17,9},{25,1},{2,26},{10... | collective-permute-start | bytes 2359304 | tf_op jit(solution)/shard_map/ppermute | solution.py:644
  662.5 64.4 %collective-permute-start.23 = (bf16[192,2048]{1,0:T(8,128)(2,1)S(1)}, bf16[192,2048]{1,0:T(8,128)(2,1)S(1)}, u32[]{:S(2)}, u32[]{:S(2)}) collective-permute-start(bf16[192,2048]{1,0:T(8,128)(2,1)S(1)} %get-tuple-element.143), channel_id=1, source_target_pairs={{0,16},{8,24},{16,0},{24,8},{1,17},{9,25},{17,1},{25,9},{2,18},{10... | collective-permute-start | bytes 2359304 | tf_op jit(solution)/shard_map/ppermute | solution.py:644
  731.8 66.3 %all-to-all-start.1 = ((bf16[4,48,4096]{2,1,0:T(8,128)(2,1)}), bf16[4,48,4096]{2,1,0:T(8,128)(2,1)S(1)}, u32[]{:S(2)}, u32[]{:S(2)}) async-start(bf16[4,48,4096]{2,1,0:T(8,128)(2,1)} %bitcast.235), calls=%async_computation.1 | async-start | bytes 3145728 | tf_op jit(solution)/shard_map/all_to_all | solution.py:631
  799.9 53.2 %collective-permute-start.31 = (bf16[256,1024]{1,0:T(8,128)(2,1)}, bf16[256,1024]{1,0:T(8,128)(2,1)}, u32[]{:S(2)}, u32[]{:S(2)}) collective-permute-start(bf16[256,1024]{1,0:T(8,128)(2,1)} %reduce-scatter.8.cloned.1.call-done), channel_id=1, source_target_pairs={{0,8},{8,0},{16,24},{24,16},{1,9},{9,1},{17,25},{25,17},{2,10},{10... | collective-permute-start | bytes 1572872 | tf_op jit(solution)/shard_map/ppermute | solution.py:644
  801.2 53.2 %collective-permute-start.32 = (bf16[256,1024]{1,0:T(8,128)(2,1)}, bf16[256,1024]{1,0:T(8,128)(2,1)}, u32[]{:S(2)}, u32[]{:S(2)}) collective-permute-start(bf16[256,1024]{1,0:T(8,128)(2,1)} %reduce-scatter.8.cloned.1.call-done), channel_id=1, source_target_pairs={{0,16},{8,24},{16,0},{24,8},{1,17},{9,25},{17,1},{25,9},{2,18},{10... | collective-permute-start | bytes 1572872 | tf_op jit(solution)/shard_map/ppermute | solution.py:644
  802.0 53.6 %collective-permute-start.33 = (bf16[256,1024]{1,0:T(8,128)(2,1)}, bf16[256,1024]{1,0:T(8,128)(2,1)}, u32[]{:S(2)}, u32[]{:S(2)}) collective-permute-start(bf16[256,1024]{1,0:T(8,128)(2,1)} %reduce-scatter.8.cloned.1.call-done), channel_id=1, source_target_pairs={{0,24},{8,16},{16,8},{24,0},{1,25},{9,17},{17,9},{25,1},{2,26},{10... | collective-permute-start | bytes 1572872 | tf_op jit(solution)/shard_map/ppermute | solution.py:644
  988.1 62.1 %collective-permute-start.39 = (bf16[256,2816]{1,0:T(8,128)(2,1)}, bf16[256,2816]{1,0:T(8,128)(2,1)}, u32[]{:S(2)}, u32[]{:S(2)}) collective-permute-start(bf16[256,2816]{1,0:T(8,128)(2,1)} %reduce-scatter.12.cloned.1.call-done), channel_id=1, source_target_pairs={{0,16},{8,24},{16,0},{24,8},{1,17},{9,25},{17,1},{25,9},{2,18},{10... | collective-permute-start | bytes 4325384 | tf_op jit(solution)/shard_map/ppermute | solution.py:644
  989.6 62.3 %collective-permute-start.40 = (bf16[256,2816]{1,0:T(8,128)(2,1)}, bf16[256,2816]{1,0:T(8,128)(2,1)}, u32[]{:S(2)}, u32[]{:S(2)}) collective-permute-start(bf16[256,2816]{1,0:T(8,128)(2,1)} %reduce-scatter.12.cloned.1.call-done), channel_id=1, source_target_pairs={{0,24},{8,16},{16,8},{24,0},{1,25},{9,17},{17,9},{25,1},{2,26},{10... | collective-permute-start | bytes 4325384 | tf_op jit(solution)/shard_map/ppermute | solution.py:644
  (85 other events, 2035.0 us)
Sparse Core Ops, SparseCore 0:
  26.8 66.5 all-gather.7
  95.6 88.7 all-gather.5
  186.6 45.6 all-gather.9
  234.3 107.2 all-gather.11
  343.6 58.6 all-gather.13
  557.7 47.8 reduce-scatter.9
  635.6 47.7 reduce-scatter.7
  686.3 70.4 reduce-scatter.13
  759.7 106.4 reduce-scatter.5
  868.9 117.6 reduce-scatter.11

commit v3 on v2

--- a/solution.py
+++ b/solution.py
@@ -16,6 +16,7 @@
 HK = 2048
 HV = 4096
 SIDE = 16
+EDGE = 32
 
 bf16 = jnp.bfloat16
 f32 = jnp.float32
@@ -31,37 +32,68 @@
     return high, (value - high.astype(f32)).astype(bf16)
 
 
-def mm_right(left, right, over=((1,), (0,))):
-    high, low = halves(right)
-    return mm(left, high, over) + mm(left, low, over)
-
-
-def mm_both(left, right, over=((1,), (0,))):
+def mm_fine(left, right):
     left_high, left_low = halves(left)
     right_high, right_low = halves(right)
-    return (
-        mm(left_high, right_high, over)
-        + mm(left_low, right_high, over)
-        + mm(left_high, right_low, over)
-    )
+    return mm(left_high, right_high) + mm(left_low, right_high) + mm(left_high, right_low)
+
+
+def mm_right(left, right, over=((1,), (0,))):
+    return mm(left, right.astype(bf16), over)
+
+
+def mm_both(left, right, over=((1,), (0,))):
+    return mm(left.astype(bf16), right.astype(bf16), over)
 
 
 ROWS = ((1,), (1,))
 COLS = ((0,), (0,))
 
 
-def unit_lower_inverse(strict):
-    parts = SPAN // 8
-    places = lax.broadcasted_iota(jnp.int32, (8, SPAN), 0)
-    columns = lax.broadcasted_iota(jnp.int32, (8, SPAN), 1)
-    done = [(places + 8 * part == columns).astype(f32) for part in range(parts)]
-    for row in range(SPAN - 1):
+def unit_lower_inverses(stricts):
+    groups = EDGE // 8
+    count = SPAN // EDGE
+    places = lax.broadcasted_iota(jnp.int32, (8, EDGE), 0)
+    columns = lax.broadcasted_iota(jnp.int32, (8, EDGE), 1)
+    blocks = {}
+    for at, strict in enumerate(stricts):
+        for block in range(count):
+            begin = block * EDGE
+            blocks[at, block] = (
+                strict[begin : begin + EDGE, begin : begin + EDGE],
+                [(places + 8 * part == columns).astype(f32) for part in range(groups)],
+            )
+    for row in range(EDGE - 1):
         first = row // 8
-        line = done[first][row - 8 * first : row - 8 * first + 1, :]
-        for part in range(first, parts):
-            column = strict[8 * part : 8 * part + 8, row : row + 1]
-            done[part] = done[part] - column * line
-    return jnp.concatenate(done, axis=0)
+        for own, done in blocks.values():
+            line = done[first][row - 8 * first : row - 8 * first + 1, :]
+            for part in range(first, groups):
+                column = own[8 * part : 8 * part + 8, row : row + 1]
+                done[part] = done[part] - column * line
+    inverses = []
+    for at, strict in enumerate(stricts):
+        parts = [jnp.concatenate(blocks[at, block][1], axis=0) for block in range(count)]
+        size = EDGE
+        while size < SPAN:
+            joined = []
+            for pair in range(0, len(parts), 2):
+                begin = pair * size
+                below = strict[begin + size : begin + 2 * size, begin : begin + size]
+                upper, lower = parts[pair], parts[pair + 1]
+                corner = mm_fine(mm_fine(lower, below), upper)
+                joined.append(
+                    jnp.concatenate(
+                        [
+                            jnp.concatenate([upper, jnp.zeros((size, size), f32)], axis=1),
+                            jnp.concatenate([-corner, lower], axis=1),
+                        ],
+                        axis=0,
+                    )
+                )
+            parts = joined
+            size *= 2
+        inverses.append(parts[0])
+    return inverses
 
 
 def silu_parts(value):
@@ -153,15 +185,17 @@
         before[...] = jnp.zeros_like(before)
 
     side = side_ref[...]
-    current = conv_ref[...].astype(f32)
+    current = conv_ref[...].astype(bf16).astype(f32)
     act, _ = silu_parts(conv_forward(current, before[...], taps_ref[...], side))
     before[...] = current[SPAN - 8 :, :]
     cols, rows, _, _, _ = side_columns(heads, gates_ref[...], side, log_ref[...], bias_ref[...])
     valid = side[:, CONV : CONV + 1]
     gain = gain_ref[...]
     scale = DK ** (-0.5)
+    terms, units, stricts = [], [], []
     for head in range(heads):
-        beta_c, lower_st, fall, growth, tail, kept = block_terms(head, heads, cols, rows)
+        terms.append(block_terms(head, heads, cols, rows))
+        beta_c, lower_st, fall = terms[-1][:3]
         unit = []
         for begin in (head * DK, (heads + head) * DK):
             row = act[:, begin : begin + DK]
@@ -169,17 +203,20 @@
             row = row.astype(bf16)
             qkv_ref[:, begin : begin + DK] = row
             unit.append(row)
-        queries, keys = unit
+        units.append(unit)
+        stricts.append(jnp.where(lower_st, beta_c * mm(unit[1], unit[1], ROWS) * fall, 0.0))
+    inverses = unit_lower_inverses(stricts)
+    for head in range(heads):
+        beta_c, lower_st, fall, growth, tail, kept = terms[head]
+        queries, keys = units[head]
+        inverse = inverses[head]
+        inv_ref[0, head] = inverse
         begin = 2 * heads * DK + head * DV
         values = act[:, begin : begin + DV].astype(bf16)
         qkv_ref[:, begin : begin + DV] = values
         state = carried[head]
         state_ref[0, head] = state
-        key_prod = mm(keys, keys, ROWS)
         query_prod = mm(queries, keys, ROWS)
-        strict = jnp.where(lower_st, beta_c * key_prod * fall, 0.0)
-        inverse = unit_lower_inverse(strict)
-        inv_ref[0, head] = inverse
         key_state = mm_right(keys, state)
         query_state = mm_right(queries, state)
         right_side = beta_c * (values.astype(f32) - growth * key_state)
@@ -211,8 +248,7 @@
     inv_ref,
     solved_ref,
     cot_ref,
-    dconv_ref,
-    dgate_ref,
+    dproj_ref,
     dgates_ref,
     dtaps_ref,
     dgain_ref,
@@ -234,8 +270,8 @@
     taps = taps_ref[...]
     gain = gain_ref[...]
     valid = side[:, CONV : CONV + 1]
-    current = conv_ref[...].astype(f32)
-    ahead = ahead_ref[8:, :].astype(f32)
+    current = conv_ref[...].astype(bf16).astype(f32)
+    ahead = ahead_ref[...].astype(bf16).astype(f32)
     conv_out = conv_forward(current, ahead, taps, side)
     act, rate = silu_parts(conv_out)
     slope = rate * (1.0 + conv_out * (1.0 - rate))
@@ -258,7 +294,8 @@
         open_gate, gate_rate = silu_parts(gate)
         with_normal = d_gated * normal
         d_gain = d_gain + jnp.sum(with_normal * open_gate, axis=0, keepdims=True)
-        dgate_ref[:, part] = (
+        begin = 2 * heads * DK + (heads + head) * DV
+        dproj_ref[:, begin : begin + DV] = (
             with_normal * gain * (gate_rate * (1.0 + gate * (1.0 - gate_rate)))
         ).astype(bf16)
         d_normal = d_gated * gain * open_gate
@@ -341,7 +378,7 @@
         reach = jnp.concatenate([masked, later * later_side[:, back : back + 1]], axis=0)
         d_in = d_in + taps[back : back + 1, :] * reach[back : back + SPAN, :]
     dtaps_ref[...] += jnp.concatenate(d_taps, axis=0)
-    dconv_ref[...] = d_in.astype(bf16)
+    dproj_ref[:, : heads * (2 * DK + DV)] = d_in.astype(bf16)
     after[...] = d_conv[:8, :]
     after_side[...] = side[:8, :]
     d_decay = ones_left(triangle(True), jnp.concatenate(d_cums, axis=1))
@@ -364,16 +401,18 @@
 MIXER_PARAMS = pltpu.CompilerParams(vmem_limit_bytes=48 * 1024 * 1024)
 
 
-def mixer_forward(conv_in, out_gate, gates, side, taps, gain, decay_log, dt_bias):
-    length, width = conv_in.shape
+def mixer_forward(proj, gates, side, taps, gain, decay_log, dt_bias):
+    length = proj.shape[0]
+    width = taps.shape[1]
     heads = decay_log.shape[1]
+    gate_at = width // (heads * DV)
     blocks = length // SPAN
     return pl.pallas_call(
         functools.partial(mixer_forward_kernel, heads),
         grid=(blocks,),
         in_specs=[
             pl.BlockSpec((SPAN, width), lambda i: (i, 0)),
-            pl.BlockSpec((SPAN, heads * DV), lambda i: (i, 0)),
+            pl.BlockSpec((SPAN, heads * DV), lambda i: (i, gate_at)),
             pl.BlockSpec((SPAN, 2 * heads), lambda i: (i, 0)),
             pl.BlockSpec((SPAN, SIDE), lambda i: (i, 0)),
             whole_block((CONV, width)),
@@ -399,16 +438,21 @@
         ],
         scratch_shapes=[pltpu.VMEM((heads, DK, DV), f32), pltpu.VMEM((8, width), f32)],
         compiler_params=MIXER_PARAMS,
+        cost_estimate=pl.CostEstimate(
+            flops=length * heads * 10**7, bytes_accessed=length * heads * 10**4, transcendentals=0
+        ),
         name="mixer_forward",
-    )(conv_in, out_gate, gates, side, taps, gain, decay_log, dt_bias)
-
-
-def mixer_backward(conv_in, out_gate, gates, side, taps, gain, decay_log, dt_bias, kept, d_gated):
-    length, width = conv_in.shape
+    )(proj, proj, gates, side, taps, gain, decay_log, dt_bias)
+
+
+def mixer_backward(proj, gates, side, taps, gain, decay_log, dt_bias, kept, d_gated):
+    length = proj.shape[0]
+    width = taps.shape[1]
     heads = decay_log.shape[1]
+    gate_at = width // (heads * DV)
     blocks = length // SPAN
     end = blocks - 1
-    ahead_rows = 16
+    ahead_rows = 8
     per = SPAN // ahead_rows
     return pl.pallas_call(
         functools.partial(mixer_backward_kernel, heads),
@@ -416,7 +460,7 @@
         in_specs=[
             pl.BlockSpec((SPAN, width), lambda i: (end - i, 0)),
             pl.BlockSpec((ahead_rows, width), lambda i: (jnp.maximum((end - i) * per - 1, 0), 0)),
-            pl.BlockSpec((SPAN, heads * DV), lambda i: (end - i, 0)),
+            pl.BlockSpec((SPAN, heads * DV), lambda i: (end - i, gate_at)),
             pl.BlockSpec((SPAN, 2 * heads), lambda i: (end - i, 0)),
             pl.BlockSpec((SPAN, SIDE), lambda i: (end - i, 0)),
             whole_block((CONV, width)),
@@ -431,16 +475,14 @@
             pl.BlockSpec((SPAN, heads * DV), lambda i: (end - i, 0)),
         ],
         out_specs=[
-            pl.BlockSpec((SPAN, width), lambda i: (end - i, 0)),
-            pl.BlockSpec((SPAN, heads * DV), lambda i: (end - i, 0)),
+            pl.BlockSpec((SPAN, width + heads * DV), lambda i: (end - i, 0)),
             pl.BlockSpec((SPAN, 2 * heads), lambda i: (end - i, 0)),
             whole_block((CONV, width)),
             whole_block((1, DV)),
             whole_block((1, 2 * heads)),
         ],
         out_shape=[
-            jax.ShapeDtypeStruct((length, width), bf16),
-            jax.ShapeDtypeStruct((length, heads * DV), bf16),
+            jax.ShapeDtypeStruct((length, width + heads * DV), bf16),
             jax.ShapeDtypeStruct((length, 2 * heads), f32),
             jax.ShapeDtypeStruct((CONV, width), f32),
             jax.ShapeDtypeStruct((1, DV), f32),
@@ -452,8 +494,11 @@
             pltpu.VMEM((8, SIDE), f32),
         ],
         compiler_params=MIXER_PARAMS,
+        cost_estimate=pl.CostEstimate(
+            flops=length * heads * 10**7, bytes_accessed=length * heads * 10**4, transcendentals=0
+        ),
         name="mixer_backward",
-    )(conv_in, conv_in, out_gate, gates, side, taps, gain, decay_log, dt_bias, *kept, d_gated)
+    )(proj, proj, proj, gates, side, taps, gain, decay_log, dt_bias, *kept, d_gated)
 
 
 MESH = pl.DeviceIdType.MESH
@@ -570,6 +615,68 @@
     )(values)
 
 
+def pick_columns_kernel(pieces, group, array_ref, out_ref):
+    part = lax.axis_index("group")
+    for own in range(group):
+
+        @pl.when(part == own)
+        def _():
+            out_ref[...] = jnp.concatenate(
+                [
+                    array_ref[:, first + own * width : first + (own + 1) * width]
+                    for first, width in pieces
+                ],
+                axis=1,
+            )
+
+
+def pick_columns(array, pieces, group):
+    rows, columns = array.shape
+    step = min(rows, 64)
+    picked = sum(width for _, width in pieces)
+    return pl.pallas_call(
+        functools.partial(pick_columns_kernel, pieces, group),
+        grid=(rows // step,),
+        in_specs=[pl.BlockSpec((step, columns), lambda i: (i, 0))],
+        out_specs=pl.BlockSpec((step, picked), lambda i: (i, 0)),
+        out_shape=jax.ShapeDtypeStruct((rows, picked), array.dtype),
+        compiler_params=MIXER_PARAMS,
+        name="pick_columns",
+    )(array)
+
+
+def join_columns_kernel(group, runs, parts_ref, out_ref):
+    source, target = 0, 0
+    for width, count in runs:
+        pack = 1
+        while pack < count and (pack * group * width) % 128:
+            pack *= 2
+        for first in range(0, count, pack):
+            pieces = []
+            for run in range(first, first + pack):
+                for part in range(group):
+                    begin = source + run * width
+                    pieces.append(parts_ref[part, :, begin : begin + width].astype(f32))
+            size = pack * group * width
+            out_ref[:, target : target + size] = jnp.concatenate(pieces, axis=1)
+            target += size
+        source += count * width
+
+
+def join_columns(parts, runs):
+    group, rows, columns = parts.shape
+    step = min(rows, 32)
+    return pl.pallas_call(
+        functools.partial(join_columns_kernel, group, runs),
+        grid=(rows // step,),
+        in_specs=[pl.BlockSpec((group, step, columns), lambda i: (0, i, 0))],
+        out_specs=pl.BlockSpec((step, group * columns), lambda i: (i, 0)),
+        out_shape=jax.ShapeDtypeStruct((rows, group * columns), f32),
+        compiler_params=MIXER_PARAMS,
+        name="join_columns",
+    )(parts)
+
+
 def rms_scale(values, gain):
     return values * lax.rsqrt(jnp.mean(values * values, axis=-1, keepdims=True) + eps_norm) * gain
 
@@ -646,40 +753,55 @@
     def gather_any(self, rows):
         return jnp.concatenate([self.swap(rows, turn) for turn in range(self.group)], axis=0)
 
-    def reduce_any(self, partial):
-        total = partial[: self.rows]
+    def reduce_any(self, partial, beside=()):
+        got = []
         for turn in range(1, self.group):
             sent = partial[turn * self.rows : (turn + 1) * self.rows].astype(bf16)
-            total = total + self.swap(sent, turn).astype(f32)
-        return total
-
-    def gather_places(self, rows):
+            got.append(self.swap(sent, turn))
+        got, beside = lax.optimization_barrier((got, beside))
+        total = partial[: self.rows]
+        for part in got:
+            total = total + part.astype(f32)
+        return total, beside
+
+    def gather_places(self, rows, beside=()):
         width = rows.shape[1]
+        got = [self.swap(rows, turn) for turn in range(1, self.group)]
+        got, beside = lax.optimization_barrier((got, beside))
         lane = jnp.zeros((self.sources, self.group, self.per, width), rows.dtype)
-        for turn in range(self.group):
-            got = self.swap(rows, turn).reshape(self.sources, 1, self.per, width)
-            lane = lax.dynamic_update_slice(lane, got, (0, self.part ^ turn, 0, 0))
-        return lane.reshape(-1, width)
-
-    def reduce_places(self, partial):
+        for turn, part in enumerate([rows] + got):
+            part = part.reshape(self.sources, 1, self.per, width)
+            lane = lax.dynamic_update_slice(lane, part, (0, self.part ^ turn, 0, 0))
+        return lane.reshape(-1, width), beside
+
+    def reduce_places(self, partial, beside=()):
         width = partial.shape[1]
         lane = partial.reshape(self.sources, self.group, self.per, width)
-        total = None
-        for turn in range(self.group):
-            mine = lax.dynamic_slice(
+        parts = [
+            lax.dynamic_slice(
                 lane, (0, self.part ^ turn, 0, 0), (self.sources, 1, self.per, width)
             ).reshape(self.rows, width)
-            if turn == 0:
-                total = mine
-            else:
-                total = total + self.swap(mine.astype(bf16), turn).astype(f32)
-        return total
+            for turn in range(self.group)
+        ]
+        got = [self.swap(parts[turn].astype(bf16), turn) for turn in range(1, self.group)]
+        got, beside = lax.optimization_barrier((got, beside))
+        total = parts[0]
+        for part in got:
+            total = total + part.astype(f32)
+        return total, beside
 
     def gather_parts(self, value):
+        if self.group == 4 and value.ndim == 2 and value.shape[0] % 2 == 0:
+            rows = value.shape[0] // 2
+            one, two = self.swap(value, 1), self.swap(value, 2)
+            three = jnp.concatenate([self.swap(two[:rows], 1), self.swap(one[rows:], 2)], axis=0)
+            turns = (value, one, two, three)
+        else:
+            turns = tuple(self.swap(value, turn) for turn in range(self.group))
         parts = jnp.zeros((self.group,) + value.shape, value.dtype)
         for turn in range(self.group):
             parts = lax.dynamic_update_slice(
-                parts, self.swap(value, turn)[None], (self.part ^ turn,) + (0,) * value.ndim
+                parts, turns[turn][None], (self.part ^ turn,) + (0,) * value.ndim
             )
         return parts
 
@@ -711,30 +833,43 @@
                 )
         return jnp.concatenate(pieces, axis=1)
 
-    def join_heads(self, parts, sections):
-        group, rows = parts.shape[:2]
-        out, begin = [], 0
-        for _, width in sections:
-            section = parts[:, :, begin : begin + self.heads * width]
-            begin += self.heads * width
-            section = section.reshape(group, rows, self.heads, width).transpose(1, 2, 0, 3)
-            out.append(section.reshape(rows, self.heads * group * width))
-        return jnp.concatenate(out, axis=1)
-
-    def hidden_columns(self, array, unit_rows_here):
-        rows = array.shape[0]
-        blocks = self.seq * self.cores
-        piece = unit_rows_here // self.group
-        split = array.reshape(rows, 2 * blocks, self.group, piece)
-        mine = lax.dynamic_slice(split, (0, 0, self.part, 0), (rows, 2 * blocks, 1, piece))
-        return mine.reshape(rows, 2 * blocks * piece)
-
-    def join_hidden(self, parts, unit_rows_here):
-        group, rows = parts.shape[:2]
-        blocks = self.seq * self.cores
-        piece = unit_rows_here // group
-        split = parts.reshape(group, rows, 2 * blocks, piece).transpose(1, 2, 0, 3)
-        return split.reshape(rows, 2 * blocks * group * piece)
+    def core_rows(self, array, core):
+        split = array.reshape(self.seq, self.cores, -1, array.shape[1])
+        return lax.dynamic_index_in_dim(split, core, 1, keepdims=False).reshape(-1, array.shape[1])
+
+    def core_sum(self, grad):
+        if self.cores != 2:
+            return grad
+        got = lax.ppermute(self.core_rows(grad, 1 - self.core), "wshard", [(0, 1), (1, 0)])
+        return (self.core_rows(grad, self.core).astype(f32) + got.astype(f32)).astype(bf16)
+
+    def core_columns(self, array):
+        if self.cores != 2:
+            return (array,)
+        rows, columns = array.shape
+        run = columns // (self.seq * 2)
+        picked = []
+        for core in (1 - self.core, self.core):
+            picked.append(
+                jnp.concatenate(
+                    [
+                        lax.dynamic_slice(array, (0, (2 * place + core) * run), (rows, run))
+                        for place in range(self.seq)
+                    ],
+                    axis=1,
+                )
+            )
+        return tuple(picked)
+
+    def weight_grad(self, lefts, right):
+        if self.cores != 2:
+            return dot_t(lefts[0], right).astype(bf16)
+        got = lax.ppermute(dot_t(lefts[0], right).astype(bf16), "wshard", [(0, 1), (1, 0)])
+        return (dot_t(lefts[1], right) + got.astype(f32)).astype(bf16)
+
+    def scatter(self, grad):
+        axes = "seq" if self.cores == 2 else SHARDED
+        return lax.psum_scatter(grad, axes, scatter_dimension=0, tiled=True)
 
     def out_rows(self, w_out):
         width = w_out.shape[1]
@@ -752,15 +887,16 @@
             every, (0, self.part, 0, 0), (self.heads, 1, DV, width)
         ).reshape(-1, width)
 
-    def out_rows_scatter(self, grad):
+    def out_grad(self, gated, d_branch):
         if self.subs == 1 and self.cores == 2:
-            return lax.psum_scatter(grad, SHARDED, scatter_dimension=0, tiled=True)
-        width = grad.shape[1]
+            return self.weight_grad(self.core_columns(gated), d_branch)
+        width = d_branch.shape[1]
+        grad = dot_t(gated, d_branch).astype(bf16)
         every = jnp.zeros((self.heads, self.group, DV, width), bf16)
         every = lax.dynamic_update_slice(
             every, grad.reshape(self.heads, 1, DV, width), (0, self.part, 0, 0)
-        )
-        return lax.psum_scatter(every.reshape(-1, width), SHARDED, scatter_dimension=0, tiled=True)
+        ).reshape(-1, width)
+        return self.core_sum(every)
 
     def out_rows_join(self, shard):
         width = shard.shape[1]
@@ -870,6 +1006,13 @@
 
     at_device = at.at_seq * at.cores + at.core
 
+    pieces = []
+    for begin, piece_width in QKV + GATE:
+        pieces += [
+            (begin + turn * at.group * piece_width, piece_width) for turn in range(heads)
+        ]
+    in_piece = pick_columns(w_in, tuple(pieces), at.group)
+
     ab_shard = at.head_columns(w_ab, ((0, 1), (H, 1)))
     conv_pieces = at.conv_pieces(conv_w)
     small = (attn_gain, ffn_gain, o_gain, ab_shard.reshape(-1), conv_pieces.reshape(-1))
@@ -877,7 +1020,11 @@
     filled = sum(lengths_small)
     rows_small = -(-filled // (16 * 128)) * 16
     packed = jnp.concatenate(small + (jnp.zeros((rows_small * 128 - filled,), bf16),))
-    packed = small_gather(packed.reshape(rows_small, 128), at.seq, at.cores).reshape(devices, -1)
+    packed, in_piece = lax.optimization_barrier((packed, in_piece))
+    in_mine = lax.all_gather(in_piece, SHARDED, axis=0, tiled=True)
+    packed = small_gather(packed.reshape(rows_small, 128), at.seq, at.cores)
+    packed, tokens, cotangent = lax.optimization_barrier((packed, tokens, cotangent))
+    packed = packed.reshape(devices, -1)
     full, begin = [], 0
     for count in lengths_small:
         full.append(packed[:, begin : begin + count])
@@ -891,101 +1038,108 @@
 
     decay_mine, dt_mine = my_heads(decay_log), my_heads(dt_bias)
 
-    in_qkv = lax.all_gather(at.head_columns(w_in, QKV), SHARDED, axis=0, tiled=True)
-    in_gate = lax.all_gather(at.head_columns(w_in, GATE), SHARDED, axis=0, tiled=True)
-    out_mine = at.out_rows(w_out)
-    gu_mine = lax.all_gather(at.hidden_columns(w_gu, device_rows), SHARDED, axis=0, tiled=True)
-    piece = device_rows // at.group
-    down_mine = lax.all_gather(
-        lax.dynamic_slice(w_down, (at.part * piece, 0), (piece, width)), SHARDED, axis=0, tiled=True
-    )
-
     member = (dealing[:, None] == jnp.arange(at.group, dtype=jnp.int32)[None, :]).astype(jnp.int32)
     before = dot(jnp.tril(jnp.ones((rows, rows), f32), -1).astype(bf16), member.astype(bf16))
     before = before.astype(jnp.int32)
     target = jnp.sum((before + at.per * jnp.arange(at.group, dtype=jnp.int32)) * member, axis=1)
     sorting = (target[None, :] == jnp.arange(rows, dtype=jnp.int32)[:, None]).astype(bf16)
-    dealt = at.deal(dot(sorting, jnp.concatenate([tokens, cotangent], axis=1)).astype(bf16))
-    tokens_f = dealt[:, :width].astype(f32)
-    cot_own = dealt[:, width:]
+    tokens_f = at.deal(dot(sorting, tokens).astype(bf16)).astype(f32)
+    normed = rms_scale(tokens_f, attn_f).astype(bf16)
+    normed, cotangent, w_out, w_gu, w_down = lax.optimization_barrier(
+        (normed, cotangent, w_out, w_gu, w_down)
+    )
+    normed_all, _ = at.gather_places(normed)
+    normed_all, normed_cores = lax.optimization_barrier(
+        (normed_all, at.core_columns(normed_all))
+    )
+
+    out_mine = at.out_rows(w_out)
+    piece = device_rows // at.group
+    gu_pieces = tuple((block * device_rows, piece) for block in range(2 * devices))
+    gu_mine = lax.all_gather(
+        pick_columns(w_gu, gu_pieces, at.group), SHARDED, axis=0, tiled=True
+    )
+    down_mine = lax.all_gather(
+        lax.dynamic_slice(w_down, (at.part * piece, 0), (piece, width)), SHARDED, axis=0, tiled=True
+    )
+    cot_own = at.deal(dot(sorting, cotangent).astype(bf16))
+    normed_all, cot_own = lax.optimization_barrier((normed_all, cot_own))
 
     lane_lengths = lax.dynamic_index_in_dim(
         at.gather_parts(lengths.reshape(-1)), at.at_seq // at.subs, 0, keepdims=False
     )
     side = side_array(lane_lengths, at.lane)
-    normed = rms_scale(tokens_f, attn_f).astype(bf16)
-    normed_all = at.gather_places(normed)
-    conv_in = at.to_lane(dot(normed_all, in_qkv).astype(bf16))
     gates_ab = at.to_lane(dot(normed_all, ab_mine))
-    out_gate = at.to_lane(dot(normed_all, in_gate))
-    mixer_args = (conv_in, out_gate, gates_ab, side, conv_mine, o_f[None], decay_mine, dt_mine)
+    proj, cot_own = lax.optimization_barrier((dot(normed_all, in_mine), cot_own))
+    cot_all = at.gather_any(cot_own)
+    proj = at.to_lane(proj)
+    mixer_args = (proj, gates_ab, side, conv_mine, o_f[None], decay_mine, dt_mine)
     gated_lane, *kept = mixer_forward(*mixer_args)
+    gated_lane, cot_all = lax.optimization_barrier((gated_lane, cot_all))
     gated = at.to_own(gated_lane)
-    branch = at.reduce_places(dot(gated, out_mine))
+    branch, _ = at.reduce_places(dot(gated, out_mine))
     resid = tokens_f + branch
 
     normed2_f, pull_norm2 = jax.vjp(rms_scale, resid, ffn_f)
     normed2_all = at.gather_any(normed2_f.astype(bf16))
-    cot_all = at.gather_any(cot_own)
+    normed2_all, normed2_cores = lax.optimization_barrier(
+        (normed2_all, at.core_columns(normed2_all))
+    )
     gate_up = dot(normed2_all, gu_mine)
     hidden_f, pull_ffn = jax.vjp(swiglu, gate_up)
     hidden = hidden_f.astype(bf16)
 
-    d_hidden = dot_back(cot_all, down_mine)
+    d_down = at.core_sum(dot_t(hidden, cot_all).astype(bf16))
+    d_down, hidden, cot_back = lax.optimization_barrier((d_down, hidden, cot_all))
+    down_shard = at.scatter(d_down)
+    d_hidden = dot_back(cot_back, down_mine)
     d_gate_up = pull_ffn(d_hidden)[0].astype(bf16)
     d_normed2_parts = dot_back(d_gate_up, gu_mine)
-    d_gu = dot_t(normed2_all, d_gate_up).astype(bf16)
-    d_down = dot_t(hidden, cot_all).astype(bf16)
-    d_normed2_parts, d_gu, d_down = lax.optimization_barrier((d_normed2_parts, d_gu, d_down))
-    gu_shard = lax.psum_scatter(d_gu, SHARDED, scatter_dimension=0, tiled=True)
-    down_shard = lax.psum_scatter(d_down, SHARDED, scatter_dimension=0, tiled=True)
-    d_normed2 = at.reduce_any(d_normed2_parts)
-    output_parts = dot(hidden, down_mine)
+    d_normed2_parts, d_gate_up = lax.optimization_barrier((d_normed2_parts, d_gate_up))
+    d_gu = at.weight_grad(normed2_cores, d_gate_up)
+    d_normed2, d_gu = at.reduce_any(d_normed2_parts, d_gu)
+    d_gu, down_shard = lax.optimization_barrier((d_gu, down_shard))
+    gu_shard = at.scatter(d_gu)
     d_resid_norm, d_ffn_gain = pull_norm2(d_normed2)
     d_resid = cot_own.astype(f32) + d_resid_norm
 
-    d_branch_all = at.gather_places(d_resid.astype(bf16))
+    d_branch_all, output_parts = at.gather_places(d_resid.astype(bf16), dot(hidden, down_mine))
     d_gated = dot_back(d_branch_all, out_mine)
-    d_out = dot_t(gated, d_branch_all).astype(bf16)
-    d_gated, d_out, output_parts = lax.optimization_barrier((d_gated, d_out, output_parts))
-    output = (resid + at.reduce_any(output_parts)).astype(bf16)
-    out_shard = at.out_rows_scatter(d_out)
-    d_conv_lane, d_gate_lane, d_gates_lane, d_conv_w, d_o_gain, d_heads = mixer_backward(
+    d_gated, output_parts, down_shard = lax.optimization_barrier(
+        (d_gated, output_parts, down_shard)
+    )
+    output_sum, _ = at.reduce_any(output_parts)
+    down_parts = at.gather_parts(down_shard)
+    d_proj_lane, d_gates_lane, d_conv_w, d_o_gain, d_heads = mixer_backward(
         *mixer_args, tuple(kept), at.to_lane(d_gated)
+    )
+    d_proj_lane, output_sum, down_parts = lax.optimization_barrier(
+        (d_proj_lane, output_sum, down_parts)
     )
     once = (at.sub == 0).astype(f32)
     d_conv_w, d_o_gain, d_heads = d_conv_w * once, d_o_gain * once, d_heads * once
-    d_conv_in = at.to_own(d_conv_lane)
-    d_gate = at.to_own(d_gate_lane)
+    d_proj = at.to_own(d_proj_lane)
     d_ab = at.to_own(d_gates_lane).astype(bf16)
-    d_in_gate = dot_t(normed_all, d_gate).astype(bf16)
-    d_in = dot_t(normed_all, d_conv_in).astype(bf16)
-    d_in, d_in_gate, d_conv_in, d_gate, d_ab = lax.optimization_barrier(
-        (d_in, d_in_gate, d_conv_in, d_gate, d_ab)
-    )
-    in_shard = lax.psum_scatter(d_in, SHARDED, scatter_dimension=0, tiled=True)
-    gate_shard = lax.psum_scatter(d_in_gate, SHARDED, scatter_dimension=0, tiled=True)
-    d_w_ab = dot_t(normed_all, d_ab)
-    d_normed = at.reduce_places(
-        dot_back(d_conv_in, in_qkv) + dot_back(d_gate, in_gate) + dot_back(d_ab, ab_mine)
-    )
+    d_in = at.weight_grad(normed_cores, d_proj)
+    d_in, d_proj, d_ab, d_branch_all, output_sum, gu_shard = lax.optimization_barrier(
+        (d_in, d_proj, d_ab, d_branch_all, output_sum, gu_shard)
+    )
+    in_shard = at.scatter(d_in)
+    output = at.undeal((resid + output_sum).astype(bf16))
+    d_normed_parts = dot_back(d_proj, in_mine) + dot_back(d_ab, ab_mine)
+    d_normed_parts, d_branch_all, d_ab = lax.optimization_barrier(
+        (d_normed_parts, d_branch_all, d_ab)
+    )
+    d_normed, (d_out, d_w_ab) = at.reduce_places(
+        d_normed_parts, (at.out_grad(gated, d_branch_all), dot_t(normed_all, d_ab))
+    )
+    d_normed, gu_shard, output = lax.optimization_barrier((d_normed, gu_shard, output))
     value_norm, pull_norm = jax.vjp(rms_scale, tokens_f, attn_f)
     d_tokens_norm, d_attn_gain = pull_norm(d_normed)
     d_tokens = (d_resid + d_tokens_norm).astype(bf16)
 
-    returned = at.undeal(jnp.concatenate([output, d_tokens], axis=1))
-    returned = dot_t(sorting, returned).astype(bf16)
-
-    grad_w_gu = at.join_hidden(at.gather_parts(gu_shard), device_rows).astype(f32)
-    grad_w_down = at.gather_parts(down_shard).reshape(device_rows, width).astype(f32)
-    grad_w_out = at.out_rows_join(out_shard)
-    grad_w_in = jnp.concatenate(
-        [
-            at.join_heads(at.gather_parts(in_shard), QKV),
-            at.join_heads(at.gather_parts(gate_shard), GATE),
-        ],
-        axis=1,
-    ).astype(f32)
+    input_grad = dot_t(sorting, at.undeal(d_tokens)).astype(bf16)
+    output = dot_t(sorting, output).astype(bf16)
 
     def to_blocks(array):
         return array.reshape(devices, -1)
@@ -1005,6 +1159,18 @@
         blocks + (jnp.zeros((devices, rows_small * 128 - filled), f32),), axis=1
     )
     summed = small_sum(packed.reshape(devices, rows_small, 128), at.seq, at.cores, at.group)
+
+    grad_w_gu = join_columns(at.gather_parts(gu_shard), ((piece, 2 * devices),))
+    grad_w_down = down_parts.reshape(device_rows, width).astype(f32)
+    in_shard, summed, input_grad, d_out = lax.optimization_barrier(
+        (in_shard, summed, input_grad, d_out)
+    )
+    out_shard = at.scatter(d_out)
+    grad_w_in = join_columns(
+        at.gather_parts(in_shard), tuple((piece_width, heads) for _, piece_width in QKV + GATE)
+    )
+    grad_w_out = at.out_rows_join(out_shard)
+
     summed = summed.reshape(at.group, -1)
     parts, begin = [], 0
     for size in sizes:
@@ -1013,8 +1179,8 @@
     grad_w_ab = parts[3].reshape(at.group, width // devices, 2, heads).transpose(1, 2, 3, 0)
     grad_heads = parts[5].reshape(at.group, 2, heads).transpose(1, 2, 0).reshape(2, H)
     return (
-        returned[:, :width],
-        returned[:, width:],
+        output,
+        input_grad,
         jnp.sum(parts[0], axis=0),
         grad_w_in,
         grad_w_ab.reshape(width // devices, 2 * H),

time: 1100 us -> 883 us (0.80)
  waiting for transfers between devices: 436 us -> 333 us
  local copies, waits for them, and re-layouts: 149 us -> 79.1 us
  Pallas kernels: 207 us -> 163 us
  matrix products: 163 us -> 151 us
    ppermute x42 -> x43, waiting for transfers between devices: 346 us -> 218 us  [swap(): lax.ppermute(value, 'group', [(i, i ^ turn) for i in range(self.group)])]
    all_to_all x1 -> x2, waiting for transfers between devices: 0.01 us -> 52.2 us  [deal(): lax.all_to_all(sorted_rows, 'seq', split_axis=0, concat_axis=0, tiled=True)]
    unnamed x129 -> x139, local copies, waits for them, and re-layouts: 60.5 us -> 15.9 us
    pallas_call x1, Pallas kernels: 50.5 us -> 9.04 us  [small_gather(): pl.pallas_call(functools.partial(small_gather_kernel, seq, cores), out_sh...]
    reduce_scatter x5 -> x4, waiting for transfers between devices: 27.2 us -> 0.01 us  [scatter(): return lax.psum_scatter(grad, axes, scatter_dimension=0, tiled=True)]
    pallas_call x0 -> x4, Pallas kernels: none -> 22.4 us  [the longest x2 15.2 us: join_columns(): pl.pallas_call(functools.partial(join_columns_kernel, group, runs), grid=...]
    convert_element_type x5 -> x7, other arithmetic: 37.1 us -> 19 us  [the longest x1 5.12 us: shards(): grad_w_down = down_parts.reshape(device_rows, width).astype(f32)]
    broadcast_in_dim x12 -> x0, local copies, waits for them, and re-layouts: 17.2 us -> none  [gather_parts(): self.swap(value, turn)[None]]
  transfers between devices with their start and end apart: 56 -> 61, of which waited for: 30 -> 28; matrix products, arithmetic and copies ran while one was open for 21% -> 27% of each run, Pallas kernels for 19% -> 18%
where the time goes in v3:
time: 883 us; the launch traced here: 872 us
  waiting for transfers between devices  333 us (38%)
  Pallas kernels  163 us (18%)
  matrix products  151 us (17%)
  local copies, waits for them, and re-layouts  79.1 us (9%)
  starting transfers between devices  66.9 us (8%)
  other arithmetic  63.4 us (7%)
  between operations  15.7 us (2%)
    ppermute x43, waiting for transfers between devices, swap(): lax.ppermute(value, 'group', [(i, i ^ turn) for i in range(self.group)])  218 us
    dot_general x8, matrix products, dot(): return jnp.dot(left, right, preferred_element_type=f32)  53.3 us
    all_to_all x2, waiting for transfers between devices, deal(): lax.all_to_all(sorted_rows, 'seq', split_axis=0, concat_axis=0, tiled=True)  52.2 us
    dot_general x5, matrix products, dot_back(): lax.dot_general(left, right, (((1,), (1,)), ((), ())), preferred_element_...  51.1 us
    pallas_call x1, Pallas kernels, mixer_backward(): pl.pallas_call(functools.partial(mixer_backward_kernel, heads), grid=(blo...  50.1 us
    ppermute x43, starting transfers between devices, swap(): lax.ppermute(value, 'group', [(i, i ^ turn) for i in range(self.group)])  48 us
    dot_general x10, matrix products, dot_t(): lax.dot_general(left, right, (((0,), (0,)), ((), ())), preferred_element_...  47 us
    pallas_call x1, Pallas kernels, mixer_forward(): pl.pallas_call(functools.partial(mixer_forward_kernel, heads), grid=(bloc...  41 us
  transfers between devices with their start and end apart: 61, of which 28 were waited for; matrix products, arithmetic and copies ran while one was open for 27% of the time, Pallas kernels for 18%

profile of v3, /device:TPU:0, one launch (start us, length us, event | category | flops | bytes accessed | tf_op | source)
XLA Modules:
  0.0 872.1 jit_solution(9390787047787958207)
XLA Ops:
  31.9 42.5 %all-to-all-done = bf16[4,48,2048]{2,1,0:T(8,128)(2,1)} async-done(((bf16[4,48,2048]{2,1,0:T(8,128)(2,1)}), bf16[4,48,2048]{2,1,0:T(8,128)(2,1)}, u32[]{:S(2)}, u32[]{:S(2)}) %all-to-all-start) | async-done | bytes 786464 | tf_op jit(solution)/shard_map/all_to_all | solution.py:723
  117.9 14.8 %collective-permute-done.1 = bf16[192,2048]{1,0:T(8,128)(2,1)} collective-permute-done((bf16[192,2048]{1,0:T(8,128)(2,1)}, bf16[192,2048]{1,0:T(8,128)(2,1)}, u32[]{:S(2)}, u32[]{:S(2)}) %collective-permute-start.1) | collective-permute-done | bytes 786464 | tf_op jit(solution)/shard_map/ppermute | solution.py:751
  152.7 15.7 %all-gather.5.cloned.1.call-done = bf16[2048,3072]{1,0:T(8,128)(2,1)} async-done(((bf16[256,3072]{1,0:T(8,128)(2,1)}), bf16[2048,3072]{1,0:T(8,128)(2,1)}) %all-gather.5.cloned.1.call-update) | async-done | bytes 12582928 | tf_op jit(solution)/shard_map/all_gather | solution.py:1024
  168.5 16.0 %fusion.65.conv_ref.gate_ref.ahead_ref = f32[768,3072]{1,0:T(8,128)} fusion(bf16[768,2048]{1,0:T(8,128)(2,1)} %bitcast.233, bf16[2048,3072]{1,0:T(8,128)(2,1)} %all-gather.5.cloned.1.call-done), kind=kOutput, calls=%fused_computation.224 | convolution fusion | flops 9663676416 | bytes 25165824 | tf_op jit(solution)/shard_map/dot_general | solution.py:690
  188.0 41.0 %mixer_forward.1 = (bf16[768,1024]{1,0:T(8,128)(2,1)S(1)}, f32[768,1024]{1,0:T(8,128)}, bf16[768,2048]{1,0:T(8,128)(2,1)}, f32[12,4,128,256]{3,2,1,0:T(8,128)}, ...) custom-call(f32[768,3072]{1,0:T(8,128)} %fusion.65.conv_ref.gate_ref.ahead_ref, ...), custom_call_target="tpu_custom_call" | custom-call | flops 30720000000 | bytes 30720000 | tf_op jit(solution)/shard_map/mixer_forward/pallas_call | solution.py:410
  248.2 14.7 %collective-permute-done.10 = bf16[192,2048]{1,0:T(8,128)(2,1)} collective-permute-done((bf16[192,2048]{1,0:T(8,128)(2,1)}, bf16[192,2048]{1,0:T(8,128)(2,1)}, u32[]{:S(2)}, u32[]{:S(2)}) %collective-permute-start.10) | collective-permute-done | bytes 786464 | tf_op jit(solution)/shard_map/ppermute | solution.py:751
  262.9 16.4 %collective-permute-done.11 = bf16[192,2048]{1,0:T(8,128)(2,1)} collective-permute-done((bf16[192,2048]{1,0:T(8,128)(2,1)}, bf16[192,2048]{1,0:T(8,128)(2,1)}, u32[]{:S(2)}, u32[]{:S(2)}) %collective-permute-start.11) | collective-permute-done | bytes 786464 | tf_op jit(solution)/shard_map/ppermute | solution.py:751
  285.7 17.1 %collective-permute-done.13 = bf16[192,2048]{1,0:T(8,128)(2,1)} collective-permute-done((bf16[192,2048]{1,0:T(8,128)(2,1)S(1)}, bf16[192,2048]{1,0:T(8,128)(2,1)}, u32[]{:S(2)}, u32[]{:S(2)}) %collective-permute-start.13) | collective-permute-done | bytes 786464 | tf_op jit(solution)/shard_map/ppermute | solution.py:751
  302.8 15.2 %collective-permute-done.14 = bf16[192,2048]{1,0:T(8,128)(2,1)} collective-permute-done((bf16[192,2048]{1,0:T(8,128)(2,1)S(1)}, bf16[192,2048]{1,0:T(8,128)(2,1)}, u32[]{:S(2)}, u32[]{:S(2)}) %collective-permute-start.14) | collective-permute-done | bytes 786464 | tf_op jit(solution)/shard_map/ppermute | solution.py:751
  324.7 13.7 %fusion.68 = f32[768,2816]{1,0:T(8,128)S(1)} fusion(bf16[768,2048]{1,0:T(8,128)(2,1)} %copy-done.17, bf16[2048,2816]{1,0:T(8,128)(2,1)} %all-gather.9.cloned.1.call-done), kind=kOutput, calls=%fused_computation.227 | convolution fusion | flops 8858370048 | bytes 23330816 | tf_op jit(solution)/shard_map/dot_general | solution.py:690
  356.9 27.8 %all-gather.11.cloned.1.call-done = bf16[1408,2048]{1,0:T(8,128)(2,1)} async-done(((bf16[176,2048]{1,0:T(8,128)(2,1)}), bf16[1408,2048]{1,0:T(8,128)(2,1)}) %all-gather.11.cloned.1.call-update) | async-done | bytes 5767184 | tf_op jit(solution)/shard_map/all_gather | solution.py:1062
  384.7 12.7 %fusion.36 = (f32[768,1408]{1,0:T(8,128)S(1)}, f32[768,1408]{1,0:T(8,128)}) fusion(f32[768,2816]{1,0:T(8,128)} %copy-done.18, bf16[768,2048]{1,0:T(8,128)(2,1)} %pad_maximum_fusion, bf16[1408,2048]{1,0:T(8,128)(2,1)} %all-gather.11.cloned.1.call-done), kind=kOutput, calls=%fused_computation.101 | convolution fusion | flops 4442161152 | bytes 26214400 | tf_op jit(solution)/shard_map/dot_general | solution.py:698
  400.1 15.2 %fusion.69 = f32[768,2048]{1,0:T(8,128)} fusion(bf16[768,2816]{1,0:T(8,128)(2,1)S(1)} %add_convert_fusion.2, bf16[2048,2816]{1,0:T(8,128)(2,1)} %all-gather.9.cloned.1.call-done), kind=kOutput, calls=%fused_computation.228 | convolution fusion | flops 8858370048 | bytes 22151168 | tf_op jit(solution)/shard_map/dot_general | solution.py:698
  447.5 17.4 %collective-permute-done.18 = bf16[192,2048]{1,0:T(8,128)(2,1)} collective-permute-done((bf16[192,2048]{1,0:T(8,128)(2,1)}, bf16[192,2048]{1,0:T(8,128)(2,1)}, u32[]{:S(2)}, u32[]{:S(2)}) %collective-permute-start.18) | collective-permute-done | bytes 786464 | tf_op jit(solution)/shard_map/ppermute | solution.py:751
  473.8 9.7 %fusion.70 = f32[768,2048]{1,0:T(8,128)} fusion(bf16[768,1408]{1,0:T(8,128)(2,1)S(1)} %copy-done.33, bf16[1408,2048]{1,0:T(8,128)(2,1)} %all-gather.11.cloned.1.call-done), kind=kOutput, calls=%fused_computation.229 | convolution fusion | flops 4429185024 | bytes 14221312 | tf_op jit(solution)/shard_map/dot_general | solution.py:690
  490.8 16.2 %collective-permute-done.22 = bf16[192,2048]{1,0:T(8,128)(2,1)S(1)} collective-permute-done((bf16[192,2048]{1,0:T(8,128)(2,1)S(1)}, bf16[192,2048]{1,0:T(8,128)(2,1)S(1)}, u32[]{:S(2)}, u32[]{:S(2)}) %collective-permute-start.22) | collective-permute-done | bytes 786464 | tf_op jit(solution)/shard_map/ppermute | solution.py:751
  521.1 50.1 %mixer_backward.1 = (bf16[768,3072]{1,0:T(8,128)(2,1)}, f32[768,8]{1,0:T(8,128)S(1)}, f32[4,2048]{1,0:T(4,128)S(1)}, f32[1,256]{1,0:T(1,128)S(1)}, f32[1,8]{1,0:T(1,128)S(1)}) custom-call(f32[768,3072]{1,0:T(8,128)} %fusion.65.conv_ref.gate_ref.ahead_ref, f32[768,3072]{1,0:T(8,128)} %fusion.65.conv_ref.gate_ref.ahead_ref, ...), custom_call_target="tpu_custom_call" | custom-call | flops 30720000000 | bytes 30720000 | tf_op jit(solution)/shard_map/mixer_backward/pallas_call | solution.py:457
  592.7 10.1 %collective-permute-done.31 = bf16[1024,3072]{1,0:T(8,128)(2,1)S(1)} collective-permute-done((bf16[1024,3072]{1,0:T(8,128)(2,1)S(1)}, bf16[1024,3072]{1,0:T(8,128)(2,1)S(1)}, u32[]{:S(2)}, u32[]{:S(2)}) %collective-permute-start.31) | collective-permute-done | bytes 6291488 | tf_op jit(solution)/shard_map/ppermute | solution.py:867
  613.7 17.0 %convolution_add_fusion = f32[768,2048]{1,0:T(8,128)} fusion(f32[768,2048]{1,0:T(8,128)S(1)} %fusion.72, bf16[768,3072]{1,0:T(8,128)(2,1)} %get-tuple-element.156, bf16[2048,3072]{1,0:T(8,128)(2,1)} %all-gather.5.cloned.1.call-done), kind=kOutput, calls=%fused_computation.15 | convolution fusion | flops 9665249280 | bytes 29884416 | tf_op jit(solution)/shard_map/dot_general | solution.py:698
  664.5 17.0 %collective-permute-done.33 = bf16[192,2048]{1,0:T(8,128)(2,1)} collective-permute-done((bf16[192,2048]{1,0:T(8,128)(2,1)}, bf16[192,2048]{1,0:T(8,128)(2,1)}, u32[]{:S(2)}, u32[]{:S(2)}) %collective-permute-start.33) | collective-permute-done | bytes 786464 | tf_op jit(solution)/shard_map/ppermute | solution.py:751
  706.8 40.3 %small_sum.1 = f32[4,32,128]{2,1,0:T(8,128)} custom-call(f32[8,32,128]{2,1,0:T(8,128)} %bitcast.256), custom_call_target="tpu_custom_call" | custom-call | tf_op jit(solution)/shard_map/small_sum/pallas_call | solution.py:601
  760.6 13.1 %collective-permute-done.47 = bf16[128,2816]{1,0:T(8,128)(2,1)S(1)} collective-permute-done((bf16[128,2816]{1,0:T(8,128)(2,1)S(1)}, bf16[128,2816]{1,0:T(8,128)(2,1)S(1)}, u32[]{:S(2)}, u32[]{:S(2)}) %collective-permute-start.47) | collective-permute-done | bytes 720928 | tf_op jit(solution)/shard_map/ppermute | solution.py:751
  794.1 13.6 %collective-permute-done.37 = bf16[256,3072]{1,0:T(8,128)(2,1)S(1)} collective-permute-done((bf16[256,3072]{1,0:T(8,128)(2,1)}, bf16[256,3072]{1,0:T(8,128)(2,1)S(1)}, u32[]{:S(2)}, u32[]{:S(2)}) %collective-permute-start.37) | collective-permute-done | bytes 1572896 | tf_op jit(solution)/shard_map/ppermute | solution.py:751
  817.9 23.2 %collective-permute-done.41 = bf16[128,2048]{1,0:T(8,128)(2,1)S(1)} collective-permute-done((bf16[128,2048]{1,0:T(8,128)(2,1)}, bf16[128,2048]{1,0:T(8,128)(2,1)S(1)}, u32[]{:S(2)}, u32[]{:S(2)}) %collective-permute-start.41) | collective-permute-done | bytes 524320 | tf_op jit(solution)/shard_map/ppermute | solution.py:751
  (433 shorter events, 365.8 us)
Async XLA Ops:
  7.2 161.3 %all-gather.5.cloned.1.call-start = ((), (), s32[]{:S(2)}) async-start(), calls=%async_computation.8 | async-start | bytes 14155776 | tf_op jit(solution)/shard_map/all_gather | solution.py:1024
  27.2 47.1 %all-to-all-start = ((bf16[4,48,2048]{2,1,0:T(8,128)(2,1)}), bf16[4,48,2048]{2,1,0:T(8,128)(2,1)}, u32[]{:S(2)}, u32[]{:S(2)}) async-start(bf16[4,48,2048]{2,1,0:T(8,128)(2,1)} %bitcast.244), calls=%async_computation | async-start | bytes 1572864 | tf_op jit(solution)/shard_map/all_to_all | solution.py:723
  31.8 200.3 %all-gather.7.cloned.1.call-start = ((), (), s32[]{:S(2)}) async-start(), calls=%async_computation.9 | async-start | bytes 4718592 | tf_op jit(solution)/shard_map/all_gather | solution.py:883
  84.1 240.5 %all-gather.9.cloned.1.call-start = ((), (), s32[]{:S(2)}) async-start(), calls=%async_computation.10 | async-start | bytes 12976128 | tf_op jit(solution)/shard_map/all_gather | solution.py:1059
  105.3 44.3 %all-to-all-start.1 = ((bf16[4,48,2048]{2,1,0:T(8,128)(2,1)}), bf16[4,48,2048]{2,1,0:T(8,128)(2,1)}, u32[]{:S(2)}, u32[]{:S(2)}) async-start(bf16[4,48,2048]{2,1,0:T(8,128)(2,1)} %bitcast.245), calls=%async_computation.1 | async-start | bytes 1572864 | tf_op jit(solution)/shard_map/all_to_all | solution.py:723
  109.5 275.2 %all-gather.11.cloned.1.call-start = ((), (), s32[]{:S(2)}) async-start(), calls=%async_computation.11 | async-start | bytes 6488064 | tf_op jit(solution)/shard_map/all_gather | solution.py:1062
  184.5 44.5 %collective-permute-start.6 = (bf16[192,2048]{1,0:T(8,128)(2,1)}, bf16[192,2048]{1,0:T(8,128)(2,1)S(1)}, u32[]{:S(2)}, u32[]{:S(2)}) collective-permute-start(bf16[192,2048]{1,0:T(8,128)(2,1)} %bitcast.13), channel_id=1, source_target_pairs={{0,8},{8,0},{16,24},{24,16},{1,9},{9,1},{17,25},{25,17},{2,10},{10... | collective-permute-start | bytes 2359304 | tf_op jit(solution)/shard_map/ppermute | solution.py:751
  185.9 43.0 %collective-permute-start.7 = (bf16[192,2048]{1,0:T(8,128)(2,1)}, bf16[192,2048]{1,0:T(8,128)(2,1)S(1)}, u32[]{:S(2)}, u32[]{:S(2)}) collective-permute-start(bf16[192,2048]{1,0:T(8,128)(2,1)} %bitcast.13), channel_id=1, source_target_pairs={{0,16},{8,24},{16,0},{24,8},{1,17},{9,25},{17,1},{25,9},{2,18},{10... | collective-permute-start | bytes 2359304 | tf_op jit(solution)/shard_map/ppermute | solution.py:751
  246.6 236.9 %reduce-scatter.5.cloned.1.call-start = ((), (), s32[]{:S(2)}) async-start(), calls=%async_computation.12 | async-start | bytes 3604480 | tf_op jit(solution)/shard_map/reduce_scatter | solution.py:872
  422.1 188.0 %reduce-scatter.7.cloned.1.call-start = ((), (), s32[]{:S(2)}) async-start(), calls=%async_computation.13 | async-start | bytes 7208960 | tf_op jit(solution)/shard_map/reduce_scatter | solution.py:872
  483.5 266.0 %reduce-scatter.9.cloned.1.call-start = ((), (), s32[]{:S(2)}) async-start(), calls=%async_computation.14 | async-start | bytes 7864320 | tf_op jit(solution)/shard_map/reduce_scatter | solution.py:872
  513.6 63.3 %collective-permute-start.27 = (bf16[176,2048]{1,0:T(8,128)(2,1)}, bf16[176,2048]{1,0:T(8,128)(2,1)}, u32[]{:S(2)}, u32[]{:S(2)}) collective-permute-start(bf16[176,2048]{1,0:T(8,128)(2,1)} %reduce-scatter.5.cloned.1.call-done), channel_id=1, source_target_pairs={{0,8},{8,0},{16,24},{24,16},{1,9},{9,1},{17,25},{25,17},{2,10},{10... | collective-permute-start | bytes 2162696 | tf_op jit(solution)/shard_map/ppermute | solution.py:751
  514.3 61.0 %collective-permute-start.28 = (bf16[176,2048]{1,0:T(8,128)(2,1)}, bf16[176,2048]{1,0:T(8,128)(2,1)}, u32[]{:S(2)}, u32[]{:S(2)}) collective-permute-start(bf16[176,2048]{1,0:T(8,128)(2,1)} %reduce-scatter.5.cloned.1.call-done), channel_id=1, source_target_pairs={{0,16},{8,24},{16,0},{24,8},{1,17},{9,25},{17,1},{25,9},{2,18},{10... | collective-permute-start | bytes 2162696 | tf_op jit(solution)/shard_map/ppermute | solution.py:751
  517.6 65.8 %collective-permute-start.24 = (bf16[192,2048]{1,0:T(8,128)(2,1)}, bf16[192,2048]{1,0:T(8,128)(2,1)S(1)}, u32[]{:S(2)}, u32[]{:S(2)}) collective-permute-start(bf16[192,2048]{1,0:T(8,128)(2,1)} %get-tuple-element.207), channel_id=1, source_target_pairs={{0,8},{8,0},{16,24},{24,16},{1,9},{9,1},{17,25},{25,17},{2,10},{10... | collective-permute-start | bytes 2359304 | tf_op jit(solution)/shard_map/ppermute | solution.py:751
  518.2 65.3 %collective-permute-start.25 = (bf16[192,2048]{1,0:T(8,128)(2,1)}, bf16[192,2048]{1,0:T(8,128)(2,1)S(1)}, u32[]{:S(2)}, u32[]{:S(2)}) collective-permute-start(bf16[192,2048]{1,0:T(8,128)(2,1)} %get-tuple-element.206), channel_id=1, source_target_pairs={{0,16},{8,24},{16,0},{24,8},{1,17},{9,25},{17,1},{25,9},{2,18},{10... | collective-permute-start | bytes 2359304 | tf_op jit(solution)/shard_map/ppermute | solution.py:751
  519.7 63.8 %collective-permute-start.26 = (bf16[192,2048]{1,0:T(8,128)(2,1)}, bf16[192,2048]{1,0:T(8,128)(2,1)S(1)}, u32[]{:S(2)}, u32[]{:S(2)}) collective-permute-start(bf16[192,2048]{1,0:T(8,128)(2,1)} %get-tuple-element.205), channel_id=1, source_target_pairs={{0,24},{8,16},{16,8},{24,0},{1,25},{9,17},{17,9},{25,1},{2,26},{10... | collective-permute-start | bytes 2359304 | tf_op jit(solution)/shard_map/ppermute | solution.py:751
  636.3 48.9 %all-to-all-start.2 = ((bf16[4,48,2048]{2,1,0:T(8,128)(2,1)}), bf16[4,48,2048]{2,1,0:T(8,128)(2,1)S(1)}, u32[]{:S(2)}, u32[]{:S(2)}) async-start(bf16[4,48,2048]{2,1,0:T(8,128)(2,1)} %bitcast.246), calls=%async_computation.4 | async-start | bytes 1572864 | tf_op jit(solution)/shard_map/all_to_all | solution.py:738
  691.8 55.3 %all-to-all-start.3 = ((bf16[4,48,2048]{2,1,0:T(8,128)(2,1)}), bf16[4,48,2048]{2,1,0:T(8,128)(2,1)}, u32[]{:S(2)}, u32[]{:S(2)}) async-start(bf16[4,48,2048]{2,1,0:T(8,128)(2,1)} %bitcast.55), calls=%async_computation.6 | async-start | bytes 1572864 | tf_op jit(solution)/shard_map/all_to_all | solution.py:738
  696.6 116.0 %reduce-scatter.11.cloned.1.call-start = ((), (), s32[]{:S(2)}) async-start(), calls=%async_computation.15 | async-start | bytes 2621440 | tf_op jit(solution)/shard_map/reduce_scatter | solution.py:872
  698.1 58.0 %collective-permute-start.45 = (bf16[256,2816]{1,0:T(8,128)(2,1)}, bf16[256,2816]{1,0:T(8,128)(2,1)S(1)}, u32[]{:S(2)}, u32[]{:S(2)}) collective-permute-start(bf16[256,2816]{1,0:T(8,128)(2,1)} %reduce-scatter.7.cloned.1.call-done), channel_id=1, source_target_pairs={{0,8},{8,0},{16,24},{24,16},{1,9},{9,1},{17,25},{25,17},{2,10},{10... | collective-permute-start | bytes 4325384 | tf_op jit(solution)/shard_map/ppermute | solution.py:751
  699.2 54.3 %collective-permute-start.46 = (bf16[256,2816]{1,0:T(8,128)(2,1)}, bf16[256,2816]{1,0:T(8,128)(2,1)}, u32[]{:S(2)}, u32[]{:S(2)}) collective-permute-start(bf16[256,2816]{1,0:T(8,128)(2,1)} %reduce-scatter.7.cloned.1.call-done), channel_id=1, source_target_pairs={{0,16},{8,24},{16,0},{24,8},{1,17},{9,25},{17,1},{25,9},{2,18},{10... | collective-permute-start | bytes 4325384 | tf_op jit(solution)/shard_map/ppermute | solution.py:751
  758.5 50.9 %collective-permute-start.36 = (bf16[256,3072]{1,0:T(8,128)(2,1)}, bf16[256,3072]{1,0:T(8,128)(2,1)}, u32[]{:S(2)}, u32[]{:S(2)}) collective-permute-start(bf16[256,3072]{1,0:T(8,128)(2,1)} %reduce-scatter.9.cloned.1.call-done), channel_id=1, source_target_pairs={{0,8},{8,0},{16,24},{24,16},{1,9},{9,1},{17,25},{25,17},{2,10},{10... | collective-permute-start | bytes 4718600 | tf_op jit(solution)/shard_map/ppermute | solution.py:751
  759.9 47.9 %collective-permute-start.37 = (bf16[256,3072]{1,0:T(8,128)(2,1)}, bf16[256,3072]{1,0:T(8,128)(2,1)S(1)}, u32[]{:S(2)}, u32[]{:S(2)}) collective-permute-start(bf16[256,3072]{1,0:T(8,128)(2,1)} %reduce-scatter.9.cloned.1.call-done), channel_id=1, source_target_pairs={{0,16},{8,24},{16,0},{24,8},{1,17},{9,25},{17,1},{25,9},{2,18},{10... | collective-permute-start | bytes 4718600 | tf_op jit(solution)/shard_map/ppermute | solution.py:751
  808.8 41.8 %collective-permute-start.38 = (bf16[128,3072]{1,0:T(8,128)(2,1)}, bf16[128,3072]{1,0:T(8,128)(2,1)}, u32[]{:S(2)}, u32[]{:S(2)}) collective-permute-start(bf16[128,3072]{1,0:T(8,128)(2,1)} %slice.153), channel_id=1, source_target_pairs={{0,8},{8,0},{16,24},{24,16},{1,9},{9,1},{17,25},{25,17},{2,10},{10... | collective-permute-start | bytes 2359304 | tf_op jit(solution)/shard_map/ppermute | solution.py:751
  (102 other events, 1929.5 us)
Sparse Core Ops, SparseCore 0:
  15.5 152.8 all-gather.4
  170.6 45.3 all-gather.6
  217.7 106.7 all-gather.8
  325.9 58.7 all-gather.10
  422.2 54.8 reduce-scatter.4
  483.6 100.0 reduce-scatter.6
  610.3 135.8 reduce-scatter.8
  749.7 51.4 reduce-scatter.10

commit v4 on v3

--- a/solution.py
+++ b/solution.py
@@ -96,6 +96,14 @@
     return inverses
 
 
+def in_turns(workers):
+    workers = list(workers)
+    while workers:
+        for worker in list(workers):
+            if next(worker, workers) is workers:
+                workers.remove(worker)
+
+
 def silu_parts(value):
     rate = 1.0 / (1.0 + jnp.exp(-value))
     return value * rate, rate
@@ -125,18 +133,42 @@
     shifted, beta, decay = gate_terms(heads, gates, decay_log, dt_bias)
     running = ones_left(triangle(False), decay)
     cols = jnp.concatenate(
-        [running, beta, side[:, :1], jnp.zeros((SPAN, 128 - 2 * heads - 1), f32)], axis=1
+        [running, beta, side[:, :CONV], jnp.zeros((SPAN, 128 - 2 * heads - CONV), f32)], axis=1
     )
     return cols, cols.T, shifted, beta, decay
 
 
-def conv_forward(current, before, taps, side):
-    extended = jnp.concatenate([before, current], axis=0)
+EDGE_ROWS = 16
+
+
+def shifted_rows(current, before, side):
+    at_i = lax.broadcasted_iota(jnp.int32, (SPAN, SPAN + EDGE_ROWS), 0)
+    at_j = lax.broadcasted_iota(jnp.int32, (SPAN, SPAN + EDGE_ROWS), 1)
+    moves = [
+        jnp.where(at_j == at_i + (EDGE_ROWS - back), side[:, back : back + 1], 0.0).astype(bf16)
+        for back in range(1, CONV)
+    ]
+    moved = mm(jnp.concatenate(moves, axis=0), jnp.concatenate([before, current], axis=0))
+    return [moved[(back - 1) * SPAN : back * SPAN, :] for back in range(1, CONV)]
+
+
+def shifted_back(d_conv, later, same_rows, later_rows):
+    at_i = lax.broadcasted_iota(jnp.int32, (SPAN, SPAN + EDGE_ROWS), 0)
+    at_j = lax.broadcasted_iota(jnp.int32, (SPAN, SPAN + EDGE_ROWS), 1)
+    moves = []
+    for back in range(1, CONV):
+        same = jnp.concatenate(
+            [same_rows[back : back + 1, :], later_rows[back : back + 1, :EDGE_ROWS]], axis=1
+        )
+        moves.append(jnp.where(at_j == at_i + back, same, 0.0).astype(bf16))
+    moved = mm(jnp.concatenate(moves, axis=0), jnp.concatenate([d_conv, later], axis=0))
+    return [moved[(back - 1) * SPAN : back * SPAN, :] for back in range(1, CONV)]
+
+
+def conv_forward(current, moved, taps):
     total = taps[0:1, :] * current
     for back in range(1, CONV):
-        total = total + taps[back : back + 1, :] * (
-            extended[8 - back : 8 - back + SPAN, :] * side[:, back : back + 1]
-        )
+        total = total + taps[back : back + 1, :] * moved[back - 1]
     return total
 
 
@@ -185,9 +217,10 @@
         before[...] = jnp.zeros_like(before)
 
     side = side_ref[...]
-    current = conv_ref[...].astype(bf16).astype(f32)
-    act, _ = silu_parts(conv_forward(current, before[...], taps_ref[...], side))
-    before[...] = current[SPAN - 8 :, :]
+    current = conv_ref[...].astype(bf16)
+    moved = shifted_rows(current, before[...], side)
+    act, _ = silu_parts(conv_forward(current.astype(f32), moved, taps_ref[...]))
+    before[...] = current[SPAN - EDGE_ROWS :, :]
     cols, rows, _, _, _ = side_columns(heads, gates_ref[...], side, log_ref[...], bias_ref[...])
     valid = side[:, CONV : CONV + 1]
     gain = gain_ref[...]
@@ -206,7 +239,8 @@
         units.append(unit)
         stricts.append(jnp.where(lower_st, beta_c * mm(unit[1], unit[1], ROWS) * fall, 0.0))
     inverses = unit_lower_inverses(stricts)
-    for head in range(heads):
+
+    def one_head(head):
         beta_c, lower_st, fall, growth, tail, kept = terms[head]
         queries, keys = units[head]
         inverse = inverses[head]
@@ -219,16 +253,25 @@
         query_prod = mm(queries, keys, ROWS)
         key_state = mm_right(keys, state)
         query_state = mm_right(queries, state)
+        yield
         right_side = beta_c * (values.astype(f32) - growth * key_state)
+        yield
         solved = mm_both(inverse, right_side)
-        mixed = scale * (growth * query_state + mm_both(query_prod * fall, solved)) * valid
+        yield
         part = slice(head * DV, (head + 1) * DV)
+        solved_ref[:, part] = solved
+        inner = mm_both(query_prod * fall, solved)
+        yield
+        carried[head] = kept * state + mm_both(tail * keys.astype(f32), solved, COLS)
+        yield
+        mixed = scale * (growth * query_state + inner) * valid
         mixed_ref[:, part] = mixed
-        solved_ref[:, part] = solved
-        carried[head] = kept * state + mm_both(tail * keys.astype(f32), solved, COLS)
         shrink = lax.rsqrt(jnp.mean(mixed * mixed, axis=1, keepdims=True) + eps_norm)
         open_gate, _ = silu_parts(gate_ref[:, part])
         gated_ref[:, part] = (mixed * shrink * gain * open_gate).astype(bf16)
+        yield
+
+    in_turns([one_head(head) for head in range(heads)])
 
 
 def mixer_backward_kernel(
@@ -270,9 +313,10 @@
     taps = taps_ref[...]
     gain = gain_ref[...]
     valid = side[:, CONV : CONV + 1]
-    current = conv_ref[...].astype(bf16).astype(f32)
-    ahead = ahead_ref[...].astype(bf16).astype(f32)
-    conv_out = conv_forward(current, ahead, taps, side)
+    current = conv_ref[...].astype(bf16)
+    moved = shifted_rows(current, ahead_ref[...].astype(bf16), side)
+    current = current.astype(f32)
+    conv_out = conv_forward(current, moved, taps)
     act, rate = silu_parts(conv_out)
     slope = rate * (1.0 + conv_out * (1.0 - rate))
     cols, rows, shifted, beta_all, decay_all = side_columns(
@@ -280,10 +324,10 @@
     )
     scale = DK ** (-0.5)
     at_last = lax.broadcasted_iota(jnp.int32, (SPAN, 1), 0) == SPAN - 1
-    d_betas, d_cums = [], []
-    d_queries, d_keys, d_values = [], [], []
-    d_gain = jnp.zeros((1, DV), f32)
-    for head in range(heads):
+    d_betas, d_cums, d_gains = [None] * heads, [None] * heads, [None] * heads
+    d_queries, d_keys, d_values = [None] * heads, [None] * heads, [None] * heads
+
+    def one_head(head):
         beta_c, lower_st, fall, growth, tail, kept = block_terms(head, heads, cols, rows)
         part = slice(head * DV, (head + 1) * DV)
         mixed = mixed_ref[:, part]
@@ -293,7 +337,7 @@
         normal = mixed * shrink
         open_gate, gate_rate = silu_parts(gate)
         with_normal = d_gated * normal
-        d_gain = d_gain + jnp.sum(with_normal * open_gate, axis=0, keepdims=True)
+        d_gains[head] = jnp.sum(with_normal * open_gate, axis=0, keepdims=True)
         begin = 2 * heads * DK + (heads + head) * DV
         dproj_ref[:, begin : begin + DV] = (
             with_normal * gain * (gate_rate * (1.0 + gate * (1.0 - gate_rate)))
@@ -301,6 +345,7 @@
         d_normal = d_gated * gain * open_gate
         d_mixed = shrink * (d_normal - normal * jnp.mean(d_normal * normal, axis=1, keepdims=True))
         d_mixed = (scale * valid) * d_mixed
+        yield
         queries = qkv_ref[:, head * DK : (head + 1) * DK]
         keys = qkv_ref[:, (heads + head) * DK : (heads + head + 1) * DK]
         begin = 2 * heads * DK + head * DV
@@ -317,14 +362,25 @@
         mixing = query_prod * fall
         key_state = mm_right(keys, state)
         query_state = mm_right(queries, state)
+        yield
         d_solved = mm_both(mixing, d_mixed, COLS) + mm_both(tail * keys_f, d_state)
+        d_mixing = mm_both(d_mixed, solved, ROWS)
+        yield
         d_right = mm_both(inverse, d_solved, COLS)
-        d_mixing = mm_both(d_mixed, solved, ROWS)
+        yield
         d_query_prod = d_mixing * fall
         d_strict = jnp.where(lower_st, -mm_both(d_right, solved, ROWS), 0.0)
         d_key_prod = d_strict * beta_c * fall
         d_key_state = -(beta_c * growth) * d_right
+        yield
+        carried[head] = (
+            kept * d_state
+            + mm_both(growth * queries_f, d_mixed, COLS)
+            + mm_right(keys, d_key_state, COLS)
+        )
+        yield
         d_query = mm_both(growth * d_mixed, state, ROWS) + mm_both(d_query_prod, keys_f)
+        yield
         both = d_key_prod + d_key_prod.T
         from_tail = mm_both(solved, d_state, ROWS)
         d_key = (
@@ -333,10 +389,10 @@
             + mm_both(d_query_prod, queries_f, COLS)
             + tail * from_tail
         )
+        yield
         residual = values.astype(f32) - growth * key_state
-        d_betas.append(
-            jnp.sum(d_right * residual, axis=1, keepdims=True)
-            + jnp.sum(d_strict * key_prod * fall, axis=1, keepdims=True)
+        d_betas[head] = jnp.sum(d_right * residual, axis=1, keepdims=True) + jnp.sum(
+            d_strict * key_prod * fall, axis=1, keepdims=True
         )
         spread = d_strict * strict + d_mixing * mixing
         from_last = tail * jnp.sum(keys_f * from_tail, axis=1, keepdims=True)
@@ -346,41 +402,38 @@
         at_end = jnp.sum(from_last, axis=0, keepdims=True) + kept * jnp.sum(
             jnp.sum(d_state * state, axis=1, keepdims=True), axis=0, keepdims=True
         )
-        d_cums.append(
+        yield
+        d_cums[head] = (
             jnp.sum(spread, axis=1, keepdims=True)
             - jnp.sum(spread.T, axis=1, keepdims=True)
             + growth * d_growth
             - from_last
             + jnp.where(at_last, at_end, 0.0)
         )
-        carried[head] = (
-            kept * d_state
-            + mm_both(growth * queries_f, d_mixed, COLS)
-            + mm_right(keys, d_key_state, COLS)
-        )
+        yield
         for grads, grad, start in ((d_queries, d_query, head * DK), (d_keys, d_key, (heads + head) * DK)):
             row = act[:, start : start + DK]
             small = lax.rsqrt(jnp.sum(row * row, axis=1, keepdims=True) + eps_norm)
             along = jnp.sum(row * grad, axis=1, keepdims=True) * small * small
-            grads.append(small * (grad - row * along))
-        d_values.append(beta_c * d_right)
-    dgain_ref[...] += d_gain
+            grads[head] = small * (grad - row * along)
+        d_values[head] = beta_c * d_right
+        yield
+
+    in_turns([one_head(head) for head in range(heads)])
+    dgain_ref[...] += sum(d_gains)
     d_conv = jnp.concatenate(d_queries + d_keys + d_values, axis=1) * slope
-    extended = jnp.concatenate([ahead, current], axis=0)
-    later, later_side = after[...], after_side[...]
+    d_low = d_conv.astype(bf16)
+    same_rows = rows[2 * heads : 2 * heads + CONV, :]
+    back_rows = shifted_back(d_low, after[...], same_rows, after_side[...])
     d_in = taps[0:1, :] * d_conv
     d_taps = [jnp.sum(d_conv * current, axis=0, keepdims=True)]
     for back in range(1, CONV):
-        masked = d_conv * side[:, back : back + 1]
-        d_taps.append(
-            jnp.sum(masked * extended[8 - back : 8 - back + SPAN, :], axis=0, keepdims=True)
-        )
-        reach = jnp.concatenate([masked, later * later_side[:, back : back + 1]], axis=0)
-        d_in = d_in + taps[back : back + 1, :] * reach[back : back + SPAN, :]
+        d_taps.append(jnp.sum(d_conv * moved[back - 1], axis=0, keepdims=True))
+        d_in = d_in + taps[back : back + 1, :] * back_rows[back - 1]
     dtaps_ref[...] += jnp.concatenate(d_taps, axis=0)
     dproj_ref[:, : heads * (2 * DK + DV)] = d_in.astype(bf16)
-    after[...] = d_conv[:8, :]
-    after_side[...] = side[:8, :]
+    after[...] = d_low[:EDGE_ROWS, :]
+    after_side[...] = same_rows
     d_decay = ones_left(triangle(True), jnp.concatenate(d_cums, axis=1))
     d_beta = jnp.concatenate(d_betas, axis=1)
     d_shifted = -d_decay * jnp.exp(log_ref[...]) / (1.0 + jnp.exp(-shifted))
@@ -436,10 +489,10 @@
             jax.ShapeDtypeStruct((blocks, heads, SPAN, SPAN), f32),
             jax.ShapeDtypeStruct((length, heads * DV), f32),
         ],
-        scratch_shapes=[pltpu.VMEM((heads, DK, DV), f32), pltpu.VMEM((8, width), f32)],
+        scratch_shapes=[pltpu.VMEM((heads, DK, DV), f32), pltpu.VMEM((EDGE_ROWS, width), bf16)],
         compiler_params=MIXER_PARAMS,
         cost_estimate=pl.CostEstimate(
-            flops=length * heads * 10**7, bytes_accessed=length * heads * 10**4, transcendentals=0
+            flops=length, bytes_accessed=length, transcendentals=0
         ),
         name="mixer_forward",
     )(proj, proj, gates, side, taps, gain, decay_log, dt_bias)
@@ -452,7 +505,7 @@
     gate_at = width // (heads * DV)
     blocks = length // SPAN
     end = blocks - 1
-    ahead_rows = 8
+    ahead_rows = EDGE_ROWS
     per = SPAN // ahead_rows
     return pl.pallas_call(
         functools.partial(mixer_backward_kernel, heads),
@@ -490,12 +543,12 @@
         ],
         scratch_shapes=[
             pltpu.VMEM((heads, DK, DV), f32),
-            pltpu.VMEM((8, width), f32),
-            pltpu.VMEM((8, SIDE), f32),
+            pltpu.VMEM((EDGE_ROWS, width), bf16),
+            pltpu.VMEM((CONV, SPAN), f32),
         ],
         compiler_params=MIXER_PARAMS,
         cost_estimate=pl.CostEstimate(
-            flops=length * heads * 10**7, bytes_accessed=length * heads * 10**4, transcendentals=0
+            flops=length, bytes_accessed=length, transcendentals=0
         ),
         name="mixer_backward",
     )(proj, proj, proj, gates, side, taps, gain, decay_log, dt_bias, *kept, d_gated)
@@ -615,6 +668,63 @@
     )(values)
 
 
+def plane_gather_kernel(in_ref, out_ref, done, send_sem, recv_sem):
+    part = lax.axis_index("group")
+    near = part + 1 - 2 * lax.rem(part, 2)
+    far = lax.rem(part + 2, 4)
+    half = in_ref.shape[0] // 2
+    first, second = pl.ds(0, half), pl.ds(half, half)
+    greet([{"group": near}, {"group": far}])
+
+    def send(source, block, rows, target, at):
+        copy = pltpu.make_async_remote_copy(
+            src_ref=source,
+            dst_ref=out_ref.at[block, rows],
+            send_sem=send_sem.at[at],
+            recv_sem=recv_sem.at[at],
+            device_id={"group": target},
+            device_id_type=MESH,
+        )
+        copy.start()
+        return copy
+
+    copies = [
+        send(in_ref.at[second], part, second, near, 0),
+        send(in_ref.at[first], part, first, far, 1),
+        send(in_ref.at[first], part, first, near, 2),
+        send(in_ref.at[second], part, second, far, 3),
+    ]
+    own = pltpu.make_async_copy(in_ref, out_ref.at[part], done)
+    own.start()
+    copies[1].wait_recv()
+    copies.append(send(out_ref.at[far, first], far, first, near, 4))
+    copies[0].wait_recv()
+    copies.append(send(out_ref.at[near, second], near, second, far, 5))
+    for at, copy in enumerate(copies):
+        copy.wait_send()
+        if at >= 2:
+            copy.wait_recv()
+    own.wait()
+
+
+def plane_gather(value):
+    return pl.pallas_call(
+        plane_gather_kernel,
+        out_shape=jax.ShapeDtypeStruct((4,) + value.shape, value.dtype),
+        in_specs=[pl.BlockSpec(memory_space=pltpu.VMEM)],
+        out_specs=pl.BlockSpec(memory_space=pltpu.VMEM),
+        scratch_shapes=[
+            pltpu.SemaphoreType.DMA,
+            pltpu.SemaphoreType.DMA((6,)),
+            pltpu.SemaphoreType.DMA((6,)),
+        ],
+        compiler_params=pltpu.CompilerParams(
+            collective_id=2, has_side_effects=True, vmem_limit_bytes=32 * 1024 * 1024
+        ),
+        name="plane_gather",
+    )(value)
+
+
 def pick_columns_kernel(pieces, group, array_ref, out_ref):
     part = lax.axis_index("group")
     for own in range(group):
@@ -645,7 +755,8 @@
     )(array)
 
 
-def join_columns_kernel(group, runs, parts_ref, out_ref):
+def join_columns_kernel(group, runs, parts_ref, *refs):
+    out_ref = refs[-1]
     source, target = 0, 0
     for width, count in runs:
         pack = 1
@@ -663,18 +774,25 @@
         source += count * width
 
 
-def join_columns(parts, runs):
+def join_columns(parts, runs, total_rows=None, into=None):
     group, rows, columns = parts.shape
     step = min(rows, 32)
+    total_rows = into.shape[0] if into is not None else total_rows or rows
+    first = (total_rows - rows) // step if into is not None else 0
+    args, specs, aliases = (parts,), [pl.BlockSpec((group, step, columns), lambda i: (0, i, 0))], {}
+    if into is not None:
+        args, aliases = (parts, into), {1: 0}
+        specs.append(pl.BlockSpec(memory_space=pl.ANY))
     return pl.pallas_call(
         functools.partial(join_columns_kernel, group, runs),
         grid=(rows // step,),
-        in_specs=[pl.BlockSpec((group, step, columns), lambda i: (0, i, 0))],
-        out_specs=pl.BlockSpec((step, group * columns), lambda i: (i, 0)),
-        out_shape=jax.ShapeDtypeStruct((rows, group * columns), f32),
+        in_specs=specs,
+        out_specs=pl.BlockSpec((step, group * columns), lambda i: (first + i, 0)),
+        out_shape=jax.ShapeDtypeStruct((total_rows, group * columns), f32),
+        input_output_aliases=aliases,
         compiler_params=MIXER_PARAMS,
         name="join_columns",
-    )(parts)
+    )(*args)
 
 
 def rms_scale(values, gain):
@@ -684,6 +802,13 @@
 def swiglu(gate_up):
     half = gate_up.shape[1] // 2
     return jax.nn.silu(gate_up[:, :half]) * gate_up[:, half:]
+
+
+def sum_parts(own, others):
+    total = own.astype(f32)
+    for part in others:
+        total = total + part.astype(f32)
+    return total
 
 
 def dot(left, right):
@@ -753,16 +878,13 @@
     def gather_any(self, rows):
         return jnp.concatenate([self.swap(rows, turn) for turn in range(self.group)], axis=0)
 
-    def reduce_any(self, partial, beside=()):
-        got = []
-        for turn in range(1, self.group):
-            sent = partial[turn * self.rows : (turn + 1) * self.rows].astype(bf16)
-            got.append(self.swap(sent, turn))
-        got, beside = lax.optimization_barrier((got, beside))
-        total = partial[: self.rows]
-        for part in got:
-            total = total + part.astype(f32)
-        return total, beside
+    def send_any(self, partial):
+        own = partial[: self.rows]
+        got = [
+            self.swap(partial[turn * self.rows : (turn + 1) * self.rows], turn)
+            for turn in range(1, self.group)
+        ]
+        return own, got
 
     def gather_places(self, rows, beside=()):
         width = rows.shape[1]
@@ -774,7 +896,7 @@
             lane = lax.dynamic_update_slice(lane, part, (0, self.part ^ turn, 0, 0))
         return lane.reshape(-1, width), beside
 
-    def reduce_places(self, partial, beside=()):
+    def send_places(self, partial):
         width = partial.shape[1]
         lane = partial.reshape(self.sources, self.group, self.per, width)
         parts = [
@@ -783,27 +905,34 @@
             ).reshape(self.rows, width)
             for turn in range(self.group)
         ]
-        got = [self.swap(parts[turn].astype(bf16), turn) for turn in range(1, self.group)]
-        got, beside = lax.optimization_barrier((got, beside))
-        total = parts[0]
-        for part in got:
-            total = total + part.astype(f32)
-        return total, beside
+        return parts[0], [self.swap(parts[turn], turn) for turn in range(1, self.group)]
+
+    def near_turns(self, value):
+        return (value, self.swap(value, 1), self.swap(value, 2))
+
+    def far_turn(self, near):
+        rows = near[0].shape[0] // 2
+        return near + ((self.swap(near[2][:rows], 1), self.swap(near[1][rows:], 2)),)
+
+    def turns_of(self, value):
+        if self.group == 4 and value.ndim == 2 and value.shape[0] % 2 == 0:
+            return self.far_turn(self.near_turns(value))
+        return tuple(self.swap(value, turn) for turn in range(self.group))
+
+    def by_owner(self, turns):
+        value = turns[0]
+        parts = jnp.zeros((self.group,) + value.shape, value.dtype)
+        for turn, got in enumerate(turns):
+            owner, begin = self.part ^ turn, 0
+            for piece in got if isinstance(got, tuple) else (got,):
+                parts = lax.dynamic_update_slice(
+                    parts, piece[None], (owner, begin) + (0,) * (value.ndim - 1)
+                )
+                begin += piece.shape[0]
+        return parts
 
     def gather_parts(self, value):
-        if self.group == 4 and value.ndim == 2 and value.shape[0] % 2 == 0:
-            rows = value.shape[0] // 2
-            one, two = self.swap(value, 1), self.swap(value, 2)
-            three = jnp.concatenate([self.swap(two[:rows], 1), self.swap(one[rows:], 2)], axis=0)
-            turns = (value, one, two, three)
-        else:
-            turns = tuple(self.swap(value, turn) for turn in range(self.group))
-        parts = jnp.zeros((self.group,) + value.shape, value.dtype)
-        for turn in range(self.group):
-            parts = lax.dynamic_update_slice(
-                parts, turns[turn][None], (self.part ^ turn,) + (0,) * value.ndim
-            )
-        return parts
+        return self.by_owner(self.turns_of(value))
 
     def to_lane(self, rows):
         if self.subs == 1:
@@ -843,29 +972,39 @@
         got = lax.ppermute(self.core_rows(grad, 1 - self.core), "wshard", [(0, 1), (1, 0)])
         return (self.core_rows(grad, self.core).astype(f32) + got.astype(f32)).astype(bf16)
 
-    def core_columns(self, array):
+    def core_columns(self, array, halves_of=1):
+        rows, columns = array.shape
+        run = columns // (self.seq * self.cores)
+        size = run // halves_of
+        out = []
+        for half in range(halves_of):
+            picked = []
+            for core in (1 - self.core, self.core) if self.cores == 2 else range(self.cores):
+                picked.append(
+                    [
+                        lax.dynamic_slice(
+                            array,
+                            (0, (place * self.cores + core) * run + half * size),
+                            (rows, size),
+                        )
+                        for place in range(self.seq)
+                    ]
+                )
+            if self.cores == 2:
+                out.append(tuple(jnp.concatenate(pieces, axis=1) for pieces in picked))
+            else:
+                every = [pieces[place] for place in range(self.seq) for pieces in picked]
+                out.append((jnp.concatenate(every, axis=1),))
+        return out
+
+    def other_grad(self, lefts, right):
         if self.cores != 2:
-            return (array,)
-        rows, columns = array.shape
-        run = columns // (self.seq * 2)
-        picked = []
-        for core in (1 - self.core, self.core):
-            picked.append(
-                jnp.concatenate(
-                    [
-                        lax.dynamic_slice(array, (0, (2 * place + core) * run), (rows, run))
-                        for place in range(self.seq)
-                    ],
-                    axis=1,
-                )
-            )
-        return tuple(picked)
-
-    def weight_grad(self, lefts, right):
-        if self.cores != 2:
-            return dot_t(lefts[0], right).astype(bf16)
-        got = lax.ppermute(dot_t(lefts[0], right).astype(bf16), "wshard", [(0, 1), (1, 0)])
-        return (dot_t(lefts[1], right) + got.astype(f32)).astype(bf16)
+            return None
+        return lax.ppermute(dot_t(lefts[0], right).astype(bf16), "wshard", [(0, 1), (1, 0)])
+
+    def own_grad(self, lefts, right, got):
+        own = dot_t(lefts[-1], right)
+        return (own if got is None else own + got.astype(f32)).astype(bf16)
 
     def scatter(self, grad):
         axes = "seq" if self.cores == 2 else SHARDED
@@ -889,7 +1028,8 @@
 
     def out_grad(self, gated, d_branch):
         if self.subs == 1 and self.cores == 2:
-            return self.weight_grad(self.core_columns(gated), d_branch)
+            lefts = self.core_columns(gated)[0]
+            return self.own_grad(lefts, d_branch, self.other_grad(lefts, d_branch))
         width = d_branch.shape[1]
         grad = dot_t(gated, d_branch).astype(bf16)
         every = jnp.zeros((self.heads, self.group, DV, width), bf16)
@@ -1050,7 +1190,7 @@
     )
     normed_all, _ = at.gather_places(normed)
     normed_all, normed_cores = lax.optimization_barrier(
-        (normed_all, at.core_columns(normed_all))
+        (normed_all, at.core_columns(normed_all)[0])
     )
 
     out_mine = at.out_rows(w_out)
@@ -1077,13 +1217,13 @@
     gated_lane, *kept = mixer_forward(*mixer_args)
     gated_lane, cot_all = lax.optimization_barrier((gated_lane, cot_all))
     gated = at.to_own(gated_lane)
-    branch, _ = at.reduce_places(dot(gated, out_mine))
-    resid = tokens_f + branch
+    own, got = at.send_places(dot(gated, out_mine).astype(bf16))
+    resid = tokens_f + sum_parts(own, got)
 
     normed2_f, pull_norm2 = jax.vjp(rms_scale, resid, ffn_f)
     normed2_all = at.gather_any(normed2_f.astype(bf16))
     normed2_all, normed2_cores = lax.optimization_barrier(
-        (normed2_all, at.core_columns(normed2_all))
+        (normed2_all, at.core_columns(normed2_all)[0])
     )
     gate_up = dot(normed2_all, gu_mine)
     hidden_f, pull_ffn = jax.vjp(swiglu, gate_up)
@@ -1094,52 +1234,55 @@
     down_shard = at.scatter(d_down)
     d_hidden = dot_back(cot_back, down_mine)
     d_gate_up = pull_ffn(d_hidden)[0].astype(bf16)
-    d_normed2_parts = dot_back(d_gate_up, gu_mine)
+    d_normed2_parts = dot_back(d_gate_up, gu_mine).astype(bf16)
     d_normed2_parts, d_gate_up = lax.optimization_barrier((d_normed2_parts, d_gate_up))
-    d_gu = at.weight_grad(normed2_cores, d_gate_up)
-    d_normed2, d_gu = at.reduce_any(d_normed2_parts, d_gu)
+    own, got = at.send_any(d_normed2_parts)
+    d_gu = at.own_grad(normed2_cores, d_gate_up, at.other_grad(normed2_cores, d_gate_up))
+    got, d_gu = lax.optimization_barrier((got, d_gu))
     d_gu, down_shard = lax.optimization_barrier((d_gu, down_shard))
     gu_shard = at.scatter(d_gu)
+    d_normed2 = sum_parts(own, got)
     d_resid_norm, d_ffn_gain = pull_norm2(d_normed2)
     d_resid = cot_own.astype(f32) + d_resid_norm
 
-    d_branch_all, output_parts = at.gather_places(d_resid.astype(bf16), dot(hidden, down_mine))
+    d_branch_all, output_parts = at.gather_places(
+        d_resid.astype(bf16), dot(hidden, down_mine).astype(bf16)
+    )
     d_gated = dot_back(d_branch_all, out_mine)
     d_gated, output_parts, down_shard = lax.optimization_barrier(
         (d_gated, output_parts, down_shard)
     )
-    output_sum, _ = at.reduce_any(output_parts)
-    down_parts = at.gather_parts(down_shard)
+    output_own, output_got = at.send_any(output_parts)
+    down_turns = at.near_turns(down_shard)
     d_proj_lane, d_gates_lane, d_conv_w, d_o_gain, d_heads = mixer_backward(
         *mixer_args, tuple(kept), at.to_lane(d_gated)
     )
-    d_proj_lane, output_sum, down_parts = lax.optimization_barrier(
-        (d_proj_lane, output_sum, down_parts)
+    d_proj_lane, output_got, down_turns = lax.optimization_barrier(
+        (d_proj_lane, output_got, down_turns)
     )
     once = (at.sub == 0).astype(f32)
     d_conv_w, d_o_gain, d_heads = d_conv_w * once, d_o_gain * once, d_heads * once
     d_proj = at.to_own(d_proj_lane)
     d_ab = at.to_own(d_gates_lane).astype(bf16)
-    d_in = at.weight_grad(normed_cores, d_proj)
-    d_in, d_proj, d_ab, d_branch_all, output_sum, gu_shard = lax.optimization_barrier(
-        (d_in, d_proj, d_ab, d_branch_all, output_sum, gu_shard)
+    d_in = at.own_grad(normed_cores, d_proj, at.other_grad(normed_cores, d_proj))
+    d_in, d_proj, d_ab, d_branch_all, output_got, gu_shard = lax.optimization_barrier(
+        (d_in, d_proj, d_ab, d_branch_all, output_got, gu_shard)
     )
     in_shard = at.scatter(d_in)
-    output = at.undeal((resid + output_sum).astype(bf16))
-    d_normed_parts = dot_back(d_proj, in_mine) + dot_back(d_ab, ab_mine)
+    output = (resid + sum_parts(output_own, output_got)).astype(bf16)
+    d_normed_parts = (dot_back(d_proj, in_mine) + dot_back(d_ab, ab_mine)).astype(bf16)
     d_normed_parts, d_branch_all, d_ab = lax.optimization_barrier(
         (d_normed_parts, d_branch_all, d_ab)
     )
-    d_normed, (d_out, d_w_ab) = at.reduce_places(
-        d_normed_parts, (at.out_grad(gated, d_branch_all), dot_t(normed_all, d_ab))
-    )
-    d_normed, gu_shard, output = lax.optimization_barrier((d_normed, gu_shard, output))
+    own, got = at.send_places(d_normed_parts)
+    d_out = at.out_grad(gated, d_branch_all)
+    d_w_ab = dot_t(normed_all, d_ab)
+    got, d_out, d_w_ab, output = lax.optimization_barrier((got, d_out, d_w_ab, output))
+    d_normed = sum_parts(own, got)
     value_norm, pull_norm = jax.vjp(rms_scale, tokens_f, attn_f)
     d_tokens_norm, d_attn_gain = pull_norm(d_normed)
     d_tokens = (d_resid + d_tokens_norm).astype(bf16)
 
-    input_grad = dot_t(sorting, at.undeal(d_tokens)).astype(bf16)
-    output = dot_t(sorting, output).astype(bf16)
 
     def to_blocks(array):
         return array.reshape(devices, -1)
@@ -1161,14 +1304,17 @@
     summed = small_sum(packed.reshape(devices, rows_small, 128), at.seq, at.cores, at.group)
 
     grad_w_gu = join_columns(at.gather_parts(gu_shard), ((piece, 2 * devices),))
-    grad_w_down = down_parts.reshape(device_rows, width).astype(f32)
-    in_shard, summed, input_grad, d_out = lax.optimization_barrier(
-        (in_shard, summed, input_grad, d_out)
+    grad_w_down = at.by_owner(at.far_turn(down_turns)).reshape(device_rows, width).astype(f32)
+    in_runs = tuple((piece_width, heads) for _, piece_width in QKV + GATE)
+    in_shard, d_out, summed, grad_w_gu, d_tokens, output = lax.optimization_barrier(
+        (in_shard, d_out, summed, grad_w_gu, d_tokens, output)
     )
     out_shard = at.scatter(d_out)
-    grad_w_in = join_columns(
-        at.gather_parts(in_shard), tuple((piece_width, heads) for _, piece_width in QKV + GATE)
-    )
+    returned = at.undeal(jnp.concatenate([output, d_tokens], axis=1))
+    in_parts = plane_gather(in_shard) if at.group == 4 else at.gather_parts(in_shard)
+    in_parts, out_shard, returned = lax.optimization_barrier((in_parts, out_shard, returned))
+    returned = dot_t(sorting, returned).astype(bf16)
+    grad_w_in = join_columns(in_parts, in_runs)
     grad_w_out = at.out_rows_join(out_shard)
 
     summed = summed.reshape(at.group, -1)
@@ -1179,8 +1325,8 @@
     grad_w_ab = parts[3].reshape(at.group, width // devices, 2, heads).transpose(1, 2, 3, 0)
     grad_heads = parts[5].reshape(at.group, 2, heads).transpose(1, 2, 0).reshape(2, H)
     return (
-        output,
-        input_grad,
+        returned[:, :width],
+        returned[:, width:],
         jnp.sum(parts[0], axis=0),
         grad_w_in,
         grad_w_ab.reshape(width // devices, 2 * H),

time: 883 us -> 842 us (0.954)
  waiting for transfers between devices: 333 us -> 315 us
  local copies, waits for them, and re-layouts: 79.1 us -> 68.6 us
    pallas_call x0 -> x1, Pallas kernels: none -> 52.6 us  [plane_gather(): pl.pallas_call(plane_gather_kernel, out_shape=jax.ShapeDtypeStruct((4,) +...]
    pallas_call x1, Pallas kernels: 40.3 us -> 12.6 us  [small_sum(): pl.pallas_call(functools.partial(small_sum_kernel, seq, cores, group), ou...]
    ppermute x43 -> x39, waiting for transfers between devices: 218 us -> 191 us  [swap(): lax.ppermute(value, 'group', [(i, i ^ turn) for i in range(self.group)])]
    pallas_call x1, Pallas kernels: 50.1 us -> 38.6 us  [mixer_backward(): pl.pallas_call(functools.partial(mixer_backward_kernel, heads), grid=(blo...]
    ppermute x43 -> x39, starting transfers between devices: 48 us -> 44.7 us  [swap(): lax.ppermute(value, 'group', [(i, i ^ turn) for i in range(self.group)])]
    dot_general x10 -> x9, matrix products: 47 us -> 44.6 us  [dot_t(): lax.dot_general(left, right, (((0,), (0,)), ((), ())), preferred_element_...]
  transfers between devices with their start and end apart: 61 -> 56, of which waited for: 28 -> 30; matrix products, arithmetic and copies ran while one was open for 27% -> 26% of each run, Pallas kernels for 18% -> 20%
where the time goes in v4:
time: 842 us; the launch traced here: 835 us
  waiting for transfers between devices  315 us (37%)
  Pallas kernels  170 us (20%)
  matrix products  146 us (17%)
  local copies, waits for them, and re-layouts  68.6 us (8%)
  starting transfers between devices  61 us (7%)
  other arithmetic  58.7 us (7%)
  between operations  15.7 us (2%)
    ppermute x39, waiting for transfers between devices, swap(): lax.ppermute(value, 'group', [(i, i ^ turn) for i in range(self.group)])  191 us
    dot_general x8, matrix products, dot(): return jnp.dot(left, right, preferred_element_type=f32)  53.1 us
    pallas_call x1, Pallas kernels, plane_gather(): pl.pallas_call(plane_gather_kernel, out_shape=jax.ShapeDtypeStruct((4,) +...  52.6 us
    all_to_all x2, waiting for transfers between devices, deal(): lax.all_to_all(sorted_rows, 'seq', split_axis=0, concat_axis=0, tiled=True)  51.3 us
    dot_general x5, matrix products, dot_back(): lax.dot_general(left, right, (((1,), (1,)), ((), ())), preferred_element_...  48 us
    ppermute x39, starting transfers between devices, swap(): lax.ppermute(value, 'group', [(i, i ^ turn) for i in range(self.group)])  44.7 us
    dot_general x9, matrix products, dot_t(): lax.dot_general(left, right, (((0,), (0,)), ((), ())), preferred_element_...  44.6 us
    pallas_call x1, Pallas kernels, mixer_backward(): pl.pallas_call(functools.partial(mixer_backward_kernel, heads), grid=(blo...  38.6 us
  transfers between devices with their start and end apart: 56, of which 30 were waited for; matrix products, arithmetic and copies ran while one was open for 26% of the time, Pallas kernels for 20%

profile of v4, /device:TPU:0, one launch (start us, length us, event | category | flops | bytes accessed | tf_op | source)
XLA Modules:
  0.0 835.2 jit_solution(5245929488894506381)
XLA Ops:
  31.9 42.5 %all-to-all-done = bf16[4,48,2048]{2,1,0:T(8,128)(2,1)} async-done(((bf16[4,48,2048]{2,1,0:T(8,128)(2,1)}), bf16[4,48,2048]{2,1,0:T(8,128)(2,1)}, u32[]{:S(2)}, u32[]{:S(2)}) %all-to-all-start) | async-done | bytes 786464 | tf_op jit(solution)/shard_map/all_to_all | solution.py:848
  117.5 14.8 %collective-permute-done.1 = bf16[192,2048]{1,0:T(8,128)(2,1)} collective-permute-done((bf16[192,2048]{1,0:T(8,128)(2,1)}, bf16[192,2048]{1,0:T(8,128)(2,1)}, u32[]{:S(2)}, u32[]{:S(2)}) %collective-permute-start.1) | collective-permute-done | bytes 786464 | tf_op jit(solution)/shard_map/ppermute | solution.py:876
  148.2 20.2 %all-gather.5.cloned.1.call-done = bf16[2048,3072]{1,0:T(8,128)(2,1)} async-done(((bf16[256,3072]{1,0:T(8,128)(2,1)}), bf16[2048,3072]{1,0:T(8,128)(2,1)}) %all-gather.5.cloned.1.call-update) | async-done | bytes 12582928 | tf_op jit(solution)/shard_map/all_gather | solution.py:1164
  168.4 16.0 %fusion.62.conv_ref.gate_ref.ahead_ref = f32[768,3072]{1,0:T(8,128)} fusion(bf16[768,2048]{1,0:T(8,128)(2,1)} %bitcast.210, bf16[2048,3072]{1,0:T(8,128)(2,1)} %all-gather.5.cloned.1.call-done), kind=kOutput, calls=%fused_computation.221 | convolution fusion | flops 9663676416 | bytes 25165824 | tf_op jit(solution)/shard_map/dot_general | solution.py:815
  193.2 32.2 %mixer_forward.1 = (bf16[768,1024]{1,0:T(8,128)(2,1)S(1)}, f32[768,1024]{1,0:T(8,128)}, bf16[768,2048]{1,0:T(8,128)(2,1)}, f32[12,4,128,256]{3,2,1,0:T(8,128)}, ...) custom-call(f32[768,3072]{1,0:T(8,128)} %fusion.62.conv_ref.gate_ref.ahead_ref, ...), custom_call_target="tpu_custom_call" | custom-call | flops 768 | bytes 768 | tf_op jit(solution)/shard_map/mixer_forward/pallas_call | solution.py:463
  242.4 16.2 %collective-permute-done.10 = bf16[192,2048]{1,0:T(8,128)(2,1)} collective-permute-done((bf16[192,2048]{1,0:T(8,128)(2,1)}, bf16[192,2048]{1,0:T(8,128)(2,1)}, u32[]{:S(2)}, u32[]{:S(2)}) %collective-permute-start.10) | collective-permute-done | bytes 786464 | tf_op jit(solution)/shard_map/ppermute | solution.py:876
  258.6 16.8 %collective-permute-done.11 = bf16[192,2048]{1,0:T(8,128)(2,1)} collective-permute-done((bf16[192,2048]{1,0:T(8,128)(2,1)}, bf16[192,2048]{1,0:T(8,128)(2,1)}, u32[]{:S(2)}, u32[]{:S(2)}) %collective-permute-start.11) | collective-permute-done | bytes 786464 | tf_op jit(solution)/shard_map/ppermute | solution.py:876
  283.0 17.1 %collective-permute-done.13 = bf16[192,2048]{1,0:T(8,128)(2,1)} collective-permute-done((bf16[192,2048]{1,0:T(8,128)(2,1)S(1)}, bf16[192,2048]{1,0:T(8,128)(2,1)}, u32[]{:S(2)}, u32[]{:S(2)}) %collective-permute-start.13) | collective-permute-done | bytes 786464 | tf_op jit(solution)/shard_map/ppermute | solution.py:876
  300.1 15.4 %collective-permute-done.14 = bf16[192,2048]{1,0:T(8,128)(2,1)} collective-permute-done((bf16[192,2048]{1,0:T(8,128)(2,1)S(1)}, bf16[192,2048]{1,0:T(8,128)(2,1)}, u32[]{:S(2)}, u32[]{:S(2)}) %collective-permute-start.14) | collective-permute-done | bytes 786464 | tf_op jit(solution)/shard_map/ppermute | solution.py:876
  324.4 13.7 %fusion.64 = f32[768,2816]{1,0:T(8,128)S(1)} fusion(bf16[768,2048]{1,0:T(8,128)(2,1)} %copy-done.19, bf16[2048,2816]{1,0:T(8,128)(2,1)} %all-gather.9.cloned.1.call-done), kind=kOutput, calls=%fused_computation.223 | convolution fusion | flops 8858370048 | bytes 23330816 | tf_op jit(solution)/shard_map/dot_general | solution.py:815
  356.8 27.8 %all-gather.11.cloned.1.call-done = bf16[1408,2048]{1,0:T(8,128)(2,1)} async-done(((bf16[176,2048]{1,0:T(8,128)(2,1)}), bf16[1408,2048]{1,0:T(8,128)(2,1)}) %all-gather.11.cloned.1.call-update) | async-done | bytes 5767184 | tf_op jit(solution)/shard_map/all_gather | solution.py:1202
  384.6 12.7 %fusion.32 = (f32[768,1408]{1,0:T(8,128)S(1)}, f32[768,1408]{1,0:T(8,128)}) fusion(f32[768,2816]{1,0:T(8,128)} %copy-done.20, bf16[768,2048]{1,0:T(8,128)(2,1)} %pad_maximum_fusion, bf16[1408,2048]{1,0:T(8,128)(2,1)} %all-gather.11.cloned.1.call-done), kind=kOutput, calls=%fused_computation.88 | convolution fusion | flops 4442161152 | bytes 26214400 | tf_op jit(solution)/shard_map/dot_general | solution.py:823
  400.0 14.8 %convolution_convert_fusion.6 = bf16[768,2048]{1,0:T(8,128)(2,1)} fusion(bf16[768,2816]{1,0:T(8,128)(2,1)S(1)} %add_convert_fusion.2, bf16[2048,2816]{1,0:T(8,128)(2,1)} %all-gather.9.cloned.1.call-done), kind=kOutput, calls=%fused_computation.19 | convolution fusion | flops 8859942912 | bytes 19005440 | tf_op jit(solution)/shard_map/dot_general | solution.py:823
  431.1 9.2 %add_convert_fusion.1 = bf16[1024,2816]{1,0:T(8,128)(2,1)} fusion(bf16[1024,2816]{1,0:T(8,128)(2,1)} %collective-permute-done.20, bf16[768,1024]{1,0:T(8,128)(2,1)} %pad_maximum_fusion.6, bf16[768,2816]{1,0:T(8,128)(2,1)S(1)} %copy-done.23), kind=kOutput, calls=%fused_computation.1 | convolution fusion | flops 4437835776 | bytes 17432576 | tf_op jit(solution)/shard_map/dot_general | solution.py:819
  445.5 17.4 %collective-permute-done.18 = bf16[192,2048]{1,0:T(8,128)(2,1)} collective-permute-done((bf16[192,2048]{1,0:T(8,128)(2,1)}, bf16[192,2048]{1,0:T(8,128)(2,1)}, u32[]{:S(2)}, u32[]{:S(2)}) %collective-permute-start.18) | collective-permute-done | bytes 786464 | tf_op jit(solution)/shard_map/ppermute | solution.py:876
  471.5 9.3 %convolution_convert_fusion.5 = bf16[768,2048]{1,0:T(8,128)(2,1)} fusion(bf16[768,1408]{1,0:T(8,128)(2,1)S(1)} %copy-done.32, bf16[1408,2048]{1,0:T(8,128)(2,1)} %all-gather.11.cloned.1.call-done), kind=kOutput, calls=%fused_computation.18 | convolution fusion | flops 4430757888 | bytes 11075584 | tf_op jit(solution)/shard_map/dot_general | solution.py:815
  488.5 16.2 %collective-permute-done.22 = bf16[192,2048]{1,0:T(8,128)(2,1)S(1)} collective-permute-done((bf16[192,2048]{1,0:T(8,128)(2,1)S(1)}, bf16[192,2048]{1,0:T(8,128)(2,1)S(1)}, u32[]{:S(2)}, u32[]{:S(2)}) %collective-permute-start.22) | collective-permute-done | bytes 786464 | tf_op jit(solution)/shard_map/ppermute | solution.py:876
  517.1 38.6 %mixer_backward.1 = (bf16[768,3072]{1,0:T(8,128)(2,1)}, f32[768,8]{1,0:T(8,128)S(1)}, f32[4,2048]{1,0:T(4,128)S(1)}, f32[1,256]{1,0:T(1,128)S(1)}, f32[1,8]{1,0:T(1,128)S(1)}) custom-call(f32[768,3072]{1,0:T(8,128)} %fusion.62.conv_ref.gate_ref.ahead_ref, f32[768,3072]{1,0:T(8,128)} %fusion.62.conv_ref.gate_ref.ahead_ref, ...), custom_call_target="tpu_custom_call" | custom-call | flops 768 | bytes 768 | tf_op jit(solution)/shard_map/mixer_backward/pallas_call | solution.py:510
  570.9 10.1 %collective-permute-done.29 = bf16[1024,3072]{1,0:T(8,128)(2,1)S(1)} collective-permute-done((bf16[1024,3072]{1,0:T(8,128)(2,1)S(1)}, bf16[1024,3072]{1,0:T(8,128)(2,1)S(1)}, u32[]{:S(2)}, u32[]{:S(2)}) %collective-permute-start.29) | collective-permute-done | bytes 6291488 | tf_op jit(solution)/shard_map/ppermute | solution.py:1003
  593.6 14.4 %fusion.66 = f32[768,2048]{1,0:T(8,128)S(1)} fusion(bf16[768,3072]{1,0:T(8,128)(2,1)} %get-tuple-element.156, bf16[2048,3072]{1,0:T(8,128)(2,1)} %all-gather.5.cloned.1.call-done), kind=kOutput, calls=%fused_computation.225 | convolution fusion | flops 9663676416 | bytes 23592960 | tf_op jit(solution)/shard_map/dot_general | solution.py:823
  643.0 18.2 %collective-permute-done.31 = bf16[192,2048]{1,0:T(8,128)(2,1)} collective-permute-done((bf16[192,2048]{1,0:T(8,128)(2,1)}, bf16[192,2048]{1,0:T(8,128)(2,1)}, u32[]{:S(2)}, u32[]{:S(2)}) %collective-permute-start.31) | collective-permute-done | bytes 786464 | tf_op jit(solution)/shard_map/ppermute | solution.py:876
  671.1 12.6 %small_sum.1 = f32[4,32,128]{2,1,0:T(8,128)} custom-call(f32[8,32,128]{2,1,0:T(8,128)} %bitcast.230), custom_call_target="tpu_custom_call" | custom-call | tf_op jit(solution)/shard_map/small_sum/pallas_call | solution.py:654
  687.8 9.4 %join_columns.2 = f32[256,11264]{1,0:T(8,128)} custom-call(bf16[4,256,2816]{2,1,0:T(8,128)(2,1)} %bitcast_dynamic-update-slice_fusion.6.parts_ref), custom_call_target="tpu_custom_call" | custom-call | tf_op jit(solution)/shard_map/join_columns/pallas_call | solution.py:786
  727.0 52.6 %plane_gather.1.parts_ref = bf16[4,256,3072]{2,1,0:T(8,128)(2,1)S(1)} custom-call(bf16[256,3072]{1,0:T(8,128)(2,1)S(1)} %copy-done.12), custom_call_target="tpu_custom_call" | custom-call | tf_op jit(solution)/shard_map/plane_gather/pallas_call | solution.py:711
  (418 shorter events, 351.4 us)
Async XLA Ops:
  7.2 161.2 %all-gather.5.cloned.1.call-start = ((), (), s32[]{:S(2)}) async-start(), calls=%async_computation.7 | async-start | bytes 14155776 | tf_op jit(solution)/shard_map/all_gather | solution.py:1164
  27.2 47.1 %all-to-all-start = ((bf16[4,48,2048]{2,1,0:T(8,128)(2,1)}), bf16[4,48,2048]{2,1,0:T(8,128)(2,1)}, u32[]{:S(2)}, u32[]{:S(2)}) async-start(bf16[4,48,2048]{2,1,0:T(8,128)(2,1)} %bitcast.222), calls=%async_computation | async-start | bytes 1572864 | tf_op jit(solution)/shard_map/all_to_all | solution.py:848
  31.8 198.2 %all-gather.7.cloned.1.call-start = ((), (), s32[]{:S(2)}) async-start(), calls=%async_computation.8 | async-start | bytes 4718592 | tf_op jit(solution)/shard_map/all_gather | solution.py:1022
  84.1 240.2 %all-gather.9.cloned.1.call-start = ((), (), s32[]{:S(2)}) async-start(), calls=%async_computation.9 | async-start | bytes 12976128 | tf_op jit(solution)/shard_map/all_gather | solution.py:1199
  102.9 45.2 %all-to-all-start.1 = ((bf16[4,48,2048]{2,1,0:T(8,128)(2,1)}), bf16[4,48,2048]{2,1,0:T(8,128)(2,1)}, u32[]{:S(2)}, u32[]{:S(2)}) async-start(bf16[4,48,2048]{2,1,0:T(8,128)(2,1)} %bitcast.223), calls=%async_computation.1 | async-start | bytes 1572864 | tf_op jit(solution)/shard_map/all_to_all | solution.py:848
  107.2 277.5 %all-gather.11.cloned.1.call-start = ((), (), s32[]{:S(2)}) async-start(), calls=%async_computation.10 | async-start | bytes 6488064 | tf_op jit(solution)/shard_map/all_gather | solution.py:1202
  184.4 41.1 %collective-permute-start.6 = (bf16[192,2048]{1,0:T(8,128)(2,1)}, bf16[192,2048]{1,0:T(8,128)(2,1)}, u32[]{:S(2)}, u32[]{:S(2)}) collective-permute-start(bf16[192,2048]{1,0:T(8,128)(2,1)} %bitcast.13), channel_id=1, source_target_pairs={{0,8},{8,0},{16,24},{24,16},{1,9},{9,1},{17,25},{25,17},{2,10},{10... | collective-permute-start | bytes 2359304 | tf_op jit(solution)/shard_map/ppermute | solution.py:876
  185.8 39.6 %collective-permute-start.7 = (bf16[192,2048]{1,0:T(8,128)(2,1)}, bf16[192,2048]{1,0:T(8,128)(2,1)}, u32[]{:S(2)}, u32[]{:S(2)}) collective-permute-start(bf16[192,2048]{1,0:T(8,128)(2,1)} %bitcast.13), channel_id=1, source_target_pairs={{0,16},{8,24},{16,0},{24,8},{1,17},{9,25},{17,1},{25,9},{2,18},{10... | collective-permute-start | bytes 2359304 | tf_op jit(solution)/shard_map/ppermute | solution.py:876
  187.3 38.1 %collective-permute-start.8 = (bf16[192,2048]{1,0:T(8,128)(2,1)}, bf16[192,2048]{1,0:T(8,128)(2,1)}, u32[]{:S(2)}, u32[]{:S(2)}) collective-permute-start(bf16[192,2048]{1,0:T(8,128)(2,1)} %bitcast.13), channel_id=1, source_target_pairs={{0,24},{8,16},{16,8},{24,0},{1,25},{9,17},{17,9},{25,1},{2,26},{10... | collective-permute-start | bytes 2359304 | tf_op jit(solution)/shard_map/ppermute | solution.py:876
  242.3 238.5 %reduce-scatter.5.cloned.1.call-start = ((), (), s32[]{:S(2)}) async-start(), calls=%async_computation.11 | async-start | bytes 3604480 | tf_op jit(solution)/shard_map/reduce_scatter | solution.py:1011
  421.6 166.7 %reduce-scatter.7.cloned.1.call-start = ((), (), s32[]{:S(2)}) async-start(), calls=%async_computation.12 | async-start | bytes 7208960 | tf_op jit(solution)/shard_map/reduce_scatter | solution.py:1011
  426.3 36.6 %collective-permute-start.18 = (bf16[192,2048]{1,0:T(8,128)(2,1)}, bf16[192,2048]{1,0:T(8,128)(2,1)}, u32[]{:S(2)}, u32[]{:S(2)}) collective-permute-start(bf16[192,2048]{1,0:T(8,128)(2,1)} %get-tuple-element.216), channel_id=1, source_target_pairs={{0,16},{8,24},{16,0},{24,8},{1,17},{9,25},{17,1},{25,9},{2,18},{10... | collective-permute-start | bytes 2359304 | tf_op jit(solution)/shard_map/ppermute | solution.py:876
  480.8 218.5 %reduce-scatter.9.cloned.1.call-start = ((), (), s32[]{:S(2)}) async-start(), calls=%async_computation.13 | async-start | bytes 7864320 | tf_op jit(solution)/shard_map/reduce_scatter | solution.py:1011
  511.5 50.3 %collective-permute-start.24 = (bf16[192,2048]{1,0:T(8,128)(2,1)S(1)}, bf16[192,2048]{1,0:T(8,128)(2,1)S(1)}, u32[]{:S(2)}, u32[]{:S(2)}) collective-permute-start(bf16[192,2048]{1,0:T(8,128)(2,1)S(1)} %get-tuple-element.214), channel_id=1, source_target_pairs={{0,8},{8,0},{16,24},{24,16},{1,9},{9,1},{17,25},{25,17},{2,10},{10... | collective-permute-start | bytes 2359304 | tf_op jit(solution)/shard_map/ppermute | solution.py:876
  512.2 49.6 %collective-permute-start.25 = (bf16[192,2048]{1,0:T(8,128)(2,1)S(1)}, bf16[192,2048]{1,0:T(8,128)(2,1)S(1)}, u32[]{:S(2)}, u32[]{:S(2)}) collective-permute-start(bf16[192,2048]{1,0:T(8,128)(2,1)S(1)} %get-tuple-element.213), channel_id=1, source_target_pairs={{0,16},{8,24},{16,0},{24,8},{1,17},{9,25},{17,1},{25,9},{2,18},{10... | collective-permute-start | bytes 2359304 | tf_op jit(solution)/shard_map/ppermute | solution.py:876
  513.6 48.2 %collective-permute-start.26 = (bf16[192,2048]{1,0:T(8,128)(2,1)S(1)}, bf16[192,2048]{1,0:T(8,128)(2,1)S(1)}, u32[]{:S(2)}, u32[]{:S(2)}) collective-permute-start(bf16[192,2048]{1,0:T(8,128)(2,1)S(1)} %get-tuple-element.212), channel_id=1, source_target_pairs={{0,24},{8,16},{16,8},{24,0},{1,25},{9,17},{17,9},{25,1},{2,26},{10... | collective-permute-start | bytes 2359304 | tf_op jit(solution)/shard_map/ppermute | solution.py:876
  515.1 46.4 %collective-permute-start.27 = (bf16[176,2048]{1,0:T(8,128)(2,1)S(1)}, bf16[176,2048]{1,0:T(8,128)(2,1)S(1)}, u32[]{:S(2)}, u32[]{:S(2)}) collective-permute-start(bf16[176,2048]{1,0:T(8,128)(2,1)S(1)} %copy-done.47), channel_id=1, source_target_pairs={{0,8},{8,0},{16,24},{24,16},{1,9},{9,1},{17,25},{25,17},{2,10},{10... | collective-permute-start | bytes 2162696 | tf_op jit(solution)/shard_map/ppermute | solution.py:876
  515.7 46.1 %collective-permute-start.28 = (bf16[176,2048]{1,0:T(8,128)(2,1)S(1)}, bf16[176,2048]{1,0:T(8,128)(2,1)S(1)}, u32[]{:S(2)}, u32[]{:S(2)}) collective-permute-start(bf16[176,2048]{1,0:T(8,128)(2,1)S(1)} %copy-done.47), channel_id=1, source_target_pairs={{0,16},{8,24},{16,0},{24,8},{1,17},{9,25},{17,1},{25,9},{2,18},{10... | collective-permute-start | bytes 2162696 | tf_op jit(solution)/shard_map/ppermute | solution.py:876
  588.3 194.2 %reduce-scatter.11.cloned.1.call-start = ((), (), s32[]{:S(2)}) async-start(), calls=%async_computation.14 | async-start | bytes 2621440 | tf_op jit(solution)/shard_map/reduce_scatter | solution.py:1011
  591.4 38.7 %collective-permute-start.34 = (bf16[256,2816]{1,0:T(8,128)(2,1)}, bf16[256,2816]{1,0:T(8,128)(2,1)S(1)}, u32[]{:S(2)}, u32[]{:S(2)}) collective-permute-start(bf16[256,2816]{1,0:T(8,128)(2,1)} %reduce-scatter.7.cloned.1.call-done), channel_id=1, source_target_pairs={{0,8},{8,0},{16,24},{24,16},{1,9},{9,1},{17,25},{25,17},{2,10},{10... | collective-permute-start | bytes 4325384 | tf_op jit(solution)/shard_map/ppermute | solution.py:876
  619.6 41.6 %collective-permute-start.31 = (bf16[192,2048]{1,0:T(8,128)(2,1)}, bf16[192,2048]{1,0:T(8,128)(2,1)}, u32[]{:S(2)}, u32[]{:S(2)}) collective-permute-start(bf16[192,2048]{1,0:T(8,128)(2,1)} %bitcast.43), channel_id=1, source_target_pairs={{0,16},{8,24},{16,0},{24,8},{1,17},{9,25},{17,1},{25,9},{2,18},{10... | collective-permute-start | bytes 2359304 | tf_op jit(solution)/shard_map/ppermute | solution.py:876
  630.1 53.6 %collective-permute-start.36 = (bf16[128,2816]{1,0:T(8,128)(2,1)}, bf16[128,2816]{1,0:T(8,128)(2,1)}, u32[]{:S(2)}, u32[]{:S(2)}) collective-permute-start(bf16[128,2816]{1,0:T(8,128)(2,1)} %slice.138), channel_id=1, source_target_pairs={{0,8},{8,0},{16,24},{24,16},{1,9},{9,1},{17,25},{25,17},{2,10},{10... | collective-permute-start | bytes 2162696 | tf_op jit(solution)/shard_map/ppermute | solution.py:876
  634.0 51.8 %collective-permute-start.37 = (bf16[128,2816]{1,0:T(8,128)(2,1)}, bf16[128,2816]{1,0:T(8,128)(2,1)}, u32[]{:S(2)}, u32[]{:S(2)}) collective-permute-start(bf16[128,2816]{1,0:T(8,128)(2,1)} %slice.139), channel_id=1, source_target_pairs={{0,16},{8,24},{16,0},{24,8},{1,17},{9,25},{17,1},{25,9},{2,18},{10... | collective-permute-start | bytes 2162696 | tf_op jit(solution)/shard_map/ppermute | solution.py:876
  703.5 78.9 %all-to-all-start.2 = ((bf16[4,48,4096]{2,1,0:T(8,128)(2,1)}), bf16[4,48,4096]{2,1,0:T(8,128)(2,1)}, u32[]{:S(2)}, u32[]{:S(2)}) async-start(bf16[4,48,4096]{2,1,0:T(8,128)(2,1)} %bitcast.54), calls=%async_computation.6 | async-start | bytes 3145728 | tf_op jit(solution)/shard_map/all_to_all | solution.py:863
  (100 other events, 1728.5 us)
Sparse Core Ops, SparseCore 0:
  15.5 152.8 all-gather.4
  170.0 45.2 all-gather.6
  217.5 106.8 all-gather.8
  325.9 58.7 all-gather.10
  421.7 54.8 reduce-scatter.4
  480.9 100.5 reduce-scatter.6
  588.4 110.8 reduce-scatter.8
  701.6 69.2 reduce-scatter.10

commit v5 on v4

--- a/solution.py
+++ b/solution.py
@@ -32,18 +32,23 @@
     return high, (value - high.astype(f32)).astype(bf16)
 
 
-def mm_fine(left, right):
+def mm_fine(left, right, over=((1,), (0,))):
     left_high, left_low = halves(left)
     right_high, right_low = halves(right)
-    return mm(left_high, right_high) + mm(left_low, right_high) + mm(left_high, right_low)
-
-
-def mm_right(left, right, over=((1,), (0,))):
-    return mm(left, right.astype(bf16), over)
+    return (
+        mm(left_high, right_high, over)
+        + mm(left_low, right_high, over)
+        + mm(left_high, right_low, over)
+    )
 
 
 def mm_both(left, right, over=((1,), (0,))):
     return mm(left.astype(bf16), right.astype(bf16), over)
+
+
+def mm_right(left, right, over=((1,), (0,))):
+    high, low = halves(right)
+    return mm(left, high, over) + mm(left, low, over)
 
 
 ROWS = ((1,), (1,))
@@ -256,13 +261,13 @@
         yield
         right_side = beta_c * (values.astype(f32) - growth * key_state)
         yield
-        solved = mm_both(inverse, right_side)
+        solved = mm_fine(inverse, right_side)
         yield
         part = slice(head * DV, (head + 1) * DV)
         solved_ref[:, part] = solved
-        inner = mm_both(query_prod * fall, solved)
-        yield
-        carried[head] = kept * state + mm_both(tail * keys.astype(f32), solved, COLS)
+        inner = mm_fine(query_prod * fall, solved)
+        yield
+        carried[head] = kept * state + mm_fine(tail * keys.astype(f32), solved, COLS)
         yield
         mixed = scale * (growth * query_state + inner) * valid
         mixed_ref[:, part] = mixed
@@ -363,10 +368,10 @@
         key_state = mm_right(keys, state)
         query_state = mm_right(queries, state)
         yield
-        d_solved = mm_both(mixing, d_mixed, COLS) + mm_both(tail * keys_f, d_state)
+        d_solved = mm_fine(mixing, d_mixed, COLS) + mm_fine(tail * keys_f, d_state)
         d_mixing = mm_both(d_mixed, solved, ROWS)
         yield
-        d_right = mm_both(inverse, d_solved, COLS)
+        d_right = mm_fine(inverse, d_solved, COLS)
         yield
         d_query_prod = d_mixing * fall
         d_strict = jnp.where(lower_st, -mm_both(d_right, solved, ROWS), 0.0)
@@ -375,7 +380,7 @@
         yield
         carried[head] = (
             kept * d_state
-            + mm_both(growth * queries_f, d_mixed, COLS)
+            + mm_fine(growth * queries_f, d_mixed, COLS)
             + mm_right(keys, d_key_state, COLS)
         )
         yield
@@ -445,6 +450,9 @@
         ],
         axis=1,
     )
+
+
+BESIDE = pl.CostEstimate(flops=1, bytes_accessed=1, transcendentals=0)
 
 
 def whole_block(shape):
@@ -491,9 +499,7 @@
         ],
         scratch_shapes=[pltpu.VMEM((heads, DK, DV), f32), pltpu.VMEM((EDGE_ROWS, width), bf16)],
         compiler_params=MIXER_PARAMS,
-        cost_estimate=pl.CostEstimate(
-            flops=length, bytes_accessed=length, transcendentals=0
-        ),
+        cost_estimate=BESIDE,
         name="mixer_forward",
     )(proj, proj, gates, side, taps, gain, decay_log, dt_bias)
 
@@ -547,9 +553,7 @@
             pltpu.VMEM((CONV, SPAN), f32),
         ],
         compiler_params=MIXER_PARAMS,
-        cost_estimate=pl.CostEstimate(
-            flops=length, bytes_accessed=length, transcendentals=0
-        ),
+        cost_estimate=BESIDE,
         name="mixer_backward",
     )(proj, proj, proj, gates, side, taps, gain, decay_log, dt_bias, *kept, d_gated)
 
@@ -604,6 +608,7 @@
         out_specs=pl.BlockSpec(memory_space=pltpu.VMEM),
         scratch_shapes=[pltpu.SemaphoreType.DMA((count - 1,)), pltpu.SemaphoreType.DMA((count - 1,))],
         compiler_params=pltpu.CompilerParams(collective_id=0, has_side_effects=True),
+        cost_estimate=BESIDE,
         name="small_gather",
     )(values)
 
@@ -664,6 +669,7 @@
             pltpu.SemaphoreType.DMA((group - 1,)),
         ],
         compiler_params=pltpu.CompilerParams(collective_id=1, has_side_effects=True),
+        cost_estimate=BESIDE,
         name="small_sum",
     )(values)
 
@@ -721,6 +727,7 @@
         compiler_params=pltpu.CompilerParams(
             collective_id=2, has_side_effects=True, vmem_limit_bytes=32 * 1024 * 1024
         ),
+        cost_estimate=BESIDE,
         name="plane_gather",
     )(value)
 
@@ -751,6 +758,7 @@
         out_specs=pl.BlockSpec((step, picked), lambda i: (i, 0)),
         out_shape=jax.ShapeDtypeStruct((rows, picked), array.dtype),
         compiler_params=MIXER_PARAMS,
+        cost_estimate=BESIDE,
         name="pick_columns",
     )(array)
 
@@ -791,6 +799,7 @@
         out_shape=jax.ShapeDtypeStruct((total_rows, group * columns), f32),
         input_output_aliases=aliases,
         compiler_params=MIXER_PARAMS,
+        cost_estimate=BESIDE,
         name="join_columns",
     )(*args)
 
@@ -1038,10 +1047,11 @@
         ).reshape(-1, width)
         return self.core_sum(every)
 
-    def out_rows_join(self, shard):
+    def out_rows_join(self, turns):
+        shard = turns[0]
         width = shard.shape[1]
         if self.subs == 1 and self.cores == 2:
-            halves_all = self.gather_parts(shard)
+            halves_all = self.by_owner(turns)
             here = lax.dynamic_slice(halves_all, (2 * self.core, 0, 0), (2, DV // 2, width))
             there = lax.dynamic_slice(halves_all, (2 - 2 * self.core, 0, 0), (2, DV // 2, width))
             got = lax.ppermute(there, "wshard", [(0, 1), (1, 0)])
@@ -1190,7 +1200,7 @@
     )
     normed_all, _ = at.gather_places(normed)
     normed_all, normed_cores = lax.optimization_barrier(
-        (normed_all, at.core_columns(normed_all)[0])
+        (normed_all, at.core_columns(normed_all, 2))
     )
 
     out_mine = at.out_rows(w_out)
@@ -1237,9 +1247,10 @@
     d_normed2_parts = dot_back(d_gate_up, gu_mine).astype(bf16)
     d_normed2_parts, d_gate_up = lax.optimization_barrier((d_normed2_parts, d_gate_up))
     own, got = at.send_any(d_normed2_parts)
-    d_gu = at.own_grad(normed2_cores, d_gate_up, at.other_grad(normed2_cores, d_gate_up))
+    gu_got = at.other_grad(normed2_cores, d_gate_up)
+    normed2_cores, down_shard = lax.optimization_barrier((normed2_cores, down_shard))
+    d_gu = at.own_grad(normed2_cores, d_gate_up, gu_got)
     got, d_gu = lax.optimization_barrier((got, d_gu))
-    d_gu, down_shard = lax.optimization_barrier((d_gu, down_shard))
     gu_shard = at.scatter(d_gu)
     d_normed2 = sum_parts(own, got)
     d_resid_norm, d_ffn_gain = pull_norm2(d_normed2)
@@ -1249,39 +1260,49 @@
         d_resid.astype(bf16), dot(hidden, down_mine).astype(bf16)
     )
     d_gated = dot_back(d_branch_all, out_mine)
-    d_gated, output_parts, down_shard = lax.optimization_barrier(
-        (d_gated, output_parts, down_shard)
-    )
+    d_out = at.out_grad(gated, d_branch_all)
+    d_gated, output_parts, down_shard, d_out = lax.optimization_barrier(
+        (d_gated, output_parts, down_shard, d_out)
+    )
+    out_shard = at.scatter(d_out)
     output_own, output_got = at.send_any(output_parts)
     down_turns = at.near_turns(down_shard)
     d_proj_lane, d_gates_lane, d_conv_w, d_o_gain, d_heads = mixer_backward(
         *mixer_args, tuple(kept), at.to_lane(d_gated)
     )
-    d_proj_lane, output_got, down_turns = lax.optimization_barrier(
-        (d_proj_lane, output_got, down_turns)
-    )
+    d_proj_lane, output_got, down_turns, gu_shard = lax.optimization_barrier(
+        (d_proj_lane, output_got, down_turns, gu_shard)
+    )
+    gu_turns = at.near_turns(gu_shard)
     once = (at.sub == 0).astype(f32)
     d_conv_w, d_o_gain, d_heads = d_conv_w * once, d_o_gain * once, d_heads * once
     d_proj = at.to_own(d_proj_lane)
     d_ab = at.to_own(d_gates_lane).astype(bf16)
-    d_in = at.own_grad(normed_cores, d_proj, at.other_grad(normed_cores, d_proj))
-    d_in, d_proj, d_ab, d_branch_all, output_got, gu_shard = lax.optimization_barrier(
-        (d_in, d_proj, d_ab, d_branch_all, output_got, gu_shard)
-    )
-    in_shard = at.scatter(d_in)
+    in_got = [at.other_grad(lefts, d_proj) for lefts in normed_cores]
+    first = at.own_grad(normed_cores[0], d_proj, in_got[0])
+    first, in_got, d_proj = lax.optimization_barrier((first, in_got[1], d_proj))
+    in_shards = [at.scatter(first)]
+    second = at.own_grad(normed_cores[1], d_proj, in_got)
+    second, d_proj, d_ab, out_shard = lax.optimization_barrier(
+        (second, d_proj, d_ab, out_shard)
+    )
+    in_shards.append(at.scatter(second))
+    d_normed_parts = (dot_back(d_proj, in_mine) + dot_back(d_ab, ab_mine)).astype(bf16)
+    d_normed_parts, d_ab, gu_turns, output_got = lax.optimization_barrier(
+        (d_normed_parts, d_ab, gu_turns, output_got)
+    )
     output = (resid + sum_parts(output_own, output_got)).astype(bf16)
-    d_normed_parts = (dot_back(d_proj, in_mine) + dot_back(d_ab, ab_mine)).astype(bf16)
-    d_normed_parts, d_branch_all, d_ab = lax.optimization_barrier(
-        (d_normed_parts, d_branch_all, d_ab)
-    )
     own, got = at.send_places(d_normed_parts)
-    d_out = at.out_grad(gated, d_branch_all)
     d_w_ab = dot_t(normed_all, d_ab)
-    got, d_out, d_w_ab, output = lax.optimization_barrier((got, d_out, d_w_ab, output))
+    got, d_w_ab = lax.optimization_barrier((got, d_w_ab))
     d_normed = sum_parts(own, got)
     value_norm, pull_norm = jax.vjp(rms_scale, tokens_f, attn_f)
     d_tokens_norm, d_attn_gain = pull_norm(d_normed)
     d_tokens = (d_resid + d_tokens_norm).astype(bf16)
+    d_tokens, gu_turns, down_turns = lax.optimization_barrier((d_tokens, gu_turns, down_turns))
+    gu_turns = at.far_turn(gu_turns)
+    down_turns = at.far_turn(down_turns)
+    back = jnp.concatenate([output, d_tokens], axis=1)
 
 
     def to_blocks(array):
@@ -1303,19 +1324,31 @@
     )
     summed = small_sum(packed.reshape(devices, rows_small, 128), at.seq, at.cores, at.group)
 
-    grad_w_gu = join_columns(at.gather_parts(gu_shard), ((piece, 2 * devices),))
-    grad_w_down = at.by_owner(at.far_turn(down_turns)).reshape(device_rows, width).astype(f32)
     in_runs = tuple((piece_width, heads) for _, piece_width in QKV + GATE)
-    in_shard, d_out, summed, grad_w_gu, d_tokens, output = lax.optimization_barrier(
-        (in_shard, d_out, summed, grad_w_gu, d_tokens, output)
-    )
-    out_shard = at.scatter(d_out)
-    returned = at.undeal(jnp.concatenate([output, d_tokens], axis=1))
-    in_parts = plane_gather(in_shard) if at.group == 4 else at.gather_parts(in_shard)
-    in_parts, out_shard, returned = lax.optimization_barrier((in_parts, out_shard, returned))
+    gather = plane_gather if at.group == 4 else at.gather_parts
+    in_first, in_second = in_shards
+    in_first, summed = lax.optimization_barrier((in_first, summed))
+    out_turns = at.turns_of(out_shard)
+    in_parts, gu_turns, down_turns, out_turns = lax.optimization_barrier(
+        (gather(in_first), gu_turns, down_turns, out_turns)
+    )
+    grad_w_in = join_columns(in_parts, in_runs, total_rows=w_in.shape[0])
+    in_second, grad_w_in, gu_turns, down_turns, out_turns, back = lax.optimization_barrier(
+        (in_second, grad_w_in, gu_turns, down_turns, out_turns, back)
+    )
+    returned = at.undeal(back)
+    in_turns = at.near_turns(in_second)
+    grad_w_gu = join_columns(at.by_owner(gu_turns), ((piece, 2 * devices),))
+    in_turns, grad_w_gu = lax.optimization_barrier((in_turns, grad_w_gu))
+    in_turns = at.far_turn(in_turns)
+    grad_w_down = at.by_owner(down_turns).reshape(device_rows, width).astype(f32)
+    grad_w_out = at.out_rows_join(out_turns)
+    in_turns, grad_w_down, grad_w_out, returned = lax.optimization_barrier(
+        (in_turns, grad_w_down, grad_w_out, returned)
+    )
+    in_parts = at.by_owner(in_turns)
+    grad_w_in = join_columns(in_parts, in_runs, into=grad_w_in)
     returned = dot_t(sorting, returned).astype(bf16)
-    grad_w_in = join_columns(in_parts, in_runs)
-    grad_w_out = at.out_rows_join(out_shard)
 
     summed = summed.reshape(at.group, -1)
     parts, begin = [], 0

time: 842 us -> 830 us (0.986)
  Pallas kernels: 170 us -> 151 us
    reduce_scatter x4 -> x5, waiting for transfers between devices: 2.16 us -> 27.5 us  [scatter(): return lax.psum_scatter(grad, axes, scatter_dimension=0, tiled=True)]
    pallas_call x1, Pallas kernels: 52.6 us -> 30 us  [plane_gather(): pl.pallas_call(plane_gather_kernel, out_shape=jax.ShapeDtypeStruct((4,) +...]
    ppermute x39 -> x43, waiting for transfers between devices: 191 us -> 175 us  [swap(): lax.ppermute(value, 'group', [(i, i ^ turn) for i in range(self.group)])]
    ppermute x3 -> x4, waiting for transfers between devices: 12.9 us -> 1.77 us  [other_grad(): lax.ppermute(dot_t(lefts[0], right).astype(bf16), 'wshard', [(0, 1), (1,...]
    pallas_call x2 -> x3, Pallas kernels: 18.2 us -> 12.8 us  [join_columns(): pl.pallas_call(functools.partial(join_columns_kernel, group, runs), grid=...]
    dot_general x9 -> x11, matrix products: 44.6 us -> 49.3 us  [dot_t(): lax.dot_general(left, right, (((0,), (0,)), ((), ())), preferred_element_...]
    ppermute x39 -> x43, starting transfers between devices: 44.7 us -> 49.3 us  [swap(): lax.ppermute(value, 'group', [(i, i ^ turn) for i in range(self.group)])]
  transfers between devices with their start and end apart: 56 -> 62, of which waited for: 30 -> 26; matrix products, arithmetic and copies ran while one was open for 26% -> 31% of each run, Pallas kernels for 20% -> 18%
where the time goes in v5:
time: 830 us; the launch traced here: 823 us
  waiting for transfers between devices  311 us (37%)
  Pallas kernels  151 us (18%)
  matrix products  147 us (18%)
  local copies, waits for them, and re-layouts  77 us (9%)
  starting transfers between devices  65.3 us (8%)
  other arithmetic  56.2 us (7%)
  between operations  15.6 us (2%)
    ppermute x43, waiting for transfers between devices, swap(): lax.ppermute(value, 'group', [(i, i ^ turn) for i in range(self.group)])  175 us
    dot_general x8, matrix products, dot(): return jnp.dot(left, right, preferred_element_type=f32)  50.4 us
    all_to_all x2, waiting for transfers between devices, deal(): lax.all_to_all(sorted_rows, 'seq', split_axis=0, concat_axis=0, tiled=True)  50.4 us
    dot_general x11, matrix products, dot_t(): lax.dot_general(left, right, (((0,), (0,)), ((), ())), preferred_element_...  49.3 us
    ppermute x43, starting transfers between devices, swap(): lax.ppermute(value, 'group', [(i, i ^ turn) for i in range(self.group)])  49.3 us
    dot_general x5, matrix products, dot_back(): lax.dot_general(left, right, (((1,), (1,)), ((), ())), preferred_element_...  47.1 us
    pallas_call x1, Pallas kernels, mixer_backward(): pl.pallas_call(functools.partial(mixer_backward_kernel, heads), grid=(blo...  41.3 us
    pallas_call x1, Pallas kernels, mixer_forward(): pl.pallas_call(functools.partial(mixer_forward_kernel, heads), grid=(bloc...  34.7 us
  transfers between devices with their start and end apart: 62, of which 26 were waited for; matrix products, arithmetic and copies ran while one was open for 31% of the time, Pallas kernels for 18%

profile of v5, /device:TPU:0, one launch (start us, length us, event | category | flops | bytes accessed | tf_op | source)
XLA Modules:
  0.0 823.2 jit_solution(16716029123613640510)
XLA Ops:
  15.4 9.1 %small_gather.1 = bf16[8,32,128]{2,1,0:T(8,128)(2,1)} custom-call(bf16[32,128]{1,0:T(8,128)(2,1)} %bitcast.273), custom_call_target="tpu_custom_call" | custom-call | flops 1 | bytes 1 | tf_op jit(solution)/shard_map/small_gather/pallas_call | solution.py:604
  31.9 42.5 %all-to-all-done = bf16[4,48,2048]{2,1,0:T(8,128)(2,1)} async-done(((bf16[4,48,2048]{2,1,0:T(8,128)(2,1)}), bf16[4,48,2048]{2,1,0:T(8,128)(2,1)}, u32[]{:S(2)}, u32[]{:S(2)}) %all-to-all-start) | async-done | bytes 786464 | tf_op jit(solution)/shard_map/all_to_all | solution.py:857
  117.6 14.8 %collective-permute-done.1 = bf16[192,2048]{1,0:T(8,128)(2,1)} collective-permute-done((bf16[192,2048]{1,0:T(8,128)(2,1)}, bf16[192,2048]{1,0:T(8,128)(2,1)}, u32[]{:S(2)}, u32[]{:S(2)}) %collective-permute-start.1) | collective-permute-done | bytes 786464 | tf_op jit(solution)/shard_map/ppermute | solution.py:885
  148.3 20.1 %all-gather.5.cloned.1.call-done = bf16[2048,3072]{1,0:T(8,128)(2,1)} async-done(((bf16[256,3072]{1,0:T(8,128)(2,1)}), bf16[2048,3072]{1,0:T(8,128)(2,1)}) %all-gather.5.cloned.1.call-update) | async-done | bytes 12582928 | tf_op jit(solution)/shard_map/all_gather | solution.py:1174
  168.4 16.0 %fusion.62.conv_ref.gate_ref.ahead_ref = f32[768,3072]{1,0:T(8,128)} fusion(bf16[768,2048]{1,0:T(8,128)(2,1)} %bitcast.224, bf16[2048,3072]{1,0:T(8,128)(2,1)} %all-gather.5.cloned.1.call-done), kind=kOutput, calls=%fused_computation.238 | convolution fusion | flops 9663676416 | bytes 25165824 | tf_op jit(solution)/shard_map/dot_general | solution.py:824
  193.3 34.7 %mixer_forward.1 = (bf16[768,1024]{1,0:T(8,128)(2,1)S(1)}, f32[768,1024]{1,0:T(8,128)}, bf16[768,2048]{1,0:T(8,128)(2,1)}, f32[12,4,128,256]{3,2,1,0:T(8,128)}, ...) custom-call(f32[768,3072]{1,0:T(8,128)} %fusion.62.conv_ref.gate_ref.ahead_ref, ...), custom_call_target="tpu_custom_call" | custom-call | flops 1 | bytes 1 | tf_op jit(solution)/shard_map/mixer_forward/pallas_call | solution.py:471
  245.0 16.1 %collective-permute-done.10 = bf16[192,2048]{1,0:T(8,128)(2,1)} collective-permute-done((bf16[192,2048]{1,0:T(8,128)(2,1)}, bf16[192,2048]{1,0:T(8,128)(2,1)}, u32[]{:S(2)}, u32[]{:S(2)}) %collective-permute-start.10) | collective-permute-done | bytes 786464 | tf_op jit(solution)/shard_map/ppermute | solution.py:885
  261.1 16.4 %collective-permute-done.11 = bf16[192,2048]{1,0:T(8,128)(2,1)} collective-permute-done((bf16[192,2048]{1,0:T(8,128)(2,1)}, bf16[192,2048]{1,0:T(8,128)(2,1)}, u32[]{:S(2)}, u32[]{:S(2)}) %collective-permute-start.11) | collective-permute-done | bytes 786464 | tf_op jit(solution)/shard_map/ppermute | solution.py:885
  285.2 17.1 %collective-permute-done.13 = bf16[192,2048]{1,0:T(8,128)(2,1)} collective-permute-done((bf16[192,2048]{1,0:T(8,128)(2,1)S(1)}, bf16[192,2048]{1,0:T(8,128)(2,1)}, u32[]{:S(2)}, u32[]{:S(2)}) %collective-permute-start.13) | collective-permute-done | bytes 786464 | tf_op jit(solution)/shard_map/ppermute | solution.py:885
  302.3 15.3 %collective-permute-done.14 = bf16[192,2048]{1,0:T(8,128)(2,1)} collective-permute-done((bf16[192,2048]{1,0:T(8,128)(2,1)S(1)}, bf16[192,2048]{1,0:T(8,128)(2,1)}, u32[]{:S(2)}, u32[]{:S(2)}) %collective-permute-start.14) | collective-permute-done | bytes 786464 | tf_op jit(solution)/shard_map/ppermute | solution.py:885
  324.4 13.7 %fusion.64 = f32[768,2816]{1,0:T(8,128)S(1)} fusion(bf16[768,2048]{1,0:T(8,128)(2,1)} %copy-done.20, bf16[2048,2816]{1,0:T(8,128)(2,1)} %all-gather.9.cloned.1.call-done), kind=kOutput, calls=%fused_computation.240 | convolution fusion | flops 8858370048 | bytes 23330816 | tf_op jit(solution)/shard_map/dot_general | solution.py:824
  356.9 27.7 %all-gather.11.cloned.1.call-done = bf16[1408,2048]{1,0:T(8,128)(2,1)} async-done(((bf16[176,2048]{1,0:T(8,128)(2,1)}), bf16[1408,2048]{1,0:T(8,128)(2,1)}) %all-gather.11.cloned.1.call-update) | async-done | bytes 5767184 | tf_op jit(solution)/shard_map/all_gather | solution.py:1212
  384.6 12.6 %fusion.32 = (f32[768,1408]{1,0:T(8,128)S(1)}, f32[768,1408]{1,0:T(8,128)}) fusion(f32[768,2816]{1,0:T(8,128)} %copy-done.21, bf16[768,2048]{1,0:T(8,128)(2,1)} %pad_maximum_fusion, bf16[1408,2048]{1,0:T(8,128)(2,1)} %all-gather.11.cloned.1.call-done), kind=kOutput, calls=%fused_computation.95 | convolution fusion | flops 4442161152 | bytes 26214400 | tf_op jit(solution)/shard_map/dot_general | solution.py:832
  399.9 13.6 %convolution_convert_fusion.7 = bf16[768,2048]{1,0:T(8,128)(2,1)S(1)} fusion(bf16[768,2816]{1,0:T(8,128)(2,1)S(1)} %add_convert_fusion.1, bf16[2048,2816]{1,0:T(8,128)(2,1)} %all-gather.9.cloned.1.call-done), kind=kOutput, calls=%fused_computation.21 | convolution fusion | flops 8859942912 | bytes 19005440 | tf_op jit(solution)/shard_map/dot_general | solution.py:832
  425.2 16.4 %reduce-scatter.6.cloned.1.call-done = bf16[176,2048]{1,0:T(8,128)(2,1)} async-done(((bf16[704,2048]{1,0:T(8,128)(2,1)}), bf16[176,2048]{1,0:T(8,128)(2,1)}) %reduce-scatter.6.cloned.1.call-update) | async-done | bytes 720912 | tf_op jit(solution)/shard_map/reduce_scatter | solution.py:1020
  441.7 9.7 %add_convert_fusion = bf16[1024,2816]{1,0:T(8,128)(2,1)} fusion(bf16[1024,2816]{1,0:T(8,128)(2,1)} %collective-permute-done.20, bf16[768,1024]{1,0:T(8,128)(2,1)S(1)} %copy-done.39, bf16[768,2816]{1,0:T(8,128)(2,1)} %copy-done.26), kind=kOutput, calls=%fused_computation | convolution fusion | flops 4437835776 | bytes 17432576 | tf_op jit(solution)/shard_map/dot_general | solution.py:828
  477.5 10.0 %collective-permute-done.21 = bf16[192,2048]{1,0:T(8,128)(2,1)S(1)} collective-permute-done((bf16[192,2048]{1,0:T(8,128)(2,1)S(1)}, bf16[192,2048]{1,0:T(8,128)(2,1)S(1)}, u32[]{:S(2)}, u32[]{:S(2)}) %collective-permute-start.21) | collective-permute-done | bytes 786464 | tf_op jit(solution)/shard_map/ppermute | solution.py:885
  487.5 16.2 %collective-permute-done.22 = bf16[192,2048]{1,0:T(8,128)(2,1)S(1)} collective-permute-done((bf16[192,2048]{1,0:T(8,128)(2,1)S(1)}, bf16[192,2048]{1,0:T(8,128)(2,1)S(1)}, u32[]{:S(2)}, u32[]{:S(2)}) %collective-permute-start.22) | collective-permute-done | bytes 786464 | tf_op jit(solution)/shard_map/ppermute | solution.py:885
  525.6 41.3 %mixer_backward.1 = (bf16[768,3072]{1,0:T(8,128)(2,1)}, f32[768,8]{1,0:T(8,128)S(1)}, f32[4,2048]{1,0:T(4,128)S(1)}, f32[1,256]{1,0:T(1,128)S(1)}, f32[1,8]{1,0:T(1,128)S(1)}) custom-call(f32[768,3072]{1,0:T(8,128)} %fusion.62.conv_ref.gate_ref.ahead_ref, f32[768,3072]{1,0:T(8,128)} %fusion.62.conv_ref.gate_ref.ahead_ref, ...), custom_call_target="tpu_custom_call" | custom-call | flops 1 | bytes 1 | tf_op jit(solution)/shard_map/mixer_backward/pallas_call | solution.py:516
  595.6 11.1 %reduce-scatter.10.cloned.1.call-done = bf16[128,2048]{1,0:T(8,128)(2,1)} async-done(((bf16[512,2048]{1,0:T(8,128)(2,1)}), bf16[128,2048]{1,0:T(8,128)(2,1)}) %reduce-scatter.10.cloned.1.call-update) | async-done | bytes 524304 | tf_op jit(solution)/shard_map/reduce_scatter | solution.py:1020
  606.7 14.8 %fusion.66 = f32[768,2048]{1,0:T(8,128)S(1)} fusion(bf16[768,3072]{1,0:T(8,128)(2,1)} %get-tuple-element.211, bf16[2048,3072]{1,0:T(8,128)(2,1)} %all-gather.5.cloned.1.call-done), kind=kOutput, calls=%fused_computation.242 | convolution fusion | flops 9663676416 | bytes 23592960 | tf_op jit(solution)/shard_map/dot_general | solution.py:832
  631.1 41.4 %collective-permute-done.42 = bf16[128,2048]{1,0:T(8,128)(2,1)S(1)} collective-permute-done((bf16[128,2048]{1,0:T(8,128)(2,1)}, bf16[128,2048]{1,0:T(8,128)(2,1)S(1)}, u32[]{:S(2)}, u32[]{:S(2)}) %collective-permute-start.42) | collective-permute-done | bytes 524320 | tf_op jit(solution)/shard_map/ppermute | solution.py:885
  694.3 16.1 %small_sum.1 = f32[4,32,128]{2,1,0:T(8,128)} custom-call(f32[8,32,128]{2,1,0:T(8,128)} %bitcast.249), custom_call_target="tpu_custom_call" | custom-call | flops 1 | bytes 1 | tf_op jit(solution)/shard_map/small_sum/pallas_call | solution.py:659
  718.4 30.0 %plane_gather.1.parts_ref = bf16[4,128,3072]{2,1,0:T(8,128)(2,1)S(1)} custom-call(bf16[128,3072]{1,0:T(8,128)(2,1)S(1)} %copy-done.11), custom_call_target="tpu_custom_call" | custom-call | flops 1 | bytes 1 | tf_op jit(solution)/shard_map/plane_gather/pallas_call | solution.py:717
  (443 shorter events, 331.1 us)
Async XLA Ops:
  7.2 161.2 %all-gather.5.cloned.1.call-start = ((), (), s32[]{:S(2)}) async-start(), calls=%async_computation.8 | async-start | bytes 14155776 | tf_op jit(solution)/shard_map/all_gather | solution.py:1174
  27.3 47.1 %all-to-all-start = ((bf16[4,48,2048]{2,1,0:T(8,128)(2,1)}), bf16[4,48,2048]{2,1,0:T(8,128)(2,1)}, u32[]{:S(2)}, u32[]{:S(2)}) async-start(bf16[4,48,2048]{2,1,0:T(8,128)(2,1)} %bitcast.238), calls=%async_computation | async-start | bytes 1572864 | tf_op jit(solution)/shard_map/all_to_all | solution.py:857
  31.8 200.6 %all-gather.7.cloned.1.call-start = ((), (), s32[]{:S(2)}) async-start(), calls=%async_computation.9 | async-start | bytes 4718592 | tf_op jit(solution)/shard_map/all_gather | solution.py:1031
  84.2 240.2 %all-gather.9.cloned.1.call-start = ((), (), s32[]{:S(2)}) async-start(), calls=%async_computation.10 | async-start | bytes 12976128 | tf_op jit(solution)/shard_map/all_gather | solution.py:1209
  103.0 45.3 %all-to-all-start.1 = ((bf16[4,48,2048]{2,1,0:T(8,128)(2,1)}), bf16[4,48,2048]{2,1,0:T(8,128)(2,1)}, u32[]{:S(2)}, u32[]{:S(2)}) async-start(bf16[4,48,2048]{2,1,0:T(8,128)(2,1)} %bitcast.237), calls=%async_computation.1 | async-start | bytes 1572864 | tf_op jit(solution)/shard_map/all_to_all | solution.py:857
  107.3 277.4 %all-gather.11.cloned.1.call-start = ((), (), s32[]{:S(2)}) async-start(), calls=%async_computation.11 | async-start | bytes 6488064 | tf_op jit(solution)/shard_map/all_gather | solution.py:1212
  244.8 196.9 %reduce-scatter.6.cloned.1.call-start = ((), (), s32[]{:S(2)}) async-start(), calls=%async_computation.12 | async-start | bytes 3604480 | tf_op jit(solution)/shard_map/reduce_scatter | solution.py:1020
  356.5 214.0 %reduce-scatter.8.cloned.1.call-start = ((), (), s32[]{:S(2)}) async-start(), calls=%async_computation.13 | async-start | bytes 7208960 | tf_op jit(solution)/shard_map/reduce_scatter | solution.py:1020
  459.9 146.8 %reduce-scatter.10.cloned.1.call-start = ((), (), s32[]{:S(2)}) async-start(), calls=%async_computation.14 | async-start | bytes 2621440 | tf_op jit(solution)/shard_map/reduce_scatter | solution.py:1020
  517.8 52.6 %collective-permute-start.25 = (bf16[192,2048]{1,0:T(8,128)(2,1)}, bf16[192,2048]{1,0:T(8,128)(2,1)}, u32[]{:S(2)}, u32[]{:S(2)}) collective-permute-start(bf16[192,2048]{1,0:T(8,128)(2,1)} %get-tuple-element.318), channel_id=1, source_target_pairs={{0,8},{8,0},{16,24},{24,16},{1,9},{9,1},{17,25},{25,17},{2,10},{10... | collective-permute-start | bytes 2359304 | tf_op jit(solution)/shard_map/ppermute | solution.py:885
  518.5 52.0 %collective-permute-start.26 = (bf16[192,2048]{1,0:T(8,128)(2,1)}, bf16[192,2048]{1,0:T(8,128)(2,1)}, u32[]{:S(2)}, u32[]{:S(2)}) collective-permute-start(bf16[192,2048]{1,0:T(8,128)(2,1)} %get-tuple-element.317), channel_id=1, source_target_pairs={{0,16},{8,24},{16,0},{24,8},{1,17},{9,25},{17,1},{25,9},{2,18},{10... | collective-permute-start | bytes 2359304 | tf_op jit(solution)/shard_map/ppermute | solution.py:885
  519.9 50.5 %collective-permute-start.27 = (bf16[192,2048]{1,0:T(8,128)(2,1)}, bf16[192,2048]{1,0:T(8,128)(2,1)}, u32[]{:S(2)}, u32[]{:S(2)}) collective-permute-start(bf16[192,2048]{1,0:T(8,128)(2,1)} %get-tuple-element.316), channel_id=1, source_target_pairs={{0,24},{8,16},{16,8},{24,0},{1,25},{9,17},{17,9},{25,1},{2,26},{10... | collective-permute-start | bytes 2359304 | tf_op jit(solution)/shard_map/ppermute | solution.py:885
  521.3 48.9 %collective-permute-start.28 = (bf16[176,2048]{1,0:T(8,128)(2,1)}, bf16[176,2048]{1,0:T(8,128)(2,1)}, u32[]{:S(2)}, u32[]{:S(2)}) collective-permute-start(bf16[176,2048]{1,0:T(8,128)(2,1)} %reduce-scatter.6.cloned.1.call-done), channel_id=1, source_target_pairs={{0,8},{8,0},{16,24},{24,16},{1,9},{9,1},{17,25},{25,17},{2,10},{10... | collective-permute-start | bytes 2162696 | tf_op jit(solution)/shard_map/ppermute | solution.py:885
  522.0 48.5 %collective-permute-start.29 = (bf16[176,2048]{1,0:T(8,128)(2,1)}, bf16[176,2048]{1,0:T(8,128)(2,1)}, u32[]{:S(2)}, u32[]{:S(2)}) collective-permute-start(bf16[176,2048]{1,0:T(8,128)(2,1)} %reduce-scatter.6.cloned.1.call-done), channel_id=1, source_target_pairs={{0,16},{8,24},{16,0},{24,8},{1,17},{9,25},{17,1},{25,9},{2,18},{10... | collective-permute-start | bytes 2162696 | tf_op jit(solution)/shard_map/ppermute | solution.py:885
  523.4 193.9 %reduce-scatter.14.cloned.1.call-start = ((), (), s32[]{:S(2)}) async-start(), calls=%async_computation.16 | async-start | bytes 3932160 | tf_op jit(solution)/shard_map/reduce_scatter | solution.py:1020
  586.5 165.3 %reduce-scatter.12.cloned.1.call-start = ((), (), s32[]{:S(2)}) async-start(), calls=%async_computation.15 | async-start | bytes 3932160 | tf_op jit(solution)/shard_map/reduce_scatter | solution.py:1020
  624.0 49.8 %collective-permute-start.34 = (bf16[192,2048]{1,0:T(8,128)(2,1)S(1)}, bf16[192,2048]{1,0:T(8,128)(2,1)S(1)}, u32[]{:S(2)}, u32[]{:S(2)}) collective-permute-start(bf16[192,2048]{1,0:T(8,128)(2,1)S(1)} %bitcast.247), channel_id=1, source_target_pairs={{0,8},{8,0},{16,24},{24,16},{1,9},{9,1},{17,25},{25,17},{2,10},{10... | collective-permute-start | bytes 2359304 | tf_op jit(solution)/shard_map/ppermute | solution.py:885
  625.5 48.3 %collective-permute-start.35 = (bf16[192,2048]{1,0:T(8,128)(2,1)S(1)}, bf16[192,2048]{1,0:T(8,128)(2,1)S(1)}, u32[]{:S(2)}, u32[]{:S(2)}) collective-permute-start(bf16[192,2048]{1,0:T(8,128)(2,1)S(1)} %bitcast.246), channel_id=1, source_target_pairs={{0,16},{8,24},{16,0},{24,8},{1,17},{9,25},{17,1},{25,9},{2,18},{10... | collective-permute-start | bytes 2359304 | tf_op jit(solution)/shard_map/ppermute | solution.py:885
  627.0 46.8 %collective-permute-start.36 = (bf16[192,2048]{1,0:T(8,128)(2,1)S(1)}, bf16[192,2048]{1,0:T(8,128)(2,1)S(1)}, u32[]{:S(2)}, u32[]{:S(2)}) collective-permute-start(bf16[192,2048]{1,0:T(8,128)(2,1)S(1)} %bitcast.245), channel_id=1, source_target_pairs={{0,24},{8,16},{16,8},{24,0},{1,25},{9,17},{17,9},{25,1},{2,26},{10... | collective-permute-start | bytes 2359304 | tf_op jit(solution)/shard_map/ppermute | solution.py:885
  629.0 61.3 %collective-permute-start.41 = (bf16[128,2048]{1,0:T(8,128)(2,1)}, bf16[128,2048]{1,0:T(8,128)(2,1)}, u32[]{:S(2)}, u32[]{:S(2)}) collective-permute-start(bf16[128,2048]{1,0:T(8,128)(2,1)} %reduce-scatter.10.cloned.1.call-done), channel_id=1, source_target_pairs={{0,8},{8,0},{16,24},{24,16},{1,9},{9,1},{17,25},{25,17},{2,10},{10... | collective-permute-start | bytes 1572872 | tf_op jit(solution)/shard_map/ppermute | solution.py:885
  685.3 63.3 %collective-permute-start.37 = (bf16[128,2816]{1,0:T(8,128)(2,1)}, bf16[128,2816]{1,0:T(8,128)(2,1)}, u32[]{:S(2)}, u32[]{:S(2)}) collective-permute-start(bf16[128,2816]{1,0:T(8,128)(2,1)} %slice.120), channel_id=1, source_target_pairs={{0,8},{8,0},{16,24},{24,16},{1,9},{9,1},{17,25},{25,17},{2,10},{10... | collective-permute-start | bytes 2162696 | tf_op jit(solution)/shard_map/ppermute | solution.py:885
  687.6 60.9 %collective-permute-start.38 = (bf16[128,2816]{1,0:T(8,128)(2,1)}, bf16[128,2816]{1,0:T(8,128)(2,1)}, u32[]{:S(2)}, u32[]{:S(2)}) collective-permute-start(bf16[128,2816]{1,0:T(8,128)(2,1)} %slice.121), channel_id=1, source_target_pairs={{0,16},{8,24},{16,0},{24,8},{1,17},{9,25},{17,1},{25,9},{2,18},{10... | collective-permute-start | bytes 2162696 | tf_op jit(solution)/shard_map/ppermute | solution.py:885
  692.0 56.5 %collective-permute-start.44 = (bf16[64,2048]{1,0:T(8,128)(2,1)}, bf16[64,2048]{1,0:T(8,128)(2,1)}, u32[]{:S(2)}, u32[]{:S(2)}) collective-permute-start(bf16[64,2048]{1,0:T(8,128)(2,1)} %slice.147), channel_id=1, source_target_pairs={{0,16},{8,24},{16,0},{24,8},{1,17},{9,25},{17,1},{25,9},{2,18},{10... | collective-permute-start | bytes 786440 | tf_op jit(solution)/shard_map/ppermute | solution.py:885
  758.7 47.2 %all-to-all-start.2 = ((bf16[4,48,4096]{2,1,0:T(8,128)(2,1)}), bf16[4,48,4096]{2,1,0:T(8,128)(2,1)}, u32[]{:S(2)}, u32[]{:S(2)}) async-start(bf16[4,48,4096]{2,1,0:T(8,128)(2,1)} %bitcast.229), calls=%async_computation.7 | async-start | bytes 3145728 | tf_op jit(solution)/shard_map/all_to_all | solution.py:872
  (106 other events, 1952.4 us)
Sparse Core Ops, SparseCore 0:
  15.5 152.8 all-gather.4
  170.0 45.2 all-gather.6
  217.6 106.7 all-gather.8
  325.9 58.7 all-gather.10
  386.8 54.8 reduce-scatter.5
  460.0 99.9 reduce-scatter.7
  562.3 44.3 reduce-scatter.9
  609.7 59.5 reduce-scatter.13
  672.3 62.3 reduce-scatter.11

commit v6 on v5

--- a/solution.py
+++ b/solution.py
@@ -804,6 +804,111 @@
     )(*args)
 
 
+def join_turns_kernel(group, runs, halfway, near_ref, one_ref, two_ref, first_ref, second_ref, *refs):
+    out_ref, far = refs[-2:]
+    part = lax.axis_index("group")
+
+    @pl.when(pl.program_id(0) < halfway)
+    def _():
+        far[...] = first_ref[...]
+
+    @pl.when(pl.program_id(0) >= halfway)
+    def _():
+        far[...] = second_ref[...]
+
+    turns = (near_ref, one_ref, two_ref, far)
+    for own in range(group):
+
+        @pl.when(part == own)
+        def _():
+            source, target = 0, 0
+            for width, count in runs:
+                pack = 1
+                while pack < count and (pack * group * width) % 128:
+                    pack *= 2
+                for first in range(0, count, pack):
+                    pieces = []
+                    for run in range(first, first + pack):
+                        begin = source + run * width
+                        for owner in range(group):
+                            pieces.append(
+                                turns[own ^ owner][:, begin : begin + width].astype(f32)
+                            )
+                    size = pack * group * width
+                    out_ref[:, target : target + size] = jnp.concatenate(pieces, axis=1)
+                    target += size
+                source += count * width
+
+
+def join_turns(turns, runs, total_rows=None, into=None):
+    near, one, two, (first_half, second_half) = turns
+    rows, columns = near.shape
+    half = first_half.shape[0]
+    step = 32 if half % 32 == 0 else 16
+    halfway = half // step
+    total_rows = into.shape[0] if into is not None else total_rows or rows
+    first = (total_rows - rows) // step if into is not None else 0
+    block = pl.BlockSpec((step, columns), lambda i: (i, 0))
+    args = [near, one, two, first_half, second_half]
+    specs = [
+        block,
+        block,
+        block,
+        pl.BlockSpec((step, columns), lambda i: (jnp.minimum(i, halfway - 1), 0)),
+        pl.BlockSpec((step, columns), lambda i: (jnp.maximum(i - halfway, 0), 0)),
+    ]
+    aliases = {}
+    if into is not None:
+        args.append(into)
+        specs.append(pl.BlockSpec(memory_space=pl.ANY))
+        aliases = {5: 0}
+    return pl.pallas_call(
+        functools.partial(join_turns_kernel, 4, runs, halfway),
+        grid=(rows // step,),
+        in_specs=specs,
+        out_specs=pl.BlockSpec((step, 4 * columns), lambda i: (first + i, 0)),
+        out_shape=jax.ShapeDtypeStruct((total_rows, 4 * columns), f32),
+        scratch_shapes=[pltpu.VMEM((step, columns), near.dtype)],
+        input_output_aliases=aliases,
+        compiler_params=MIXER_PARAMS,
+        cost_estimate=BESIDE,
+        name="join_turns",
+    )(*args)
+
+
+def stack_turns_kernel(near_ref, one_ref, two_ref, first_ref, second_ref, out_ref):
+    turn = lax.bitwise_xor(lax.axis_index("group"), pl.program_id(0))
+    half = first_ref.shape[0]
+    for at, ref in enumerate((near_ref, one_ref, two_ref)):
+
+        @pl.when(turn == at)
+        def _():
+            out_ref[0] = ref[...].astype(out_ref.dtype)
+
+    @pl.when(turn == 3)
+    def _():
+        out_ref[0, :half] = first_ref[...].astype(out_ref.dtype)
+        out_ref[0, half:] = second_ref[...].astype(out_ref.dtype)
+
+
+def stack_turns(turns, dtype):
+    near, one, two, (first_half, second_half) = turns
+    rows, columns = near.shape
+    half = first_half.shape[0]
+    whole = pl.BlockSpec((rows, columns), lambda i: (0, 0))
+    halved = pl.BlockSpec((half, columns), lambda i: (0, 0))
+    return pl.pallas_call(
+        stack_turns_kernel,
+        grid=(4,),
+        in_specs=[whole, whole, whole, halved, halved],
+        out_specs=pl.BlockSpec((1, rows, columns), lambda i: (i, 0, 0)),
+        out_shape=jax.ShapeDtypeStruct((4, rows, columns), dtype),
+        compiler_params=MIXER_PARAMS,
+        cost_estimate=BESIDE,
+        name="stack_turns",
+    )(near, one, two, first_half, second_half)
+
+
 def rms_scale(values, gain):
     return values * lax.rsqrt(jnp.mean(values * values, axis=-1, keepdims=True) + eps_norm) * gain
 
@@ -927,6 +1032,16 @@
         if self.group == 4 and value.ndim == 2 and value.shape[0] % 2 == 0:
             return self.far_turn(self.near_turns(value))
         return tuple(self.swap(value, turn) for turn in range(self.group))
+
+    def joined(self, turns, runs, total_rows=None, into=None):
+        if isinstance(turns[-1], tuple) and turns[-1][0].shape[0] % 16 == 0:
+            return join_turns(turns, runs, total_rows, into)
+        return join_columns(self.by_owner(turns), runs, total_rows, into)
+
+    def stacked(self, turns, dtype):
+        if isinstance(turns[-1], tuple) and turns[-1][0].shape[0] % 8 == 0:
+            return stack_turns(turns, dtype)
+        return self.by_owner(turns).astype(dtype)
 
     def by_owner(self, turns):
         value = turns[0]
@@ -1051,7 +1166,7 @@
         shard = turns[0]
         width = shard.shape[1]
         if self.subs == 1 and self.cores == 2:
-            halves_all = self.by_owner(turns)
+            halves_all = self.stacked(turns, bf16)
             here = lax.dynamic_slice(halves_all, (2 * self.core, 0, 0), (2, DV // 2, width))
             there = lax.dynamic_slice(halves_all, (2 - 2 * self.core, 0, 0), (2, DV // 2, width))
             got = lax.ppermute(there, "wshard", [(0, 1), (1, 0)])
@@ -1283,25 +1398,22 @@
     first, in_got, d_proj = lax.optimization_barrier((first, in_got[1], d_proj))
     in_shards = [at.scatter(first)]
     second = at.own_grad(normed_cores[1], d_proj, in_got)
-    second, d_proj, d_ab, out_shard = lax.optimization_barrier(
-        (second, d_proj, d_ab, out_shard)
-    )
+    second, d_proj, d_ab = lax.optimization_barrier((second, d_proj, d_ab))
     in_shards.append(at.scatter(second))
     d_normed_parts = (dot_back(d_proj, in_mine) + dot_back(d_ab, ab_mine)).astype(bf16)
-    d_normed_parts, d_ab, gu_turns, output_got = lax.optimization_barrier(
-        (d_normed_parts, d_ab, gu_turns, output_got)
+    d_normed_parts, d_ab, output_got, out_shard = lax.optimization_barrier(
+        (d_normed_parts, d_ab, output_got, out_shard)
     )
     output = (resid + sum_parts(output_own, output_got)).astype(bf16)
     own, got = at.send_places(d_normed_parts)
     d_w_ab = dot_t(normed_all, d_ab)
-    got, d_w_ab = lax.optimization_barrier((got, d_w_ab))
+    got, d_w_ab, gu_turns = lax.optimization_barrier((got, d_w_ab, gu_turns))
     d_normed = sum_parts(own, got)
     value_norm, pull_norm = jax.vjp(rms_scale, tokens_f, attn_f)
     d_tokens_norm, d_attn_gain = pull_norm(d_normed)
     d_tokens = (d_resid + d_tokens_norm).astype(bf16)
     d_tokens, gu_turns, down_turns = lax.optimization_barrier((d_tokens, gu_turns, down_turns))
     gu_turns = at.far_turn(gu_turns)
-    down_turns = at.far_turn(down_turns)
     back = jnp.concatenate([output, d_tokens], axis=1)
 
 
@@ -1325,29 +1437,31 @@
     summed = small_sum(packed.reshape(devices, rows_small, 128), at.seq, at.cores, at.group)
 
     in_runs = tuple((piece_width, heads) for _, piece_width in QKV + GATE)
-    gather = plane_gather if at.group == 4 else at.gather_parts
     in_first, in_second = in_shards
-    in_first, summed = lax.optimization_barrier((in_first, summed))
-    out_turns = at.turns_of(out_shard)
-    in_parts, gu_turns, down_turns, out_turns = lax.optimization_barrier(
-        (gather(in_first), gu_turns, down_turns, out_turns)
-    )
-    grad_w_in = join_columns(in_parts, in_runs, total_rows=w_in.shape[0])
-    in_second, grad_w_in, gu_turns, down_turns, out_turns, back = lax.optimization_barrier(
-        (in_second, grad_w_in, gu_turns, down_turns, out_turns, back)
-    )
+    out_turns = at.near_turns(out_shard)
+    in_first, summed, gu_turns, down_turns, out_turns = lax.optimization_barrier(
+        (in_first, summed, gu_turns, down_turns, out_turns)
+    )
+    out_turns = at.far_turn(out_turns)
+    down_turns = at.far_turn(down_turns)
+    first_turns = at.near_turns(in_first)
+    grad_w_gu = at.joined(gu_turns, ((piece, 2 * devices),))
+    first_turns, grad_w_gu = lax.optimization_barrier((first_turns, grad_w_gu))
+    first_turns = at.far_turn(first_turns)
+    grad_w_down = at.stacked(down_turns, f32).reshape(device_rows, width)
+    first_turns, grad_w_down, in_second, back = lax.optimization_barrier(
+        (first_turns, grad_w_down, in_second, back)
+    )
+    second_turns = at.near_turns(in_second)
     returned = at.undeal(back)
-    in_turns = at.near_turns(in_second)
-    grad_w_gu = join_columns(at.by_owner(gu_turns), ((piece, 2 * devices),))
-    in_turns, grad_w_gu = lax.optimization_barrier((in_turns, grad_w_gu))
-    in_turns = at.far_turn(in_turns)
-    grad_w_down = at.by_owner(down_turns).reshape(device_rows, width).astype(f32)
+    grad_w_in = at.joined(first_turns, in_runs, total_rows=w_in.shape[0])
     grad_w_out = at.out_rows_join(out_turns)
-    in_turns, grad_w_down, grad_w_out, returned = lax.optimization_barrier(
-        (in_turns, grad_w_down, grad_w_out, returned)
-    )
-    in_parts = at.by_owner(in_turns)
-    grad_w_in = join_columns(in_parts, in_runs, into=grad_w_in)
+    second_turns, grad_w_in, grad_w_out = lax.optimization_barrier(
+        (second_turns, grad_w_in, grad_w_out)
+    )
+    second_turns = at.far_turn(second_turns)
+    second_turns, returned = lax.optimization_barrier((second_turns, returned))
+    grad_w_in = at.joined(second_turns, in_runs, into=grad_w_in)
     returned = dot_t(sorting, returned).astype(bf16)
 
     summed = summed.reshape(at.group, -1)

time: 830 us -> 796 us (0.959)
  Pallas kernels: 151 us -> 136 us
  local copies, waits for them, and re-layouts: 77 us -> 62.4 us
    pallas_call x4 -> x5, Pallas kernels: 42.9 us -> 22.8 us  [the longest x3 17.1 us: join_turns(): pl.pallas_call(functools.partial(join_turns_kernel, 4, runs, halfway), gr...]
    dynamic_update_slice x24 -> x4, local copies, waits for them, and re-layouts: 15.8 us -> 0.15 us  [by_owner(): lax.dynamic_update_slice(parts, piece[None], (owner, begin) + (0,) * (val...]
    reduce_scatter x5, waiting for transfers between devices: 27.5 us -> 16.5 us  [scatter(): return lax.psum_scatter(grad, axes, scatter_dimension=0, tiled=True)]
    ppermute x43 -> x47, waiting for transfers between devices: 175 us -> 182 us  [swap(): lax.ppermute(value, 'group', [(i, i ^ turn) for i in range(self.group)])]
    ppermute x43 -> x47, starting transfers between devices: 49.3 us -> 53.3 us  [swap(): lax.ppermute(value, 'group', [(i, i ^ turn) for i in range(self.group)])]
  transfers between devices with their start and end apart: 62 -> 66, of which waited for: 26 -> 35; matrix products, arithmetic and copies ran while one was open for 31% -> 30% of each run, Pallas kernels for 18% -> 16%
where the time goes in v6:
time: 796 us; the launch traced here: 790 us
  waiting for transfers between devices  307 us (39%)
  matrix products  149 us (19%)
  Pallas kernels  136 us (17%)
  starting transfers between devices  69.8 us (9%)
  local copies, waits for them, and re-layouts  62.4 us (8%)
  other arithmetic  49.8 us (6%)
  between operations  15.5 us (2%)
    ppermute x47, waiting for transfers between devices, swap(): lax.ppermute(value, 'group', [(i, i ^ turn) for i in range(self.group)])  182 us
    ppermute x47, starting transfers between devices, swap(): lax.ppermute(value, 'group', [(i, i ^ turn) for i in range(self.group)])  53.3 us
    all_to_all x2, waiting for transfers between devices, deal(): lax.all_to_all(sorted_rows, 'seq', split_axis=0, concat_axis=0, tiled=True)  50.5 us
    dot_general x11, matrix products, dot_t(): lax.dot_general(left, right, (((0,), (0,)), ((), ())), preferred_element_...  50.4 us
    dot_general x8, matrix products, dot(): return jnp.dot(left, right, preferred_element_type=f32)  50.4 us
    dot_general x5, matrix products, dot_back(): lax.dot_general(left, right, (((1,), (1,)), ((), ())), preferred_element_...  48.6 us
    pallas_call x1, Pallas kernels, mixer_backward(): pl.pallas_call(functools.partial(mixer_backward_kernel, heads), grid=(blo...  41.2 us
    pallas_call x1, Pallas kernels, mixer_forward(): pl.pallas_call(functools.partial(mixer_forward_kernel, heads), grid=(bloc...  34.7 us
  transfers between devices with their start and end apart: 66, of which 35 were waited for; matrix products, arithmetic and copies ran while one was open for 30% of the time, Pallas kernels for 16%

profile of v6, /device:TPU:0, one launch (start us, length us, event | category | flops | bytes accessed | tf_op | source)
XLA Modules:
  0.0 790.1 jit_solution(6161897080741863336)
XLA Ops:
  15.4 9.1 %small_gather.1 = bf16[8,32,128]{2,1,0:T(8,128)(2,1)} custom-call(bf16[32,128]{1,0:T(8,128)(2,1)} %bitcast.233), custom_call_target="tpu_custom_call" | custom-call | flops 1 | bytes 1 | tf_op jit(solution)/shard_map/small_gather/pallas_call | solution.py:604
  31.9 42.5 %all-to-all-done = bf16[4,48,2048]{2,1,0:T(8,128)(2,1)} async-done(((bf16[4,48,2048]{2,1,0:T(8,128)(2,1)}), bf16[4,48,2048]{2,1,0:T(8,128)(2,1)}, u32[]{:S(2)}, u32[]{:S(2)}) %all-to-all-start) | async-done | bytes 786464 | tf_op jit(solution)/shard_map/all_to_all | solution.py:962
  117.5 14.8 %collective-permute-done.1 = bf16[192,2048]{1,0:T(8,128)(2,1)} collective-permute-done((bf16[192,2048]{1,0:T(8,128)(2,1)}, bf16[192,2048]{1,0:T(8,128)(2,1)}, u32[]{:S(2)}, u32[]{:S(2)}) %collective-permute-start.1) | collective-permute-done | bytes 786464 | tf_op jit(solution)/shard_map/ppermute | solution.py:990
  148.3 20.2 %all-gather.5.cloned.1.call-done = bf16[2048,3072]{1,0:T(8,128)(2,1)} async-done(((bf16[256,3072]{1,0:T(8,128)(2,1)}), bf16[2048,3072]{1,0:T(8,128)(2,1)}) %all-gather.5.cloned.1.call-update) | async-done | bytes 12582928 | tf_op jit(solution)/shard_map/all_gather | solution.py:1289
  168.4 16.0 %fusion.62.conv_ref.gate_ref.ahead_ref = f32[768,3072]{1,0:T(8,128)} fusion(bf16[768,2048]{1,0:T(8,128)(2,1)} %bitcast.182, bf16[2048,3072]{1,0:T(8,128)(2,1)} %all-gather.5.cloned.1.call-done), kind=kOutput, calls=%fused_computation.216 | convolution fusion | flops 9663676416 | bytes 25165824 | tf_op jit(solution)/shard_map/dot_general | solution.py:929
  193.2 34.7 %mixer_forward.1 = (bf16[768,1024]{1,0:T(8,128)(2,1)S(1)}, f32[768,1024]{1,0:T(8,128)}, bf16[768,2048]{1,0:T(8,128)(2,1)}, f32[12,4,128,256]{3,2,1,0:T(8,128)}, ...) custom-call(f32[768,3072]{1,0:T(8,128)} %fusion.62.conv_ref.gate_ref.ahead_ref, ...), custom_call_target="tpu_custom_call" | custom-call | flops 1 | bytes 1 | tf_op jit(solution)/shard_map/mixer_forward/pallas_call | solution.py:471
  245.0 16.1 %collective-permute-done.10 = bf16[192,2048]{1,0:T(8,128)(2,1)} collective-permute-done((bf16[192,2048]{1,0:T(8,128)(2,1)}, bf16[192,2048]{1,0:T(8,128)(2,1)}, u32[]{:S(2)}, u32[]{:S(2)}) %collective-permute-start.10) | collective-permute-done | bytes 786464 | tf_op jit(solution)/shard_map/ppermute | solution.py:990
  261.1 16.5 %collective-permute-done.11 = bf16[192,2048]{1,0:T(8,128)(2,1)} collective-permute-done((bf16[192,2048]{1,0:T(8,128)(2,1)}, bf16[192,2048]{1,0:T(8,128)(2,1)}, u32[]{:S(2)}, u32[]{:S(2)}) %collective-permute-start.11) | collective-permute-done | bytes 786464 | tf_op jit(solution)/shard_map/ppermute | solution.py:990
  285.2 17.1 %collective-permute-done.13 = bf16[192,2048]{1,0:T(8,128)(2,1)} collective-permute-done((bf16[192,2048]{1,0:T(8,128)(2,1)S(1)}, bf16[192,2048]{1,0:T(8,128)(2,1)}, u32[]{:S(2)}, u32[]{:S(2)}) %collective-permute-start.13) | collective-permute-done | bytes 786464 | tf_op jit(solution)/shard_map/ppermute | solution.py:990
  302.3 15.3 %collective-permute-done.14 = bf16[192,2048]{1,0:T(8,128)(2,1)} collective-permute-done((bf16[192,2048]{1,0:T(8,128)(2,1)S(1)}, bf16[192,2048]{1,0:T(8,128)(2,1)}, u32[]{:S(2)}, u32[]{:S(2)}) %collective-permute-start.14) | collective-permute-done | bytes 786464 | tf_op jit(solution)/shard_map/ppermute | solution.py:990
  324.4 13.7 %fusion.64 = f32[768,2816]{1,0:T(8,128)S(1)} fusion(bf16[768,2048]{1,0:T(8,128)(2,1)} %copy-done.34, bf16[2048,2816]{1,0:T(8,128)(2,1)} %all-gather.9.cloned.1.call-done), kind=kOutput, calls=%fused_computation.218 | convolution fusion | flops 8858370048 | bytes 23330816 | tf_op jit(solution)/shard_map/dot_general | solution.py:929
  356.7 27.9 %all-gather.11.cloned.1.call-done = bf16[1408,2048]{1,0:T(8,128)(2,1)} async-done(((bf16[176,2048]{1,0:T(8,128)(2,1)}), bf16[1408,2048]{1,0:T(8,128)(2,1)}) %all-gather.11.cloned.1.call-update) | async-done | bytes 5767184 | tf_op jit(solution)/shard_map/all_gather | solution.py:1327
  384.6 12.5 %fusion.32 = (f32[768,1408]{1,0:T(8,128)S(1)}, f32[768,1408]{1,0:T(8,128)}) fusion(f32[768,2816]{1,0:T(8,128)} %copy-done.35, bf16[768,2048]{1,0:T(8,128)(2,1)} %pad_maximum_fusion, bf16[1408,2048]{1,0:T(8,128)(2,1)} %all-gather.11.cloned.1.call-done), kind=kOutput, calls=%fused_computation.79 | convolution fusion | flops 4442161152 | bytes 26214400 | tf_op jit(solution)/shard_map/dot_general | solution.py:937
  399.9 13.6 %convolution_convert_fusion.7 = bf16[768,2048]{1,0:T(8,128)(2,1)S(1)} fusion(bf16[768,2816]{1,0:T(8,128)(2,1)S(1)} %add_convert_fusion.1, bf16[2048,2816]{1,0:T(8,128)(2,1)} %all-gather.9.cloned.1.call-done), kind=kOutput, calls=%fused_computation.21 | convolution fusion | flops 8859942912 | bytes 19005440 | tf_op jit(solution)/shard_map/dot_general | solution.py:937
  425.2 16.4 %reduce-scatter.6.cloned.1.call-done.near_ref = bf16[176,2048]{1,0:T(8,128)(2,1)} async-done(((bf16[704,2048]{1,0:T(8,128)(2,1)}), bf16[176,2048]{1,0:T(8,128)(2,1)}) %reduce-scatter.6.cloned.1.call-update) | async-done | bytes 720912 | tf_op jit(solution)/shard_map/reduce_scatter | solution.py:1135
  441.7 9.6 %add_convert_fusion = bf16[1024,2816]{1,0:T(8,128)(2,1)} fusion(bf16[1024,2816]{1,0:T(8,128)(2,1)} %collective-permute-done.20, bf16[768,1024]{1,0:T(8,128)(2,1)S(1)} %copy-done.47, bf16[768,2816]{1,0:T(8,128)(2,1)} %copy-done.38), kind=kOutput, calls=%fused_computation | convolution fusion | flops 4437835776 | bytes 17432576 | tf_op jit(solution)/shard_map/dot_general | solution.py:933
  478.1 10.0 %collective-permute-done.21 = bf16[192,2048]{1,0:T(8,128)(2,1)S(1)} collective-permute-done((bf16[192,2048]{1,0:T(8,128)(2,1)S(1)}, bf16[192,2048]{1,0:T(8,128)(2,1)S(1)}, u32[]{:S(2)}, u32[]{:S(2)}) %collective-permute-start.21) | collective-permute-done | bytes 786464 | tf_op jit(solution)/shard_map/ppermute | solution.py:990
  488.1 15.9 %collective-permute-done.22 = bf16[192,2048]{1,0:T(8,128)(2,1)S(1)} collective-permute-done((bf16[192,2048]{1,0:T(8,128)(2,1)S(1)}, bf16[192,2048]{1,0:T(8,128)(2,1)S(1)}, u32[]{:S(2)}, u32[]{:S(2)}) %collective-permute-start.22) | collective-permute-done | bytes 786464 | tf_op jit(solution)/shard_map/ppermute | solution.py:990
  525.8 41.2 %mixer_backward.1 = (bf16[768,3072]{1,0:T(8,128)(2,1)}, f32[768,8]{1,0:T(8,128)S(1)}, f32[4,2048]{1,0:T(4,128)S(1)}, f32[1,256]{1,0:T(1,128)S(1)}, f32[1,8]{1,0:T(1,128)S(1)}) custom-call(f32[768,3072]{1,0:T(8,128)} %fusion.62.conv_ref.gate_ref.ahead_ref, f32[768,3072]{1,0:T(8,128)} %fusion.62.conv_ref.gate_ref.ahead_ref, ...), custom_call_target="tpu_custom_call" | custom-call | flops 1 | bytes 1 | tf_op jit(solution)/shard_map/mixer_backward/pallas_call | solution.py:516
  596.9 14.6 %fusion.66 = f32[768,2048]{1,0:T(8,128)S(1)} fusion(bf16[768,3072]{1,0:T(8,128)(2,1)} %get-tuple-element.197, bf16[2048,3072]{1,0:T(8,128)(2,1)} %all-gather.5.cloned.1.call-done), kind=kOutput, calls=%fused_computation.220 | convolution fusion | flops 9663676416 | bytes 23592960 | tf_op jit(solution)/shard_map/dot_general | solution.py:937
  623.1 15.4 %collective-permute-done.32 = bf16[192,2048]{1,0:T(8,128)(2,1)S(1)} collective-permute-done((bf16[192,2048]{1,0:T(8,128)(2,1)S(1)}, bf16[192,2048]{1,0:T(8,128)(2,1)S(1)}, u32[]{:S(2)}, u32[]{:S(2)}) %collective-permute-start.32) | collective-permute-done | bytes 786464 | tf_op jit(solution)/shard_map/ppermute | solution.py:990
  638.5 17.2 %collective-permute-done.33 = bf16[192,2048]{1,0:T(8,128)(2,1)S(1)} collective-permute-done((bf16[192,2048]{1,0:T(8,128)(2,1)S(1)}, bf16[192,2048]{1,0:T(8,128)(2,1)S(1)}, u32[]{:S(2)}, u32[]{:S(2)}) %collective-permute-start.33) | collective-permute-done | bytes 786464 | tf_op jit(solution)/shard_map/ppermute | solution.py:990
  675.5 21.2 %small_sum.1 = f32[4,32,128]{2,1,0:T(8,128)} custom-call(f32[8,32,128]{2,1,0:T(8,128)} %bitcast.209), custom_call_target="tpu_custom_call" | custom-call | flops 1 | bytes 1 | tf_op jit(solution)/shard_map/small_sum/pallas_call | solution.py:659
  705.6 9.0 %join_turns.3 = f32[256,11264]{1,0:T(8,128)} custom-call(bf16[256,2816]{1,0:T(8,128)(2,1)} %reduce-scatter.8.cloned.1.call-done.near_ref, bf16[256,2816]{1,0:T(8,128)(2,1)S(1)} %copy-done.7, bf16[256,2816]{1,0:T(8,128)(2,1)S(1)} %copy-done.9, bf16[128,2816]{1,0:T(8,128)(2,1)} %collective-permute-done.37.first_ref, ...), custom_call_target="tpu_custom_call" | custom-call | flops 1 | bytes 1 | tf_op jit(solution)/shard_map/join_turns/pallas_call | solution.py:865
  (433 shorter events, 334.2 us)
Async XLA Ops:
  7.2 161.2 %all-gather.5.cloned.1.call-start = ((), (), s32[]{:S(2)}) async-start(), calls=%async_computation.8 | async-start | bytes 14155776 | tf_op jit(solution)/shard_map/all_gather | solution.py:1289
  27.2 47.1 %all-to-all-start = ((bf16[4,48,2048]{2,1,0:T(8,128)(2,1)}), bf16[4,48,2048]{2,1,0:T(8,128)(2,1)}, u32[]{:S(2)}, u32[]{:S(2)}) async-start(bf16[4,48,2048]{2,1,0:T(8,128)(2,1)} %bitcast.198), calls=%async_computation | async-start | bytes 1572864 | tf_op jit(solution)/shard_map/all_to_all | solution.py:962
  31.8 200.6 %all-gather.7.cloned.1.call-start = ((), (), s32[]{:S(2)}) async-start(), calls=%async_computation.9 | async-start | bytes 4718592 | tf_op jit(solution)/shard_map/all_gather | solution.py:1146
  84.1 240.2 %all-gather.9.cloned.1.call-start = ((), (), s32[]{:S(2)}) async-start(), calls=%async_computation.10 | async-start | bytes 12976128 | tf_op jit(solution)/shard_map/all_gather | solution.py:1324
  103.0 45.3 %all-to-all-start.1 = ((bf16[4,48,2048]{2,1,0:T(8,128)(2,1)}), bf16[4,48,2048]{2,1,0:T(8,128)(2,1)}, u32[]{:S(2)}, u32[]{:S(2)}) async-start(bf16[4,48,2048]{2,1,0:T(8,128)(2,1)} %bitcast.197), calls=%async_computation.1 | async-start | bytes 1572864 | tf_op jit(solution)/shard_map/all_to_all | solution.py:962
  107.2 277.4 %all-gather.11.cloned.1.call-start = ((), (), s32[]{:S(2)}) async-start(), calls=%async_computation.11 | async-start | bytes 6488064 | tf_op jit(solution)/shard_map/all_gather | solution.py:1327
  184.4 43.6 %collective-permute-start.6 = (bf16[192,2048]{1,0:T(8,128)(2,1)}, bf16[192,2048]{1,0:T(8,128)(2,1)}, u32[]{:S(2)}, u32[]{:S(2)}) collective-permute-start(bf16[192,2048]{1,0:T(8,128)(2,1)} %bitcast.13), channel_id=1, source_target_pairs={{0,8},{8,0},{16,24},{24,16},{1,9},{9,1},{17,25},{25,17},{2,10},{10... | collective-permute-start | bytes 2359304 | tf_op jit(solution)/shard_map/ppermute | solution.py:990
  185.8 42.1 %collective-permute-start.7 = (bf16[192,2048]{1,0:T(8,128)(2,1)}, bf16[192,2048]{1,0:T(8,128)(2,1)}, u32[]{:S(2)}, u32[]{:S(2)}) collective-permute-start(bf16[192,2048]{1,0:T(8,128)(2,1)} %bitcast.13), channel_id=1, source_target_pairs={{0,16},{8,24},{16,0},{24,8},{1,17},{9,25},{17,1},{25,9},{2,18},{10... | collective-permute-start | bytes 2359304 | tf_op jit(solution)/shard_map/ppermute | solution.py:990
  187.3 40.7 %collective-permute-start.8 = (bf16[192,2048]{1,0:T(8,128)(2,1)}, bf16[192,2048]{1,0:T(8,128)(2,1)}, u32[]{:S(2)}, u32[]{:S(2)}) collective-permute-start(bf16[192,2048]{1,0:T(8,128)(2,1)} %bitcast.13), channel_id=1, source_target_pairs={{0,24},{8,16},{16,8},{24,0},{1,25},{9,17},{17,9},{25,1},{2,26},{10... | collective-permute-start | bytes 2359304 | tf_op jit(solution)/shard_map/ppermute | solution.py:990
  241.8 35.8 %collective-permute-start.11 = (bf16[192,2048]{1,0:T(8,128)(2,1)}, bf16[192,2048]{1,0:T(8,128)(2,1)}, u32[]{:S(2)}, u32[]{:S(2)}) collective-permute-start(bf16[192,2048]{1,0:T(8,128)(2,1)} %bitcast.27), channel_id=1, source_target_pairs={{0,16},{8,24},{16,0},{24,8},{1,17},{9,25},{17,1},{25,9},{2,18},{10... | collective-permute-start | bytes 2359304 | tf_op jit(solution)/shard_map/ppermute | solution.py:990
  244.8 196.9 %reduce-scatter.6.cloned.1.call-start = ((), (), s32[]{:S(2)}) async-start(), calls=%async_computation.12 | async-start | bytes 3604480 | tf_op jit(solution)/shard_map/reduce_scatter | solution.py:1135
  356.5 214.4 %reduce-scatter.8.cloned.1.call-start = ((), (), s32[]{:S(2)}) async-start(), calls=%async_computation.13 | async-start | bytes 7208960 | tf_op jit(solution)/shard_map/reduce_scatter | solution.py:1135
  423.2 36.6 %collective-permute-start.18 = (bf16[192,2048]{1,0:T(8,128)(2,1)}, bf16[192,2048]{1,0:T(8,128)(2,1)}, u32[]{:S(2)}, u32[]{:S(2)}) collective-permute-start(bf16[192,2048]{1,0:T(8,128)(2,1)} %get-tuple-element.296), channel_id=1, source_target_pairs={{0,16},{8,24},{16,0},{24,8},{1,17},{9,25},{17,1},{25,9},{2,18},{10... | collective-permute-start | bytes 2359304 | tf_op jit(solution)/shard_map/ppermute | solution.py:990
  459.9 154.4 %reduce-scatter.12.cloned.1.call-start = ((), (), s32[]{:S(2)}) async-start(), calls=%async_computation.15 | async-start | bytes 2621440 | tf_op jit(solution)/shard_map/reduce_scatter | solution.py:1135
  518.1 52.7 %collective-permute-start.25 = (bf16[192,2048]{1,0:T(8,128)(2,1)}, bf16[192,2048]{1,0:T(8,128)(2,1)}, u32[]{:S(2)}, u32[]{:S(2)}) collective-permute-start(bf16[192,2048]{1,0:T(8,128)(2,1)} %get-tuple-element.294), channel_id=1, source_target_pairs={{0,8},{8,0},{16,24},{24,16},{1,9},{9,1},{17,25},{25,17},{2,10},{10... | collective-permute-start | bytes 2359304 | tf_op jit(solution)/shard_map/ppermute | solution.py:990
  518.8 52.0 %collective-permute-start.26 = (bf16[192,2048]{1,0:T(8,128)(2,1)}, bf16[192,2048]{1,0:T(8,128)(2,1)}, u32[]{:S(2)}, u32[]{:S(2)}) collective-permute-start(bf16[192,2048]{1,0:T(8,128)(2,1)} %get-tuple-element.293), channel_id=1, source_target_pairs={{0,16},{8,24},{16,0},{24,8},{1,17},{9,25},{17,1},{25,9},{2,18},{10... | collective-permute-start | bytes 2359304 | tf_op jit(solution)/shard_map/ppermute | solution.py:990
  520.2 50.6 %collective-permute-start.27 = (bf16[192,2048]{1,0:T(8,128)(2,1)}, bf16[192,2048]{1,0:T(8,128)(2,1)}, u32[]{:S(2)}, u32[]{:S(2)}) collective-permute-start(bf16[192,2048]{1,0:T(8,128)(2,1)} %get-tuple-element.292), channel_id=1, source_target_pairs={{0,24},{8,16},{16,8},{24,0},{1,25},{9,17},{17,9},{25,1},{2,26},{10... | collective-permute-start | bytes 2359304 | tf_op jit(solution)/shard_map/ppermute | solution.py:990
  521.6 48.9 %collective-permute-start.28 = (bf16[176,2048]{1,0:T(8,128)(2,1)}, bf16[176,2048]{1,0:T(8,128)(2,1)}, u32[]{:S(2)}, u32[]{:S(2)}) collective-permute-start(bf16[176,2048]{1,0:T(8,128)(2,1)} %reduce-scatter.6.cloned.1.call-done.near_ref), channel_id=1, source_target_pairs={{0,8},{8,0},{16,24},{24,16},{1,9},{9,1},{17,25},{25,17},{2,10},{10... | collective-permute-start | bytes 2162696 | tf_op jit(solution)/shard_map/ppermute | solution.py:990
  522.3 48.5 %collective-permute-start.29 = (bf16[176,2048]{1,0:T(8,128)(2,1)}, bf16[176,2048]{1,0:T(8,128)(2,1)}, u32[]{:S(2)}, u32[]{:S(2)}) collective-permute-start(bf16[176,2048]{1,0:T(8,128)(2,1)} %reduce-scatter.6.cloned.1.call-done.near_ref), channel_id=1, source_target_pairs={{0,16},{8,24},{16,0},{24,8},{1,17},{9,25},{17,1},{25,9},{2,18},{10... | collective-permute-start | bytes 2162696 | tf_op jit(solution)/shard_map/ppermute | solution.py:990
  523.7 173.1 %reduce-scatter.10.cloned.1.call-start = ((), (), s32[]{:S(2)}) async-start(), calls=%async_computation.14 | async-start | bytes 3932160 | tf_op jit(solution)/shard_map/reduce_scatter | solution.py:1135
  586.8 149.9 %reduce-scatter.14.cloned.1.call-start = ((), (), s32[]{:S(2)}) async-start(), calls=%async_computation.16 | async-start | bytes 3932160 | tf_op jit(solution)/shard_map/reduce_scatter | solution.py:1135
  618.5 37.1 %collective-permute-start.33 = (bf16[192,2048]{1,0:T(8,128)(2,1)S(1)}, bf16[192,2048]{1,0:T(8,128)(2,1)S(1)}, u32[]{:S(2)}, u32[]{:S(2)}) collective-permute-start(bf16[192,2048]{1,0:T(8,128)(2,1)S(1)} %bitcast.206), channel_id=1, source_target_pairs={{0,16},{8,24},{16,0},{24,8},{1,17},{9,25},{17,1},{25,9},{2,18},{10... | collective-permute-start | bytes 2359304 | tf_op jit(solution)/shard_map/ppermute | solution.py:990
  618.7 37.0 %collective-permute-start.34 = (bf16[192,2048]{1,0:T(8,128)(2,1)S(1)}, bf16[192,2048]{1,0:T(8,128)(2,1)S(1)}, u32[]{:S(2)}, u32[]{:S(2)}) collective-permute-start(bf16[192,2048]{1,0:T(8,128)(2,1)S(1)} %bitcast.205), channel_id=1, source_target_pairs={{0,24},{8,16},{16,8},{24,0},{1,25},{9,17},{17,9},{25,1},{2,26},{10... | collective-permute-start | bytes 2359304 | tf_op jit(solution)/shard_map/ppermute | solution.py:990
  737.3 39.0 %all-to-all-start.2 = ((bf16[4,48,4096]{2,1,0:T(8,128)(2,1)}), bf16[4,48,4096]{2,1,0:T(8,128)(2,1)}, u32[]{:S(2)}, u32[]{:S(2)}) async-start(bf16[4,48,4096]{2,1,0:T(8,128)(2,1)} %bitcast.187), calls=%async_computation.7 | async-start | bytes 3145728 | tf_op jit(solution)/shard_map/all_to_all | solution.py:977
  (112 other events, 1909.5 us)
Sparse Core Ops, SparseCore 0:
  15.5 152.8 all-gather.4
  170.0 45.2 all-gather.6
  217.6 106.7 all-gather.8
  325.9 58.7 all-gather.10
  386.8 54.8 reduce-scatter.5
  460.0 99.9 reduce-scatter.7
  562.2 44.3 reduce-scatter.11
  609.6 59.5 reduce-scatter.9
  671.6 61.9 reduce-scatter.13

commit v7 on v6

--- a/solution.py
+++ b/solution.py
@@ -1134,7 +1134,7 @@
         axes = "seq" if self.cores == 2 else SHARDED
         return lax.psum_scatter(grad, axes, scatter_dimension=0, tiled=True)
 
-    def out_rows(self, w_out):
+    def out_rows(self, w_out, down_piece):
         width = w_out.shape[1]
         if self.subs == 1 and self.cores == 2:
             mine = lax.dynamic_slice(w_out, ((self.part % 2) * DV, 0), (DV, width))
@@ -1143,12 +1143,15 @@
             other = lax.dynamic_slice(mine, ((1 - self.core) * half, 0), (half, width))
             got = lax.ppermute(other, "wshard", [(0, 1), (1, 0)])
             piece = jnp.where(self.core == self.part // 2, kept, got)
-            return lax.all_gather(piece, SHARDED, axis=0, tiled=True)
+            both = lax.all_gather(jnp.concatenate([piece, down_piece], axis=0), SHARDED, axis=0)
+            both = both.reshape(self.seq * self.cores, -1, width)
+            return both[:, :half].reshape(-1, width), both[:, half:].reshape(-1, width)
         every = lax.all_gather(w_out, SHARDED, axis=0, tiled=True)
         every = every.reshape(self.heads, self.group, DV, width)
-        return lax.dynamic_slice(
+        out_mine = lax.dynamic_slice(
             every, (0, self.part, 0, 0), (self.heads, 1, DV, width)
         ).reshape(-1, width)
+        return out_mine, lax.all_gather(down_piece, SHARDED, axis=0, tiled=True)
 
     def out_grad(self, gated, d_branch):
         if self.subs == 1 and self.cores == 2:
@@ -1318,14 +1321,13 @@
         (normed_all, at.core_columns(normed_all, 2))
     )
 
-    out_mine = at.out_rows(w_out)
     piece = device_rows // at.group
+    out_mine, down_mine = at.out_rows(
+        w_out, lax.dynamic_slice(w_down, (at.part * piece, 0), (piece, width))
+    )
     gu_pieces = tuple((block * device_rows, piece) for block in range(2 * devices))
     gu_mine = lax.all_gather(
         pick_columns(w_gu, gu_pieces, at.group), SHARDED, axis=0, tiled=True
-    )
-    down_mine = lax.all_gather(
-        lax.dynamic_slice(w_down, (at.part * piece, 0), (piece, width)), SHARDED, axis=0, tiled=True
     )
     cot_own = at.deal(dot(sorting, cotangent).astype(bf16))
     normed_all, cot_own = lax.optimization_barrier((normed_all, cot_own))
@@ -1340,7 +1342,9 @@
     proj = at.to_lane(proj)
     mixer_args = (proj, gates_ab, side, conv_mine, o_f[None], decay_mine, dt_mine)
     gated_lane, *kept = mixer_forward(*mixer_args)
-    gated_lane, cot_all = lax.optimization_barrier((gated_lane, cot_all))
+    gated_lane, cot_all, out_mine, down_mine = lax.optimization_barrier(
+        (gated_lane, cot_all, out_mine, down_mine)
+    )
     gated = at.to_own(gated_lane)
     own, got = at.send_places(dot(gated, out_mine).astype(bf16))
     resid = tokens_f + sum_parts(own, got)

time: 796 us -> 850 us (1.068)
  waiting for transfers between devices: 307 us -> 353 us
    all_gather x2 -> x1, waiting for transfers between devices: 27.9 us -> 71.3 us  [out_rows(): lax.all_gather(jnp.concatenate([piece, down_piece], axis=0), SHARDED, axi...]
    slice x0 -> x2, local copies, waits for them, and re-layouts: none -> 9.4 us  [the longest x1 6.16 us: out_rows(): both[:, half:].reshape(-1, width)]
  transfers between devices with their start and end apart: 66 -> 65, of which waited for: 35 -> 35; matrix products, arithmetic and copies ran while one was open for 30% -> 26% of each run, Pallas kernels for 16% -> 16%
where the time goes in v7:
time: 850 us; the launch traced here: 843 us
  waiting for transfers between devices  353 us (42%)
  matrix products  150 us (18%)
  Pallas kernels  140 us (16%)
  starting transfers between devices  67.5 us (8%)
  local copies, waits for them, and re-layouts  66.5 us (8%)
  other arithmetic  49.7 us (6%)
  between operations  15.7 us (2%)
    ppermute x47, waiting for transfers between devices, swap(): lax.ppermute(value, 'group', [(i, i ^ turn) for i in range(self.group)])  190 us
    all_gather x1, waiting for transfers between devices, out_rows(): lax.all_gather(jnp.concatenate([piece, down_piece], axis=0), SHARDED, axi...  71.3 us
    ppermute x47, starting transfers between devices, swap(): lax.ppermute(value, 'group', [(i, i ^ turn) for i in range(self.group)])  53 us
    dot_general x11, matrix products, dot_t(): lax.dot_general(left, right, (((0,), (0,)), ((), ())), preferred_element_...  52.7 us
    all_to_all x2, waiting for transfers between devices, deal(): lax.all_to_all(sorted_rows, 'seq', split_axis=0, concat_axis=0, tiled=True)  51 us
    dot_general x5, matrix products, dot_back(): lax.dot_general(left, right, (((1,), (1,)), ((), ())), preferred_element_...  49.5 us
    dot_general x8, matrix products, dot(): return jnp.dot(left, right, preferred_element_type=f32)  48.3 us
    pallas_call x1, Pallas kernels, mixer_backward(): pl.pallas_call(functools.partial(mixer_backward_kernel, heads), grid=(blo...  41.7 us
  transfers between devices with their start and end apart: 65, of which 35 were waited for; matrix products, arithmetic and copies ran while one was open for 26% of the time, Pallas kernels for 16%

profile of v7, /device:TPU:0, one launch (start us, length us, event | category | flops | bytes accessed | tf_op | source)
XLA Modules:
  0.0 842.6 jit_solution(11192839464840149913)
XLA Ops:
  31.9 42.5 %all-to-all-done = bf16[4,48,2048]{2,1,0:T(8,128)(2,1)} async-done(((bf16[4,48,2048]{2,1,0:T(8,128)(2,1)}), bf16[4,48,2048]{2,1,0:T(8,128)(2,1)}, u32[]{:S(2)}, u32[]{:S(2)}) %all-to-all-start) | async-done | bytes 786464 | tf_op jit(solution)/shard_map/all_to_all | solution.py:962
  108.2 9.5 %collective-permute-done = bf16[192,2048]{1,0:T(8,128)(2,1)S(1)} collective-permute-done((bf16[192,2048]{1,0:T(8,128)(2,1)S(1)}, bf16[192,2048]{1,0:T(8,128)(2,1)S(1)}, u32[]{:S(2)}, u32[]{:S(2)}) %collective-permute-start) | collective-permute-done | bytes 786464 | tf_op jit(solution)/shard_map/ppermute | solution.py:990
  117.7 14.9 %collective-permute-done.1 = bf16[192,2048]{1,0:T(8,128)(2,1)} collective-permute-done((bf16[192,2048]{1,0:T(8,128)(2,1)S(1)}, bf16[192,2048]{1,0:T(8,128)(2,1)}, u32[]{:S(2)}, u32[]{:S(2)}) %collective-permute-start.1) | collective-permute-done | bytes 786464 | tf_op jit(solution)/shard_map/ppermute | solution.py:990
  148.7 19.8 %all-gather.5.cloned.1.call-done = bf16[2048,3072]{1,0:T(8,128)(2,1)} async-done(((bf16[256,3072]{1,0:T(8,128)(2,1)}), bf16[2048,3072]{1,0:T(8,128)(2,1)}) %all-gather.5.cloned.1.call-update) | async-done | bytes 12582928 | tf_op jit(solution)/shard_map/all_gather | solution.py:1292
  168.5 16.2 %fusion.62.conv_ref.gate_ref.ahead_ref = f32[768,3072]{1,0:T(8,128)} fusion(bf16[768,2048]{1,0:T(8,128)(2,1)} %bitcast.185, bf16[2048,3072]{1,0:T(8,128)(2,1)} %all-gather.5.cloned.1.call-done), kind=kOutput, calls=%fused_computation.217 | convolution fusion | flops 9663676416 | bytes 25165824 | tf_op jit(solution)/shard_map/dot_general | solution.py:929
  192.6 71.3 %all-gather.9.cloned.1.call-done = bf16[2432,2048]{1,0:T(8,128)(2,1)} async-done(((bf16[304,2048]{1,0:T(8,128)(2,1)}), bf16[2432,2048]{1,0:T(8,128)(2,1)}) %all-gather.9.cloned.1.call-update) | async-done | bytes 9961488 | tf_op jit(solution)/shard_map/all_gather | solution.py:1146
  273.3 35.5 %mixer_forward.1 = (bf16[768,1024]{1,0:T(8,128)(2,1)S(1)}, f32[768,1024]{1,0:T(8,128)}, bf16[768,2048]{1,0:T(8,128)(2,1)}, f32[12,4,128,256]{3,2,1,0:T(8,128)}, ...) custom-call(f32[768,3072]{1,0:T(8,128)} %fusion.62.conv_ref.gate_ref.ahead_ref, ...), custom_call_target="tpu_custom_call" | custom-call | flops 1 | bytes 1 | tf_op jit(solution)/shard_map/mixer_forward/pallas_call | solution.py:471
  320.2 16.9 %collective-permute-done.10 = bf16[192,2048]{1,0:T(8,128)(2,1)S(1)} collective-permute-done((bf16[192,2048]{1,0:T(8,128)(2,1)S(1)}, bf16[192,2048]{1,0:T(8,128)(2,1)S(1)}, u32[]{:S(2)}, u32[]{:S(2)}) %collective-permute-start.10) | collective-permute-done | bytes 786464 | tf_op jit(solution)/shard_map/ppermute | solution.py:990
  337.1 17.4 %collective-permute-done.11 = bf16[192,2048]{1,0:T(8,128)(2,1)S(1)} collective-permute-done((bf16[192,2048]{1,0:T(8,128)(2,1)S(1)}, bf16[192,2048]{1,0:T(8,128)(2,1)S(1)}, u32[]{:S(2)}, u32[]{:S(2)}) %collective-permute-start.11) | collective-permute-done | bytes 786464 | tf_op jit(solution)/shard_map/ppermute | solution.py:990
  363.0 17.3 %collective-permute-done.13 = bf16[192,2048]{1,0:T(8,128)(2,1)} collective-permute-done((bf16[192,2048]{1,0:T(8,128)(2,1)}, bf16[192,2048]{1,0:T(8,128)(2,1)}, u32[]{:S(2)}, u32[]{:S(2)}) %collective-permute-start.13) | collective-permute-done | bytes 786464 | tf_op jit(solution)/shard_map/ppermute | solution.py:990
  380.3 16.2 %collective-permute-done.14 = bf16[192,2048]{1,0:T(8,128)(2,1)} collective-permute-done((bf16[192,2048]{1,0:T(8,128)(2,1)}, bf16[192,2048]{1,0:T(8,128)(2,1)}, u32[]{:S(2)}, u32[]{:S(2)}) %collective-permute-start.14) | collective-permute-done | bytes 786464 | tf_op jit(solution)/shard_map/ppermute | solution.py:990
  403.1 13.9 %fusion.64 = f32[768,2816]{1,0:T(8,128)S(1)} fusion(bf16[768,2048]{1,0:T(8,128)(2,1)} %copy-done.29, bf16[2048,2816]{1,0:T(8,128)(2,1)} %all-gather.7.cloned.1.call-done), kind=kOutput, calls=%fused_computation.219 | convolution fusion | flops 8858370048 | bytes 23330816 | tf_op jit(solution)/shard_map/dot_general | solution.py:929
  435.4 13.6 %fusion.32 = (f32[768,1408]{1,0:T(8,128)S(1)}, f32[768,1408]{1,0:T(8,128)}) fusion(f32[768,2816]{1,0:T(8,128)} %copy-done.30, bf16[768,2048]{1,0:T(8,128)(2,1)} %pad_maximum_fusion, bf16[1408,2048]{1,0:T(8,128)(2,1)} %bitcast.193), kind=kOutput, calls=%fused_computation.80 | convolution fusion | flops 4442161152 | bytes 26214400 | tf_op jit(solution)/shard_map/dot_general | solution.py:937
  451.8 13.6 %convolution_convert_fusion.7 = bf16[768,2048]{1,0:T(8,128)(2,1)S(1)} fusion(bf16[768,2816]{1,0:T(8,128)(2,1)S(1)} %add_convert_fusion.1, bf16[2048,2816]{1,0:T(8,128)(2,1)} %all-gather.7.cloned.1.call-done), kind=kOutput, calls=%fused_computation.21 | convolution fusion | flops 8859942912 | bytes 19005440 | tf_op jit(solution)/shard_map/dot_general | solution.py:937
  477.2 11.7 %reduce-scatter.6.cloned.1.call-done.near_ref = bf16[176,2048]{1,0:T(8,128)(2,1)} async-done(((bf16[704,2048]{1,0:T(8,128)(2,1)}), bf16[176,2048]{1,0:T(8,128)(2,1)}) %reduce-scatter.6.cloned.1.call-update) | async-done | bytes 720912 | tf_op jit(solution)/shard_map/reduce_scatter | solution.py:1135
  488.9 11.7 %add_convert_fusion = bf16[1024,2816]{1,0:T(8,128)(2,1)} fusion(bf16[1024,2816]{1,0:T(8,128)(2,1)} %collective-permute-done.20, bf16[768,1024]{1,0:T(8,128)(2,1)} %pad_maximum_fusion.3, bf16[768,2816]{1,0:T(8,128)(2,1)} %copy-done.34), kind=kOutput, calls=%fused_computation | convolution fusion | flops 4437835776 | bytes 17432576 | tf_op jit(solution)/shard_map/dot_general | solution.py:933
  500.6 10.4 %collective-permute-done.18 = bf16[192,2048]{1,0:T(8,128)(2,1)} collective-permute-done((bf16[192,2048]{1,0:T(8,128)(2,1)}, bf16[192,2048]{1,0:T(8,128)(2,1)}, u32[]{:S(2)}, u32[]{:S(2)}) %collective-permute-start.18) | collective-permute-done | bytes 786464 | tf_op jit(solution)/shard_map/ppermute | solution.py:990
  528.9 9.9 %collective-permute-done.21 = bf16[192,2048]{1,0:T(8,128)(2,1)S(1)} collective-permute-done((bf16[192,2048]{1,0:T(8,128)(2,1)S(1)}, bf16[192,2048]{1,0:T(8,128)(2,1)S(1)}, u32[]{:S(2)}, u32[]{:S(2)}) %collective-permute-start.21) | collective-permute-done | bytes 786464 | tf_op jit(solution)/shard_map/ppermute | solution.py:990
  538.8 16.0 %collective-permute-done.22 = bf16[192,2048]{1,0:T(8,128)(2,1)S(1)} collective-permute-done((bf16[192,2048]{1,0:T(8,128)(2,1)S(1)}, bf16[192,2048]{1,0:T(8,128)(2,1)S(1)}, u32[]{:S(2)}, u32[]{:S(2)}) %collective-permute-start.22) | collective-permute-done | bytes 786464 | tf_op jit(solution)/shard_map/ppermute | solution.py:990
  576.5 41.7 %mixer_backward.1 = (bf16[768,3072]{1,0:T(8,128)(2,1)}, f32[768,8]{1,0:T(8,128)S(1)}, f32[4,2048]{1,0:T(4,128)S(1)}, f32[1,256]{1,0:T(1,128)S(1)}, f32[1,8]{1,0:T(1,128)S(1)}) custom-call(f32[768,3072]{1,0:T(8,128)} %fusion.62.conv_ref.gate_ref.ahead_ref, f32[768,3072]{1,0:T(8,128)} %fusion.62.conv_ref.gate_ref.ahead_ref, ...), custom_call_target="tpu_custom_call" | custom-call | flops 1 | bytes 1 | tf_op jit(solution)/shard_map/mixer_backward/pallas_call | solution.py:516
  647.7 14.6 %fusion.66 = f32[768,2048]{1,0:T(8,128)S(1)} fusion(bf16[768,3072]{1,0:T(8,128)(2,1)} %get-tuple-element.201, bf16[2048,3072]{1,0:T(8,128)(2,1)} %all-gather.5.cloned.1.call-done), kind=kOutput, calls=%fused_computation.221 | convolution fusion | flops 9663676416 | bytes 23592960 | tf_op jit(solution)/shard_map/dot_general | solution.py:937
  673.7 15.5 %collective-permute-done.32 = bf16[192,2048]{1,0:T(8,128)(2,1)S(1)} collective-permute-done((bf16[192,2048]{1,0:T(8,128)(2,1)S(1)}, bf16[192,2048]{1,0:T(8,128)(2,1)S(1)}, u32[]{:S(2)}, u32[]{:S(2)}) %collective-permute-start.32) | collective-permute-done | bytes 786464 | tf_op jit(solution)/shard_map/ppermute | solution.py:990
  689.2 17.1 %collective-permute-done.33 = bf16[192,2048]{1,0:T(8,128)(2,1)S(1)} collective-permute-done((bf16[192,2048]{1,0:T(8,128)(2,1)S(1)}, bf16[192,2048]{1,0:T(8,128)(2,1)S(1)}, u32[]{:S(2)}, u32[]{:S(2)}) %collective-permute-start.33) | collective-permute-done | bytes 786464 | tf_op jit(solution)/shard_map/ppermute | solution.py:990
  726.2 21.3 %small_sum.1 = f32[4,32,128]{2,1,0:T(8,128)} custom-call(f32[8,32,128]{2,1,0:T(8,128)} %bitcast.223), custom_call_target="tpu_custom_call" | custom-call | flops 1 | bytes 1 | tf_op jit(solution)/shard_map/small_sum/pallas_call | solution.py:659
  (425 shorter events, 338.6 us)
Async XLA Ops:
  7.2 161.3 %all-gather.5.cloned.1.call-start = ((), (), s32[]{:S(2)}) async-start(), calls=%async_computation.8 | async-start | bytes 14155776 | tf_op jit(solution)/shard_map/all_gather | solution.py:1292
  27.2 47.1 %all-to-all-start = ((bf16[4,48,2048]{2,1,0:T(8,128)(2,1)}), bf16[4,48,2048]{2,1,0:T(8,128)(2,1)}, u32[]{:S(2)}, u32[]{:S(2)}) async-start(bf16[4,48,2048]{2,1,0:T(8,128)(2,1)} %bitcast.208), calls=%async_computation | async-start | bytes 1572864 | tf_op jit(solution)/shard_map/all_to_all | solution.py:962
  31.8 232.1 %all-gather.9.cloned.1.call-start = ((), (), s32[]{:S(2)}) async-start(), calls=%async_computation.15 | async-start | bytes 11206656 | tf_op jit(solution)/shard_map/all_gather | solution.py:1146
  84.5 318.6 %all-gather.7.cloned.1.call-start = ((), (), s32[]{:S(2)}) async-start(), calls=%async_computation.9 | async-start | bytes 12976128 | tf_op jit(solution)/shard_map/all_gather | solution.py:1329
  103.4 45.3 %all-to-all-start.1 = ((bf16[4,48,2048]{2,1,0:T(8,128)(2,1)}), bf16[4,48,2048]{2,1,0:T(8,128)(2,1)}, u32[]{:S(2)}, u32[]{:S(2)}) async-start(bf16[4,48,2048]{2,1,0:T(8,128)(2,1)} %bitcast.12), calls=%async_computation.1 | async-start | bytes 1572864 | tf_op jit(solution)/shard_map/all_to_all | solution.py:962
  107.6 381.3 %reduce-scatter.6.cloned.1.call-start = ((), (), s32[]{:S(2)}) async-start(), calls=%async_computation.10 | async-start | bytes 3604480 | tf_op jit(solution)/shard_map/reduce_scatter | solution.py:1135
  184.6 124.2 %collective-permute-start.6 = (bf16[192,2048]{1,0:T(8,128)(2,1)}, bf16[192,2048]{1,0:T(8,128)(2,1)}, u32[]{:S(2)}, u32[]{:S(2)}) collective-permute-start(bf16[192,2048]{1,0:T(8,128)(2,1)} %bitcast.13), channel_id=1, source_target_pairs={{0,8},{8,0},{16,24},{24,16},{1,9},{9,1},{17,25},{25,17},{2,10},{10... | collective-permute-start | bytes 2359304 | tf_op jit(solution)/shard_map/ppermute | solution.py:990
  186.0 122.8 %collective-permute-start.7 = (bf16[192,2048]{1,0:T(8,128)(2,1)}, bf16[192,2048]{1,0:T(8,128)(2,1)}, u32[]{:S(2)}, u32[]{:S(2)}) collective-permute-start(bf16[192,2048]{1,0:T(8,128)(2,1)} %bitcast.13), channel_id=1, source_target_pairs={{0,16},{8,24},{16,0},{24,8},{1,17},{9,25},{17,1},{25,9},{2,18},{10... | collective-permute-start | bytes 2359304 | tf_op jit(solution)/shard_map/ppermute | solution.py:990
  187.5 121.3 %collective-permute-start.8 = (bf16[192,2048]{1,0:T(8,128)(2,1)}, bf16[192,2048]{1,0:T(8,128)(2,1)}, u32[]{:S(2)}, u32[]{:S(2)}) collective-permute-start(bf16[192,2048]{1,0:T(8,128)(2,1)} %bitcast.13), channel_id=1, source_target_pairs={{0,24},{8,16},{16,8},{24,0},{1,25},{9,17},{17,9},{25,1},{2,26},{10... | collective-permute-start | bytes 2359304 | tf_op jit(solution)/shard_map/ppermute | solution.py:990
  318.2 36.3 %collective-permute-start.11 = (bf16[192,2048]{1,0:T(8,128)(2,1)S(1)}, bf16[192,2048]{1,0:T(8,128)(2,1)S(1)}, u32[]{:S(2)}, u32[]{:S(2)}) collective-permute-start(bf16[192,2048]{1,0:T(8,128)(2,1)S(1)} %bitcast.220), channel_id=1, source_target_pairs={{0,16},{8,24},{16,0},{24,8},{1,17},{9,25},{17,1},{25,9},{2,18},{10... | collective-permute-start | bytes 2359304 | tf_op jit(solution)/shard_map/ppermute | solution.py:990
  360.7 35.9 %collective-permute-start.14 = (bf16[192,2048]{1,0:T(8,128)(2,1)}, bf16[192,2048]{1,0:T(8,128)(2,1)}, u32[]{:S(2)}, u32[]{:S(2)}) collective-permute-start(bf16[192,2048]{1,0:T(8,128)(2,1)} %multiply_convert_fusion.1), channel_id=1, source_target_pairs={{0,16},{8,24},{16,0},{24,8},{1,17},{9,25},{17,1},{25,9},{2,18},{10... | collective-permute-start | bytes 2359304 | tf_op jit(solution)/shard_map/ppermute | solution.py:990
  435.4 186.2 %reduce-scatter.8.cloned.1.call-start = ((), (), s32[]{:S(2)}) async-start(), calls=%async_computation.11 | async-start | bytes 7208960 | tf_op jit(solution)/shard_map/reduce_scatter | solution.py:1135
  474.4 36.7 %collective-permute-start.18 = (bf16[192,2048]{1,0:T(8,128)(2,1)}, bf16[192,2048]{1,0:T(8,128)(2,1)}, u32[]{:S(2)}, u32[]{:S(2)}) collective-permute-start(bf16[192,2048]{1,0:T(8,128)(2,1)} %get-tuple-element.300), channel_id=1, source_target_pairs={{0,16},{8,24},{16,0},{24,8},{1,17},{9,25},{17,1},{25,9},{2,18},{10... | collective-permute-start | bytes 2359304 | tf_op jit(solution)/shard_map/ppermute | solution.py:990
  511.1 153.9 %reduce-scatter.12.cloned.1.call-start = ((), (), s32[]{:S(2)}) async-start(), calls=%async_computation.13 | async-start | bytes 2621440 | tf_op jit(solution)/shard_map/reduce_scatter | solution.py:1135
  568.8 52.8 %collective-permute-start.25 = (bf16[192,2048]{1,0:T(8,128)(2,1)}, bf16[192,2048]{1,0:T(8,128)(2,1)}, u32[]{:S(2)}, u32[]{:S(2)}) collective-permute-start(bf16[192,2048]{1,0:T(8,128)(2,1)} %get-tuple-element.298), channel_id=1, source_target_pairs={{0,8},{8,0},{16,24},{24,16},{1,9},{9,1},{17,25},{25,17},{2,10},{10... | collective-permute-start | bytes 2359304 | tf_op jit(solution)/shard_map/ppermute | solution.py:990
  569.5 52.0 %collective-permute-start.26 = (bf16[192,2048]{1,0:T(8,128)(2,1)}, bf16[192,2048]{1,0:T(8,128)(2,1)}, u32[]{:S(2)}, u32[]{:S(2)}) collective-permute-start(bf16[192,2048]{1,0:T(8,128)(2,1)} %get-tuple-element.297), channel_id=1, source_target_pairs={{0,16},{8,24},{16,0},{24,8},{1,17},{9,25},{17,1},{25,9},{2,18},{10... | collective-permute-start | bytes 2359304 | tf_op jit(solution)/shard_map/ppermute | solution.py:990
  571.0 50.5 %collective-permute-start.27 = (bf16[192,2048]{1,0:T(8,128)(2,1)}, bf16[192,2048]{1,0:T(8,128)(2,1)}, u32[]{:S(2)}, u32[]{:S(2)}) collective-permute-start(bf16[192,2048]{1,0:T(8,128)(2,1)} %get-tuple-element.296), channel_id=1, source_target_pairs={{0,24},{8,16},{16,8},{24,0},{1,25},{9,17},{17,9},{25,1},{2,26},{10... | collective-permute-start | bytes 2359304 | tf_op jit(solution)/shard_map/ppermute | solution.py:990
  572.3 48.9 %collective-permute-start.28 = (bf16[176,2048]{1,0:T(8,128)(2,1)}, bf16[176,2048]{1,0:T(8,128)(2,1)}, u32[]{:S(2)}, u32[]{:S(2)}) collective-permute-start(bf16[176,2048]{1,0:T(8,128)(2,1)} %reduce-scatter.6.cloned.1.call-done.near_ref), channel_id=1, source_target_pairs={{0,8},{8,0},{16,24},{24,16},{1,9},{9,1},{17,25},{25,17},{2,10},{10... | collective-permute-start | bytes 2162696 | tf_op jit(solution)/shard_map/ppermute | solution.py:990
  573.0 48.5 %collective-permute-start.29 = (bf16[176,2048]{1,0:T(8,128)(2,1)}, bf16[176,2048]{1,0:T(8,128)(2,1)}, u32[]{:S(2)}, u32[]{:S(2)}) collective-permute-start(bf16[176,2048]{1,0:T(8,128)(2,1)} %reduce-scatter.6.cloned.1.call-done.near_ref), channel_id=1, source_target_pairs={{0,16},{8,24},{16,0},{24,8},{1,17},{9,25},{17,1},{25,9},{2,18},{10... | collective-permute-start | bytes 2162696 | tf_op jit(solution)/shard_map/ppermute | solution.py:990
  574.5 173.0 %reduce-scatter.10.cloned.1.call-start = ((), (), s32[]{:S(2)}) async-start(), calls=%async_computation.12 | async-start | bytes 3932160 | tf_op jit(solution)/shard_map/reduce_scatter | solution.py:1135
  637.6 149.8 %reduce-scatter.14.cloned.1.call-start = ((), (), s32[]{:S(2)}) async-start(), calls=%async_computation.14 | async-start | bytes 3932160 | tf_op jit(solution)/shard_map/reduce_scatter | solution.py:1135
  669.3 37.0 %collective-permute-start.33 = (bf16[192,2048]{1,0:T(8,128)(2,1)S(1)}, bf16[192,2048]{1,0:T(8,128)(2,1)S(1)}, u32[]{:S(2)}, u32[]{:S(2)}) collective-permute-start(bf16[192,2048]{1,0:T(8,128)(2,1)S(1)} %bitcast.217), channel_id=1, source_target_pairs={{0,16},{8,24},{16,0},{24,8},{1,17},{9,25},{17,1},{25,9},{2,18},{10... | collective-permute-start | bytes 2359304 | tf_op jit(solution)/shard_map/ppermute | solution.py:990
  669.5 36.8 %collective-permute-start.34 = (bf16[192,2048]{1,0:T(8,128)(2,1)S(1)}, bf16[192,2048]{1,0:T(8,128)(2,1)S(1)}, u32[]{:S(2)}, u32[]{:S(2)}) collective-permute-start(bf16[192,2048]{1,0:T(8,128)(2,1)S(1)} %bitcast.216), channel_id=1, source_target_pairs={{0,24},{8,16},{16,8},{24,0},{1,25},{9,17},{17,9},{25,1},{2,26},{10... | collective-permute-start | bytes 2359304 | tf_op jit(solution)/shard_map/ppermute | solution.py:990
  788.4 38.9 %all-to-all-start.2 = ((bf16[4,48,4096]{2,1,0:T(8,128)(2,1)}), bf16[4,48,4096]{2,1,0:T(8,128)(2,1)}, u32[]{:S(2)}, u32[]{:S(2)}) async-start(bf16[4,48,4096]{2,1,0:T(8,128)(2,1)} %bitcast.192), calls=%async_computation.7 | async-start | bytes 3145728 | tf_op jit(solution)/shard_map/all_to_all | solution.py:977
  (107 other events, 1769.7 us)
Sparse Core Ops, SparseCore 0:
  15.5 152.8 all-gather.4
  170.7 93.1 all-gather.8
  265.5 106.4 all-gather.6
  435.5 53.3 reduce-scatter.5
  511.2 99.5 reduce-scatter.7
  612.9 44.3 reduce-scatter.11
  660.3 59.5 reduce-scatter.9
  722.9 61.3 reduce-scatter.13
